TPU v7x, 32 devices: a whole 2x2x4 slice. The times are simulated.
32 devices in a mesh: groups: 2 (over y), mp: 4 (over z), section: 2 (over x), rows: 2 (over core).
Axes of the slice: x: 2, y: 2, z: 4, core: 2. Of those that a mesh axis runs over, the one named last changes fastest.
Arguments:
- thinker_act: bfloat16 [1536, 18944], P(('groups', 'section', 'rows'), 'mp'), parts along dimension 0, may hold values from -6 to 6
- w_think: bfloat16 [18944, 3584], P('mp', ('section', 'rows')), may hold values from -0.046875 to 0.046875
- w_proj: bfloat16 [3584, 896], P('mp'), may hold values from -0.09375 to 0.09375
- talker_gain: float32 [896], replicated, may hold values from 0.25 to 1.75
- w_query: bfloat16 [896, 1536], P(None, ('section', 'rows')), may hold values from -0.1875 to 0.1875
- w_key: bfloat16 [896, 512], P(None, ('section', 'rows')), may hold values from -0.1875 to 0.1875
- w_value: bfloat16 [896, 512], P(None, ('section', 'rows')), may hold values from -0.1875 to 0.1875
- talker_slot: int32 [8, 192], P(('groups', 'section', 'rows')), parts along dimension 0, may hold values from 0 to 191, each once within a row
- kv_len: int32 [1536], P(('groups', 'mp', 'section', 'rows')), parts along dimension 0, may hold values from 1 to 256, 98304 in all
- kv_cache: bfloat16 [1536, 256, 1024], P(('groups', 'mp', 'section', 'rows')), parts along dimension 0, may hold values from -6 to 6
Outputs:
- thinker_out: bfloat16 [1536, 3584], P(('groups', 'section', 'rows'), 'mp'), parts along dimension 0
- talker_kv: bfloat16 [1536, 1024], P(('groups', 'mp', 'section', 'rows')), parts along dimension 0
- talker_ctx: float32 [1536, 1536], P(('groups', 'mp', 'section', 'rows')), parts along dimension 0
There are 2 independent parts, one for each index of `groups`. A program takes and returns all parts, laid end to end along the dimension named above; an argument that names none is the same for every part. Nothing has to cross between parts.
Inputs may be any that keep to these rules, and one draw needn't show every extreme that they name: Each row of talker_slot holds every number of 0 to 191 once.
All inputs are finite; a program needn't handle non-finite values. No bound on the sum of `kv_len` on one device may be relied on, other than what follows from the above.
Results may differ from a plain program's by a relative error of at most 0.008.
Values may be sent and summed in bfloat16 or wider, within the bound.
No kernel may reach another device: no remote copies, remote signals or barrier semaphores. Data moves between devices by JAX's collectives and lax.ppermute only.
A program may use at most 192 MiB of HBM per device.

v0:
```python
import jax
import jax.numpy as jnp
from jax import lax
from jax.sharding import PartitionSpec as P

HEAD_DIM = 128


def talker_step(talker_in, talker_gain, w_query, w_key, w_value, kv_len, kv_cache):
    owned = talker_in.shape[0]
    cached = kv_cache.shape[1]
    kv_width = w_key.shape[1]
    head_dim = HEAD_DIM
    kv_heads = kv_width // head_dim
    group = w_query.shape[1] // kv_width
    scale = lax.rsqrt(jnp.mean(talker_in * talker_in, axis=1, keepdims=True) + 1e-06)
    normed = (talker_in * scale * talker_gain).astype(jnp.bfloat16)
    query = jnp.dot(normed, w_query, preferred_element_type=jnp.float32).astype(jnp.bfloat16)
    new_key = jnp.dot(normed, w_key, preferred_element_type=jnp.float32).astype(jnp.bfloat16)
    new_value = jnp.dot(normed, w_value, preferred_element_type=jnp.float32).astype(jnp.bfloat16)
    talker_kv = jnp.concatenate([new_key, new_value], axis=1)
    qb = query.reshape(owned, kv_heads, group, head_dim)
    keys = kv_cache[:, :, :kv_width].reshape(owned, cached, kv_heads, head_dim)
    values = kv_cache[:, :, kv_width:].reshape(owned, cached, kv_heads, head_dim)
    nk = new_key.reshape(owned, kv_heads, head_dim)
    nv = new_value.reshape(owned, kv_heads, head_dim)
    inv = 1.0 / head_dim**0.5
    scores = jnp.einsum("rgjd,rpgd->rgjp", qb, keys, preferred_element_type=jnp.float32) * inv
    own = jnp.einsum("rgjd,rgd->rgj", qb, nk, preferred_element_type=jnp.float32) * inv
    valid = (jnp.arange(cached, dtype=jnp.int32)[None, :] < kv_len[:, None])[:, None, None, :]
    scores = jnp.where(valid, scores, -jnp.inf)
    top = jnp.maximum(jnp.max(scores, axis=3), own)
    expo = jnp.where(valid, jnp.exp(scores - top[..., None]), 0.0)
    own_expo = jnp.exp(own - top)
    total = jnp.sum(expo, axis=3) + own_expo
    probs = (expo / total[..., None]).astype(jnp.bfloat16)
    own_prob = (own_expo / total).astype(jnp.bfloat16)
    ctx = jnp.einsum("rgjp,rpgd->rgjd", probs, values, preferred_element_type=jnp.float32)
    ctx = ctx + own_prob.astype(jnp.float32)[..., None] * nv.astype(jnp.float32)[:, :, None, :]
    return (talker_kv, ctx.reshape(owned, w_query.shape[1]))


def shards(
    thinker_act,
    w_think,
    w_proj,
    talker_gain,
    w_query,
    w_key,
    w_value,
    talker_slot,
    kv_len,
    kv_cache,
):
    partial_sums = jnp.dot(
        thinker_act,
        lax.all_gather(w_think, ("section", "rows"), axis=1, tiled=True),
        preferred_element_type=jnp.float32,
    )
    full_query, full_key, full_value = (
        lax.all_gather(w_query, ("section", "rows"), axis=1, tiled=True),
        lax.all_gather(w_key, ("section", "rows"), axis=1, tiled=True),
        lax.all_gather(w_value, ("section", "rows"), axis=1, tiled=True),
    )
    mine = lax.psum_scatter(partial_sums, "mp", scatter_dimension=1, tiled=True)
    thinker_out = mine.astype(jnp.bfloat16)
    order = jnp.argsort(talker_slot[0], stable=True)
    sorted_out = thinker_out[order]
    talker_in = lax.psum_scatter(
        jnp.dot(sorted_out, w_proj, preferred_element_type=jnp.float32),
        "mp",
        scatter_dimension=0,
        tiled=True,
    )
    talker_kv, talker_ctx = talker_step(
        talker_in, talker_gain, full_query, full_key, full_value, kv_len, kv_cache
    )
    return (thinker_out, talker_kv, talker_ctx)


def solution(mesh):
    in_specs = (
        P(("groups", "section", "rows"), "mp"),
        P("mp", ("section", "rows")),
        P("mp", None),
        P(),
        P(None, ("section", "rows")),
        P(None, ("section", "rows")),
        P(None, ("section", "rows")),
        P(("groups", "section", "rows"), None),
        P(("groups", "mp", "section", "rows")),
        P(("groups", "mp", "section", "rows"), None, None),
    )
    out_specs = (
        P(("groups", "section", "rows"), "mp"),
        P(("groups", "mp", "section", "rows"), None),
        P(("groups", "mp", "section", "rows"), None),
    )
    return jax.shard_map(shards, mesh=mesh, in_specs=in_specs, out_specs=out_specs, check_vma=False)
```

profile of v0, /device:TPU:0, one launch (start us, length us, event | category | flops | bytes accessed | tf_op | source)
XLA Modules:
  0.0 391.6 jit_solution(2065255700790779534)
XLA Ops:
  7.2 0.7 all-gather.3.cloned.1.call-update
  8.0 210.3 %all-gather.3.cloned.1.call-done = bf16[4736,3584]{1,0:T(8,128)(2,1)} async-done(((bf16[4736,896]{1,0:T(8,128)(2,1)}), bf16[4736,3584]{1,0:T(8,128)(2,1)}) %all-gather.3.cloned.1.call-update) | async-done | bytes 33947664 | tf_op jit(solution)/shard_map/all_gather | solution.py:57
  218.3 16.0 %fusion.12 = f32[192,3584]{1,0:T(8,128)} fusion(bf16[192,4736]{1,0:T(8,128)(2,1)S(1)} %copy-done, bf16[4736,3584]{1,0:T(8,128)(2,1)} %all-gather.3.cloned.1.call-done), kind=kOutput, calls=%fused_computation.30 | convolution fusion | flops 6517948416 | bytes 38518784 | tf_op jit(solution)/shard_map/dot_general | solution.py:55
  234.4 3.2 sort.17
  237.5 51.1 %reduce-scatter.3.cloned.1.call-done = f32[192,896]{1,0:T(8,128)} async-done(((f32[192,3584]{1,0:T(8,128)}), f32[192,896]{1,0:T(8,128)}) %reduce-scatter.3.cloned.1.call-update) | async-done | bytes 688144 | tf_op jit(solution)/shard_map/reduce_scatter | solution.py:65
  288.7 1.1 convert_element_type.34
  289.8 1.0 gather_fusion
  290.9 1.4 fusion.13
  292.4 0.5 all-gather.5.cloned.1.call-update
  292.9 17.2 %fusion.10 = (bf16[48,256,512]{2,1,0:T(8,128)(2,1)}, bf16[48,256,512]{2,1,0:T(8,128)(2,1)}) fusion(bf16[48,256,1024]{2,1,0:T(8,128)(2,1)} %param.19), kind=kLoop, calls=%fused_computation.28 | loop fusion | bytes 50331648 | tf_op jit(solution)/shard_map/slice | solution.py:23
  310.1 16.7 %copy.37 = bf16[48,256,512]{1,2,0:T(8,128)(2,1)} copy(bf16[48,256,512]{2,1,0:T(8,128)(2,1)} %get-tuple-element.5) | data formatting | bytes 25165824
  326.8 16.4 %copy.38 = bf16[48,256,512]{1,2,0:T(8,128)(2,1)} copy(bf16[48,256,512]{2,1,0:T(8,128)(2,1)} %get-tuple-element.6) | data formatting | bytes 25165824
  343.3 9.1 %all_gather.13 = bf16[896,512]{1,0:T(8,128)(2,1)S(1)} all-gather(bf16[896,128]{1,0:T(8,128)(2,1)S(1)} %copy-done.4), channel_id=1, replica_groups=mesh['groups'=2,'mp'=4,'section'=2,'rows'=2] {'section','rows'}, dimensions={1}, use_global_device_ids=true | all-gather | bytes 1146880 | tf_op jit(solution)/shard_map/all_gather | solution.py:62
  352.4 9.6 %all_gather.14 = bf16[896,512]{1,0:T(8,128)(2,1)S(1)} all-gather(bf16[896,128]{1,0:T(8,128)(2,1)S(1)} %copy-done.5), channel_id=1, replica_groups=mesh['groups'=2,'mp'=4,'section'=2,'rows'=2] {'section','rows'}, dimensions={1}, use_global_device_ids=true | all-gather | bytes 1146880 | tf_op jit(solution)/shard_map/all_gather | solution.py:63
  362.1 1.0 multiply_reduce_fusion
  363.1 1.0 multiply_convert_fusion
  364.4 0.3 convolution_convert_fusion.1
  364.8 0.6 pad_maximum_fusion
  365.4 2.4 convolution_convert_fusion
  367.9 0.3 fusion.14
  368.3 6.6 %fusion.11 = (f32[48,4,3]{2,1,0:T(4,128)S(1)}, f32[48,4,3,256]{3,2,1,0:T(4,128)S(1)}) fusion(bf16[48,4,3,128]{3,2,1,0:T(4,128)(2,1)S(1)} %reshape.58, bf16[48,256,4,128]{1,3,2,0:T(8,128)(2,1)} %bitcast.34, pred[48,256]{1,0:T(8,128)(4,1)S(1)} %iota_compare_fusion), kind=kOutput, calls=%fused_computation.29 | convolution fusion | flops 38190528 | bytes 13334784 | tf_op jit(solution)/shard_map/rgjd,rpgd->rgjp/dot_general | solution.py:28
  375.2 0.6 fusion.1
  376.2 8.0 %convolution_add_fusion = f32[48,4,3,128]{3,2,1,0:T(4,128)S(1)} fusion(bf16[48,256,4,128]{1,3,2,0:T(8,128)(2,1)} %bitcast.35, f32[48,4,3,256]{3,2,1,0:T(4,128)S(1)} %get-tuple-element.10, f32[48,4,3]{2,1,0:T(4,128)S(1)} %copy.29, f32[48,4,3]{2,1,0:T(4,128)S(1)} %copy.27, pred[48,256]{1,0:T(8,128)(4,1)S(1)} %iota_compare_fusion, ...), kind=kOutput, calls=%fused_computation.4 | convolution fusion | flops 38486016 | bytes 13585152 | tf_op jit(solution)/shard_map/rgjp,rpgd->rgjd/dot_general | solution.py:38
  384.2 0.9 reshape.62
  (43 shorter events, 1.5 us)
Async XLA Ops:
  7.2 211.1 %copy-start = (bf16[192,4736]{1,0:T(8,128)(2,1)S(1)}, bf16[192,4736]{1,0:T(8,128)(2,1)}, u32[]{:S(2)}) copy-start(bf16[192,4736]{1,0:T(8,128)(2,1)} %param.10) | copy-start | bytes 5455876
  7.2 211.1 %all-gather.3.cloned.1.call-start = ((), (), s32[]{:S(2)}) async-start(), calls=%async_computation.2 | async-start | bytes 42434560 | tf_op jit(solution)/shard_map/all_gather | solution.py:57
  7.9 226.4 %copy-start.7 = (s32[1,192]{1,0:T(1,128)S(1)}, s32[1,192]{1,0:T(1,128)}, u32[]{:S(2)}) copy-start(s32[1,192]{1,0:T(1,128)} %param.17) | copy-start | bytes 2308
  7.9 282.9 %copy-start.3 = (bf16[896,896]{1,0:T(8,128)(2,1)S(1)}, bf16[896,896]{1,0:T(8,128)(2,1)}, u32[]{:S(2)}) copy-start(bf16[896,896]{1,0:T(8,128)(2,1)} %param.12) | copy-start | bytes 4816900
  7.9 280.7 %reduce-scatter.3.cloned.1.call-start = ((), (), s32[]{:S(2)}) async-start(), calls=%async_computation.3 | async-start | bytes 3440640 | tf_op jit(solution)/shard_map/reduce_scatter | solution.py:65
  234.3 127.8 %reduce-scatter.5.cloned.1.call-start = ((), (), s32[]{:S(2)}) async-start(), calls=%async_computation.4 | async-start | bytes 860160 | tf_op jit(solution)/shard_map/reduce_scatter | solution.py:69
  289.8 20.3 %copy-start.2 = (bf16[192,896]{1,0:T(8,128)(2,1)}, bf16[192,896]{1,0:T(8,128)(2,1)S(1)}, u32[]{:S(2)}) copy-start(bf16[192,896]{1,0:T(8,128)(2,1)S(1)} %convert_element_type.34) | copy-start | bytes 1032196
  292.3 73.1 %all-gather.5.cloned.1.call-start = ((), (), s32[]{:S(2)}) async-start(), calls=%async_computation.5 | async-start | bytes 3440640 | tf_op jit(solution)/shard_map/all_gather | solution.py:61
  326.8 16.5 %copy-start.8 = (s32[48]{0:T(128)S(1)}, s32[48]{0:T(128)}, u32[]{:S(2)}) copy-start(s32[48]{0:T(128)} %param.18) | copy-start | bytes 580
  326.8 16.5 %copy-start.4 = (bf16[896,128]{1,0:T(8,128)(2,1)S(1)}, bf16[896,128]{1,0:T(8,128)(2,1)}, u32[]{:S(2)}) copy-start(bf16[896,128]{1,0:T(8,128)(2,1)} %param.15) | copy-start | bytes 688132
  326.8 25.7 %copy-start.5 = (bf16[896,128]{1,0:T(8,128)(2,1)S(1)}, bf16[896,128]{1,0:T(8,128)(2,1)}, u32[]{:S(2)}) copy-start(bf16[896,128]{1,0:T(8,128)(2,1)} %param.16) | copy-start | bytes 688132
  326.8 36.3 %copy-start.6 = (f32[896]{0:T(1024)S(1)}, f32[896]{0:T(1024)}, u32[]{:S(2)}) copy-start(f32[896]{0:T(1024)} %param.13) | copy-start | bytes 10756
  368.3 16.7 %copy-start.1 = (bf16[192,4736]{1,0:T(8,128)(2,1)S(1)}, bf16[192,4736]{1,0:T(8,128)(2,1)}, u32[]{:S(2)}) copy-start(bf16[192,4736]{1,0:T(8,128)(2,1)} %param.10) | copy-start | bytes 5455876
Sparse Core Ops, SparseCore 0:
  9.6 208.6 all-gather.2
  234.4 54.2 reduce-scatter.2
  292.4 22.2 reduce-scatter.4
  316.2 25.1 all-gather.4
where the time goes:
time: 393 us; the launch traced here: 392 us
  waiting for transfers between devices  263 us (67%)
  local copies, waits for them, and re-layouts  53.1 us (14%)
  matrix products  35.2 us (9%)
  blocking collectives  18.7 us (5%)
  between operations  14 us (4%)
  other arithmetic  7.77 us (2%)
    all_gather x1, waiting for transfers between devices, shards(): lax.all_gather(w_think, ('section', 'rows'), axis=1, tiled=True)  210 us
    reduce_scatter x1, waiting for transfers between devices, shards(): mine = lax.psum_scatter(partial_sums, 'mp', scatter_dimension=1, tiled=True)  51.1 us
    unnamed x20, local copies, waits for them, and re-layouts  33.2 us
    slice x1, local copies, waits for them, and re-layouts, talker_step(): keys = kv_cache[:, :, :kv_width].reshape(owned, cached, kv_heads, head_dim)  17.2 us
    dot_general x1, matrix products, shards(): jnp.dot(thinker_act, lax.all_gather(w_think, ('section', 'rows'), axis=1,...  16 us
    all_gather x1, blocking collectives, shards(): lax.all_gather(w_value, ('section', 'rows'), axis=1, tiled=True)  9.63 us
    all_gather x1, blocking collectives, shards(): lax.all_gather(w_key, ('section', 'rows'), axis=1, tiled=True)  9.12 us
    dot_general x1, matrix products, talker_step(): jnp.einsum('rgjp,rpgd->rgjd', probs, values, preferred_element_type=jnp.f...  7.99 us
  transfers between devices with their start and end apart: 4, of which 2 were waited for; matrix products, arithmetic and copies ran while one was open for 15% of the time, Pallas kernels for 0%

commit v1 on v0

--- a/solution.py
+++ b/solution.py
@@ -1,9 +1,106 @@
+import functools
+
 import jax
 import jax.numpy as jnp
 from jax import lax
+from jax.experimental import pallas as pl
+from jax.experimental.pallas import tpu as pltpu
 from jax.sharding import PartitionSpec as P
 
 HEAD_DIM = 128
+ROW_STEP = 8
+
+
+def attention_kernel(first_row, kv_heads, group, len_ref, q_ref, nkv_ref, kv_ref, out_ref):
+    rows, cached, _ = kv_ref.shape
+    width = kv_heads * HEAD_DIM
+    lanes = 16
+    step = pl.program_id(0)
+    inv = 1.0 / HEAD_DIM**0.5
+    which = lax.broadcasted_iota(jnp.int32, (lanes, width), 0)
+    head = lax.broadcasted_iota(jnp.int32, (lanes, width), 1) // HEAD_DIM
+    picks = [(which == j * kv_heads + head).astype(jnp.float32) for j in range(group)]
+    position = lax.broadcasted_iota(jnp.int32, (lanes, cached), 1)
+    for r in range(rows):
+        q = q_ref[r : r + 1, :].astype(jnp.float32)
+        spread = jnp.zeros((lanes, width), jnp.float32)
+        for j in range(group):
+            part = jnp.concatenate(
+                [
+                    q[:, (g * group + j) * HEAD_DIM : (g * group + j + 1) * HEAD_DIM]
+                    for g in range(kv_heads)
+                ],
+                axis=1,
+            )
+            spread = spread + picks[j] * part
+        nk = nkv_ref[r : r + 1, :width].astype(jnp.float32)
+        nv = nkv_ref[r : r + 1, width:].astype(jnp.float32)
+        own = jnp.sum(spread * nk, axis=1, keepdims=True) * inv
+        scores = (
+            lax.dot_general(
+                spread.astype(jnp.bfloat16),
+                kv_ref[r, :, :width],
+                (((1,), (1,)), ((), ())),
+                preferred_element_type=jnp.float32,
+            )
+            * inv
+        )
+        valid = position < len_ref[first_row + step * rows + r]
+        scores = jnp.where(valid, scores, -jnp.inf)
+        top = jnp.maximum(jnp.max(scores, axis=1, keepdims=True), own)
+        expo = jnp.where(valid, jnp.exp(scores - top), 0.0)
+        own_expo = jnp.exp(own - top)
+        total = jnp.sum(expo, axis=1, keepdims=True) + own_expo
+        probs = (expo / total).astype(jnp.bfloat16)
+        own_prob = (own_expo / total).astype(jnp.bfloat16).astype(jnp.float32)
+        ctx = lax.dot_general(
+            probs,
+            kv_ref[r, :, width:],
+            (((1,), (0,)), ((), ())),
+            preferred_element_type=jnp.float32,
+        )
+        ctx = ctx + own_prob * nv
+        for g in range(kv_heads):
+            for j in range(group):
+                h = g * group + j
+                i = j * kv_heads + g
+                out_ref[r : r + 1, h * HEAD_DIM : (h + 1) * HEAD_DIM] = ctx[
+                    i : i + 1, g * HEAD_DIM : (g + 1) * HEAD_DIM
+                ]
+
+
+def attention(first_row, query, new_kv, kv_len, kv_cache):
+    rows, q_width = query.shape
+    _, cached, kv_width = kv_cache.shape
+    kv_heads = kv_width // 2 // HEAD_DIM
+    group = q_width // (kv_width // 2)
+    step = ROW_STEP
+    offset = first_row // step
+    return pl.pallas_call(
+        functools.partial(attention_kernel, first_row, kv_heads, group),
+        out_shape=jax.ShapeDtypeStruct((rows, q_width), jnp.float32),
+        grid_spec=pltpu.PrefetchScalarGridSpec(
+            num_scalar_prefetch=1,
+            grid=(rows // step,),
+            in_specs=[
+                pl.BlockSpec((step, q_width), lambda i, _: (i, 0)),
+                pl.BlockSpec((step, kv_width), lambda i, _: (i, 0)),
+                pl.BlockSpec((step, cached, kv_width), lambda i, _: (i + offset, 0, 0)),
+            ],
+            out_specs=pl.BlockSpec((step, q_width), lambda i, _: (i, 0)),
+        ),
+        cost_estimate=pl.CostEstimate(
+            flops=4 * rows * cached * q_width,
+            bytes_accessed=2 * rows * cached * kv_width,
+            transcendentals=rows * cached * q_width // HEAD_DIM,
+        ),
+        compiler_params=pltpu.CompilerParams(vmem_limit_bytes=32 * 1024 * 1024),
+    )(kv_len, query, new_kv, kv_cache)
+
+
+def rms_norm(talker_in, talker_gain):
+    scale = lax.rsqrt(jnp.mean(talker_in * talker_in, axis=1, keepdims=True) + 1e-06)
+    return (talker_in * scale * talker_gain).astype(jnp.bfloat16)
 
 
 def talker_step(talker_in, talker_gain, w_query, w_key, w_value, kv_len, kv_cache):
@@ -13,8 +110,7 @@
     head_dim = HEAD_DIM
     kv_heads = kv_width // head_dim
     group = w_query.shape[1] // kv_width
-    scale = lax.rsqrt(jnp.mean(talker_in * talker_in, axis=1, keepdims=True) + 1e-06)
-    normed = (talker_in * scale * talker_gain).astype(jnp.bfloat16)
+    normed = rms_norm(talker_in, talker_gain)
     query = jnp.dot(normed, w_query, preferred_element_type=jnp.float32).astype(jnp.bfloat16)
     new_key = jnp.dot(normed, w_key, preferred_element_type=jnp.float32).astype(jnp.bfloat16)
     new_value = jnp.dot(normed, w_value, preferred_element_type=jnp.float32).astype(jnp.bfloat16)
@@ -40,7 +136,7 @@
     return (talker_kv, ctx.reshape(owned, w_query.shape[1]))
 
 
-def shards(
+def any_mesh(
     thinker_act,
     w_think,
     w_proj,
@@ -78,6 +174,133 @@
     return (thinker_out, talker_kv, talker_ctx)
 
 
+PLANE = ("section", "rows")
+GROUP = ("mp", "section", "rows")
+
+
+def over_core(x):
+    return lax.ppermute(x, "rows", [(0, 1), (1, 0)])
+
+
+def over_section(x):
+    return lax.ppermute(x, "section", [(0, 1), (1, 0)])
+
+
+def gathered_qkv(w_query, w_key, w_value, after):
+    mine = jnp.concatenate([w_query, w_key, w_value], axis=1)
+    half = mine.shape[0] // 2
+    g = lax.axis_index("groups")
+    piece = lax.dynamic_slice_in_dim(mine, g * half, half, axis=0)
+    piece, _ = lax.optimization_barrier((piece, after))
+    crossed = over_section(piece)
+    other = lax.ppermute(crossed, "groups", [(0, 1), (1, 0)])
+    pair = jnp.stack([crossed, other])
+    across = pair[jnp.arange(2) ^ g].reshape(mine.shape)
+    four = [mine, over_core(mine), across, over_core(across)]
+    c = lax.axis_index(PLANE)
+    return jnp.stack(four)[jnp.arange(4) ^ c]
+
+
+def four_planes(
+    thinker_act,
+    w_think,
+    w_proj,
+    talker_gain,
+    w_query,
+    w_key,
+    w_value,
+    talker_slot,
+    kv_len,
+    kv_cache,
+):
+    planes = 4
+    owned = kv_cache.shape[0]
+    m = lax.axis_index("mp")
+    c = lax.axis_index(PLANE)
+    columns = w_think.shape[1]
+    slots = talker_slot[0]
+    chunks = [(0, 32), (32, 16)]
+
+    sent = []
+    for first, n in chunks:
+        plane = (m + jnp.arange(planes, dtype=jnp.int32)) % planes
+        want = (plane[:, None] * owned + first + jnp.arange(n, dtype=jnp.int32)[None, :]).reshape(-1)
+        pick = (want[:, None] == slots[None, :]).astype(jnp.bfloat16)
+        rows = jnp.dot(pick, thinker_act, preferred_element_type=jnp.float32).astype(jnp.bfloat16)
+        sent.append(rows)
+
+    crossed = []
+    for rows in sent:
+        if crossed:
+            rows, _ = lax.optimization_barrier((rows, crossed[-1]))
+        crossed.append(over_section(rows))
+    w_qkv = gathered_qkv(w_query, w_key, w_value, crossed[-1])
+
+    returned, kvs, ctxs = [], [], []
+    for (first, n), own_rows, across in zip(chunks, sent, crossed):
+        blocks = []
+        for near, far in ((own_rows, over_core(own_rows)), (across, over_core(across))):
+            sums = [
+                jnp.dot(x, w_think, preferred_element_type=jnp.float32).reshape(planes, n, columns)
+                for x in (near, far)
+            ]
+            total = jnp.stack([s[0] for s in sums])
+            for d in range(1, planes):
+                out = jnp.stack([s[d] for s in sums]).astype(jnp.bfloat16)
+                got = lax.ppermute(out, "mp", [(i, (i + d) % planes) for i in range(planes)])
+                total = total + got.astype(jnp.float32)
+            blocks.append(total.astype(jnp.bfloat16))
+        mine = jnp.concatenate(blocks, axis=0)
+        home = []
+        for k in range(planes):
+            out = lax.dynamic_index_in_dim(mine, m ^ k, axis=0, keepdims=False)
+            pairs = [
+                (p * 4 + b, b * 4 + (b ^ p ^ k)) for p in range(planes) for b in range(4)
+            ]
+            home.append(lax.ppermute(out, GROUP, pairs))
+        home = jnp.stack(home)
+        returned.append(home)
+        projected = jnp.dot(
+            home.reshape(planes * n, columns), w_proj, preferred_element_type=jnp.float32
+        ).astype(jnp.bfloat16)
+        projected = projected.reshape(planes, n, -1)
+        talker_in = 0.0
+        for k in range(planes):
+            pairs = [
+                (p * 4 + b, (p ^ b ^ k) * 4 + b) for p in range(planes) for b in range(4)
+            ]
+            talker_in = talker_in + lax.ppermute(projected[k], GROUP, pairs).astype(jnp.float32)
+        normed = rms_norm(talker_in, talker_gain)
+        qkv = jnp.einsum("rk,bkn->brn", normed, w_qkv, preferred_element_type=jnp.float32)
+        qkv = qkv.astype(jnp.bfloat16)
+        q_cols, k_cols = w_query.shape[1], w_key.shape[1]
+
+        def across_blocks(x):
+            return jnp.moveaxis(x, 0, 1).reshape(n, -1)
+
+        query = across_blocks(qkv[:, :, :q_cols])
+        new_kv = jnp.concatenate(
+            [
+                across_blocks(qkv[:, :, q_cols : q_cols + k_cols]),
+                across_blocks(qkv[:, :, q_cols + k_cols :]),
+            ],
+            axis=1,
+        )
+        kvs.append(new_kv)
+        ctxs.append(attention(first, query, new_kv, kv_len, kv_cache))
+
+    where_to = []
+    for first, n in chunks:
+        plane = m ^ c ^ jnp.arange(planes, dtype=jnp.int32)
+        where_to.append(
+            (plane[:, None] * owned + first + jnp.arange(n, dtype=jnp.int32)[None, :]).reshape(-1)
+        )
+    pick = (slots[:, None] == jnp.concatenate(where_to)[None, :]).astype(jnp.bfloat16)
+    home = jnp.concatenate([h.reshape(-1, columns) for h in returned], axis=0)
+    thinker_out = jnp.dot(pick, home, preferred_element_type=jnp.float32).astype(jnp.bfloat16)
+    return (thinker_out, jnp.concatenate(kvs, axis=0), jnp.concatenate(ctxs, axis=0))
+
+
 def solution(mesh):
     in_specs = (
         P(("groups", "section", "rows"), "mp"),
@@ -96,4 +319,6 @@
         P(("groups", "mp", "section", "rows"), None),
         P(("groups", "mp", "section", "rows"), None),
     )
+    sizes = tuple(mesh.shape[a] for a in ("groups", "section", "rows", "mp"))
+    shards = four_planes if sizes == (2, 2, 2, 4) else any_mesh
     return jax.shard_map(shards, mesh=mesh, in_specs=in_specs, out_specs=out_specs, check_vma=False)

time: 393 us -> 190 us (0.48)
  waiting for transfers between devices: 263 us -> 26.6 us
  starting transfers between devices: 0.16 us -> 75.9 us
  local copies, waits for them, and re-layouts: 53.1 us -> 16.3 us
  Pallas kernels: 0 us -> 28.2 us
  blocking collectives: 18.7 us -> 0 us
  between operations: 14 us -> 1.56 us
  matrix products: 35.2 us -> 30.9 us
    all_gather x2 -> x0, waiting for transfers between devices: 210 us -> none  [the longest x1 210 us: shards(): lax.all_gather(w_think, ('section', 'rows'), axis=1, tiled=True)]
    ppermute x0 -> x38, starting transfers between devices: none -> 75.9 us  [the longest x12 21.8 us: four_planes(): lax.ppermute(out, 'mp', [(i, (i + d) % planes) for i in range(planes)])]
    reduce_scatter x2 -> x0, waiting for transfers between devices: 51.1 us -> none  [the longest x1 51.1 us: shards(): mine = lax.psum_scatter(partial_sums, 'mp', scatter_dimension=1, tiled=True)]
    unnamed x20 -> x48, local copies, waits for them, and re-layouts: 33.2 us -> 4.07 us
    pallas_call x0 -> x2, Pallas kernels: none -> 28.2 us  [attention(): pl.pallas_call(functools.partial(attention_kernel, first_row, kv_heads, g...]
    ppermute x0 -> x38, waiting for transfers between devices: none -> 26.6 us  [the longest x12 15.7 us: four_planes(): lax.ppermute(out, 'mp', [(i, (i + d) % planes) for i in range(planes)])]
    all_gather x2 -> x0, blocking collectives: 18.7 us -> none  [the longest x1 9.63 us: shards(): lax.all_gather(w_value, ('section', 'rows'), axis=1, tiled=True)]
    slice x1 -> x18, local copies, waits for them, and re-layouts: 17.2 us -> 1.83 us  [the longest x8 1.74 us: four_planes(): out = jnp.stack([s[d] for s in sums]).astype(jnp.bfloat16)]
  transfers between devices with their start and end apart: 4 -> 38, of which waited for: 2 -> 9; matrix products, arithmetic and copies ran while one was open for 15% -> 20% of each run, Pallas kernels for 0% -> 0%
where the time goes in v1:
time: 190 us; the launch traced here: 189 us
  starting transfers between devices  75.9 us (40%)
  matrix products  30.9 us (16%)
  Pallas kernels  28.2 us (15%)
  waiting for transfers between devices  26.6 us (14%)
  local copies, waits for them, and re-layouts  16.3 us (9%)
  other arithmetic  9.04 us (5%)
    pallas_call x2, Pallas kernels, attention(): pl.pallas_call(functools.partial(attention_kernel, first_row, kv_heads, g...  28.2 us
    dot_general x8, matrix products, four_planes(): jnp.dot(x, w_think, preferred_element_type=jnp.float32)  22.4 us
    ppermute x12, starting transfers between devices, four_planes(): lax.ppermute(out, 'mp', [(i, (i + d) % planes) for i in range(planes)])  21.8 us
    ppermute x8, starting transfers between devices, four_planes(): lax.ppermute(projected[k], GROUP, pairs).astype(jnp.float32)  21.6 us
    ppermute x8, starting transfers between devices, four_planes(): home.append(lax.ppermute(out, GROUP, pairs))  19.9 us
    ppermute x12, waiting for transfers between devices, four_planes(): lax.ppermute(out, 'mp', [(i, (i + d) % planes) for i in range(planes)])  15.7 us
    ppermute x3, waiting for transfers between devices, over_section(): return lax.ppermute(x, 'section', [(0, 1), (1, 0)])  8.86 us
    ppermute x6, starting transfers between devices, over_core(): return lax.ppermute(x, 'rows', [(0, 1), (1, 0)])  5.83 us
  transfers between devices with their start and end apart: 38, of which 9 were waited for; matrix products, arithmetic and copies ran while one was open for 20% of the time, Pallas kernels for 0%

profile of v1, /device:TPU:0, one launch (start us, length us, event | category | flops | bytes accessed | tf_op | source)
XLA Modules:
  0.0 188.6 jit_solution(13017130474630169183)
XLA Ops:
  3.3 3.0 %collective-permute-start.4 = (bf16[128,4736]{1,0:T(8,128)(2,1)S(1)}, bf16[128,4736]{1,0:T(8,128)(2,1)}, u32[]{:S(2)}, u32[]{:S(2)}) collective-permute-start(bf16[128,4736]{1,0:T(8,128)(2,1)S(1)} %convolution_convert_fusion), channel_id=1, source_target_pairs={{0,2},{2,0},{1,3},{3,1},{4,6},{6,4},{5,7},{7,5},{8,10},{10,8},{9,1... | collective-permute-start | bytes 3637256 | tf_op jit(solution)/shard_map/ppermute | solution.py:186
  8.4 5.3 %fusion.58 = (bf16[64,896]{1,0:T(8,128)(2,1)S(1)}, f32[64,896]{1,0:T(8,128)S(1)}) fusion(bf16[64,4736]{1,0:T(8,128)(2,1)} %convolution_convert_fusion.1, bf16[4736,896]{1,0:T(8,128)(2,1)} %param.11), kind=kOutput, calls=%fused_computation.172 | convolution fusion | flops 543219712 | bytes 9437184 | tf_op jit(solution)/shard_map/dot_general | solution.py:244
  23.5 5.0 %fusion.57 = (bf16[64,896]{1,0:T(8,128)(2,1)S(1)}, f32[64,896]{1,0:T(8,128)S(1)}) fusion(bf16[64,4736]{1,0:T(8,128)(2,1)S(1)} %collective-permute-done.13, bf16[4736,896]{1,0:T(8,128)(2,1)} %param.11), kind=kOutput, calls=%fused_computation.171 | convolution fusion | flops 543219712 | bytes 9437184 | tf_op jit(solution)/shard_map/dot_general | solution.py:244
  28.6 3.7 %collective-permute-start.16 = (bf16[2,16,896]{2,1,0:T(8,128)(2,1)S(1)}, bf16[2,16,896]{2,1,0:T(8,128)(2,1)S(1)}, u32[]{:S(2)}, u32[]{:S(2)}) collective-permute-start(bf16[2,16,896]{2,1,0:T(8,128)(2,1)S(1)} %pad_maximum_fusion.14), channel_id=1, source_target_pairs={{0,12},{4,0},{8,4},{12,8},{1,13},{5,1},{9,5},{13,9},{2,14},{6,2},{... | collective-permute-start | bytes 172040 | tf_op jit(solution)/shard_map/ppermute | solution.py:250
  34.6 3.0 %collective-permute-done.15 = bf16[2,16,896]{2,1,0:T(8,128)(2,1)S(1)} collective-permute-done((bf16[2,16,896]{2,1,0:T(8,128)(2,1)S(1)}, bf16[2,16,896]{2,1,0:T(8,128)(2,1)S(1)}, u32[]{:S(2)}, u32[]{:S(2)}) %collective-permute-start.15) | collective-permute-done | bytes 57376 | tf_op jit(solution)/shard_map/ppermute | solution.py:250
  39.1 2.8 %fusion.61 = (bf16[128,896]{1,0:T(8,128)(2,1)S(1)}, f32[128,896]{1,0:T(8,128)S(1)}) fusion(bf16[128,4736]{1,0:T(8,128)(2,1)} %collective-permute-done, bf16[4736,896]{1,0:T(8,128)(2,1)S(1)} %bitcast.169), kind=kOutput, calls=%fused_computation.175 | convolution fusion | flops 1086439424 | bytes 10387456 | tf_op jit(solution)/shard_map/dot_general | solution.py:244
  45.7 2.8 %fusion.64 = (bf16[128,896]{1,0:T(8,128)(2,1)S(1)}, f32[128,896]{1,0:T(8,128)S(1)}) fusion(bf16[128,4736]{1,0:T(8,128)(2,1)} %collective-permute-done.4, bf16[4736,896]{1,0:T(8,128)(2,1)S(1)} %bitcast.169), kind=kOutput, calls=%fused_computation.178 | convolution fusion | flops 1086439424 | bytes 10387456 | tf_op jit(solution)/shard_map/dot_general | solution.py:244
  48.6 4.9 %collective-permute-done.2 = bf16[2,32,896]{2,1,0:T(8,128)(2,1)S(1)} collective-permute-done((bf16[2,32,896]{2,1,0:T(8,128)(2,1)S(1)}, bf16[2,32,896]{2,1,0:T(8,128)(2,1)S(1)}, u32[]{:S(2)}, u32[]{:S(2)}) %collective-permute-start.2) | collective-permute-done | bytes 114720 | tf_op jit(solution)/shard_map/ppermute | solution.py:250
  56.6 8.9 %collective-permute-done.27 = bf16[448,640]{1,0:T(8,128)(2,1)S(1)} collective-permute-done((bf16[448,640]{1,0:T(8,128)(2,1)S(1)}, bf16[448,640]{1,0:T(8,128)(2,1)S(1)}, u32[]{:S(2)}, u32[]{:S(2)}) %collective-permute-start.27) | collective-permute-done | bytes 573472 | tf_op jit(solution)/shard_map/ppermute | solution.py:186
  80.8 3.4 %collective-permute-start.24 = (bf16[16,896]{1,0:T(8,128)(2,1)S(1)}, bf16[16,896]{1,0:T(8,128)(2,1)S(1)}, u32[]{:S(2)}, u32[]{:S(2)}) collective-permute-start(bf16[16,896]{1,0:T(8,128)(2,1)S(1)} %get-tuple-element.35), channel_id=1, source_target_pairs={{0,2},{1,7},{2,8},{3,13},{4,3},{5,6},{6,9},{7,12},{8,0},{9,5},{10,... | collective-permute-start | bytes 86024 | tf_op jit(solution)/shard_map/ppermute | solution.py:260
  86.9 6.4 %collective-permute-start.8 = (bf16[2,32,896]{2,1,0:T(8,128)(2,1)S(1)}, bf16[2,32,896]{2,1,0:T(8,128)(2,1)S(1)}, u32[]{:S(2)}, u32[]{:S(2)}) collective-permute-start(bf16[2,32,896]{2,1,0:T(8,128)(2,1)S(1)} %pad_maximum_fusion.9), channel_id=1, source_target_pairs={{0,12},{4,0},{8,4},{12,8},{1,13},{5,1},{9,5},{13,9},{2,14},{6,2},{... | collective-permute-start | bytes 344072 | tf_op jit(solution)/shard_map/ppermute | solution.py:250
  94.3 5.1 %collective-permute-start.37 = (bf16[16,896]{1,0:T(8,128)(2,1)S(1)}, bf16[16,896]{1,0:T(8,128)(2,1)S(1)}, u32[]{:S(2)}, u32[]{:S(2)}) collective-permute-start(bf16[16,896]{1,0:T(8,128)(2,1)S(1)} %get-tuple-element.30), channel_id=1, source_target_pairs={{0,12},{1,9},{2,6},{3,3},{4,8},{5,13},{6,2},{7,7},{8,4},{9,1},{10,... | collective-permute-start | bytes 86024 | tf_op jit(solution)/shard_map/ppermute | solution.py:272
  99.5 3.0 %collective-permute-start.36 = (bf16[16,896]{1,0:T(8,128)(2,1)S(1)}, bf16[16,896]{1,0:T(8,128)(2,1)S(1)}, u32[]{:S(2)}, u32[]{:S(2)}) collective-permute-start(bf16[16,896]{1,0:T(8,128)(2,1)S(1)} %get-tuple-element.31), channel_id=1, source_target_pairs={{0,8},{1,13},{2,2},{3,7},{4,12},{5,9},{6,6},{7,3},{8,0},{9,5},{10,... | collective-permute-start | bytes 86024 | tf_op jit(solution)/shard_map/ppermute | solution.py:272
  102.5 3.4 %collective-permute-done.7 = bf16[2,32,896]{2,1,0:T(8,128)(2,1)S(1)} collective-permute-done((bf16[2,32,896]{2,1,0:T(8,128)(2,1)S(1)}, bf16[2,32,896]{2,1,0:T(8,128)(2,1)S(1)}, u32[]{:S(2)}, u32[]{:S(2)}) %collective-permute-start.7) | collective-permute-done | bytes 114720 | tf_op jit(solution)/shard_map/ppermute | solution.py:250
  108.7 5.1 %collective-permute-start.12 = (bf16[32,896]{1,0:T(8,128)(2,1)S(1)}, bf16[32,896]{1,0:T(8,128)(2,1)S(1)}, u32[]{:S(2)}, u32[]{:S(2)}) collective-permute-start(bf16[32,896]{1,0:T(8,128)(2,1)S(1)} %get-tuple-element.14), channel_id=1, source_target_pairs={{0,3},{1,6},{2,9},{3,12},{4,2},{5,7},{6,8},{7,13},{8,1},{9,4},{10,... | collective-permute-start | bytes 172040 | tf_op jit(solution)/shard_map/ppermute | solution.py:260
  115.8 4.4 %collective-permute-start.10 = (bf16[32,896]{1,0:T(8,128)(2,1)S(1)}, bf16[32,896]{1,0:T(8,128)(2,1)S(1)}, u32[]{:S(2)}, u32[]{:S(2)}) collective-permute-start(bf16[32,896]{1,0:T(8,128)(2,1)S(1)} %get-tuple-element.12), channel_id=1, source_target_pairs={{0,1},{1,4},{2,11},{3,14},{4,0},{5,5},{6,10},{7,15},{8,3},{9,6},{1... | collective-permute-start | bytes 172040 | tf_op jit(solution)/shard_map/ppermute | solution.py:260
  123.5 3.0 %gather_fusion = bf16[2,448,640]{2,1,0:T(8,128)(2,1)} fusion(bf16[2,448,640]{2,1,0:T(8,128)(2,1)} %pad_maximum_fusion.1, s32[1024]{0:T(1024)S(1)} %pad_clamp_fusion.1), kind=kCustom, calls=%fused_computation | custom fusion | bytes 2293768 | tf_op jit(solution)/shard_map/gather | solution.py:198
  126.5 3.9 %collective-permute-start.29 = (bf16[896,640]{1,0:T(8,128)(2,1)}, bf16[896,640]{1,0:T(8,128)(2,1)S(1)}, u32[]{:S(2)}, u32[]{:S(2)}) collective-permute-start(bf16[896,640]{1,0:T(8,128)(2,1)} %bitcast.171), channel_id=1, source_target_pairs={{0,1},{1,0},{2,3},{3,2},{4,5},{5,4},{6,7},{7,6},{8,9},{9,8},{10,11... | collective-permute-start | bytes 3440648 | tf_op jit(solution)/shard_map/ppermute | solution.py:182
  130.9 5.9 %collective-permute-start.33 = (bf16[32,896]{1,0:T(8,128)(2,1)S(1)}, bf16[32,896]{1,0:T(8,128)(2,1)S(1)}, u32[]{:S(2)}, u32[]{:S(2)}) collective-permute-start(bf16[32,896]{1,0:T(8,128)(2,1)S(1)} %get-tuple-element.8), channel_id=1, source_target_pairs={{0,12},{1,9},{2,6},{3,3},{4,8},{5,13},{6,2},{7,7},{8,4},{9,1},{10,... | collective-permute-start | bytes 172040 | tf_op jit(solution)/shard_map/ppermute | solution.py:272
  145.1 3.5 %pad_maximum_fusion = bf16[4,896,640]{2,1,0:T(8,128)(2,1)} fusion(bf16[1,896,640]{2,1,0:T(8,128)(2,1)S(1)} %bitcast.173, bf16[1,896,640]{2,1,0:T(8,128)(2,1)S(1)} %bitcast.172, bf16[1,896,640]{2,1,0:T(8,128)(2,1)} %bitcast.52, bf16[1,896,640]{2,1,0:T(8,128)(2,1)S(1)} %bitcast.170), kind=kLoop, calls=%fused_computation.4 | loop fusion | flops 6881280 | bytes 9175040 | tf_op jit(solution)/shard_map/stack | solution.py:201
  148.7 5.6 %gather_fusion.1 = bf16[4,896,640]{2,1,0:T(8,128)(2,1)} fusion(bf16[4,896,640]{2,1,0:T(8,128)(2,1)} %pad_maximum_fusion, s32[1024]{0:T(1024)S(1)} %pad_clamp_fusion), kind=kCustom, calls=%fused_computation.1 | custom fusion | bytes 9175056 | tf_op jit(solution)/shard_map/gather | solution.py:201
  154.2 3.2 %fusion.1 = bf16[4,16,640]{2,1,0:T(8,128)(2,1)S(1)} fusion(bf16[4,896,640]{2,1,0:T(8,128)(2,1)} %gather_fusion.1, f32[896]{0:T(1024)S(1)} %copy-done.9, f32[16]{0:T(128)S(1)} %add_rsqrt_fusion, bf16[16,896]{1,0:T(8,128)(2,1)S(1)} %collective-permute-done.37, bf16[16,896]{1,0:T(8,128)(2,1)S(1)} %collective-permute-done.36, ...), kind=kOutput, calls=%fused_computation.12 | convolution fusion | flops 73584640 | bytes 4787776 | tf_op jit(solution)/shard_map/rk,bkn->brn/dot_general | solution.py:274
  159.6 10.3 %shard_map.122 = f32[16,1536]{1,0:T(8,128)S(1)} custom-call(s32[48]{0:T(128)S(1)} %copy-done.2, bf16[16,1536]{1,0:T(8,128)(2,1)S(1)} %bitcast.165, bf16[16,1024]{1,0:T(8,128)(2,1)S(1)} %bitcast_dynamic-update-slice_fusion.2.nkv_ref, bf16[48,256,1024]{2,1,0:T(8,128)(2,1)} %kv_ref.3), custom_call_target="tpu_custom_call" | custom-call | flops 25165824 | bytes 8388608 | tf_op jit(solution)/shard_map/pallas_call | solution.py:79
  169.9 17.9 %shard_map.121 = f32[32,1536]{1,0:T(8,128)S(1)} custom-call(s32[48]{0:T(128)S(1)} %copy-done.2, bf16[32,1536]{1,0:T(8,128)(2,1)S(1)} %bitcast.164, bf16[32,1024]{1,0:T(8,128)(2,1)S(1)} %bitcast_dynamic-update-slice_fusion.nkv_ref, bf16[48,256,1024]{2,1,0:T(8,128)(2,1)} %kv_ref.3), custom_call_target="tpu_custom_call" | custom-call | flops 50331648 | bytes 16777216 | tf_op jit(solution)/shard_map/pallas_call | solution.py:79
  (188 shorter events, 63.7 us)
Async XLA Ops:
  3.3 35.1 %collective-permute-start.4 = (bf16[128,4736]{1,0:T(8,128)(2,1)S(1)}, bf16[128,4736]{1,0:T(8,128)(2,1)}, u32[]{:S(2)}, u32[]{:S(2)}) collective-permute-start(bf16[128,4736]{1,0:T(8,128)(2,1)S(1)} %convolution_convert_fusion), channel_id=1, source_target_pairs={{0,2},{2,0},{1,3},{3,1},{4,6},{6,4},{5,7},{7,5},{8,10},{10,8},{9,1... | collective-permute-start | bytes 3637256 | tf_op jit(solution)/shard_map/ppermute | solution.py:186
  6.4 32.7 %collective-permute-start = (bf16[128,4736]{1,0:T(8,128)(2,1)S(1)}, bf16[128,4736]{1,0:T(8,128)(2,1)}, u32[]{:S(2)}, u32[]{:S(2)}) collective-permute-start(bf16[128,4736]{1,0:T(8,128)(2,1)S(1)} %convolution_convert_fusion), channel_id=1, source_target_pairs={{0,1},{1,0},{2,3},{3,2},{4,5},{5,4},{6,7},{7,6},{8,9},{9,8},{10,11... | collective-permute-start | bytes 3637256 | tf_op jit(solution)/shard_map/ppermute | solution.py:182
  7.9 15.6 %collective-permute-start.13 = (bf16[64,4736]{1,0:T(8,128)(2,1)}, bf16[64,4736]{1,0:T(8,128)(2,1)S(1)}, u32[]{:S(2)}, u32[]{:S(2)}) collective-permute-start(bf16[64,4736]{1,0:T(8,128)(2,1)} %convolution_convert_fusion.1), channel_id=1, source_target_pairs={{0,1},{1,0},{2,3},{3,2},{4,5},{5,4},{6,7},{7,6},{8,9},{9,8},{10,11... | collective-permute-start | bytes 1818632 | tf_op jit(solution)/shard_map/ppermute | solution.py:182
  38.4 15.2 %collective-permute-start.17 = (bf16[64,4736]{1,0:T(8,128)(2,1)}, bf16[64,4736]{1,0:T(8,128)(2,1)S(1)}, u32[]{:S(2)}, u32[]{:S(2)}) collective-permute-start(bf16[64,4736]{1,0:T(8,128)(2,1)} %convolution_convert_fusion.1), channel_id=1, source_target_pairs={{0,2},{2,0},{1,3},{3,1},{4,6},{6,4},{5,7},{7,5},{8,10},{10,8},{9,1... | collective-permute-start | bytes 1818632 | tf_op jit(solution)/shard_map/ppermute | solution.py:186
  43.7 9.9 %collective-permute-start.2 = (bf16[2,32,896]{2,1,0:T(8,128)(2,1)S(1)}, bf16[2,32,896]{2,1,0:T(8,128)(2,1)S(1)}, u32[]{:S(2)}, u32[]{:S(2)}) collective-permute-start(bf16[2,32,896]{2,1,0:T(8,128)(2,1)S(1)} %pad_maximum_fusion.5), channel_id=1, source_target_pairs={{0,8},{4,12},{8,0},{12,4},{1,9},{5,13},{9,1},{13,5},{2,10},{6,14},... | collective-permute-start | bytes 344072 | tf_op jit(solution)/shard_map/ppermute | solution.py:250
  43.8 9.8 %collective-permute-start.1 = (bf16[2,32,896]{2,1,0:T(8,128)(2,1)S(1)}, bf16[2,32,896]{2,1,0:T(8,128)(2,1)S(1)}, u32[]{:S(2)}, u32[]{:S(2)}) collective-permute-start(bf16[2,32,896]{2,1,0:T(8,128)(2,1)S(1)} %pad_maximum_fusion.4), channel_id=1, source_target_pairs={{0,4},{4,8},{8,12},{12,0},{1,5},{5,9},{9,13},{13,1},{2,6},{6,10},{... | collective-permute-start | bytes 344072 | tf_op jit(solution)/shard_map/ppermute | solution.py:250
  48.5 26.3 %collective-permute-start.5 = (bf16[128,4736]{1,0:T(8,128)(2,1)}, bf16[128,4736]{1,0:T(8,128)(2,1)S(1)}, u32[]{:S(2)}, u32[]{:S(2)}) collective-permute-start(bf16[128,4736]{1,0:T(8,128)(2,1)} %collective-permute-done.4), channel_id=1, source_target_pairs={{0,1},{1,0},{2,3},{3,2},{4,5},{5,4},{6,7},{7,6},{8,9},{9,8},{10,11... | collective-permute-start | bytes 3637256 | tf_op jit(solution)/shard_map/ppermute | solution.py:182
  53.6 11.9 %collective-permute-start.27 = (bf16[448,640]{1,0:T(8,128)(2,1)S(1)}, bf16[448,640]{1,0:T(8,128)(2,1)S(1)}, u32[]{:S(2)}, u32[]{:S(2)}) collective-permute-start(bf16[448,640]{1,0:T(8,128)(2,1)S(1)} %constant_dynamic-slice_fusion), channel_id=1, source_target_pairs={{0,2},{2,0},{1,3},{3,1},{4,6},{6,4},{5,7},{7,5},{8,10},{10,8},{9,1... | collective-permute-start | bytes 1720328 | tf_op jit(solution)/shard_map/ppermute | solution.py:186
  55.2 11.8 %collective-permute-start.18 = (bf16[64,4736]{1,0:T(8,128)(2,1)S(1)}, bf16[64,4736]{1,0:T(8,128)(2,1)S(1)}, u32[]{:S(2)}, u32[]{:S(2)}) collective-permute-start(bf16[64,4736]{1,0:T(8,128)(2,1)S(1)} %collective-permute-done.17), channel_id=1, source_target_pairs={{0,1},{1,0},{2,3},{3,2},{4,5},{5,4},{6,7},{7,6},{8,9},{9,8},{10,11... | collective-permute-start | bytes 1818632 | tf_op jit(solution)/shard_map/ppermute | solution.py:182
  65.5 56.9 %collective-permute-start.28 = (bf16[448,640]{1,0:T(8,128)(2,1)S(1)}, bf16[448,640]{1,0:T(8,128)(2,1)S(1)}, u32[]{:S(2)}, u32[]{:S(2)}) collective-permute-start(bf16[448,640]{1,0:T(8,128)(2,1)S(1)} %collective-permute-done.27), channel_id=1, source_target_pairs={{0,16},{16,0},{1,17},{17,1},{2,18},{18,2},{3,19},{19,3},{4,20},{20... | collective-permute-start | bytes 1720328 | tf_op jit(solution)/shard_map/ppermute | solution.py:196
  80.8 12.4 %collective-permute-start.24 = (bf16[16,896]{1,0:T(8,128)(2,1)S(1)}, bf16[16,896]{1,0:T(8,128)(2,1)S(1)}, u32[]{:S(2)}, u32[]{:S(2)}) collective-permute-start(bf16[16,896]{1,0:T(8,128)(2,1)S(1)} %get-tuple-element.35), channel_id=1, source_target_pairs={{0,2},{1,7},{2,8},{3,13},{4,3},{5,6},{6,9},{7,12},{8,0},{9,5},{10,... | collective-permute-start | bytes 86024 | tf_op jit(solution)/shard_map/ppermute | solution.py:260
  84.2 9.0 %collective-permute-start.23 = (bf16[16,896]{1,0:T(8,128)(2,1)S(1)}, bf16[16,896]{1,0:T(8,128)(2,1)S(1)}, u32[]{:S(2)}, u32[]{:S(2)}) collective-permute-start(bf16[16,896]{1,0:T(8,128)(2,1)S(1)} %get-tuple-element.34), channel_id=1, source_target_pairs={{0,1},{1,4},{2,11},{3,14},{4,0},{5,5},{6,10},{7,15},{8,3},{9,6},{1... | collective-permute-start | bytes 86024 | tf_op jit(solution)/shard_map/ppermute | solution.py:260
  86.9 12.6 %collective-permute-start.8 = (bf16[2,32,896]{2,1,0:T(8,128)(2,1)S(1)}, bf16[2,32,896]{2,1,0:T(8,128)(2,1)S(1)}, u32[]{:S(2)}, u32[]{:S(2)}) collective-permute-start(bf16[2,32,896]{2,1,0:T(8,128)(2,1)S(1)} %pad_maximum_fusion.9), channel_id=1, source_target_pairs={{0,12},{4,0},{8,4},{12,8},{1,13},{5,1},{9,5},{13,9},{2,14},{6,2},{... | collective-permute-start | bytes 344072 | tf_op jit(solution)/shard_map/ppermute | solution.py:250
  93.2 12.6 %collective-permute-start.7 = (bf16[2,32,896]{2,1,0:T(8,128)(2,1)S(1)}, bf16[2,32,896]{2,1,0:T(8,128)(2,1)S(1)}, u32[]{:S(2)}, u32[]{:S(2)}) collective-permute-start(bf16[2,32,896]{2,1,0:T(8,128)(2,1)S(1)} %pad_maximum_fusion.8), channel_id=1, source_target_pairs={{0,8},{4,12},{8,0},{12,4},{1,9},{5,13},{9,1},{13,5},{2,10},{6,14},... | collective-permute-start | bytes 344072 | tf_op jit(solution)/shard_map/ppermute | solution.py:250
  93.3 14.6 %collective-permute-start.6 = (bf16[2,32,896]{2,1,0:T(8,128)(2,1)S(1)}, bf16[2,32,896]{2,1,0:T(8,128)(2,1)S(1)}, u32[]{:S(2)}, u32[]{:S(2)}) collective-permute-start(bf16[2,32,896]{2,1,0:T(8,128)(2,1)S(1)} %pad_maximum_fusion.7), channel_id=1, source_target_pairs={{0,4},{4,8},{8,12},{12,0},{1,5},{5,9},{9,13},{13,1},{2,6},{6,10},{... | collective-permute-start | bytes 344072 | tf_op jit(solution)/shard_map/ppermute | solution.py:250
  94.3 14.4 %collective-permute-start.37 = (bf16[16,896]{1,0:T(8,128)(2,1)S(1)}, bf16[16,896]{1,0:T(8,128)(2,1)S(1)}, u32[]{:S(2)}, u32[]{:S(2)}) collective-permute-start(bf16[16,896]{1,0:T(8,128)(2,1)S(1)} %get-tuple-element.30), channel_id=1, source_target_pairs={{0,12},{1,9},{2,6},{3,3},{4,8},{5,13},{6,2},{7,7},{8,4},{9,1},{10,... | collective-permute-start | bytes 86024 | tf_op jit(solution)/shard_map/ppermute | solution.py:272
  99.5 14.3 %collective-permute-start.36 = (bf16[16,896]{1,0:T(8,128)(2,1)S(1)}, bf16[16,896]{1,0:T(8,128)(2,1)S(1)}, u32[]{:S(2)}, u32[]{:S(2)}) collective-permute-start(bf16[16,896]{1,0:T(8,128)(2,1)S(1)} %get-tuple-element.31), channel_id=1, source_target_pairs={{0,8},{1,13},{2,2},{3,7},{4,12},{5,9},{6,6},{7,3},{8,0},{9,5},{10,... | collective-permute-start | bytes 86024 | tf_op jit(solution)/shard_map/ppermute | solution.py:272
  105.9 9.8 %collective-permute-start.35 = (bf16[16,896]{1,0:T(8,128)(2,1)S(1)}, bf16[16,896]{1,0:T(8,128)(2,1)S(1)}, u32[]{:S(2)}, u32[]{:S(2)}) collective-permute-start(bf16[16,896]{1,0:T(8,128)(2,1)S(1)} %get-tuple-element.32), channel_id=1, source_target_pairs={{0,4},{1,1},{2,14},{3,11},{4,0},{5,5},{6,10},{7,15},{8,12},{9,9},{... | collective-permute-start | bytes 86024 | tf_op jit(solution)/shard_map/ppermute | solution.py:272
  107.8 12.3 %collective-permute-start.34 = (bf16[16,896]{1,0:T(8,128)(2,1)S(1)}, bf16[16,896]{1,0:T(8,128)(2,1)S(1)}, u32[]{:S(2)}, u32[]{:S(2)}) collective-permute-start(bf16[16,896]{1,0:T(8,128)(2,1)S(1)} %get-tuple-element.29), channel_id=1, source_target_pairs={{0,0},{1,5},{2,10},{3,15},{4,4},{5,1},{6,14},{7,11},{8,8},{9,13},{... | collective-permute-start | bytes 86024 | tf_op jit(solution)/shard_map/ppermute | solution.py:272
  108.7 12.2 %collective-permute-start.12 = (bf16[32,896]{1,0:T(8,128)(2,1)S(1)}, bf16[32,896]{1,0:T(8,128)(2,1)S(1)}, u32[]{:S(2)}, u32[]{:S(2)}) collective-permute-start(bf16[32,896]{1,0:T(8,128)(2,1)S(1)} %get-tuple-element.14), channel_id=1, source_target_pairs={{0,3},{1,6},{2,9},{3,12},{4,2},{5,7},{6,8},{7,13},{8,1},{9,4},{10,... | collective-permute-start | bytes 172040 | tf_op jit(solution)/shard_map/ppermute | solution.py:260
  113.8 8.5 %collective-permute-start.11 = (bf16[32,896]{1,0:T(8,128)(2,1)S(1)}, bf16[32,896]{1,0:T(8,128)(2,1)S(1)}, u32[]{:S(2)}, u32[]{:S(2)}) collective-permute-start(bf16[32,896]{1,0:T(8,128)(2,1)S(1)} %get-tuple-element.13), channel_id=1, source_target_pairs={{0,2},{1,7},{2,8},{3,13},{4,3},{5,6},{6,9},{7,12},{8,0},{9,5},{10,... | collective-permute-start | bytes 172040 | tf_op jit(solution)/shard_map/ppermute | solution.py:260
  121.0 24.2 %collective-permute-start.26 = (bf16[896,640]{1,0:T(8,128)(2,1)S(1)}, bf16[896,640]{1,0:T(8,128)(2,1)}, u32[]{:S(2)}, u32[]{:S(2)}) collective-permute-start(bf16[896,640]{1,0:T(8,128)(2,1)S(1)} %copy-done.6), channel_id=1, source_target_pairs={{0,1},{1,0},{2,3},{3,2},{4,5},{5,4},{6,7},{7,6},{8,9},{9,8},{10,11... | collective-permute-start | bytes 3440648 | tf_op jit(solution)/shard_map/ppermute | solution.py:182
  126.5 18.6 %collective-permute-start.29 = (bf16[896,640]{1,0:T(8,128)(2,1)}, bf16[896,640]{1,0:T(8,128)(2,1)S(1)}, u32[]{:S(2)}, u32[]{:S(2)}) collective-permute-start(bf16[896,640]{1,0:T(8,128)(2,1)} %bitcast.171), channel_id=1, source_target_pairs={{0,1},{1,0},{2,3},{3,2},{4,5},{5,4},{6,7},{7,6},{8,9},{9,8},{10,11... | collective-permute-start | bytes 3440648 | tf_op jit(solution)/shard_map/ppermute | solution.py:182
  130.9 10.3 %collective-permute-start.33 = (bf16[32,896]{1,0:T(8,128)(2,1)S(1)}, bf16[32,896]{1,0:T(8,128)(2,1)S(1)}, u32[]{:S(2)}, u32[]{:S(2)}) collective-permute-start(bf16[32,896]{1,0:T(8,128)(2,1)S(1)} %get-tuple-element.8), channel_id=1, source_target_pairs={{0,12},{1,9},{2,6},{3,3},{4,8},{5,13},{6,2},{7,7},{8,4},{9,1},{10,... | collective-permute-start | bytes 172040 | tf_op jit(solution)/shard_map/ppermute | solution.py:272
  (34 other events, 305.7 us)

commit v2 on v0

--- a/solution.py
+++ b/solution.py
@@ -1,9 +1,157 @@
+import functools
+
 import jax
 import jax.numpy as jnp
 from jax import lax
+from jax.experimental import pallas as pl
+from jax.experimental.pallas import tpu as pltpu
 from jax.sharding import PartitionSpec as P
 
 HEAD_DIM = 128
+ROW_STEP = 8
+LANES = 128
+
+
+def talker_kernel(
+    first_row, heads, len_ref, block_ref, sums_ref, gain_ref, w0, w1, w2, w3, kv_ref,
+    new_kv_ref, out_ref, qkv, spread, gathered,
+):
+    step = pl.program_id(0)
+    blocks = qkv.shape[0]
+    group = heads // blocks
+    slot = LANES // ROW_STEP
+    cached = kv_ref.shape[1]
+    width = blocks * HEAD_DIM
+    inv = 1.0 / HEAD_DIM**0.5
+
+    @pl.when(step == 0)
+    def _():
+        talker_in = sums_ref[0].astype(jnp.float32)
+        for k in range(1, sums_ref.shape[0]):
+            talker_in = talker_in + sums_ref[k].astype(jnp.float32)
+        scale = lax.rsqrt(jnp.mean(talker_in * talker_in, axis=1, keepdims=True) + 1e-06)
+        normed = (talker_in * scale * gain_ref[...]).astype(jnp.bfloat16)
+        for e, w in enumerate((w0, w1, w2, w3)):
+            made = jnp.dot(normed, w[...], preferred_element_type=jnp.float32)
+            qkv[e ^ block_ref[0]] = made.astype(jnp.bfloat16).astype(jnp.float32)
+        for g in range(blocks):
+            key, value = group * HEAD_DIM, (group + 1) * HEAD_DIM
+            new_kv_ref[:, g * HEAD_DIM : (g + 1) * HEAD_DIM] = qkv[g, :, key:value].astype(
+                jnp.bfloat16
+            )
+            new_kv_ref[:, width + g * HEAD_DIM : width + (g + 1) * HEAD_DIM] = qkv[
+                g, :, value:
+            ].astype(jnp.bfloat16)
+        spread[...] = jnp.zeros_like(spread)
+
+    here = pl.ds(pl.multiple_of(step * ROW_STEP, ROW_STEP), ROW_STEP)
+    for h in range(heads):
+        g, j = h // group, h % group
+        spread[pl.ds(h, ROW_STEP, stride=slot), :] = qkv[
+            g, here, j * HEAD_DIM : (j + 1) * HEAD_DIM
+        ]
+    query = spread[...].T
+    lane = lax.broadcasted_iota(jnp.int32, (HEAD_DIM, LANES), 1)
+    lane_row, lane_block = lane // slot, lane % slot // group
+    by_block = [
+        jnp.where(lane_block == g, query, 0.0).astype(jnp.bfloat16) for g in range(blocks)
+    ]
+
+    scores = jnp.zeros((cached, LANES), jnp.float32)
+    for r in range(ROW_STEP):
+        mine = lane_row == r
+        right = jnp.concatenate(
+            [jnp.where(mine, q, jnp.zeros_like(q)) for q in by_block], axis=0
+        )
+        scores = scores + jnp.dot(
+            kv_ref[r, :, :width], right, preferred_element_type=jnp.float32
+        )
+    own = jnp.zeros((ROW_STEP, LANES), jnp.float32)
+    for g in range(blocks):
+        key = qkv[g, here, group * HEAD_DIM : (group + 1) * HEAD_DIM].astype(jnp.bfloat16)
+        own = own + jnp.dot(key, by_block[g], preferred_element_type=jnp.float32)
+    own_row = lax.broadcasted_iota(jnp.int32, own.shape, 0)
+    own = jnp.sum(jnp.where(own_row == lane_row[:ROW_STEP], own, 0.0), axis=0, keepdims=True)
+
+    scores, own = scores * inv, own * inv
+    lens = jnp.zeros((1, LANES), jnp.int32)
+    for r in range(ROW_STEP):
+        lens = jnp.where(lane_row[:1] == r, len_ref[first_row + step * ROW_STEP + r], lens)
+    valid = lax.broadcasted_iota(jnp.int32, scores.shape, 0) < lens
+    scores = jnp.where(valid, scores, -jnp.inf)
+    top = jnp.maximum(jnp.max(scores, axis=0, keepdims=True), own)
+    expo = jnp.where(valid, jnp.exp(scores - top), 0.0)
+    own_expo = jnp.exp(own - top)
+    total = jnp.sum(expo, axis=0, keepdims=True) + own_expo
+    probs = (expo / total).T.astype(jnp.bfloat16)
+    own_prob = (own_expo / total).astype(jnp.bfloat16).astype(jnp.float32)
+    own_prob = jnp.broadcast_to(own_prob, (LANES, LANES)).T
+
+    row_block = lax.broadcasted_iota(jnp.int32, (slot, HEAD_DIM), 0) // group
+    for r in range(ROW_STEP):
+        rows = slice(r * slot, (r + 1) * slot)
+        made = jnp.dot(
+            probs[rows], kv_ref[r, :, width:], preferred_element_type=jnp.float32
+        )
+        values = qkv.at[:, here]
+        ctx = jnp.zeros((slot, HEAD_DIM), jnp.float32)
+        value = jnp.zeros((slot, HEAD_DIM), jnp.float32)
+        for g in range(blocks):
+            new = values[g, r : r + 1, (group + 1) * HEAD_DIM :]
+            ctx = jnp.where(row_block == g, made[:, g * HEAD_DIM : (g + 1) * HEAD_DIM], ctx)
+            value = jnp.where(row_block == g, new, value)
+        gathered[rows, :] = ctx + own_prob[rows] * value
+    for h in range(heads):
+        out_ref[:, h * HEAD_DIM : (h + 1) * HEAD_DIM] = gathered[
+            pl.ds(h, ROW_STEP, stride=slot), :
+        ]
+
+
+def talker_rows(first_row, block, sums, talker_gain, weights, kv_len, kv_cache):
+    terms, rows, wide = sums.shape
+    _, cached, kv_width = kv_cache.shape
+    columns = weights[0].shape[1]
+    q_width = len(weights) * columns - kv_width
+    heads = q_width // HEAD_DIM
+    offset = first_row // ROW_STEP
+    whole = lambda *shape: pl.BlockSpec(shape, lambda i, *_: (0,) * len(shape))
+    return pl.pallas_call(
+        functools.partial(talker_kernel, first_row, heads),
+        out_shape=(
+            jax.ShapeDtypeStruct((rows, kv_width), jnp.bfloat16),
+            jax.ShapeDtypeStruct((rows, q_width), jnp.float32),
+        ),
+        grid_spec=pltpu.PrefetchScalarGridSpec(
+            num_scalar_prefetch=2,
+            grid=(rows // ROW_STEP,),
+            in_specs=[
+                whole(terms, rows, wide),
+                whole(1, wide),
+                *[whole(wide, columns) for _ in weights],
+                pl.BlockSpec((ROW_STEP, cached, kv_width), lambda i, *_: (i + offset, 0, 0)),
+            ],
+            out_specs=(
+                whole(rows, kv_width),
+                pl.BlockSpec((ROW_STEP, q_width), lambda i, *_: (i, 0)),
+            ),
+            scratch_shapes=[
+                pltpu.VMEM((len(weights), rows, columns), jnp.float32),
+                pltpu.VMEM((LANES, HEAD_DIM), jnp.float32),
+                pltpu.VMEM((LANES, HEAD_DIM), jnp.float32),
+            ],
+        ),
+        cost_estimate=pl.CostEstimate(
+            flops=4 * rows * cached * q_width,
+            bytes_accessed=2 * rows * cached * kv_width,
+            transcendentals=rows * cached * heads,
+        ),
+        compiler_params=pltpu.CompilerParams(vmem_limit_bytes=32 * 1024 * 1024),
+    )(kv_len, block, sums, talker_gain.reshape(1, wide), *weights, kv_cache)
+
+
+def rms_norm(talker_in, talker_gain):
+    scale = lax.rsqrt(jnp.mean(talker_in * talker_in, axis=1, keepdims=True) + 1e-06)
+    return (talker_in * scale * talker_gain).astype(jnp.bfloat16)
 
 
 def talker_step(talker_in, talker_gain, w_query, w_key, w_value, kv_len, kv_cache):
@@ -13,8 +161,7 @@
     head_dim = HEAD_DIM
     kv_heads = kv_width // head_dim
     group = w_query.shape[1] // kv_width
-    scale = lax.rsqrt(jnp.mean(talker_in * talker_in, axis=1, keepdims=True) + 1e-06)
-    normed = (talker_in * scale * talker_gain).astype(jnp.bfloat16)
+    normed = rms_norm(talker_in, talker_gain)
     query = jnp.dot(normed, w_query, preferred_element_type=jnp.float32).astype(jnp.bfloat16)
     new_key = jnp.dot(normed, w_key, preferred_element_type=jnp.float32).astype(jnp.bfloat16)
     new_value = jnp.dot(normed, w_value, preferred_element_type=jnp.float32).astype(jnp.bfloat16)
@@ -40,7 +187,7 @@
     return (talker_kv, ctx.reshape(owned, w_query.shape[1]))
 
 
-def shards(
+def any_mesh(
     thinker_act,
     w_think,
     w_proj,
@@ -78,6 +225,86 @@
     return (thinker_out, talker_kv, talker_ctx)
 
 
+PLANE = ("section", "rows")
+
+
+def over_core(x):
+    return lax.ppermute(x, "rows", [(0, 1), (1, 0)])
+
+
+def over_section(x):
+    return lax.ppermute(x, "section", [(0, 1), (1, 0)])
+
+
+def after(x, *others):
+    return lax.optimization_barrier((x, *others))[0]
+
+
+def four_planes(
+    thinker_act,
+    w_think,
+    w_proj,
+    talker_gain,
+    w_query,
+    w_key,
+    w_value,
+    talker_slot,
+    kv_len,
+    kv_cache,
+):
+    planes = 4
+    owned = kv_cache.shape[0]
+    g, m, c = lax.axis_index("groups"), lax.axis_index("mp"), lax.axis_index(PLANE)
+    columns = w_think.shape[1]
+    slots = talker_slot[0]
+    chunks = [(0, 32), (32, 16)]
+
+    wanted, sent = [], []
+    for first, n in chunks:
+        plane = jnp.arange(planes, dtype=jnp.int32)[:, None] * owned
+        want = (plane + first + jnp.arange(n, dtype=jnp.int32)[None, :]).reshape(-1)
+        pick = (want[:, None] == slots[None, :]).astype(jnp.bfloat16)
+        rows = jnp.dot(pick, thinker_act, preferred_element_type=jnp.float32)
+        wanted.append(want)
+        sent.append(rows.astype(jnp.bfloat16))
+
+    mine = jnp.concatenate([w_query, w_key, w_value], axis=1)
+    depth = mine.shape[0] // (2 * planes)
+    piece = lax.dynamic_slice_in_dim(mine, (g * planes + m) * depth, depth, axis=0)
+    piece = over_section(piece)
+    crossed = [over_section(after(sent[0], piece))]
+    other = lax.all_gather(piece, ("groups", "mp"), axis=0, tiled=True)
+    crossed.append(over_section(after(sent[1], crossed[0])))
+    weights = [mine, over_core(mine), other, over_core(other)]
+
+    def times_w(x):
+        return jnp.dot(x, w_think, preferred_element_type=jnp.float32).astype(jnp.bfloat16)
+
+    near = [(times_w(rows), times_w(over_core(rows))) for rows in sent]
+    returned, kvs, ctxs = [], [], []
+    for (first, n), own, across in zip(chunks, near, crossed):
+        four = [*own, times_w(across), times_w(over_core(across))]
+        swapped = [jnp.where(c & 1, four[e ^ 1], four[e]) for e in range(4)]
+        blocks = jnp.stack([jnp.where(c & 2, swapped[e ^ 2], swapped[e]) for e in range(4)])
+        mixed = lax.all_to_all(blocks, PLANE, 0, 0)
+        terms = lax.all_to_all(mixed, "mp", 0, 0)
+        home = jnp.sum(terms.astype(jnp.float32), axis=0).astype(jnp.bfloat16)
+        returned.append(home)
+        projected = jnp.dot(home, w_proj, preferred_element_type=jnp.float32)
+        projected = projected.astype(jnp.bfloat16).reshape(planes, n, -1)
+        sums = lax.all_to_all(projected, "mp", 0, 0)
+        new_kv, ctx = talker_rows(
+            first, c.reshape(1), sums, talker_gain, weights, kv_len, kv_cache
+        )
+        kvs.append(new_kv)
+        ctxs.append(ctx)
+
+    pick = (slots[:, None] == jnp.concatenate(wanted)[None, :]).astype(jnp.bfloat16)
+    home = jnp.concatenate(returned, axis=0)
+    thinker_out = jnp.dot(pick, home, preferred_element_type=jnp.float32).astype(jnp.bfloat16)
+    return (thinker_out, jnp.concatenate(kvs, axis=0), jnp.concatenate(ctxs, axis=0))
+
+
 def solution(mesh):
     in_specs = (
         P(("groups", "section", "rows"), "mp"),
@@ -96,4 +323,6 @@
         P(("groups", "mp", "section", "rows"), None),
         P(("groups", "mp", "section", "rows"), None),
     )
+    sizes = tuple(mesh.shape[a] for a in ("groups", "section", "rows", "mp"))
+    shards = four_planes if sizes == (2, 2, 2, 4) else any_mesh
     return jax.shard_map(shards, mesh=mesh, in_specs=in_specs, out_specs=out_specs, check_vma=False)

time: 393 us -> 183 us (0.47)
  waiting for transfers between devices: 263 us -> 42.6 us
  local copies, waits for them, and re-layouts: 53.1 us -> 5.17 us
  starting transfers between devices: 0.16 us -> 22 us
  Pallas kernels: 0 us -> 18 us
  blocking collectives: 18.7 us -> 34.6 us
  matrix products: 35.2 us -> 40.1 us
    all_gather x2 -> x1, waiting for transfers between devices: 210 us -> 0.02 us  [four_planes(): other = lax.all_gather(piece, ('groups', 'mp'), axis=0, tiled=True)]
    reduce_scatter x2 -> x0, waiting for transfers between devices: 51.1 us -> none  [the longest x1 51.1 us: shards(): mine = lax.psum_scatter(partial_sums, 'mp', scatter_dimension=1, tiled=True)]
    all_to_all x0 -> x2, blocking collectives: none -> 34.6 us  [the longest x1 17.4 us: four_planes(): mixed = lax.all_to_all(blocks, PLANE, 0, 0)]
    unnamed x20 -> x34, local copies, waits for them, and re-layouts: 33.2 us -> 4.92 us
    all_to_all x0 -> x4, waiting for transfers between devices: none -> 22.4 us  [the longest x1 19.1 us: four_planes(): terms = lax.all_to_all(mixed, 'mp', 0, 0)]
    ppermute x0 -> x9, waiting for transfers between devices: none -> 20.2 us  [the longest x3 20.2 us: over_section(): return lax.ppermute(x, 'section', [(0, 1), (1, 0)])]
    all_gather x2 -> x0, blocking collectives: 18.7 us -> none  [the longest x1 9.63 us: shards(): lax.all_gather(w_value, ('section', 'rows'), axis=1, tiled=True)]
    pallas_call x0 -> x2, Pallas kernels: none -> 18 us  [talker_rows(): pl.pallas_call(functools.partial(talker_kernel, first_row, heads), out_sh...]
  transfers between devices with their start and end apart: 4 -> 14, of which waited for: 2 -> 6; matrix products, arithmetic and copies ran while one was open for 15% -> 24% of each run, Pallas kernels for 0% -> 4%
where the time goes in v2:
time: 183 us; the launch traced here: 182 us
  waiting for transfers between devices  42.6 us (23%)
  matrix products  40.1 us (22%)
  blocking collectives  34.6 us (19%)
  starting transfers between devices  22 us (12%)
  Pallas kernels  18 us (10%)
  between operations  14.4 us (8%)
  local copies, waits for them, and re-layouts  5.17 us (3%)
  other arithmetic  4.86 us (3%)
    dot_general x8, matrix products, times_w(): jnp.dot(x, w_think, preferred_element_type=jnp.float32).astype(jnp.bfloat16)  31 us
    ppermute x3, waiting for transfers between devices, over_section(): return lax.ppermute(x, 'section', [(0, 1), (1, 0)])  20.2 us
    all_to_all x1, waiting for transfers between devices, four_planes(): terms = lax.all_to_all(mixed, 'mp', 0, 0)  19.1 us
    pallas_call x2, Pallas kernels, talker_rows(): pl.pallas_call(functools.partial(talker_kernel, first_row, heads), out_sh...  18 us
    all_to_all x1, blocking collectives, four_planes(): mixed = lax.all_to_all(blocks, PLANE, 0, 0)  17.4 us
    all_to_all x1, blocking collectives, four_planes(): terms = lax.all_to_all(mixed, 'mp', 0, 0)  17.2 us
    all_to_all x2, starting transfers between devices, four_planes(): sums = lax.all_to_all(projected, 'mp', 0, 0)  6.7 us
    ppermute x3, starting transfers between devices, over_section(): return lax.ppermute(x, 'section', [(0, 1), (1, 0)])  6.17 us
  transfers between devices with their start and end apart: 14, of which 6 were waited for; matrix products, arithmetic and copies ran while one was open for 24% of the time, Pallas kernels for 4%

profile of v2, /device:TPU:0, one launch (start us, length us, event | category | flops | bytes accessed | tf_op | source)
XLA Modules:
  0.0 181.7 jit_solution(11991782089728519464)
XLA Ops:
  9.7 3.0 %collective-permute-start = (bf16[112,640]{1,0:T(8,128)(2,1)S(1)}, bf16[112,640]{1,0:T(8,128)(2,1)S(1)}, u32[]{:S(2)}, u32[]{:S(2)}) collective-permute-start(bf16[112,640]{1,0:T(8,128)(2,1)S(1)} %constant_dynamic-slice_fusion), channel_id=1, source_target_pairs={{0,2},{2,0},{1,3},{3,1},{4,6},{6,4},{5,7},{7,5},{8,10},{10,8},{9,1... | collective-permute-start | bytes 430088 | tf_op jit(solution)/shard_map/ppermute | solution.py:236
  12.9 1.6 convolution_convert_fusion
  14.6 1.9 %collective-permute-done = bf16[112,640]{1,0:T(8,128)(2,1)S(1)} collective-permute-done((bf16[112,640]{1,0:T(8,128)(2,1)S(1)}, bf16[112,640]{1,0:T(8,128)(2,1)S(1)}, u32[]{:S(2)}, u32[]{:S(2)}) %collective-permute-start) | collective-permute-done | bytes 143392 | tf_op jit(solution)/shard_map/ppermute | solution.py:236
  16.5 1.7 collective-permute-start.1
  19.6 5.0 %convolution_convert_fusion.9 = bf16[64,896]{1,0:T(8,128)(2,1)S(1)} fusion(bf16[64,4736]{1,0:T(8,128)(2,1)} %convolution_convert_fusion.1, bf16[4736,896]{1,0:T(8,128)(2,1)} %param.11), kind=kOutput, calls=%fused_computation.9 | convolution fusion | flops 543219712 | bytes 9207808 | tf_op jit(solution)/shard_map/dot_general | solution.py:281
  24.6 6.0 %convolution_convert_fusion.4 = bf16[128,896]{1,0:T(8,128)(2,1)} fusion(bf16[128,4736]{1,0:T(8,128)(2,1)} %convolution_convert_fusion, bf16[4736,896]{1,0:T(8,128)(2,1)} %param.11), kind=kOutput, calls=%fused_computation.4 | convolution fusion | flops 1086439424 | bytes 9928704 | tf_op jit(solution)/shard_map/dot_general | solution.py:281
  30.6 14.1 %collective-permute-done.1 = bf16[128,4736]{1,0:T(8,128)(2,1)} collective-permute-done((bf16[128,4736]{1,0:T(8,128)(2,1)}, bf16[128,4736]{1,0:T(8,128)(2,1)}, u32[]{:S(2)}, u32[]{:S(2)}) %collective-permute-start.1) | collective-permute-done | bytes 1212448 | tf_op jit(solution)/shard_map/ppermute | solution.py:236
  46.1 5.0 %convolution_convert_fusion.10 = bf16[64,896]{1,0:T(8,128)(2,1)S(1)} fusion(bf16[64,4736]{1,0:T(8,128)(2,1)} %collective-permute-done.6, bf16[4736,896]{1,0:T(8,128)(2,1)} %param.11), kind=kOutput, calls=%fused_computation.10 | convolution fusion | flops 543219712 | bytes 9207808 | tf_op jit(solution)/shard_map/dot_general | solution.py:281
  51.1 3.4 %convolution_convert_fusion.5 = bf16[128,896]{1,0:T(8,128)(2,1)} fusion(bf16[128,4736]{1,0:T(8,128)(2,1)} %collective-permute-done.3, bf16[4736,896]{1,0:T(8,128)(2,1)S(1)} %bitcast.43), kind=kOutput, calls=%fused_computation.5 | convolution fusion | flops 1086439424 | bytes 9928704 | tf_op jit(solution)/shard_map/dot_general | solution.py:281
  54.6 4.2 %collective-permute-done.4 = bf16[64,4736]{1,0:T(8,128)(2,1)S(1)} collective-permute-done((bf16[64,4736]{1,0:T(8,128)(2,1)}, bf16[64,4736]{1,0:T(8,128)(2,1)S(1)}, u32[]{:S(2)}, u32[]{:S(2)}) %collective-permute-start.4) | collective-permute-done | bytes 606240 | tf_op jit(solution)/shard_map/ppermute | solution.py:236
  58.8 3.4 %convolution_convert_fusion.6 = bf16[128,896]{1,0:T(8,128)(2,1)} fusion(bf16[128,4736]{1,0:T(8,128)(2,1)} %collective-permute-done.1, bf16[4736,896]{1,0:T(8,128)(2,1)S(1)} %bitcast.43), kind=kOutput, calls=%fused_computation.6 | convolution fusion | flops 1086439424 | bytes 9928704 | tf_op jit(solution)/shard_map/dot_general | solution.py:281
  66.4 3.6 %all-to-all-start.2 = ((bf16[4,64,896]{2,1,0:T(8,128)(2,1)}), bf16[4,64,896]{2,1,0:T(8,128)(2,1)S(1)}, u32[]{:S(2)}, u32[]{:S(2)}) async-start(bf16[4,64,896]{2,1,0:T(8,128)(2,1)} %pad_maximum_fusion.1), calls=%async_computation.2 | async-start | bytes 917504 | tf_op jit(solution)/shard_map/all_to_all | solution.py:289
  70.1 5.3 %select_bitcast_fusion.3 = (bf16[1,128,896]{2,1,0:T(8,128)(2,1)S(1)}, bf16[1,128,896]{2,1,0:T(8,128)(2,1)S(1)}, bf16[1,128,896]{2,1,0:T(8,128)(2,1)S(1)}, bf16[1,128,896]{2,1,0:T(8,128)(2,1)S(1)}) fusion(pred[]{:T(512)S(6)} %ne.22, bf16[128,896]{1,0:T(8,128)(2,1)} %convolution_convert_fusion.6, pred[]{:T(512)S(6)} %ne.23, ...), kind=kOutput, calls=%fused_computation.22 | convolution fusion | flops 1087356928 | bytes 11304962 | tf_op jit(solution)/shard_map/dot_general | solution.py:281
  78.0 17.4 %all_to_all.30 = bf16[4,128,896]{2,1,0:T(8,128)(2,1)} all-to-all(bf16[4,128,896]{2,1,0:T(8,128)(2,1)} %pad_maximum_fusion), channel_id=1, replica_groups=mesh['groups'=2,'mp'=4,'section'=2,'rows'=2] {'section','rows'}, dimensions={0} | all-to-all | bytes 1835008 | tf_op jit(solution)/shard_map/all_to_all | solution.py:289
  95.4 17.2 %all_to_all.31 = bf16[4,64,896]{2,1,0:T(8,128)(2,1)} all-to-all(bf16[4,64,896]{2,1,0:T(8,128)(2,1)S(1)} %all-to-all-done.2), channel_id=1, replica_groups=mesh['groups'=2,'mp'=4,'section'=2,'rows'=2] {'mp'}, dimensions={0} | all-to-all | bytes 917504 | tf_op jit(solution)/shard_map/all_to_all | solution.py:290
  112.6 4.4 %all-to-all-start.1 = ((bf16[4,128,896]{2,1,0:T(8,128)(2,1)}), bf16[4,128,896]{2,1,0:T(8,128)(2,1)}, u32[]{:S(2)}, u32[]{:S(2)}) async-start(bf16[4,128,896]{2,1,0:T(8,128)(2,1)} %all_to_all.30), calls=%async_computation.1 | async-start | bytes 1835008 | tf_op jit(solution)/shard_map/all_to_all | solution.py:290
  117.7 2.5 %convolution_convert_fusion.8 = bf16[64,896]{1,0:T(8,128)(2,1)} fusion(bf16[64,896]{1,0:T(8,128)(2,1)S(1)} %reduce_sum.25, bf16[896,896]{1,0:T(8,128)(2,1)} %param.12), kind=kOutput, calls=%fused_computation.8 | convolution fusion | flops 102817792 | bytes 1835008 | tf_op jit(solution)/shard_map/dot_general | solution.py:293
  120.1 19.1 %all-to-all-done.1 = bf16[4,128,896]{2,1,0:T(8,128)(2,1)} async-done(((bf16[4,128,896]{2,1,0:T(8,128)(2,1)}), bf16[4,128,896]{2,1,0:T(8,128)(2,1)}, u32[]{:S(2)}, u32[]{:S(2)}) %all-to-all-start.1) | async-done | bytes 917536 | tf_op jit(solution)/shard_map/all_to_all | solution.py:290
  139.2 3.3 %all-to-all-start.5 = ((bf16[4,16,896]{2,1,0:T(8,128)(2,1)}), bf16[4,16,896]{2,1,0:T(8,128)(2,1)S(1)}, u32[]{:S(2)}, u32[]{:S(2)}) async-start(bf16[4,16,896]{2,1,0:T(8,128)(2,1)} %bitcast.11), calls=%async_computation.5 | async-start | bytes 229376 | tf_op jit(solution)/shard_map/all_to_all | solution.py:295
  143.9 2.7 %convolution_convert_fusion.3 = bf16[128,896]{1,0:T(8,128)(2,1)} fusion(bf16[128,896]{1,0:T(8,128)(2,1)S(1)} %reduce_sum.24, bf16[896,896]{1,0:T(8,128)(2,1)} %param.12), kind=kOutput, calls=%fused_computation.3 | convolution fusion | flops 205635584 | bytes 2064384 | tf_op jit(solution)/shard_map/dot_general | solution.py:293
  146.6 1.8 all-to-all-done.5.sums_ref
  148.4 3.4 %all-to-all-start.4 = ((bf16[4,32,896]{2,1,0:T(8,128)(2,1)}), bf16[4,32,896]{2,1,0:T(8,128)(2,1)S(1)}, u32[]{:S(2)}, u32[]{:S(2)}) async-start(bf16[4,32,896]{2,1,0:T(8,128)(2,1)} %bitcast.44), calls=%async_computation.4 | async-start | bytes 458752 | tf_op jit(solution)/shard_map/all_to_all | solution.py:295
  153.1 7.0 %shard_map.122 = (bf16[16,1024]{1,0:T(8,128)(2,1)S(1)}, f32[16,1536]{1,0:T(8,128)S(1)}) custom-call(s32[48]{0:T(128)S(1)} %copy-done.3, s32[1]{0:T(128)} %bitcast.9.block_ref, bf16[4,16,896]{2,1,0:T(8,128)(2,1)S(1)} %all-to-all-done.5.sums_ref, f32[1,896]{1,0:T(1,128)S(1)} %reshape.66.gain_ref, bf16[896,640]{1,0:T(8,128)(2,1)S(1)} %constant_dynamic-update-slice_fusion.w0, ...), custom_call_target="tpu_custom_call" | custom-call | flops 25165824 | bytes 8388608 | tf_op jit(solution)/shard_map/pallas_call | solution.py:118
  162.4 11.0 %shard_map.121 = (bf16[32,1024]{1,0:T(8,128)(2,1)S(1)}, f32[32,1536]{1,0:T(8,128)S(1)}) custom-call(s32[48]{0:T(128)S(1)} %copy-done.3, s32[1]{0:T(128)} %bitcast.9.block_ref, bf16[4,32,896]{2,1,0:T(8,128)(2,1)S(1)} %all-to-all-done.4.sums_ref, f32[1,896]{1,0:T(1,128)S(1)} %reshape.66.gain_ref, bf16[896,640]{1,0:T(8,128)(2,1)S(1)} %constant_dynamic-update-slice_fusion.w0, ...), custom_call_target="tpu_custom_call" | custom-call | flops 50331648 | bytes 16777216 | tf_op jit(solution)/shard_map/pallas_call | solution.py:118
  (73 shorter events, 19.3 us)
Async XLA Ops:
  7.2 5.7 %copy-start = (bf16[192,4736]{1,0:T(8,128)(2,1)S(1)}, bf16[192,4736]{1,0:T(8,128)(2,1)}, u32[]{:S(2)}) copy-start(bf16[192,4736]{1,0:T(8,128)(2,1)} %param.10) | copy-start | bytes 5455876
  7.2 109.9 %all-gather.2.cloned.1.call-start = ((), (), s32[]{:S(2)}) async-start(), calls=%async_computation.6 | async-start | bytes 1290240 | tf_op jit(solution)/shard_map/all_gather | solution.py:276
  9.7 6.8 %collective-permute-start = (bf16[112,640]{1,0:T(8,128)(2,1)S(1)}, bf16[112,640]{1,0:T(8,128)(2,1)S(1)}, u32[]{:S(2)}, u32[]{:S(2)}) collective-permute-start(bf16[112,640]{1,0:T(8,128)(2,1)S(1)} %constant_dynamic-slice_fusion), channel_id=1, source_target_pairs={{0,2},{2,0},{1,3},{3,1},{4,6},{6,4},{5,7},{7,5},{8,10},{10,8},{9,1... | collective-permute-start | bytes 430088 | tf_op jit(solution)/shard_map/ppermute | solution.py:236
  14.4 36.6 %collective-permute-start.3 = (bf16[128,4736]{1,0:T(8,128)(2,1)}, bf16[128,4736]{1,0:T(8,128)(2,1)}, u32[]{:S(2)}, u32[]{:S(2)}) collective-permute-start(bf16[128,4736]{1,0:T(8,128)(2,1)} %convolution_convert_fusion), channel_id=1, source_target_pairs={{0,1},{1,0},{2,3},{3,2},{4,5},{5,4},{6,7},{7,6},{8,9},{9,8},{10,11... | collective-permute-start | bytes 3637256 | tf_op jit(solution)/shard_map/ppermute | solution.py:232
  16.5 8.1 %copy-start.10 = (bf16[112,640]{1,0:T(8,128)(2,1)}, bf16[112,640]{1,0:T(8,128)(2,1)S(1)}, u32[]{:S(2)}) copy-start(bf16[112,640]{1,0:T(8,128)(2,1)S(1)} %collective-permute-done) | copy-start | bytes 430084
  16.5 28.2 %collective-permute-start.1 = (bf16[128,4736]{1,0:T(8,128)(2,1)}, bf16[128,4736]{1,0:T(8,128)(2,1)}, u32[]{:S(2)}, u32[]{:S(2)}) collective-permute-start(bf16[128,4736]{1,0:T(8,128)(2,1)} %convolution_convert_fusion), channel_id=1, source_target_pairs={{0,2},{2,0},{1,3},{3,1},{4,6},{6,4},{5,7},{7,5},{8,10},{10,8},{9,1... | collective-permute-start | bytes 3637256 | tf_op jit(solution)/shard_map/ppermute | solution.py:236
  19.6 26.5 %collective-permute-start.6 = (bf16[64,4736]{1,0:T(8,128)(2,1)}, bf16[64,4736]{1,0:T(8,128)(2,1)}, u32[]{:S(2)}, u32[]{:S(2)}) collective-permute-start(bf16[64,4736]{1,0:T(8,128)(2,1)} %convolution_convert_fusion.1), channel_id=1, source_target_pairs={{0,1},{1,0},{2,3},{3,2},{4,5},{5,4},{6,7},{7,6},{8,9},{9,8},{10,11... | collective-permute-start | bytes 1818632 | tf_op jit(solution)/shard_map/ppermute | solution.py:232
  30.5 20.5 %slice-start = ((s8[8486912]{0:T(1024)(128)(4,1)}), s8[98304]{0:T(1024)(128)(4,1)S(1)}, s32[]{:S(2)}) async-start(s8[8486912]{0:T(1024)(128)(4,1)} %bitcast.42), calls=%async_computation.7 | async-start | bytes 196608
  30.6 20.5 %slice-start.1 = ((s8[8486912]{0:T(1024)(128)(4,1)}), s8[4194304]{0:T(1024)(128)(4,1)S(1)}, s32[]{:S(2)}) async-start(s8[8486912]{0:T(1024)(128)(4,1)} %bitcast.42), calls=%async_computation.8 | async-start | bytes 8388608
  30.6 20.5 %slice-start.2 = ((s8[8486912]{0:T(1024)(128)(4,1)}), s8[4194304]{0:T(1024)(128)(4,1)S(1)}, s32[]{:S(2)}) async-start(s8[8486912]{0:T(1024)(128)(4,1)} %bitcast.42), calls=%async_computation.9 | async-start | bytes 8388608
  44.6 14.2 %collective-permute-start.4 = (bf16[64,4736]{1,0:T(8,128)(2,1)}, bf16[64,4736]{1,0:T(8,128)(2,1)S(1)}, u32[]{:S(2)}, u32[]{:S(2)}) collective-permute-start(bf16[64,4736]{1,0:T(8,128)(2,1)} %convolution_convert_fusion.1), channel_id=1, source_target_pairs={{0,2},{2,0},{1,3},{3,1},{4,6},{6,4},{5,7},{7,5},{8,10},{10,8},{9,1... | collective-permute-start | bytes 1818632 | tf_op jit(solution)/shard_map/ppermute | solution.py:236
  58.8 5.4 %collective-permute-start.5 = (bf16[64,4736]{1,0:T(8,128)(2,1)S(1)}, bf16[64,4736]{1,0:T(8,128)(2,1)S(1)}, u32[]{:S(2)}, u32[]{:S(2)}) collective-permute-start(bf16[64,4736]{1,0:T(8,128)(2,1)S(1)} %collective-permute-done.4), channel_id=1, source_target_pairs={{0,1},{1,0},{2,3},{3,2},{4,5},{5,4},{6,7},{7,6},{8,9},{9,8},{10,11... | collective-permute-start | bytes 1818632 | tf_op jit(solution)/shard_map/ppermute | solution.py:232
  62.2 7.9 %collective-permute-start.2 = (bf16[128,4736]{1,0:T(8,128)(2,1)}, bf16[128,4736]{1,0:T(8,128)(2,1)}, u32[]{:S(2)}, u32[]{:S(2)}) collective-permute-start(bf16[128,4736]{1,0:T(8,128)(2,1)} %collective-permute-done.1), channel_id=1, source_target_pairs={{0,1},{1,0},{2,3},{3,2},{4,5},{5,4},{6,7},{7,6},{8,9},{9,8},{10,11... | collective-permute-start | bytes 3637256 | tf_op jit(solution)/shard_map/ppermute | solution.py:232
  66.4 11.6 %all-to-all-start.2 = ((bf16[4,64,896]{2,1,0:T(8,128)(2,1)}), bf16[4,64,896]{2,1,0:T(8,128)(2,1)S(1)}, u32[]{:S(2)}, u32[]{:S(2)}) async-start(bf16[4,64,896]{2,1,0:T(8,128)(2,1)} %pad_maximum_fusion.1), calls=%async_computation.2 | async-start | bytes 917504 | tf_op jit(solution)/shard_map/all_to_all | solution.py:289
  95.4 22.2 %copy-start.12 = (f32[896]{0:T(1024)S(1)}, f32[896]{0:T(1024)}, u32[]{:S(2)}) copy-start(f32[896]{0:T(1024)} %param.13) | copy-start | bytes 10756
  112.6 26.6 %all-to-all-start.1 = ((bf16[4,128,896]{2,1,0:T(8,128)(2,1)}), bf16[4,128,896]{2,1,0:T(8,128)(2,1)}, u32[]{:S(2)}, u32[]{:S(2)}) async-start(bf16[4,128,896]{2,1,0:T(8,128)(2,1)} %all_to_all.30), calls=%async_computation.1 | async-start | bytes 1835008 | tf_op jit(solution)/shard_map/all_to_all | solution.py:290
  117.0 34.8 %collective-permute-start.7 = (bf16[896,640]{1,0:T(8,128)(2,1)S(1)}, bf16[896,640]{1,0:T(8,128)(2,1)}, u32[]{:S(2)}, u32[]{:S(2)}) collective-permute-start(bf16[896,640]{1,0:T(8,128)(2,1)S(1)} %constant_dynamic-update-slice_fusion.w0), channel_id=1, source_target_pairs={{0,1},{1,0},{2,3},{3,2},{4,5},{5,4},{6,7},{7,6},{8,9},{9,8},{10,11... | collective-permute-start | bytes 3440648 | tf_op jit(solution)/shard_map/ppermute | solution.py:232
  117.1 34.7 %collective-permute-start.8 = (bf16[896,640]{1,0:T(8,128)(2,1)}, bf16[896,640]{1,0:T(8,128)(2,1)}, u32[]{:S(2)}, u32[]{:S(2)}) collective-permute-start(bf16[896,640]{1,0:T(8,128)(2,1)} %all-gather.2.cloned.1.call-done.w2), channel_id=1, source_target_pairs={{0,1},{1,0},{2,3},{3,2},{4,5},{5,4},{6,7},{7,6},{8,9},{9,8},{10,11... | collective-permute-start | bytes 3440648 | tf_op jit(solution)/shard_map/ppermute | solution.py:232
  117.7 26.2 %copy-start.7 = (bf16[64,896]{1,0:T(8,128)(2,1)}, bf16[64,896]{1,0:T(8,128)(2,1)S(1)}, u32[]{:S(2)}) copy-start(bf16[64,896]{1,0:T(8,128)(2,1)S(1)} %reduce_sum.25) | copy-start | bytes 344068
  139.2 9.2 %all-to-all-start.5 = ((bf16[4,16,896]{2,1,0:T(8,128)(2,1)}), bf16[4,16,896]{2,1,0:T(8,128)(2,1)S(1)}, u32[]{:S(2)}, u32[]{:S(2)}) async-start(bf16[4,16,896]{2,1,0:T(8,128)(2,1)} %bitcast.11), calls=%async_computation.5 | async-start | bytes 229376 | tf_op jit(solution)/shard_map/all_to_all | solution.py:295
  142.5 9.3 %copy-start.3 = (s32[48]{0:T(128)S(1)}, s32[48]{0:T(128)}, u32[]{:S(2)}) copy-start(s32[48]{0:T(128)} %len_ref.3) | copy-start | bytes 580
  148.4 12.8 %all-to-all-start.4 = ((bf16[4,32,896]{2,1,0:T(8,128)(2,1)}), bf16[4,32,896]{2,1,0:T(8,128)(2,1)S(1)}, u32[]{:S(2)}, u32[]{:S(2)}) async-start(bf16[4,32,896]{2,1,0:T(8,128)(2,1)} %bitcast.44), calls=%async_computation.4 | async-start | bytes 458752 | tf_op jit(solution)/shard_map/all_to_all | solution.py:295
  153.1 7.1 %copy-start.6 = (bf16[128,896]{1,0:T(8,128)(2,1)S(1)}, bf16[128,896]{1,0:T(8,128)(2,1)}, u32[]{:S(2)}) copy-start(bf16[128,896]{1,0:T(8,128)(2,1)} %copy-done.5) | copy-start | bytes 688132
  153.1 7.1 %copy-start.8 = (bf16[64,896]{1,0:T(8,128)(2,1)S(1)}, bf16[64,896]{1,0:T(8,128)(2,1)}, u32[]{:S(2)}) copy-start(bf16[64,896]{1,0:T(8,128)(2,1)} %copy-done.7) | copy-start | bytes 344068
  (6 other events, 20.1 us)
Sparse Core Ops, SparseCore 0:
  30.7 41.3 all-gather.1

commit v3 on v2

--- a/solution.py
+++ b/solution.py
@@ -12,10 +12,144 @@
 LANES = 128
 
 
-def talker_kernel(
-    first_row, heads, len_ref, block_ref, sums_ref, gain_ref, w0, w1, w2, w3, kv_ref,
-    new_kv_ref, out_ref, qkv, spread, gathered,
-):
+def down_kernel(counts, planes, cuts, *refs):
+    groups = len(counts)
+    xs, (w, out, x_all, w_all, acc, x_sem, w_sem) = refs[:groups], refs[groups:]
+    first = [planes * sum(counts[:i]) for i in range(groups)]
+    pulls = [
+        pltpu.make_async_copy(
+            xs[i], x_all.at[pl.ds(first[i], planes * counts[i])], x_sem.at[i]
+        )
+        for i in range(groups)
+    ]
+    loads = [
+        pltpu.make_async_copy(w.at[pl.ds(lo, hi - lo)], w_all.at[pl.ds(lo, hi - lo)], w_sem.at[i])
+        for i, (lo, hi) in enumerate(cuts)
+    ]
+    for copy in (*pulls, *loads):
+        copy.start()
+    for copy in pulls:
+        copy.wait()
+    for i, (lo, hi) in enumerate(cuts):
+        loads[i].wait()
+        part = jnp.dot(x_all[:, lo:hi], w_all[lo:hi, :], preferred_element_type=jnp.float32)
+        acc[...] = part if i == 0 else acc[...] + part
+    for i, n in enumerate(counts):
+        row = sum(counts[:i])
+        for p in range(planes):
+            at = first[i] + p * n
+            out[p, row : row + n, :] = acc[at : at + n, :].astype(out.dtype)
+
+
+def down(xs, w, planes):
+    depth, columns = w.shape
+    counts = [x.shape[0] // planes for x in xs]
+    rows = sum(counts)
+    tiles, parts = depth // LANES, 4
+    ends = [LANES * (tiles * i // parts) for i in range(parts)] + [depth]
+    return pl.pallas_call(
+        functools.partial(down_kernel, counts, planes, list(zip(ends[:-1], ends[1:]))),
+        out_shape=jax.ShapeDtypeStruct((planes, rows, columns), jnp.bfloat16),
+        in_specs=[pl.BlockSpec(memory_space=pl.ANY)] * (len(xs) + 1),
+        out_specs=pl.BlockSpec(memory_space=pltpu.VMEM),
+        scratch_shapes=[
+            pltpu.VMEM((planes * rows, depth), jnp.bfloat16),
+            pltpu.VMEM((depth, columns), jnp.bfloat16),
+            pltpu.VMEM((planes * rows, columns), jnp.float32),
+            pltpu.SemaphoreType.DMA((len(xs),)),
+            pltpu.SemaphoreType.DMA((parts,)),
+        ],
+        cost_estimate=pl.CostEstimate(
+            flops=2 * planes * rows * depth * columns,
+            bytes_accessed=2 * depth * (columns + planes * rows),
+            transcendentals=0,
+        ),
+        compiler_params=pltpu.CompilerParams(vmem_limit_bytes=28 * 1024 * 1024),
+    )(*xs, w)
+
+
+def finish_kernel(terms, w, near, far):
+    total = terms[0].astype(jnp.float32)
+    for k in range(1, terms.shape[0]):
+        total = total + terms[k].astype(jnp.float32)
+    features = total.astype(jnp.bfloat16)
+    projected = jnp.dot(features, w[...], preferred_element_type=jnp.float32)
+    projected = projected.astype(jnp.bfloat16)
+    n = features.shape[0] // 2
+    for out, at in ((near, 0), (far, n)):
+        out[0] = features[at : at + n]
+        out[1] = projected[at : at + n]
+
+
+def finish(terms, w_proj):
+    _, rows, columns = terms.shape
+    half = jax.ShapeDtypeStruct((2, rows // 2, columns), jnp.bfloat16)
+    vmem = pl.BlockSpec(memory_space=pltpu.VMEM)
+    return pl.pallas_call(
+        finish_kernel,
+        out_shape=(half, half),
+        in_specs=[vmem, vmem],
+        out_specs=(vmem, vmem),
+        cost_estimate=pl.CostEstimate(
+            flops=2 * rows * columns * columns,
+            bytes_accessed=2 * columns * (columns + 6 * rows),
+            transcendentals=0,
+        ),
+        compiler_params=pltpu.CompilerParams(vmem_limit_bytes=16 * 1024 * 1024),
+    )(terms, w_proj)
+
+
+def prepare_kernel(group, spans, block_ref, gain, w0, w1, w2, w3, *refs):
+    pieces, (home, new_kv, qkv) = refs[: sum(map(len, spans))], refs[sum(map(len, spans)) :]
+    at = 0
+    total = None
+    for e, span in enumerate(spans):
+        terms = []
+        for first, n in span:
+            home[e ^ block_ref[0], first : first + n, :] = pieces[at][0]
+            terms.append(pieces[at][1].astype(jnp.float32))
+            at += 1
+        term = jnp.concatenate(terms, axis=0) if len(terms) > 1 else terms[0]
+        total = term if total is None else total + term
+    scale = lax.rsqrt(jnp.mean(total * total, axis=1, keepdims=True) + 1e-06)
+    normed = (total * scale * gain[...]).astype(jnp.bfloat16)
+    for e, w in enumerate((w0, w1, w2, w3)):
+        made = jnp.dot(normed, w[...], preferred_element_type=jnp.float32)
+        qkv[e ^ block_ref[0]] = made.astype(jnp.bfloat16).astype(jnp.float32)
+    blocks = qkv.shape[0]
+    key, value = group * HEAD_DIM, (group + 1) * HEAD_DIM
+    for g in range(blocks):
+        for place, start in ((g, key), (blocks + g, value)):
+            new_kv[:, place * HEAD_DIM : (place + 1) * HEAD_DIM] = qkv[
+                g, :, start : start + HEAD_DIM
+            ].astype(jnp.bfloat16)
+
+
+def prepare(block, pieces, spans, talker_gain, weights):
+    flat = [p for piece in pieces for p in piece]
+    rows = sum(n for _, n in spans[0])
+    wide, columns = weights[0].shape
+    group = columns // HEAD_DIM - 2
+    vmem = pl.BlockSpec(memory_space=pltpu.VMEM)
+    return pl.pallas_call(
+        functools.partial(prepare_kernel, group, spans),
+        out_shape=(
+            jax.ShapeDtypeStruct((len(weights), rows, flat[0].shape[2]), jnp.bfloat16),
+            jax.ShapeDtypeStruct((rows, 2 * len(weights) * HEAD_DIM), jnp.bfloat16),
+            jax.ShapeDtypeStruct((len(weights), rows, columns), jnp.float32),
+        ),
+        in_specs=[pl.BlockSpec(memory_space=pltpu.SMEM)] + [vmem] * (5 + len(flat)),
+        out_specs=(vmem, vmem, vmem),
+        cost_estimate=pl.CostEstimate(
+            flops=2 * rows * wide * columns * len(weights),
+            bytes_accessed=2 * wide * columns * len(weights),
+            transcendentals=rows,
+        ),
+        compiler_params=pltpu.CompilerParams(vmem_limit_bytes=24 * 1024 * 1024),
+    )(block, talker_gain.reshape(1, wide), *weights, *flat)
+
+
+def attention_kernel(heads, len_ref, qkv, kv_ref, out_ref, spread, gathered):
     step = pl.program_id(0)
     blocks = qkv.shape[0]
     group = heads // blocks
@@ -26,30 +160,11 @@
 
     @pl.when(step == 0)
     def _():
-        talker_in = sums_ref[0].astype(jnp.float32)
-        for k in range(1, sums_ref.shape[0]):
-            talker_in = talker_in + sums_ref[k].astype(jnp.float32)
-        scale = lax.rsqrt(jnp.mean(talker_in * talker_in, axis=1, keepdims=True) + 1e-06)
-        normed = (talker_in * scale * gain_ref[...]).astype(jnp.bfloat16)
-        for e, w in enumerate((w0, w1, w2, w3)):
-            made = jnp.dot(normed, w[...], preferred_element_type=jnp.float32)
-            qkv[e ^ block_ref[0]] = made.astype(jnp.bfloat16).astype(jnp.float32)
-        for g in range(blocks):
-            key, value = group * HEAD_DIM, (group + 1) * HEAD_DIM
-            new_kv_ref[:, g * HEAD_DIM : (g + 1) * HEAD_DIM] = qkv[g, :, key:value].astype(
-                jnp.bfloat16
-            )
-            new_kv_ref[:, width + g * HEAD_DIM : width + (g + 1) * HEAD_DIM] = qkv[
-                g, :, value:
-            ].astype(jnp.bfloat16)
         spread[...] = jnp.zeros_like(spread)
 
-    here = pl.ds(pl.multiple_of(step * ROW_STEP, ROW_STEP), ROW_STEP)
     for h in range(heads):
         g, j = h // group, h % group
-        spread[pl.ds(h, ROW_STEP, stride=slot), :] = qkv[
-            g, here, j * HEAD_DIM : (j + 1) * HEAD_DIM
-        ]
+        spread[pl.ds(h, ROW_STEP, stride=slot), :] = qkv[g, :, j * HEAD_DIM : (j + 1) * HEAD_DIM]
     query = spread[...].T
     lane = lax.broadcasted_iota(jnp.int32, (HEAD_DIM, LANES), 1)
     lane_row, lane_block = lane // slot, lane % slot // group
@@ -68,7 +183,7 @@
         )
     own = jnp.zeros((ROW_STEP, LANES), jnp.float32)
     for g in range(blocks):
-        key = qkv[g, here, group * HEAD_DIM : (group + 1) * HEAD_DIM].astype(jnp.bfloat16)
+        key = qkv[g, :, group * HEAD_DIM : (group + 1) * HEAD_DIM].astype(jnp.bfloat16)
         own = own + jnp.dot(key, by_block[g], preferred_element_type=jnp.float32)
     own_row = lax.broadcasted_iota(jnp.int32, own.shape, 0)
     own = jnp.sum(jnp.where(own_row == lane_row[:ROW_STEP], own, 0.0), axis=0, keepdims=True)
@@ -76,7 +191,7 @@
     scores, own = scores * inv, own * inv
     lens = jnp.zeros((1, LANES), jnp.int32)
     for r in range(ROW_STEP):
-        lens = jnp.where(lane_row[:1] == r, len_ref[first_row + step * ROW_STEP + r], lens)
+        lens = jnp.where(lane_row[:1] == r, len_ref[step * ROW_STEP + r], lens)
     valid = lax.broadcasted_iota(jnp.int32, scores.shape, 0) < lens
     scores = jnp.where(valid, scores, -jnp.inf)
     top = jnp.maximum(jnp.max(scores, axis=0, keepdims=True), own)
@@ -93,11 +208,10 @@
         made = jnp.dot(
             probs[rows], kv_ref[r, :, width:], preferred_element_type=jnp.float32
         )
-        values = qkv.at[:, here]
         ctx = jnp.zeros((slot, HEAD_DIM), jnp.float32)
         value = jnp.zeros((slot, HEAD_DIM), jnp.float32)
         for g in range(blocks):
-            new = values[g, r : r + 1, (group + 1) * HEAD_DIM :]
+            new = qkv[g, r : r + 1, (group + 1) * HEAD_DIM :]
             ctx = jnp.where(row_block == g, made[:, g * HEAD_DIM : (g + 1) * HEAD_DIM], ctx)
             value = jnp.where(row_block == g, new, value)
         gathered[rows, :] = ctx + own_prob[rows] * value
@@ -107,35 +221,23 @@
         ]
 
 
-def talker_rows(first_row, block, sums, talker_gain, weights, kv_len, kv_cache):
-    terms, rows, wide = sums.shape
+def attention(qkv, kv_len, kv_cache):
+    blocks, rows, columns = qkv.shape
     _, cached, kv_width = kv_cache.shape
-    columns = weights[0].shape[1]
-    q_width = len(weights) * columns - kv_width
+    q_width = blocks * columns - kv_width
     heads = q_width // HEAD_DIM
-    offset = first_row // ROW_STEP
-    whole = lambda *shape: pl.BlockSpec(shape, lambda i, *_: (0,) * len(shape))
     return pl.pallas_call(
-        functools.partial(talker_kernel, first_row, heads),
-        out_shape=(
-            jax.ShapeDtypeStruct((rows, kv_width), jnp.bfloat16),
-            jax.ShapeDtypeStruct((rows, q_width), jnp.float32),
-        ),
+        functools.partial(attention_kernel, heads),
+        out_shape=jax.ShapeDtypeStruct((rows, q_width), jnp.float32),
         grid_spec=pltpu.PrefetchScalarGridSpec(
-            num_scalar_prefetch=2,
+            num_scalar_prefetch=1,
             grid=(rows // ROW_STEP,),
             in_specs=[
-                whole(terms, rows, wide),
-                whole(1, wide),
-                *[whole(wide, columns) for _ in weights],
-                pl.BlockSpec((ROW_STEP, cached, kv_width), lambda i, *_: (i + offset, 0, 0)),
+                pl.BlockSpec((blocks, ROW_STEP, columns), lambda i, *_: (0, i, 0)),
+                pl.BlockSpec((ROW_STEP, cached, kv_width), lambda i, *_: (i, 0, 0)),
             ],
-            out_specs=(
-                whole(rows, kv_width),
-                pl.BlockSpec((ROW_STEP, q_width), lambda i, *_: (i, 0)),
-            ),
+            out_specs=pl.BlockSpec((ROW_STEP, q_width), lambda i, *_: (i, 0)),
             scratch_shapes=[
-                pltpu.VMEM((len(weights), rows, columns), jnp.float32),
                 pltpu.VMEM((LANES, HEAD_DIM), jnp.float32),
                 pltpu.VMEM((LANES, HEAD_DIM), jnp.float32),
             ],
@@ -146,7 +248,7 @@
             transcendentals=rows * cached * heads,
         ),
         compiler_params=pltpu.CompilerParams(vmem_limit_bytes=32 * 1024 * 1024),
-    )(kv_len, block, sums, talker_gain.reshape(1, wide), *weights, kv_cache)
+    )(kv_len, qkv, kv_cache)
 
 
 def rms_norm(talker_in, talker_gain):
@@ -226,6 +328,7 @@
 
 
 PLANE = ("section", "rows")
+GROUP = ("mp", "section", "rows")
 
 
 def over_core(x):
@@ -236,8 +339,31 @@
     return lax.ppermute(x, "section", [(0, 1), (1, 0)])
 
 
+def over_groups(x):
+    return lax.ppermute(x, "groups", [(0, 1), (1, 0)])
+
+
+def over_plane(x, e):
+    return lax.ppermute(x, PLANE, [(b, b ^ e) for b in range(4)])
+
+
 def after(x, *others):
     return lax.optimization_barrier((x, *others))[0]
+
+
+def feature_block(w_proj, g, m, c):
+    half = w_proj.shape[0] // 2
+    piece = lax.dynamic_slice_in_dim(w_proj, g * half, half, axis=0)
+    got = lax.ppermute(piece, GROUP, [(b * 4 + b, (b ^ 2) * 4 + b) for b in range(4)])
+    piece = jnp.where(m == c, piece, got)
+    pairs = [(b * 4 + b, (b ^ 1) * 4 + b) for b in range(4)]
+    pairs += [((b ^ 2) * 4 + b, (b ^ 3) * 4 + b) for b in range(4)]
+    got = lax.ppermute(piece, GROUP, pairs)
+    piece = jnp.where((m == c) | (m == c ^ 2), piece, got)
+    other = over_groups(piece)
+    return jnp.concatenate(
+        [jnp.where(g == 0, piece, other), jnp.where(g == 0, other, piece)], axis=0
+    )
 
 
 def four_planes(
@@ -255,54 +381,51 @@
     planes = 4
     owned = kv_cache.shape[0]
     g, m, c = lax.axis_index("groups"), lax.axis_index("mp"), lax.axis_index(PLANE)
-    columns = w_think.shape[1]
     slots = talker_slot[0]
     chunks = [(0, 32), (32, 16)]
 
-    wanted, sent = [], []
+    depth = w_query.shape[0] // (2 * planes)
+    piece = jnp.concatenate(
+        [
+            lax.dynamic_slice_in_dim(w, (g * planes + m) * depth, depth, axis=0)
+            for w in (w_query, w_key, w_value)
+        ],
+        axis=1,
+    )
+    piece = over_section(piece)
+
+    sent = []
     for first, n in chunks:
         plane = jnp.arange(planes, dtype=jnp.int32)[:, None] * owned
         want = (plane + first + jnp.arange(n, dtype=jnp.int32)[None, :]).reshape(-1)
         pick = (want[:, None] == slots[None, :]).astype(jnp.bfloat16)
         rows = jnp.dot(pick, thinker_act, preferred_element_type=jnp.float32)
-        wanted.append(want)
         sent.append(rows.astype(jnp.bfloat16))
-
+    crossed = [over_section(sent[0])]
+    crossed.append(over_section(after(sent[1], crossed[0])))
+
+    near = down([*sent, *[over_core(x) for x in sent]], w_think, planes)
+    near = lax.all_to_all(near, "mp", 0, 0)
+    block_w = feature_block(w_proj, g, m, c)
     mine = jnp.concatenate([w_query, w_key, w_value], axis=1)
-    depth = mine.shape[0] // (2 * planes)
-    piece = lax.dynamic_slice_in_dim(mine, (g * planes + m) * depth, depth, axis=0)
-    piece = over_section(piece)
-    crossed = [over_section(after(sent[0], piece))]
     other = lax.all_gather(piece, ("groups", "mp"), axis=0, tiled=True)
-    crossed.append(over_section(after(sent[1], crossed[0])))
     weights = [mine, over_core(mine), other, over_core(other)]
-
-    def times_w(x):
-        return jnp.dot(x, w_think, preferred_element_type=jnp.float32).astype(jnp.bfloat16)
-
-    near = [(times_w(rows), times_w(over_core(rows))) for rows in sent]
-    returned, kvs, ctxs = [], [], []
-    for (first, n), own, across in zip(chunks, near, crossed):
-        four = [*own, times_w(across), times_w(over_core(across))]
-        swapped = [jnp.where(c & 1, four[e ^ 1], four[e]) for e in range(4)]
-        blocks = jnp.stack([jnp.where(c & 2, swapped[e ^ 2], swapped[e]) for e in range(4)])
-        mixed = lax.all_to_all(blocks, PLANE, 0, 0)
-        terms = lax.all_to_all(mixed, "mp", 0, 0)
-        home = jnp.sum(terms.astype(jnp.float32), axis=0).astype(jnp.bfloat16)
-        returned.append(home)
-        projected = jnp.dot(home, w_proj, preferred_element_type=jnp.float32)
-        projected = projected.astype(jnp.bfloat16).reshape(planes, n, -1)
-        sums = lax.all_to_all(projected, "mp", 0, 0)
-        new_kv, ctx = talker_rows(
-            first, c.reshape(1), sums, talker_gain, weights, kv_len, kv_cache
-        )
-        kvs.append(new_kv)
-        ctxs.append(ctx)
-
-    pick = (slots[:, None] == jnp.concatenate(wanted)[None, :]).astype(jnp.bfloat16)
-    home = jnp.concatenate(returned, axis=0)
-    thinker_out = jnp.dot(pick, home, preferred_element_type=jnp.float32).astype(jnp.bfloat16)
-    return (thinker_out, jnp.concatenate(kvs, axis=0), jnp.concatenate(ctxs, axis=0))
+    own, next_core = finish(near, block_w)
+    pieces = [[own], [over_core(next_core)], [], []]
+    for x in crossed:
+        far = lax.all_to_all(down([x, over_core(x)], w_think, planes), "mp", 0, 0)
+        across = finish(far, block_w)
+        pieces[2].append(over_plane(across[0], 2))
+        pieces[3].append(over_plane(across[1], 3))
+    spans = [[(0, owned)], [(0, owned)], chunks, chunks]
+    home, new_kv, qkv = prepare(c.reshape(1), pieces, spans, talker_gain, weights)
+    home = lax.all_to_all(home, "mp", 0, 0)
+    ctx = attention(qkv, kv_len, kv_cache)
+    pick = (slots[:, None] == jnp.arange(planes * owned)[None, :]).astype(jnp.bfloat16)
+    thinker_out = jnp.dot(
+        pick, home.reshape(planes * owned, -1), preferred_element_type=jnp.float32
+    )
+    return (thinker_out.astype(jnp.bfloat16), new_kv, ctx)
 
 
 def solution(mesh):

time: 183 us -> 160 us (0.87)
  matrix products: 40.1 us -> 3.69 us
  blocking collectives: 34.6 us -> 0 us
  Pallas kernels: 18 us -> 37.6 us
  local copies, waits for them, and re-layouts: 5.17 us -> 21.3 us
  starting transfers between devices: 22 us -> 37.2 us
  waiting for transfers between devices: 42.6 us -> 38.9 us
    dot_general x11 -> x1, matrix products: 37.1 us -> 1.04 us  [four_planes(): jnp.dot(pick, home.reshape(planes * owned, -1), preferred_element_type=jn...]
    all_to_all x2 -> x0, blocking collectives: 34.6 us -> none  [the longest x1 17.4 us: four_planes(): mixed = lax.all_to_all(blocks, PLANE, 0, 0)]
    pallas_call x2 -> x8, Pallas kernels: 18 us -> 37.6 us  [the longest x3 16.8 us: down(): pl.pallas_call(functools.partial(down_kernel, counts, planes, list(zip(en...]
    all_to_all x4, waiting for transfers between devices: 22.4 us -> 5.63 us  [the longest x2 3.08 us: four_planes(): far = lax.all_to_all(down([x, over_core(x)], w_think, planes), 'mp', 0, 0)]
    ppermute x0 -> x7, starting transfers between devices: none -> 15.5 us  [the longest x1 5.51 us: feature_block(): lax.ppermute(piece, GROUP, [(b * 4 + b, (b ^ 2) * 4 + b) for b in range(4)])]
    unnamed x34 -> x40, local copies, waits for them, and re-layouts: 4.92 us -> 16.6 us
    ppermute x3, waiting for transfers between devices: 20.2 us -> 28.3 us  [over_section(): return lax.ppermute(x, 'section', [(0, 1), (1, 0)])]
    select_n x0 -> x3, other arithmetic: none -> 5.98 us  [the longest x1 2.26 us: feature_block(): piece = jnp.where(m == c, piece, got)]
  transfers between devices with their start and end apart: 14 -> 22, of which waited for: 6 -> 7; matrix products, arithmetic and copies ran while one was open for 24% -> 9% of each run, Pallas kernels for 4% -> 21%
where the time goes in v3:
time: 160 us; the launch traced here: 159 us
  waiting for transfers between devices  38.9 us (24%)
  Pallas kernels  37.6 us (24%)
  starting transfers between devices  37.2 us (23%)
  local copies, waits for them, and re-layouts  21.3 us (13%)
  between operations  14.3 us (9%)
  other arithmetic  6.28 us (4%)
  matrix products  3.69 us (2%)
    ppermute x3, waiting for transfers between devices, over_section(): return lax.ppermute(x, 'section', [(0, 1), (1, 0)])  28.3 us
    pallas_call x3, Pallas kernels, down(): pl.pallas_call(functools.partial(down_kernel, counts, planes, list(zip(en...  16.8 us
    unnamed x40, local copies, waits for them, and re-layouts  16.6 us
    pallas_call x1, Pallas kernels, attention(): pl.pallas_call(functools.partial(attention_kernel, heads), out_shape=jax....  13.7 us
    all_to_all x2, starting transfers between devices, four_planes(): far = lax.all_to_all(down([x, over_core(x)], w_think, planes), 'mp', 0, 0)  7.68 us
    ppermute x1, starting transfers between devices, feature_block(): lax.ppermute(piece, GROUP, [(b * 4 + b, (b ^ 2) * 4 + b) for b in range(4)])  5.51 us
    ppermute x4, waiting for transfers between devices, over_plane(): return lax.ppermute(x, PLANE, [(b, b ^ e) for b in range(4)])  4.96 us
    ppermute x1, starting transfers between devices, feature_block(): got = lax.ppermute(piece, GROUP, pairs)  4.86 us
  transfers between devices with their start and end apart: 22, of which 7 were waited for; matrix products, arithmetic and copies ran while one was open for 9% of the time, Pallas kernels for 21%

profile of v3, /device:TPU:0, one launch (start us, length us, event | category | flops | bytes accessed | tf_op | source)
XLA Modules:
  0.0 159.3 jit_solution(9751898116225646473)
XLA Ops:
  10.0 3.0 %collective-permute-start.9 = (bf16[128,4736]{1,0:T(8,128)(2,1)S(1)}, bf16[128,4736]{1,0:T(8,128)(2,1)}, u32[]{:S(2)}, u32[]{:S(2)}) collective-permute-start(bf16[128,4736]{1,0:T(8,128)(2,1)S(1)} %convolution_convert_fusion.refs_0_), channel_id=1, source_target_pairs={{0,2},{2,0},{1,3},{3,1},{4,6},{6,4},{5,7},{7,5},{8,10},{10,8},{9,1... | collective-permute-start | bytes 3637256 | tf_op jit(solution)/shard_map/ppermute | solution.py:339
  13.0 2.1 %constant_dynamic-slice_fusion = bf16[448,896]{1,0:T(8,128)(2,1)} fusion(bf16[896,896]{1,0:T(8,128)(2,1)} %param.12, s32[]{:T(128)S(6)} %select_n.36), kind=kLoop, calls=%fused_computation.22 | loop fusion | bytes 1605636 | tf_op jit(solution)/shard_map/dynamic_slice | solution.py:356
  15.1 5.5 %collective-permute-start.5 = (bf16[448,896]{1,0:T(8,128)(2,1)}, bf16[448,896]{1,0:T(8,128)(2,1)}, u32[]{:S(2)}, u32[]{:S(2)}) collective-permute-start(bf16[448,896]{1,0:T(8,128)(2,1)} %constant_dynamic-slice_fusion), channel_id=1, source_target_pairs={{0,8},{5,13},{10,2},{15,7},{16,24},{21,29},{26,18},{31,23}} | collective-permute-start | bytes 2408456 | tf_op jit(solution)/shard_map/ppermute | solution.py:357
  23.9 18.8 %collective-permute-done.1 = bf16[112,640]{1,0:T(8,128)(2,1)S(1)} collective-permute-done((bf16[112,640]{1,0:T(8,128)(2,1)S(1)}, bf16[112,640]{1,0:T(8,128)(2,1)S(1)}, u32[]{:S(2)}, u32[]{:S(2)}) %collective-permute-start.1) | collective-permute-done | bytes 143392 | tf_op jit(solution)/shard_map/ppermute | solution.py:339
  43.5 2.3 %broadcast_select_fusion = bf16[448,896]{1,0:T(8,128)(2,1)} fusion(bf16[448,896]{1,0:T(8,128)(2,1)} %collective-permute-done.5, pred[]{:T(512)S(6)} %eq.63, bf16[896,896]{1,0:T(8,128)(2,1)} %param.12, s32[]{:T(128)S(6)} %select_n.36), kind=kLoop, calls=%fused_computation.4 | loop fusion | flops 401408 | bytes 2408453 | tf_op jit(solution)/shard_map/jit(_where)/select_n | solution.py:358
  45.8 4.9 %collective-permute-start.6 = (bf16[448,896]{1,0:T(8,128)(2,1)}, bf16[448,896]{1,0:T(8,128)(2,1)}, u32[]{:S(2)}, u32[]{:S(2)}) collective-permute-start(bf16[448,896]{1,0:T(8,128)(2,1)} %broadcast_select_fusion), channel_id=1, source_target_pairs={{0,4},{5,1},{10,14},{15,11},{8,12},{13,9},{2,6},{7,3},{16,20},{21,... | collective-permute-start | bytes 2408456 | tf_op jit(solution)/shard_map/ppermute | solution.py:361
  50.6 3.6 %copy-done.1 = bf16[4736,896]{1,0:T(8,128)(2,1)S(1)} copy-done((bf16[4736,896]{1,0:T(8,128)(2,1)S(1)}, bf16[4736,896]{1,0:T(8,128)(2,1)}, u32[]{:S(2)}) %copy-start.1) | copy-done | bytes 8486936
  54.2 6.7 %shard_map.121 = bf16[4,96,896]{2,1,0:T(8,128)(2,1)S(1)} custom-call(bf16[128,4736]{1,0:T(8,128)(2,1)S(1)} %convolution_convert_fusion.refs_0_, bf16[64,4736]{1,0:T(8,128)(2,1)} %convolution_convert_fusion.1.refs_1_, bf16[128,4736]{1,0:T(8,128)(2,1)} %collective-permute-done.3.refs_2_, bf16[64,4736]{1,0:T(8,128)(2,1)} %collective-permute-done.4.refs_3_, ...), custom_call_target="tpu_custom_call" | custom-call | flops 3258974208 | bytes 12124160 | tf_op jit(solution)/shard_map/pallas_call | solution.py:50
  61.7 4.0 %all-to-all-start = ((bf16[4,96,896]{2,1,0:T(8,128)(2,1)}), bf16[4,96,896]{2,1,0:T(8,128)(2,1)S(1)}, u32[]{:S(2)}, u32[]{:S(2)}) async-start(bf16[4,96,896]{2,1,0:T(8,128)(2,1)} %copy-done.6), calls=%async_computation | async-start | bytes 1376256 | tf_op jit(solution)/shard_map/all_to_all | solution.py:408
  68.1 2.2 %broadcast_select_fusion.1 = bf16[448,896]{1,0:T(8,128)(2,1)} fusion(bf16[448,896]{1,0:T(8,128)(2,1)} %broadcast_select_fusion, bf16[448,896]{1,0:T(8,128)(2,1)} %collective-permute-done.6, pred[]{:T(512)S(6)} %or.3), kind=kLoop, calls=%fused_computation.5 | loop fusion | flops 401408 | bytes 2408449 | tf_op jit(solution)/shard_map/jit(_where)/select_n | solution.py:362
  71.8 9.5 %collective-permute-done.12.refs_0_ = bf16[64,4736]{1,0:T(8,128)(2,1)} collective-permute-done((bf16[64,4736]{1,0:T(8,128)(2,1)}, bf16[64,4736]{1,0:T(8,128)(2,1)}, u32[]{:S(2)}, u32[]{:S(2)}) %collective-permute-start.12) | collective-permute-done | bytes 606240 | tf_op jit(solution)/shard_map/ppermute | solution.py:339
  81.3 3.4 %copy-done.2 = bf16[4736,896]{1,0:T(8,128)(2,1)S(1)} copy-done((bf16[4736,896]{1,0:T(8,128)(2,1)S(1)}, bf16[4736,896]{1,0:T(8,128)(2,1)}, u32[]{:S(2)}) %copy-start.2) | copy-done | bytes 8486936
  84.7 5.8 %shard_map.123 = bf16[4,64,896]{2,1,0:T(8,128)(2,1)} custom-call(bf16[128,4736]{1,0:T(8,128)(2,1)} %collective-permute-done.9.refs_0_, bf16[128,4736]{1,0:T(8,128)(2,1)} %collective-permute-done.10.refs_1_, bf16[4736,896]{1,0:T(8,128)(2,1)S(1)} %copy-done.2), custom_call_target="tpu_custom_call" | custom-call | flops 2172649472 | bytes 10911744 | tf_op jit(solution)/shard_map/pallas_call | solution.py:50
  90.5 2.5 %all-to-all-done.terms = bf16[4,96,896]{2,1,0:T(8,128)(2,1)S(1)} async-done(((bf16[4,96,896]{2,1,0:T(8,128)(2,1)}), bf16[4,96,896]{2,1,0:T(8,128)(2,1)S(1)}, u32[]{:S(2)}, u32[]{:S(2)}) %all-to-all-start) | async-done | bytes 688160 | tf_op jit(solution)/shard_map/all_to_all | solution.py:408
  93.1 3.5 %all-to-all-start.1 = ((bf16[4,64,896]{2,1,0:T(8,128)(2,1)}), bf16[4,64,896]{2,1,0:T(8,128)(2,1)S(1)}, u32[]{:S(2)}, u32[]{:S(2)}) async-start(bf16[4,64,896]{2,1,0:T(8,128)(2,1)} %shard_map.123), calls=%async_computation.1 | async-start | bytes 917504 | tf_op jit(solution)/shard_map/all_to_all | solution.py:416
  98.6 3.4 %copy-done.3 = bf16[4736,896]{1,0:T(8,128)(2,1)S(1)} copy-done((bf16[4736,896]{1,0:T(8,128)(2,1)S(1)}, bf16[4736,896]{1,0:T(8,128)(2,1)}, u32[]{:S(2)}) %copy-start.3) | copy-done | bytes 8486936
  102.0 4.3 %shard_map.125 = bf16[4,32,896]{2,1,0:T(8,128)(2,1)} custom-call(bf16[64,4736]{1,0:T(8,128)(2,1)} %collective-permute-done.12.refs_0_, bf16[64,4736]{1,0:T(8,128)(2,1)} %collective-permute-done.13.refs_1_, bf16[4736,896]{1,0:T(8,128)(2,1)S(1)} %copy-done.3), custom_call_target="tpu_custom_call" | custom-call | flops 1086324736 | bytes 9699328 | tf_op jit(solution)/shard_map/pallas_call | solution.py:50
  106.4 2.8 %all-to-all-done.1.terms = bf16[4,64,896]{2,1,0:T(8,128)(2,1)S(1)} async-done(((bf16[4,64,896]{2,1,0:T(8,128)(2,1)}), bf16[4,64,896]{2,1,0:T(8,128)(2,1)S(1)}, u32[]{:S(2)}, u32[]{:S(2)}) %all-to-all-start.1) | async-done | bytes 458784 | tf_op jit(solution)/shard_map/all_to_all | solution.py:416
  109.1 4.2 %all-to-all-start.2 = ((bf16[4,32,896]{2,1,0:T(8,128)(2,1)}), bf16[4,32,896]{2,1,0:T(8,128)(2,1)}, u32[]{:S(2)}, u32[]{:S(2)}) async-start(bf16[4,32,896]{2,1,0:T(8,128)(2,1)} %shard_map.125), calls=%async_computation.2 | async-start | bytes 458752 | tf_op jit(solution)/shard_map/all_to_all | solution.py:416
  122.4 1.8 %collective-permute-start.14 = (bf16[2,16,896]{2,1,0:T(8,128)(2,1)S(1)}, bf16[2,16,896]{2,1,0:T(8,128)(2,1)S(1)}, u32[]{:S(2)}, u32[]{:S(2)}) collective-permute-start(bf16[2,16,896]{2,1,0:T(8,128)(2,1)S(1)} %get-tuple-element.17), channel_id=1, source_target_pairs={{0,2},{1,3},{2,0},{3,1},{4,6},{5,7},{6,4},{7,5},{8,10},{9,11},{10,... | collective-permute-start | bytes 172040 | tf_op jit(solution)/shard_map/ppermute | solution.py:347
  124.1 4.5 %collective-permute-done.14.refs_3_ = bf16[2,16,896]{2,1,0:T(8,128)(2,1)S(1)} collective-permute-done((bf16[2,16,896]{2,1,0:T(8,128)(2,1)S(1)}, bf16[2,16,896]{2,1,0:T(8,128)(2,1)S(1)}, u32[]{:S(2)}, u32[]{:S(2)}) %collective-permute-start.14) | collective-permute-done | bytes 57376 | tf_op jit(solution)/shard_map/ppermute | solution.py:347
  129.1 3.7 %shard_map.127 = (bf16[4,48,896]{2,1,0:T(8,128)(2,1)}, bf16[48,1024]{1,0:T(8,128)(2,1)}, f32[4,48,640]{2,1,0:T(8,128)S(1)}) custom-call(s32[1]{0:T(128)} %bitcast.1.block_ref, f32[1,896]{1,0:T(1,128)S(1)} %reshape.53.gain, bf16[896,640]{1,0:T(8,128)(2,1)} %constant_dynamic-update-slice_fusion.w0, bf16[896,640]{1,0:T(8,128)(2,1)} %collective-permute-done.w1, ...), custom_call_target="tpu_custom_call" | custom-call | flops 220200960 | bytes 4587520 | tf_op jit(solution)/shard_map/pallas_call | solution.py:134
  132.8 4.9 %all-to-all-start.3 = ((bf16[4,48,896]{2,1,0:T(8,128)(2,1)}), bf16[4,48,896]{2,1,0:T(8,128)(2,1)S(1)}, u32[]{:S(2)}, u32[]{:S(2)}) async-start(bf16[4,48,896]{2,1,0:T(8,128)(2,1)} %get-tuple-element.20), calls=%async_computation.3 | async-start | bytes 688128 | tf_op jit(solution)/shard_map/all_to_all | solution.py:422
  137.6 13.7 %shard_map.128 = f32[48,1536]{1,0:T(8,128)} custom-call(s32[48]{0:T(128)S(1)} %copy-done.12, f32[4,48,640]{2,1,0:T(8,128)S(1)} %get-tuple-element.22.qkv, bf16[48,256,1024]{2,1,0:T(8,128)(2,1)} %kv_ref.1), custom_call_target="tpu_custom_call" | custom-call | flops 75497472 | bytes 25165824 | tf_op jit(solution)/shard_map/pallas_call | solution.py:229
  (88 shorter events, 24.2 us)
Async XLA Ops:
  7.2 90.9 %all-gather.2.cloned.1.call-start = ((), (), s32[]{:S(2)}) async-start(), calls=%async_computation.4 | async-start | bytes 1290240 | tf_op jit(solution)/shard_map/all_gather | solution.py:411
  10.0 33.4 %collective-permute-start.9 = (bf16[128,4736]{1,0:T(8,128)(2,1)S(1)}, bf16[128,4736]{1,0:T(8,128)(2,1)}, u32[]{:S(2)}, u32[]{:S(2)}) collective-permute-start(bf16[128,4736]{1,0:T(8,128)(2,1)S(1)} %convolution_convert_fusion.refs_0_), channel_id=1, source_target_pairs={{0,2},{2,0},{1,3},{3,1},{4,6},{6,4},{5,7},{7,5},{8,10},{10,8},{9,1... | collective-permute-start | bytes 3637256 | tf_op jit(solution)/shard_map/ppermute | solution.py:339
  13.0 37.7 %collective-permute-start.3 = (bf16[128,4736]{1,0:T(8,128)(2,1)S(1)}, bf16[128,4736]{1,0:T(8,128)(2,1)}, u32[]{:S(2)}, u32[]{:S(2)}) collective-permute-start(bf16[128,4736]{1,0:T(8,128)(2,1)S(1)} %convolution_convert_fusion.refs_0_), channel_id=1, source_target_pairs={{0,1},{1,0},{2,3},{3,2},{4,5},{5,4},{6,7},{7,6},{8,9},{9,8},{10,11... | collective-permute-start | bytes 3637256 | tf_op jit(solution)/shard_map/ppermute | solution.py:335
  15.1 28.4 %collective-permute-start.5 = (bf16[448,896]{1,0:T(8,128)(2,1)}, bf16[448,896]{1,0:T(8,128)(2,1)}, u32[]{:S(2)}, u32[]{:S(2)}) collective-permute-start(bf16[448,896]{1,0:T(8,128)(2,1)} %constant_dynamic-slice_fusion), channel_id=1, source_target_pairs={{0,8},{5,13},{10,2},{15,7},{16,24},{21,29},{26,18},{31,23}} | collective-permute-start | bytes 2408456 | tf_op jit(solution)/shard_map/ppermute | solution.py:357
  22.1 28.5 %collective-permute-start.4 = (bf16[64,4736]{1,0:T(8,128)(2,1)}, bf16[64,4736]{1,0:T(8,128)(2,1)}, u32[]{:S(2)}, u32[]{:S(2)}) collective-permute-start(bf16[64,4736]{1,0:T(8,128)(2,1)} %convolution_convert_fusion.1.refs_1_), channel_id=1, source_target_pairs={{0,1},{1,0},{2,3},{3,2},{4,5},{5,4},{6,7},{7,6},{8,9},{9,8},{10,11... | collective-permute-start | bytes 1818632 | tf_op jit(solution)/shard_map/ppermute | solution.py:335
  23.8 18.9 %collective-permute-start.1 = (bf16[112,640]{1,0:T(8,128)(2,1)S(1)}, bf16[112,640]{1,0:T(8,128)(2,1)S(1)}, u32[]{:S(2)}, u32[]{:S(2)}) collective-permute-start(bf16[112,640]{1,0:T(8,128)(2,1)S(1)} %pad_maximum_fusion.1), channel_id=1, source_target_pairs={{0,2},{2,0},{1,3},{3,1},{4,6},{6,4},{5,7},{7,5},{8,10},{10,8},{9,1... | collective-permute-start | bytes 430088 | tf_op jit(solution)/shard_map/ppermute | solution.py:339
  43.4 37.9 %collective-permute-start.10 = (bf16[128,4736]{1,0:T(8,128)(2,1)}, bf16[128,4736]{1,0:T(8,128)(2,1)}, u32[]{:S(2)}, u32[]{:S(2)}) collective-permute-start(bf16[128,4736]{1,0:T(8,128)(2,1)} %collective-permute-done.9.refs_0_), channel_id=1, source_target_pairs={{0,1},{1,0},{2,3},{3,2},{4,5},{5,4},{6,7},{7,6},{8,9},{9,8},{10,11... | collective-permute-start | bytes 3637256 | tf_op jit(solution)/shard_map/ppermute | solution.py:335
  45.8 22.4 %collective-permute-start.6 = (bf16[448,896]{1,0:T(8,128)(2,1)}, bf16[448,896]{1,0:T(8,128)(2,1)}, u32[]{:S(2)}, u32[]{:S(2)}) collective-permute-start(bf16[448,896]{1,0:T(8,128)(2,1)} %broadcast_select_fusion), channel_id=1, source_target_pairs={{0,4},{5,1},{10,14},{15,11},{8,12},{13,9},{2,6},{7,3},{16,20},{21,... | collective-permute-start | bytes 2408456 | tf_op jit(solution)/shard_map/ppermute | solution.py:361
  61.7 31.4 %all-to-all-start = ((bf16[4,96,896]{2,1,0:T(8,128)(2,1)}), bf16[4,96,896]{2,1,0:T(8,128)(2,1)S(1)}, u32[]{:S(2)}, u32[]{:S(2)}) async-start(bf16[4,96,896]{2,1,0:T(8,128)(2,1)} %copy-done.6), calls=%async_computation | async-start | bytes 1376256 | tf_op jit(solution)/shard_map/all_to_all | solution.py:408
  65.7 15.6 %collective-permute-start.12 = (bf16[64,4736]{1,0:T(8,128)(2,1)}, bf16[64,4736]{1,0:T(8,128)(2,1)}, u32[]{:S(2)}, u32[]{:S(2)}) collective-permute-start(bf16[64,4736]{1,0:T(8,128)(2,1)} %convolution_convert_fusion.1.refs_1_), channel_id=1, source_target_pairs={{0,2},{2,0},{1,3},{3,1},{4,6},{6,4},{5,7},{7,5},{8,10},{10,8},{9,1... | collective-permute-start | bytes 1818632 | tf_op jit(solution)/shard_map/ppermute | solution.py:339
  68.1 29.2 %copy-start.15 = (bf16[896,128]{1,0:T(8,128)(2,1)S(1)}, bf16[896,128]{1,0:T(8,128)(2,1)}, u32[]{:S(2)}) copy-start(bf16[896,128]{1,0:T(8,128)(2,1)} %param.16) | copy-start | bytes 688132
  70.3 43.0 %collective-permute-start.7 = (bf16[448,896]{1,0:T(8,128)(2,1)}, bf16[448,896]{1,0:T(8,128)(2,1)}, u32[]{:S(2)}, u32[]{:S(2)}) collective-permute-start(bf16[448,896]{1,0:T(8,128)(2,1)} %broadcast_select_fusion.1), channel_id=1, source_target_pairs={{0,16},{16,0},{1,17},{17,1},{2,18},{18,2},{3,19},{19,3},{4,20},{20... | collective-permute-start | bytes 2408456 | tf_op jit(solution)/shard_map/ppermute | solution.py:343
  81.3 17.3 %collective-permute-start.13 = (bf16[64,4736]{1,0:T(8,128)(2,1)}, bf16[64,4736]{1,0:T(8,128)(2,1)}, u32[]{:S(2)}, u32[]{:S(2)}) collective-permute-start(bf16[64,4736]{1,0:T(8,128)(2,1)} %collective-permute-done.12.refs_0_), channel_id=1, source_target_pairs={{0,1},{1,0},{2,3},{3,2},{4,5},{5,4},{6,7},{7,6},{8,9},{9,8},{10,11... | collective-permute-start | bytes 1818632 | tf_op jit(solution)/shard_map/ppermute | solution.py:335
  93.1 13.3 %copy-start.4 = (bf16[4,96,896]{2,1,0:T(8,128)(2,1)}, bf16[4,96,896]{2,1,0:T(8,128)(2,1)S(1)}, u32[]{:S(2)}) copy-start(bf16[4,96,896]{2,1,0:T(8,128)(2,1)S(1)} %all-to-all-done.terms) | copy-start | bytes 2064388
  93.1 16.1 %all-to-all-start.1 = ((bf16[4,64,896]{2,1,0:T(8,128)(2,1)}), bf16[4,64,896]{2,1,0:T(8,128)(2,1)S(1)}, u32[]{:S(2)}, u32[]{:S(2)}) async-start(bf16[4,64,896]{2,1,0:T(8,128)(2,1)} %shard_map.123), calls=%async_computation.1 | async-start | bytes 917504 | tf_op jit(solution)/shard_map/all_to_all | solution.py:416
  98.1 24.3 %collective-permute-start = (bf16[896,640]{1,0:T(8,128)(2,1)}, bf16[896,640]{1,0:T(8,128)(2,1)}, u32[]{:S(2)}, u32[]{:S(2)}) collective-permute-start(bf16[896,640]{1,0:T(8,128)(2,1)} %constant_dynamic-update-slice_fusion.w0), channel_id=1, source_target_pairs={{0,1},{1,0},{2,3},{3,2},{4,5},{5,4},{6,7},{7,6},{8,9},{9,8},{10,11... | collective-permute-start | bytes 3440648 | tf_op jit(solution)/shard_map/ppermute | solution.py:335
  98.1 31.0 %collective-permute-start.2 = (bf16[896,640]{1,0:T(8,128)(2,1)}, bf16[896,640]{1,0:T(8,128)(2,1)}, u32[]{:S(2)}, u32[]{:S(2)}) collective-permute-start(bf16[896,640]{1,0:T(8,128)(2,1)} %all-gather.2.cloned.1.call-done.w2), channel_id=1, source_target_pairs={{0,1},{1,0},{2,3},{3,2},{4,5},{5,4},{6,7},{7,6},{8,9},{9,8},{10,11... | collective-permute-start | bytes 3440648 | tf_op jit(solution)/shard_map/ppermute | solution.py:335
  109.1 11.8 %all-to-all-start.2 = ((bf16[4,32,896]{2,1,0:T(8,128)(2,1)}), bf16[4,32,896]{2,1,0:T(8,128)(2,1)}, u32[]{:S(2)}, u32[]{:S(2)}) async-start(bf16[4,32,896]{2,1,0:T(8,128)(2,1)} %shard_map.125), calls=%async_computation.2 | async-start | bytes 458752 | tf_op jit(solution)/shard_map/all_to_all | solution.py:416
  117.8 6.4 %collective-permute-start.8 = (bf16[2,48,896]{2,1,0:T(8,128)(2,1)}, bf16[2,48,896]{2,1,0:T(8,128)(2,1)}, u32[]{:S(2)}, u32[]{:S(2)}) collective-permute-start(bf16[2,48,896]{2,1,0:T(8,128)(2,1)} %get-tuple-element.14), channel_id=1, source_target_pairs={{0,1},{1,0},{2,3},{3,2},{4,5},{5,4},{6,7},{7,6},{8,9},{9,8},{10,11... | collective-permute-start | bytes 516104 | tf_op jit(solution)/shard_map/ppermute | solution.py:335
  118.8 10.3 %collective-permute-start.11 = (bf16[2,32,896]{2,1,0:T(8,128)(2,1)}, bf16[2,32,896]{2,1,0:T(8,128)(2,1)S(1)}, u32[]{:S(2)}, u32[]{:S(2)}) collective-permute-start(bf16[2,32,896]{2,1,0:T(8,128)(2,1)} %get-tuple-element.15), channel_id=1, source_target_pairs={{0,2},{1,3},{2,0},{3,1},{4,6},{5,7},{6,4},{7,5},{8,10},{9,11},{10,... | collective-permute-start | bytes 344072 | tf_op jit(solution)/shard_map/ppermute | solution.py:347
  120.3 8.8 %collective-permute-start.15 = (bf16[2,32,896]{2,1,0:T(8,128)(2,1)}, bf16[2,32,896]{2,1,0:T(8,128)(2,1)}, u32[]{:S(2)}, u32[]{:S(2)}) collective-permute-start(bf16[2,32,896]{2,1,0:T(8,128)(2,1)} %get-tuple-element.18), channel_id=1, source_target_pairs={{0,3},{1,2},{2,1},{3,0},{4,7},{5,6},{6,5},{7,4},{8,11},{9,10},{10,... | collective-permute-start | bytes 344072 | tf_op jit(solution)/shard_map/ppermute | solution.py:347
  122.4 6.3 %collective-permute-start.14 = (bf16[2,16,896]{2,1,0:T(8,128)(2,1)S(1)}, bf16[2,16,896]{2,1,0:T(8,128)(2,1)S(1)}, u32[]{:S(2)}, u32[]{:S(2)}) collective-permute-start(bf16[2,16,896]{2,1,0:T(8,128)(2,1)S(1)} %get-tuple-element.17), channel_id=1, source_target_pairs={{0,2},{1,3},{2,0},{3,1},{4,6},{5,7},{6,4},{7,5},{8,10},{9,11},{10,... | collective-permute-start | bytes 172040 | tf_op jit(solution)/shard_map/ppermute | solution.py:347
  124.1 5.0 %collective-permute-start.16 = (bf16[2,16,896]{2,1,0:T(8,128)(2,1)S(1)}, bf16[2,16,896]{2,1,0:T(8,128)(2,1)S(1)}, u32[]{:S(2)}, u32[]{:S(2)}) collective-permute-start(bf16[2,16,896]{2,1,0:T(8,128)(2,1)S(1)} %get-tuple-element.19), channel_id=1, source_target_pairs={{0,3},{1,2},{2,1},{3,0},{4,7},{5,6},{6,5},{7,4},{8,11},{9,10},{10,... | collective-permute-start | bytes 172040 | tf_op jit(solution)/shard_map/ppermute | solution.py:347
  132.8 18.6 %all-to-all-start.3 = ((bf16[4,48,896]{2,1,0:T(8,128)(2,1)}), bf16[4,48,896]{2,1,0:T(8,128)(2,1)S(1)}, u32[]{:S(2)}, u32[]{:S(2)}) async-start(bf16[4,48,896]{2,1,0:T(8,128)(2,1)} %get-tuple-element.20), calls=%async_computation.3 | async-start | bytes 688128 | tf_op jit(solution)/shard_map/all_to_all | solution.py:422
  (17 other events, 78.5 us)
Sparse Core Ops, SparseCore 0:
  43.5 49.9 all-gather.1

commit v4 on v3

--- a/solution.py
+++ b/solution.py
@@ -16,24 +16,25 @@
     groups = len(counts)
     xs, (w, out, x_all, w_all, acc, x_sem, w_sem) = refs[:groups], refs[groups:]
     first = [planes * sum(counts[:i]) for i in range(groups)]
-    pulls = [
-        pltpu.make_async_copy(
-            xs[i], x_all.at[pl.ds(first[i], planes * counts[i])], x_sem.at[i]
-        )
-        for i in range(groups)
-    ]
-    loads = [
-        pltpu.make_async_copy(w.at[pl.ds(lo, hi - lo)], w_all.at[pl.ds(lo, hi - lo)], w_sem.at[i])
-        for i, (lo, hi) in enumerate(cuts)
-    ]
-    for copy in (*pulls, *loads):
-        copy.start()
-    for copy in pulls:
-        copy.wait()
-    for i, (lo, hi) in enumerate(cuts):
-        loads[i].wait()
+    loads = []
+    for s, (lo, hi) in enumerate(cuts):
+        deep = pl.ds(lo, hi - lo)
+        copies = [pltpu.make_async_copy(w.at[deep], w_all.at[deep], w_sem.at[s])]
+        for i in range(groups):
+            here = pl.ds(first[i], planes * counts[i])
+            copies.append(
+                pltpu.make_async_copy(
+                    xs[i].at[:, deep], x_all.at[here, deep], x_sem.at[s, i]
+                )
+            )
+        for copy in copies:
+            copy.start()
+        loads.append(copies)
+    for s, (lo, hi) in enumerate(cuts):
+        for copy in loads[s]:
+            copy.wait()
         part = jnp.dot(x_all[:, lo:hi], w_all[lo:hi, :], preferred_element_type=jnp.float32)
-        acc[...] = part if i == 0 else acc[...] + part
+        acc[...] = part if s == 0 else acc[...] + part
     for i, n in enumerate(counts):
         row = sum(counts[:i])
         for p in range(planes):
@@ -45,7 +46,7 @@
     depth, columns = w.shape
     counts = [x.shape[0] // planes for x in xs]
     rows = sum(counts)
-    tiles, parts = depth // LANES, 4
+    tiles, parts = depth // LANES, 6
     ends = [LANES * (tiles * i // parts) for i in range(parts)] + [depth]
     return pl.pallas_call(
         functools.partial(down_kernel, counts, planes, list(zip(ends[:-1], ends[1:]))),
@@ -56,7 +57,7 @@
             pltpu.VMEM((planes * rows, depth), jnp.bfloat16),
             pltpu.VMEM((depth, columns), jnp.bfloat16),
             pltpu.VMEM((planes * rows, columns), jnp.float32),
-            pltpu.SemaphoreType.DMA((len(xs),)),
+            pltpu.SemaphoreType.DMA((parts, len(xs))),
             pltpu.SemaphoreType.DMA((parts,)),
         ],
         cost_estimate=pl.CostEstimate(
@@ -64,7 +65,7 @@
             bytes_accessed=2 * depth * (columns + planes * rows),
             transcendentals=0,
         ),
-        compiler_params=pltpu.CompilerParams(vmem_limit_bytes=28 * 1024 * 1024),
+        compiler_params=pltpu.CompilerParams(vmem_limit_bytes=56 * 1024 * 1024),
     )(*xs, w)
 
 
@@ -149,76 +150,84 @@
     )(block, talker_gain.reshape(1, wide), *weights, *flat)
 
 
-def attention_kernel(heads, len_ref, qkv, kv_ref, out_ref, spread, gathered):
+def attention_kernel(heads, len_ref, qkv, kv_ref, out_ref, spreads, gathereds):
     step = pl.program_id(0)
     blocks = qkv.shape[0]
     group = heads // blocks
     slot = LANES // ROW_STEP
-    cached = kv_ref.shape[1]
+    rows, cached, _ = kv_ref.shape
     width = blocks * HEAD_DIM
     inv = 1.0 / HEAD_DIM**0.5
 
     @pl.when(step == 0)
     def _():
-        spread[...] = jnp.zeros_like(spread)
-
-    for h in range(heads):
-        g, j = h // group, h % group
-        spread[pl.ds(h, ROW_STEP, stride=slot), :] = qkv[g, :, j * HEAD_DIM : (j + 1) * HEAD_DIM]
-    query = spread[...].T
+        spreads[...] = jnp.zeros_like(spreads)
+
     lane = lax.broadcasted_iota(jnp.int32, (HEAD_DIM, LANES), 1)
     lane_row, lane_block = lane // slot, lane % slot // group
-    by_block = [
-        jnp.where(lane_block == g, query, 0.0).astype(jnp.bfloat16) for g in range(blocks)
-    ]
-
-    scores = jnp.zeros((cached, LANES), jnp.float32)
-    for r in range(ROW_STEP):
-        mine = lane_row == r
-        right = jnp.concatenate(
-            [jnp.where(mine, q, jnp.zeros_like(q)) for q in by_block], axis=0
-        )
-        scores = scores + jnp.dot(
-            kv_ref[r, :, :width], right, preferred_element_type=jnp.float32
-        )
-    own = jnp.zeros((ROW_STEP, LANES), jnp.float32)
-    for g in range(blocks):
-        key = qkv[g, :, group * HEAD_DIM : (group + 1) * HEAD_DIM].astype(jnp.bfloat16)
-        own = own + jnp.dot(key, by_block[g], preferred_element_type=jnp.float32)
-    own_row = lax.broadcasted_iota(jnp.int32, own.shape, 0)
-    own = jnp.sum(jnp.where(own_row == lane_row[:ROW_STEP], own, 0.0), axis=0, keepdims=True)
-
-    scores, own = scores * inv, own * inv
-    lens = jnp.zeros((1, LANES), jnp.int32)
-    for r in range(ROW_STEP):
-        lens = jnp.where(lane_row[:1] == r, len_ref[step * ROW_STEP + r], lens)
-    valid = lax.broadcasted_iota(jnp.int32, scores.shape, 0) < lens
-    scores = jnp.where(valid, scores, -jnp.inf)
-    top = jnp.maximum(jnp.max(scores, axis=0, keepdims=True), own)
-    expo = jnp.where(valid, jnp.exp(scores - top), 0.0)
-    own_expo = jnp.exp(own - top)
-    total = jnp.sum(expo, axis=0, keepdims=True) + own_expo
-    probs = (expo / total).T.astype(jnp.bfloat16)
-    own_prob = (own_expo / total).astype(jnp.bfloat16).astype(jnp.float32)
-    own_prob = jnp.broadcast_to(own_prob, (LANES, LANES)).T
-
     row_block = lax.broadcasted_iota(jnp.int32, (slot, HEAD_DIM), 0) // group
-    for r in range(ROW_STEP):
-        rows = slice(r * slot, (r + 1) * slot)
-        made = jnp.dot(
-            probs[rows], kv_ref[r, :, width:], preferred_element_type=jnp.float32
-        )
-        ctx = jnp.zeros((slot, HEAD_DIM), jnp.float32)
-        value = jnp.zeros((slot, HEAD_DIM), jnp.float32)
+    own_row = lax.broadcasted_iota(jnp.int32, (ROW_STEP, LANES), 0)
+    for part in range(rows // ROW_STEP):
+        at = part * ROW_STEP
+        here = slice(at, at + ROW_STEP)
+        spread, gathered = spreads.at[part], gathereds.at[part]
+        for h in range(heads):
+            g, j = h // group, h % group
+            spread[pl.ds(h, ROW_STEP, stride=slot), :] = qkv[
+                g, here, j * HEAD_DIM : (j + 1) * HEAD_DIM
+            ]
+        query = spread[...].T
+        by_block = [
+            jnp.where(lane_block == g, query, 0.0).astype(jnp.bfloat16) for g in range(blocks)
+        ]
+
+        scores = jnp.zeros((cached, LANES), jnp.float32)
+        for r in range(ROW_STEP):
+            mine = lane_row == r
+            right = jnp.concatenate(
+                [jnp.where(mine, q, jnp.zeros_like(q)) for q in by_block], axis=0
+            )
+            scores = scores + jnp.dot(
+                kv_ref[at + r, :, :width], right, preferred_element_type=jnp.float32
+            )
+        own = jnp.zeros((ROW_STEP, LANES), jnp.float32)
         for g in range(blocks):
-            new = qkv[g, r : r + 1, (group + 1) * HEAD_DIM :]
-            ctx = jnp.where(row_block == g, made[:, g * HEAD_DIM : (g + 1) * HEAD_DIM], ctx)
-            value = jnp.where(row_block == g, new, value)
-        gathered[rows, :] = ctx + own_prob[rows] * value
-    for h in range(heads):
-        out_ref[:, h * HEAD_DIM : (h + 1) * HEAD_DIM] = gathered[
-            pl.ds(h, ROW_STEP, stride=slot), :
-        ]
+            key = qkv[g, here, group * HEAD_DIM : (group + 1) * HEAD_DIM].astype(jnp.bfloat16)
+            own = own + jnp.dot(key, by_block[g], preferred_element_type=jnp.float32)
+        own = jnp.where(own_row == lane_row[:ROW_STEP], own, 0.0)
+        own = jnp.sum(own, axis=0, keepdims=True)
+
+        scores, own = scores * inv, own * inv
+        lens = jnp.zeros((1, LANES), jnp.int32)
+        for r in range(ROW_STEP):
+            lens = jnp.where(lane_row[:1] == r, len_ref[step * rows + at + r], lens)
+        valid = lax.broadcasted_iota(jnp.int32, scores.shape, 0) < lens
+        scores = jnp.where(valid, scores, -jnp.inf)
+        top = jnp.maximum(jnp.max(scores, axis=0, keepdims=True), own)
+        expo = jnp.where(valid, jnp.exp(scores - top), 0.0)
+        own_expo = jnp.exp(own - top)
+        total = jnp.sum(expo, axis=0, keepdims=True) + own_expo
+        probs = (expo / total).T.astype(jnp.bfloat16)
+        own_prob = (own_expo / total).astype(jnp.bfloat16).astype(jnp.float32)
+        own_prob = jnp.broadcast_to(own_prob, (LANES, LANES)).T
+
+        for r in range(ROW_STEP):
+            lanes = slice(r * slot, (r + 1) * slot)
+            made = jnp.dot(
+                probs[lanes], kv_ref[at + r, :, width:], preferred_element_type=jnp.float32
+            )
+            ctx = jnp.zeros((slot, HEAD_DIM), jnp.float32)
+            value = jnp.zeros((slot, HEAD_DIM), jnp.float32)
+            for g in range(blocks):
+                new = qkv[g, at + r : at + r + 1, (group + 1) * HEAD_DIM :]
+                block = made[:, g * HEAD_DIM : (g + 1) * HEAD_DIM]
+                ctx = jnp.where(row_block == g, block, ctx)
+                value = jnp.where(row_block == g, new, value)
+            gathered[lanes, :] = ctx + own_prob[lanes] * value
+        for h in range(heads):
+            out_ref[here, h * HEAD_DIM : (h + 1) * HEAD_DIM] = gathered[
+                pl.ds(h, ROW_STEP, stride=slot), :
+            ]
 
 
 def attention(qkv, kv_len, kv_cache):
@@ -226,20 +235,21 @@
     _, cached, kv_width = kv_cache.shape
     q_width = blocks * columns - kv_width
     heads = q_width // HEAD_DIM
+    step = 2 * ROW_STEP
     return pl.pallas_call(
         functools.partial(attention_kernel, heads),
         out_shape=jax.ShapeDtypeStruct((rows, q_width), jnp.float32),
         grid_spec=pltpu.PrefetchScalarGridSpec(
             num_scalar_prefetch=1,
-            grid=(rows // ROW_STEP,),
+            grid=(rows // step,),
             in_specs=[
-                pl.BlockSpec((blocks, ROW_STEP, columns), lambda i, *_: (0, i, 0)),
-                pl.BlockSpec((ROW_STEP, cached, kv_width), lambda i, *_: (i, 0, 0)),
+                pl.BlockSpec((blocks, step, columns), lambda i, *_: (0, i, 0)),
+                pl.BlockSpec((step, cached, kv_width), lambda i, *_: (i, 0, 0)),
             ],
-            out_specs=pl.BlockSpec((ROW_STEP, q_width), lambda i, *_: (i, 0)),
+            out_specs=pl.BlockSpec((step, q_width), lambda i, *_: (i, 0)),
             scratch_shapes=[
-                pltpu.VMEM((LANES, HEAD_DIM), jnp.float32),
-                pltpu.VMEM((LANES, HEAD_DIM), jnp.float32),
+                pltpu.VMEM((step // ROW_STEP, LANES, HEAD_DIM), jnp.float32),
+                pltpu.VMEM((step // ROW_STEP, LANES, HEAD_DIM), jnp.float32),
             ],
         ),
         cost_estimate=pl.CostEstimate(
@@ -247,7 +257,7 @@
             bytes_accessed=2 * rows * cached * kv_width,
             transcendentals=rows * cached * heads,
         ),
-        compiler_params=pltpu.CompilerParams(vmem_limit_bytes=32 * 1024 * 1024),
+        compiler_params=pltpu.CompilerParams(vmem_limit_bytes=40 * 1024 * 1024),
     )(kv_len, qkv, kv_cache)
 
 
@@ -351,15 +361,15 @@
     return lax.optimization_barrier((x, *others))[0]
 
 
-def feature_block(w_proj, g, m, c):
+def feature_block(w_proj, g, m, c, first, second):
     half = w_proj.shape[0] // 2
     piece = lax.dynamic_slice_in_dim(w_proj, g * half, half, axis=0)
     got = lax.ppermute(piece, GROUP, [(b * 4 + b, (b ^ 2) * 4 + b) for b in range(4)])
-    piece = jnp.where(m == c, piece, got)
+    piece = jnp.where(m == c, piece, after(got, first))
     pairs = [(b * 4 + b, (b ^ 1) * 4 + b) for b in range(4)]
     pairs += [((b ^ 2) * 4 + b, (b ^ 3) * 4 + b) for b in range(4)]
     got = lax.ppermute(piece, GROUP, pairs)
-    piece = jnp.where((m == c) | (m == c ^ 2), piece, got)
+    piece = jnp.where((m == c) | (m == c ^ 2), piece, after(got, second))
     other = over_groups(piece)
     return jnp.concatenate(
         [jnp.where(g == 0, piece, other), jnp.where(g == 0, other, piece)], axis=0
@@ -384,16 +394,6 @@
     slots = talker_slot[0]
     chunks = [(0, 32), (32, 16)]
 
-    depth = w_query.shape[0] // (2 * planes)
-    piece = jnp.concatenate(
-        [
-            lax.dynamic_slice_in_dim(w, (g * planes + m) * depth, depth, axis=0)
-            for w in (w_query, w_key, w_value)
-        ],
-        axis=1,
-    )
-    piece = over_section(piece)
-
     sent = []
     for first, n in chunks:
         plane = jnp.arange(planes, dtype=jnp.int32)[:, None] * owned
@@ -401,20 +401,25 @@
         pick = (want[:, None] == slots[None, :]).astype(jnp.bfloat16)
         rows = jnp.dot(pick, thinker_act, preferred_element_type=jnp.float32)
         sent.append(rows.astype(jnp.bfloat16))
+
     crossed = [over_section(sent[0])]
-    crossed.append(over_section(after(sent[1], crossed[0])))
-
     near = down([*sent, *[over_core(x) for x in sent]], w_think, planes)
-    near = lax.all_to_all(near, "mp", 0, 0)
-    block_w = feature_block(w_proj, g, m, c)
+    crossed.append(over_section(after(sent[1], near)))
+    near_terms = lax.all_to_all(near, "mp", 0, 0)
+    far = [down([crossed[0], over_core(crossed[0])], w_think, planes)]
+    late = after(crossed[1], far[0])
+    far.append(down([late, over_core(late)], w_think, planes))
+    far_terms = [lax.all_to_all(x, "mp", 0, 0) for x in far]
+
+    block_w = feature_block(w_proj, g, m, c, near, far[0])
     mine = jnp.concatenate([w_query, w_key, w_value], axis=1)
-    other = lax.all_gather(piece, ("groups", "mp"), axis=0, tiled=True)
+    other = over_section(after(mine, late))
     weights = [mine, over_core(mine), other, over_core(other)]
-    own, next_core = finish(near, block_w)
+
+    own, next_core = finish(near_terms, block_w)
     pieces = [[own], [over_core(next_core)], [], []]
-    for x in crossed:
-        far = lax.all_to_all(down([x, over_core(x)], w_think, planes), "mp", 0, 0)
-        across = finish(far, block_w)
+    for terms in far_terms:
+        across = finish(terms, block_w)
         pieces[2].append(over_plane(across[0], 2))
         pieces[3].append(over_plane(across[1], 3))
     spans = [[(0, owned)], [(0, owned)], chunks, chunks]

time: 160 us -> 149 us (0.931)
  local copies, waits for them, and re-layouts: 21.3 us -> 7.61 us
  between operations: 14.3 us -> 0.86 us
  starting transfers between devices: 37.2 us -> 46.2 us
  waiting for transfers between devices: 38.9 us -> 45.8 us
  Pallas kernels: 37.6 us -> 40.3 us
  other arithmetic: 6.28 us -> 4.13 us
    unnamed x40 -> x30, local copies, waits for them, and re-layouts: 16.6 us -> 4.57 us
    ppermute x3, waiting for transfers between devices: 28.3 us -> 40.1 us  [over_section(): return lax.ppermute(x, 'section', [(0, 1), (1, 0)])]
    ppermute x3, starting transfers between devices: 4.57 us -> 12.9 us  [over_section(): return lax.ppermute(x, 'section', [(0, 1), (1, 0)])]
    ppermute x7, starting transfers between devices: 0.59 us -> 5.7 us  [over_core(): return lax.ppermute(x, 'rows', [(0, 1), (1, 0)])]
    all_to_all x3, waiting for transfers between devices: 5.62 us -> 1.44 us  [the longest x2 1.44 us: four_planes(): far_terms = [lax.all_to_all(x, 'mp', 0, 0) for x in far]]
    pallas_call x3, Pallas kernels: 16.8 us -> 19.9 us  [down(): pl.pallas_call(functools.partial(down_kernel, counts, planes, list(zip(en...]
    ppermute x1, starting transfers between devices: 4.86 us -> 2.25 us  [feature_block(): got = lax.ppermute(piece, GROUP, pairs)]
    select_n x2, other arithmetic: 4.44 us -> 2.31 us  [the longest x1 1.33 us: feature_block(): piece = jnp.where(m == c, piece, after(got, first))]
  transfers between devices with their start and end apart: 22 -> 21, of which waited for: 7 -> 5; matrix products, arithmetic and copies ran while one was open for 9% -> 7% of each run, Pallas kernels for 21% -> 24%
where the time goes in v4:
time: 149 us
  starting transfers between devices  46.2 us (31%)
  waiting for transfers between devices  45.8 us (31%)
  Pallas kernels  40.3 us (27%)
  local copies, waits for them, and re-layouts  7.61 us (5%)
  other arithmetic  4.13 us (3%)
  matrix products  3.65 us (2%)
    ppermute x3, waiting for transfers between devices, over_section(): return lax.ppermute(x, 'section', [(0, 1), (1, 0)])  40.1 us
    pallas_call x3, Pallas kernels, down(): pl.pallas_call(functools.partial(down_kernel, counts, planes, list(zip(en...  19.9 us
    pallas_call x1, Pallas kernels, attention(): pl.pallas_call(functools.partial(attention_kernel, heads), out_shape=jax....  13.1 us
    ppermute x3, starting transfers between devices, over_section(): return lax.ppermute(x, 'section', [(0, 1), (1, 0)])  12.9 us
    all_to_all x2, starting transfers between devices, four_planes(): far_terms = [lax.all_to_all(x, 'mp', 0, 0) for x in far]  8.19 us
    ppermute x7, starting transfers between devices, over_core(): return lax.ppermute(x, 'rows', [(0, 1), (1, 0)])  5.7 us
    ppermute x1, starting transfers between devices, feature_block(): lax.ppermute(piece, GROUP, [(b * 4 + b, (b ^ 2) * 4 + b) for b in range(4)])  5.63 us
    unnamed x30, local copies, waits for them, and re-layouts  4.57 us
  transfers between devices with their start and end apart: 21, of which 5 were waited for; matrix products, arithmetic and copies ran while one was open for 7% of the time, Pallas kernels for 24%

profile of v4, /device:TPU:0, one launch (start us, length us, event | category | flops | bytes accessed | tf_op | source)
XLA Modules:
  0.0 148.5 jit_solution(8718963825152102458)
XLA Ops:
  3.4 3.0 %collective-permute-start.4 = (bf16[128,4736]{1,0:T(8,128)(2,1)S(1)}, bf16[128,4736]{1,0:T(8,128)(2,1)}, u32[]{:S(2)}, u32[]{:S(2)}) collective-permute-start(bf16[128,4736]{1,0:T(8,128)(2,1)S(1)} %convolution_convert_fusion.refs_0_), channel_id=1, source_target_pairs={{0,2},{2,0},{1,3},{3,1},{4,6},{6,4},{5,7},{7,5},{8,10},{10,8},{9,1... | collective-permute-start | bytes 3637256 | tf_op jit(solution)/shard_map/ppermute | solution.py:349
  6.5 1.4 convolution_convert_fusion.1.refs_1_
  8.4 24.7 %collective-permute-done.4.refs_0_ = bf16[128,4736]{1,0:T(8,128)(2,1)} collective-permute-done((bf16[128,4736]{1,0:T(8,128)(2,1)S(1)}, bf16[128,4736]{1,0:T(8,128)(2,1)}, u32[]{:S(2)}, u32[]{:S(2)}) %collective-permute-start.4) | collective-permute-done | bytes 1212448 | tf_op jit(solution)/shard_map/ppermute | solution.py:349
  33.1 2.1 %constant_dynamic-slice_fusion = bf16[448,896]{1,0:T(8,128)(2,1)} fusion(bf16[896,896]{1,0:T(8,128)(2,1)} %param.12, s32[]{:T(128)S(6)} %select_n.30), kind=kLoop, calls=%fused_computation.22 | loop fusion | bytes 1605636 | tf_op jit(solution)/shard_map/dynamic_slice | solution.py:366
  35.2 5.6 %collective-permute-start.8 = (bf16[448,896]{1,0:T(8,128)(2,1)}, bf16[448,896]{1,0:T(8,128)(2,1)}, u32[]{:S(2)}, u32[]{:S(2)}) collective-permute-start(bf16[448,896]{1,0:T(8,128)(2,1)} %constant_dynamic-slice_fusion), channel_id=1, source_target_pairs={{0,8},{5,13},{10,2},{15,7},{16,24},{21,29},{26,18},{31,23}} | collective-permute-start | bytes 2408456 | tf_op jit(solution)/shard_map/ppermute | solution.py:367
  41.8 8.3 %shard_map.121 = bf16[4,96,896]{2,1,0:T(8,128)(2,1)} custom-call(bf16[128,4736]{1,0:T(8,128)(2,1)} %copy-done.8, bf16[64,4736]{1,0:T(8,128)(2,1)} %convolution_convert_fusion.1.refs_1_, bf16[128,4736]{1,0:T(8,128)(2,1)} %collective-permute-done.1.refs_2_, bf16[64,4736]{1,0:T(8,128)(2,1)} %collective-permute-done.2.refs_3_, bf16[4736,896]{1,0:T(8,128)(2,1)} %refs_2_.3), custom_call_target="tpu_custom_call" | custom-call | flops 3258974208 | bytes 12124160 | tf_op jit(solution)/shard_map/pallas_call | solution.py:51
  51.0 1.3 broadcast_select_fusion
  52.3 2.2 %collective-permute-start.9 = (bf16[448,896]{1,0:T(8,128)(2,1)S(1)}, bf16[448,896]{1,0:T(8,128)(2,1)}, u32[]{:S(2)}, u32[]{:S(2)}) collective-permute-start(bf16[448,896]{1,0:T(8,128)(2,1)S(1)} %broadcast_select_fusion), channel_id=1, source_target_pairs={{0,4},{5,1},{10,14},{15,11},{8,12},{13,9},{2,6},{7,3},{16,20},{21,... | collective-permute-start | bytes 2408456 | tf_op jit(solution)/shard_map/ppermute | solution.py:371
  55.3 3.9 %all-to-all-start = ((bf16[4,96,896]{2,1,0:T(8,128)(2,1)}), bf16[4,96,896]{2,1,0:T(8,128)(2,1)S(1)}, u32[]{:S(2)}, u32[]{:S(2)}) async-start(bf16[4,96,896]{2,1,0:T(8,128)(2,1)} %shard_map.121), calls=%async_computation | async-start | bytes 1376256 | tf_op jit(solution)/shard_map/all_to_all | solution.py:408
  59.2 6.3 %shard_map.122 = bf16[4,64,896]{2,1,0:T(8,128)(2,1)} custom-call(bf16[128,4736]{1,0:T(8,128)(2,1)} %collective-permute-done.4.refs_0_, bf16[128,4736]{1,0:T(8,128)(2,1)} %collective-permute-done.5.refs_1_, bf16[4736,896]{1,0:T(8,128)(2,1)} %refs_2_.3), custom_call_target="tpu_custom_call" | custom-call | flops 2172649472 | bytes 10911744 | tf_op jit(solution)/shard_map/pallas_call | solution.py:51
  65.6 9.8 %collective-permute-start.6 = (bf16[896,640]{1,0:T(8,128)(2,1)}, bf16[896,640]{1,0:T(8,128)(2,1)}, u32[]{:S(2)}, u32[]{:S(2)}) collective-permute-start(bf16[896,640]{1,0:T(8,128)(2,1)} %constant_dynamic-update-slice_fusion.w0), channel_id=1, source_target_pairs={{0,2},{2,0},{1,3},{3,1},{4,6},{6,4},{5,7},{7,5},{8,10},{10,8},{9,1... | collective-permute-start | bytes 3440648 | tf_op jit(solution)/shard_map/ppermute | solution.py:349
  76.4 1.5 %collective-permute-start.10 = (bf16[448,896]{1,0:T(8,128)(2,1)}, bf16[448,896]{1,0:T(8,128)(2,1)}, u32[]{:S(2)}, u32[]{:S(2)}) collective-permute-start(bf16[448,896]{1,0:T(8,128)(2,1)} %broadcast_select_fusion.1), channel_id=1, source_target_pairs={{0,16},{16,0},{1,17},{17,1},{2,18},{18,2},{3,19},{19,3},{4,20},{20... | collective-permute-start | bytes 2408456 | tf_op jit(solution)/shard_map/ppermute | solution.py:353
  77.9 4.7 %collective-permute-start.13 = (bf16[64,4736]{1,0:T(8,128)(2,1)}, bf16[64,4736]{1,0:T(8,128)(2,1)}, u32[]{:S(2)}, u32[]{:S(2)}) collective-permute-start(bf16[64,4736]{1,0:T(8,128)(2,1)} %collective-permute-done.3.refs_0_), channel_id=1, source_target_pairs={{0,1},{1,0},{2,3},{3,2},{4,5},{5,4},{6,7},{7,6},{8,9},{9,8},{10,11... | collective-permute-start | bytes 1818632 | tf_op jit(solution)/shard_map/ppermute | solution.py:345
  82.6 3.5 %all-to-all-start.1 = ((bf16[4,64,896]{2,1,0:T(8,128)(2,1)}), bf16[4,64,896]{2,1,0:T(8,128)(2,1)S(1)}, u32[]{:S(2)}, u32[]{:S(2)}) async-start(bf16[4,64,896]{2,1,0:T(8,128)(2,1)} %shard_map.122), calls=%async_computation.1 | async-start | bytes 917504 | tf_op jit(solution)/shard_map/all_to_all | solution.py:412
  86.4 15.4 %collective-permute-done.6.w2 = bf16[896,640]{1,0:T(8,128)(2,1)} collective-permute-done((bf16[896,640]{1,0:T(8,128)(2,1)}, bf16[896,640]{1,0:T(8,128)(2,1)}, u32[]{:S(2)}, u32[]{:S(2)}) %collective-permute-start.6) | collective-permute-done | bytes 1146912 | tf_op jit(solution)/shard_map/ppermute | solution.py:349
  101.9 5.2 %shard_map.125 = bf16[4,32,896]{2,1,0:T(8,128)(2,1)} custom-call(bf16[64,4736]{1,0:T(8,128)(2,1)} %collective-permute-done.3.refs_0_, bf16[64,4736]{1,0:T(8,128)(2,1)} %collective-permute-done.13.refs_1_, bf16[4736,896]{1,0:T(8,128)(2,1)} %refs_2_.3), custom_call_target="tpu_custom_call" | custom-call | flops 1086324736 | bytes 9699328 | tf_op jit(solution)/shard_map/pallas_call | solution.py:51
  107.2 4.7 %all-to-all-start.2 = ((bf16[4,32,896]{2,1,0:T(8,128)(2,1)}), bf16[4,32,896]{2,1,0:T(8,128)(2,1)}, u32[]{:S(2)}, u32[]{:S(2)}) async-start(bf16[4,32,896]{2,1,0:T(8,128)(2,1)} %shard_map.125), calls=%async_computation.2 | async-start | bytes 458752 | tf_op jit(solution)/shard_map/all_to_all | solution.py:412
  111.9 1.5 %broadcast_select_fusion.3 = (bf16[448,896]{1,0:T(8,128)(2,1)S(1)}, bf16[448,896]{1,0:T(8,128)(2,1)S(1)}) fusion(bf16[448,896]{1,0:T(8,128)(2,1)} %broadcast_select_fusion.1, bf16[448,896]{1,0:T(8,128)(2,1)} %collective-permute-done.10, pred[]{:T(512)S(6)} %eq.62), kind=kLoop, calls=%fused_computation.7 | loop fusion | flops 802816 | bytes 3211265 | tf_op jit(solution)/shard_map/jit(_where)/select_n | solution.py:375
  117.5 1.9 %collective-permute-start.15 = (bf16[2,32,896]{2,1,0:T(8,128)(2,1)}, bf16[2,32,896]{2,1,0:T(8,128)(2,1)}, u32[]{:S(2)}, u32[]{:S(2)}) collective-permute-start(bf16[2,32,896]{2,1,0:T(8,128)(2,1)} %get-tuple-element.26), channel_id=1, source_target_pairs={{0,3},{1,2},{2,1},{3,0},{4,7},{5,6},{6,5},{7,4},{8,11},{9,10},{10,... | collective-permute-start | bytes 344072 | tf_op jit(solution)/shard_map/ppermute | solution.py:357
  119.4 1.4 all-to-all-done.2.terms
  123.2 3.5 %collective-permute-done.14.refs_3_ = bf16[2,16,896]{2,1,0:T(8,128)(2,1)S(1)} collective-permute-done((bf16[2,16,896]{2,1,0:T(8,128)(2,1)S(1)}, bf16[2,16,896]{2,1,0:T(8,128)(2,1)S(1)}, u32[]{:S(2)}, u32[]{:S(2)}) %collective-permute-start.14) | collective-permute-done | bytes 57376 | tf_op jit(solution)/shard_map/ppermute | solution.py:357
  126.8 4.0 %shard_map.127 = (bf16[4,48,896]{2,1,0:T(8,128)(2,1)}, bf16[48,1024]{1,0:T(8,128)(2,1)}, f32[4,48,640]{2,1,0:T(8,128)S(1)}) custom-call(s32[1]{0:T(128)} %bitcast.1.block_ref, f32[1,896]{1,0:T(1,128)S(1)} %reshape.53.gain, bf16[896,640]{1,0:T(8,128)(2,1)} %constant_dynamic-update-slice_fusion.w0, bf16[896,640]{1,0:T(8,128)(2,1)} %collective-permute-done.w1, ...), custom_call_target="tpu_custom_call" | custom-call | flops 220200960 | bytes 4587520 | tf_op jit(solution)/shard_map/pallas_call | solution.py:135
  130.8 3.6 %all-to-all-start.3 = ((bf16[4,48,896]{2,1,0:T(8,128)(2,1)}), bf16[4,48,896]{2,1,0:T(8,128)(2,1)S(1)}, u32[]{:S(2)}, u32[]{:S(2)}) async-start(bf16[4,48,896]{2,1,0:T(8,128)(2,1)} %get-tuple-element.28), calls=%async_computation.3 | async-start | bytes 688128 | tf_op jit(solution)/shard_map/all_to_all | solution.py:427
  134.4 13.1 %shard_map.128 = f32[48,1536]{1,0:T(8,128)} custom-call(s32[48]{0:T(128)S(1)} %copy-done.7, f32[4,48,640]{2,1,0:T(8,128)S(1)} %get-tuple-element.30.qkv, bf16[48,256,1024]{2,1,0:T(8,128)(2,1)} %kv_ref.1), custom_call_target="tpu_custom_call" | custom-call | flops 75497472 | bytes 25165824 | tf_op jit(solution)/shard_map/pallas_call | solution.py:239
  (72 shorter events, 14.9 us)
Async XLA Ops:
  3.3 31.9 %copy-start.8 = (bf16[128,4736]{1,0:T(8,128)(2,1)}, bf16[128,4736]{1,0:T(8,128)(2,1)S(1)}, u32[]{:S(2)}) copy-start(bf16[128,4736]{1,0:T(8,128)(2,1)S(1)} %convolution_convert_fusion.refs_0_) | copy-start | bytes 3637252
  3.4 29.8 %collective-permute-start.4 = (bf16[128,4736]{1,0:T(8,128)(2,1)S(1)}, bf16[128,4736]{1,0:T(8,128)(2,1)}, u32[]{:S(2)}, u32[]{:S(2)}) collective-permute-start(bf16[128,4736]{1,0:T(8,128)(2,1)S(1)} %convolution_convert_fusion.refs_0_), channel_id=1, source_target_pairs={{0,2},{2,0},{1,3},{3,1},{4,6},{6,4},{5,7},{7,5},{8,10},{10,8},{9,1... | collective-permute-start | bytes 3637256 | tf_op jit(solution)/shard_map/ppermute | solution.py:349
  6.4 35.5 %collective-permute-start.1 = (bf16[128,4736]{1,0:T(8,128)(2,1)S(1)}, bf16[128,4736]{1,0:T(8,128)(2,1)}, u32[]{:S(2)}, u32[]{:S(2)}) collective-permute-start(bf16[128,4736]{1,0:T(8,128)(2,1)S(1)} %convolution_convert_fusion.refs_0_), channel_id=1, source_target_pairs={{0,1},{1,0},{2,3},{3,2},{4,5},{5,4},{6,7},{7,6},{8,9},{9,8},{10,11... | collective-permute-start | bytes 3637256 | tf_op jit(solution)/shard_map/ppermute | solution.py:345
  7.9 33.9 %collective-permute-start.2 = (bf16[64,4736]{1,0:T(8,128)(2,1)}, bf16[64,4736]{1,0:T(8,128)(2,1)}, u32[]{:S(2)}, u32[]{:S(2)}) collective-permute-start(bf16[64,4736]{1,0:T(8,128)(2,1)} %convolution_convert_fusion.1.refs_1_), channel_id=1, source_target_pairs={{0,1},{1,0},{2,3},{3,2},{4,5},{5,4},{6,7},{7,6},{8,9},{9,8},{10,11... | collective-permute-start | bytes 1818632 | tf_op jit(solution)/shard_map/ppermute | solution.py:345
  8.4 32.4 %copy-start.9 = (bf16[896,384]{1,0:T(8,128)(2,1)S(1)}, bf16[896,384]{1,0:T(8,128)(2,1)}, u32[]{:S(2)}) copy-start(bf16[896,384]{1,0:T(8,128)(2,1)} %param.14) | copy-start | bytes 2064388
  33.1 26.1 %collective-permute-start.5 = (bf16[128,4736]{1,0:T(8,128)(2,1)}, bf16[128,4736]{1,0:T(8,128)(2,1)}, u32[]{:S(2)}, u32[]{:S(2)}) collective-permute-start(bf16[128,4736]{1,0:T(8,128)(2,1)} %collective-permute-done.4.refs_0_), channel_id=1, source_target_pairs={{0,1},{1,0},{2,3},{3,2},{4,5},{5,4},{6,7},{7,6},{8,9},{9,8},{10,11... | collective-permute-start | bytes 3637256 | tf_op jit(solution)/shard_map/ppermute | solution.py:345
  35.2 15.7 %collective-permute-start.8 = (bf16[448,896]{1,0:T(8,128)(2,1)}, bf16[448,896]{1,0:T(8,128)(2,1)}, u32[]{:S(2)}, u32[]{:S(2)}) collective-permute-start(bf16[448,896]{1,0:T(8,128)(2,1)} %constant_dynamic-slice_fusion), channel_id=1, source_target_pairs={{0,8},{5,13},{10,2},{15,7},{16,24},{21,29},{26,18},{31,23}} | collective-permute-start | bytes 2408456 | tf_op jit(solution)/shard_map/ppermute | solution.py:367
  50.2 15.4 %collective-permute-start.3 = (bf16[64,4736]{1,0:T(8,128)(2,1)}, bf16[64,4736]{1,0:T(8,128)(2,1)}, u32[]{:S(2)}, u32[]{:S(2)}) collective-permute-start(bf16[64,4736]{1,0:T(8,128)(2,1)} %convolution_convert_fusion.1.refs_1_), channel_id=1, source_target_pairs={{0,2},{2,0},{1,3},{3,1},{4,6},{6,4},{5,7},{7,5},{8,10},{10,8},{9,1... | collective-permute-start | bytes 1818632 | tf_op jit(solution)/shard_map/ppermute | solution.py:349
  52.3 23.1 %collective-permute-start.9 = (bf16[448,896]{1,0:T(8,128)(2,1)S(1)}, bf16[448,896]{1,0:T(8,128)(2,1)}, u32[]{:S(2)}, u32[]{:S(2)}) collective-permute-start(bf16[448,896]{1,0:T(8,128)(2,1)S(1)} %broadcast_select_fusion), channel_id=1, source_target_pairs={{0,4},{5,1},{10,14},{15,11},{8,12},{13,9},{2,6},{7,3},{16,20},{21,... | collective-permute-start | bytes 2408456 | tf_op jit(solution)/shard_map/ppermute | solution.py:371
  55.3 27.2 %all-to-all-start = ((bf16[4,96,896]{2,1,0:T(8,128)(2,1)}), bf16[4,96,896]{2,1,0:T(8,128)(2,1)S(1)}, u32[]{:S(2)}, u32[]{:S(2)}) async-start(bf16[4,96,896]{2,1,0:T(8,128)(2,1)} %shard_map.121), calls=%async_computation | async-start | bytes 1376256 | tf_op jit(solution)/shard_map/all_to_all | solution.py:408
  65.6 36.2 %collective-permute-start.6 = (bf16[896,640]{1,0:T(8,128)(2,1)}, bf16[896,640]{1,0:T(8,128)(2,1)}, u32[]{:S(2)}, u32[]{:S(2)}) collective-permute-start(bf16[896,640]{1,0:T(8,128)(2,1)} %constant_dynamic-update-slice_fusion.w0), channel_id=1, source_target_pairs={{0,2},{2,0},{1,3},{3,1},{4,6},{6,4},{5,7},{7,5},{8,10},{10,8},{9,1... | collective-permute-start | bytes 3440648 | tf_op jit(solution)/shard_map/ppermute | solution.py:349
  76.4 35.5 %collective-permute-start.10 = (bf16[448,896]{1,0:T(8,128)(2,1)}, bf16[448,896]{1,0:T(8,128)(2,1)}, u32[]{:S(2)}, u32[]{:S(2)}) collective-permute-start(bf16[448,896]{1,0:T(8,128)(2,1)} %broadcast_select_fusion.1), channel_id=1, source_target_pairs={{0,16},{16,0},{1,17},{17,1},{2,18},{18,2},{3,19},{19,3},{4,20},{20... | collective-permute-start | bytes 2408456 | tf_op jit(solution)/shard_map/ppermute | solution.py:353
  77.9 24.0 %collective-permute-start.13 = (bf16[64,4736]{1,0:T(8,128)(2,1)}, bf16[64,4736]{1,0:T(8,128)(2,1)}, u32[]{:S(2)}, u32[]{:S(2)}) collective-permute-start(bf16[64,4736]{1,0:T(8,128)(2,1)} %collective-permute-done.3.refs_0_), channel_id=1, source_target_pairs={{0,1},{1,0},{2,3},{3,2},{4,5},{5,4},{6,7},{7,6},{8,9},{9,8},{10,11... | collective-permute-start | bytes 1818632 | tf_op jit(solution)/shard_map/ppermute | solution.py:345
  82.6 24.6 %copy-start.1 = (bf16[4,96,896]{2,1,0:T(8,128)(2,1)}, bf16[4,96,896]{2,1,0:T(8,128)(2,1)S(1)}, u32[]{:S(2)}) copy-start(bf16[4,96,896]{2,1,0:T(8,128)(2,1)S(1)} %all-to-all-done.terms) | copy-start | bytes 2064388
  82.6 24.6 %all-to-all-start.1 = ((bf16[4,64,896]{2,1,0:T(8,128)(2,1)}), bf16[4,64,896]{2,1,0:T(8,128)(2,1)S(1)}, u32[]{:S(2)}, u32[]{:S(2)}) async-start(bf16[4,64,896]{2,1,0:T(8,128)(2,1)} %shard_map.122), calls=%async_computation.1 | async-start | bytes 917504 | tf_op jit(solution)/shard_map/all_to_all | solution.py:412
  86.0 36.1 %collective-permute-start = (bf16[896,640]{1,0:T(8,128)(2,1)}, bf16[896,640]{1,0:T(8,128)(2,1)}, u32[]{:S(2)}, u32[]{:S(2)}) collective-permute-start(bf16[896,640]{1,0:T(8,128)(2,1)} %constant_dynamic-update-slice_fusion.w0), channel_id=1, source_target_pairs={{0,1},{1,0},{2,3},{3,2},{4,5},{5,4},{6,7},{7,6},{8,9},{9,8},{10,11... | collective-permute-start | bytes 3440648 | tf_op jit(solution)/shard_map/ppermute | solution.py:345
  101.8 24.9 %collective-permute-start.7 = (bf16[896,640]{1,0:T(8,128)(2,1)}, bf16[896,640]{1,0:T(8,128)(2,1)}, u32[]{:S(2)}, u32[]{:S(2)}) collective-permute-start(bf16[896,640]{1,0:T(8,128)(2,1)} %collective-permute-done.6.w2), channel_id=1, source_target_pairs={{0,1},{1,0},{2,3},{3,2},{4,5},{5,4},{6,7},{7,6},{8,9},{9,8},{10,11... | collective-permute-start | bytes 3440648 | tf_op jit(solution)/shard_map/ppermute | solution.py:345
  107.2 13.7 %all-to-all-start.2 = ((bf16[4,32,896]{2,1,0:T(8,128)(2,1)}), bf16[4,32,896]{2,1,0:T(8,128)(2,1)}, u32[]{:S(2)}, u32[]{:S(2)}) async-start(bf16[4,32,896]{2,1,0:T(8,128)(2,1)} %shard_map.125), calls=%async_computation.2 | async-start | bytes 458752 | tf_op jit(solution)/shard_map/all_to_all | solution.py:412
  115.5 7.0 %collective-permute-start.12 = (bf16[2,32,896]{2,1,0:T(8,128)(2,1)}, bf16[2,32,896]{2,1,0:T(8,128)(2,1)S(1)}, u32[]{:S(2)}, u32[]{:S(2)}) collective-permute-start(bf16[2,32,896]{2,1,0:T(8,128)(2,1)} %get-tuple-element.24), channel_id=1, source_target_pairs={{0,2},{1,3},{2,0},{3,1},{4,6},{5,7},{6,4},{7,5},{8,10},{9,11},{10,... | collective-permute-start | bytes 344072 | tf_op jit(solution)/shard_map/ppermute | solution.py:357
  117.5 5.7 %collective-permute-start.11 = (bf16[2,48,896]{2,1,0:T(8,128)(2,1)}, bf16[2,48,896]{2,1,0:T(8,128)(2,1)}, u32[]{:S(2)}, u32[]{:S(2)}) collective-permute-start(bf16[2,48,896]{2,1,0:T(8,128)(2,1)} %get-tuple-element.23), channel_id=1, source_target_pairs={{0,1},{1,0},{2,3},{3,2},{4,5},{5,4},{6,7},{7,6},{8,9},{9,8},{10,11... | collective-permute-start | bytes 516104 | tf_op jit(solution)/shard_map/ppermute | solution.py:345
  117.5 5.7 %collective-permute-start.15 = (bf16[2,32,896]{2,1,0:T(8,128)(2,1)}, bf16[2,32,896]{2,1,0:T(8,128)(2,1)}, u32[]{:S(2)}, u32[]{:S(2)}) collective-permute-start(bf16[2,32,896]{2,1,0:T(8,128)(2,1)} %get-tuple-element.26), channel_id=1, source_target_pairs={{0,3},{1,2},{2,1},{3,0},{4,7},{5,6},{6,5},{7,4},{8,11},{9,10},{10,... | collective-permute-start | bytes 344072 | tf_op jit(solution)/shard_map/ppermute | solution.py:357
  122.2 4.6 %collective-permute-start.14 = (bf16[2,16,896]{2,1,0:T(8,128)(2,1)S(1)}, bf16[2,16,896]{2,1,0:T(8,128)(2,1)S(1)}, u32[]{:S(2)}, u32[]{:S(2)}) collective-permute-start(bf16[2,16,896]{2,1,0:T(8,128)(2,1)S(1)} %get-tuple-element.25), channel_id=1, source_target_pairs={{0,2},{1,3},{2,0},{3,1},{4,6},{5,7},{6,4},{7,5},{8,10},{9,11},{10,... | collective-permute-start | bytes 172040 | tf_op jit(solution)/shard_map/ppermute | solution.py:357
  122.5 4.2 %collective-permute-start.16 = (bf16[2,16,896]{2,1,0:T(8,128)(2,1)S(1)}, bf16[2,16,896]{2,1,0:T(8,128)(2,1)S(1)}, u32[]{:S(2)}, u32[]{:S(2)}) collective-permute-start(bf16[2,16,896]{2,1,0:T(8,128)(2,1)S(1)} %get-tuple-element.27), channel_id=1, source_target_pairs={{0,3},{1,2},{2,1},{3,0},{4,7},{5,6},{6,5},{7,4},{8,11},{9,10},{10,... | collective-permute-start | bytes 172040 | tf_op jit(solution)/shard_map/ppermute | solution.py:357
  130.8 16.8 %all-to-all-start.3 = ((bf16[4,48,896]{2,1,0:T(8,128)(2,1)}), bf16[4,48,896]{2,1,0:T(8,128)(2,1)S(1)}, u32[]{:S(2)}, u32[]{:S(2)}) async-start(bf16[4,48,896]{2,1,0:T(8,128)(2,1)} %get-tuple-element.28), calls=%async_computation.3 | async-start | bytes 688128 | tf_op jit(solution)/shard_map/all_to_all | solution.py:427
  (11 other events, 50.1 us)

commit v5 on v4

--- a/solution.py
+++ b/solution.py
@@ -10,30 +10,20 @@
 HEAD_DIM = 128
 ROW_STEP = 8
 LANES = 128
+DOWN_LIMIT = 28
+PAGES = 2
 
 
 def down_kernel(counts, planes, cuts, *refs):
     groups = len(counts)
-    xs, (w, out, x_all, w_all, acc, x_sem, w_sem) = refs[:groups], refs[groups:]
+    xs, (w, out, x_part, acc) = refs[:groups], refs[groups:]
     first = [planes * sum(counts[:i]) for i in range(groups)]
-    loads = []
     for s, (lo, hi) in enumerate(cuts):
-        deep = pl.ds(lo, hi - lo)
-        copies = [pltpu.make_async_copy(w.at[deep], w_all.at[deep], w_sem.at[s])]
         for i in range(groups):
-            here = pl.ds(first[i], planes * counts[i])
-            copies.append(
-                pltpu.make_async_copy(
-                    xs[i].at[:, deep], x_all.at[here, deep], x_sem.at[s, i]
-                )
-            )
-        for copy in copies:
-            copy.start()
-        loads.append(copies)
-    for s, (lo, hi) in enumerate(cuts):
-        for copy in loads[s]:
-            copy.wait()
-        part = jnp.dot(x_all[:, lo:hi], w_all[lo:hi, :], preferred_element_type=jnp.float32)
+            x_part[first[i] : first[i] + planes * counts[i], : hi - lo] = xs[i][:, lo:hi]
+        part = jnp.dot(
+            x_part[:, : hi - lo], w[lo:hi, :], preferred_element_type=jnp.float32
+        )
         acc[...] = part if s == 0 else acc[...] + part
     for i, n in enumerate(counts):
         row = sum(counts[:i])
@@ -46,26 +36,25 @@
     depth, columns = w.shape
     counts = [x.shape[0] // planes for x in xs]
     rows = sum(counts)
-    tiles, parts = depth // LANES, 6
+    tiles, parts = depth // LANES, 4
     ends = [LANES * (tiles * i // parts) for i in range(parts)] + [depth]
+    most = max(hi - lo for lo, hi in zip(ends[:-1], ends[1:]))
+    vmem = pl.BlockSpec(memory_space=pltpu.VMEM)
     return pl.pallas_call(
         functools.partial(down_kernel, counts, planes, list(zip(ends[:-1], ends[1:]))),
         out_shape=jax.ShapeDtypeStruct((planes, rows, columns), jnp.bfloat16),
-        in_specs=[pl.BlockSpec(memory_space=pl.ANY)] * (len(xs) + 1),
-        out_specs=pl.BlockSpec(memory_space=pltpu.VMEM),
+        in_specs=[vmem] * (len(xs) + 1),
+        out_specs=vmem,
         scratch_shapes=[
-            pltpu.VMEM((planes * rows, depth), jnp.bfloat16),
-            pltpu.VMEM((depth, columns), jnp.bfloat16),
+            pltpu.VMEM((planes * rows, most), jnp.bfloat16),
             pltpu.VMEM((planes * rows, columns), jnp.float32),
-            pltpu.SemaphoreType.DMA((parts, len(xs))),
-            pltpu.SemaphoreType.DMA((parts,)),
         ],
         cost_estimate=pl.CostEstimate(
             flops=2 * planes * rows * depth * columns,
             bytes_accessed=2 * depth * (columns + planes * rows),
             transcendentals=0,
         ),
-        compiler_params=pltpu.CompilerParams(vmem_limit_bytes=56 * 1024 * 1024),
+        compiler_params=pltpu.CompilerParams(vmem_limit_bytes=DOWN_LIMIT * 1024 * 1024),
     )(*xs, w)
 
 
@@ -100,16 +89,68 @@
     )(terms, w_proj)
 
 
-def prepare_kernel(group, spans, block_ref, gain, w0, w1, w2, w3, *refs):
-    pieces, (home, new_kv, qkv) = refs[: sum(map(len, spans))], refs[sum(map(len, spans)) :]
+def collect_kernel(spans, block_ref, *refs):
+    pieces, home = refs[:-1], refs[-1]
+    at = 0
+    for e, span in enumerate(spans):
+        for first, n in span:
+            home[e ^ block_ref[0], first : first + n, :] = pieces[at][0]
+            at += 1
+
+
+def collect(block, pieces, spans):
+    flat = [p for piece in pieces for p in piece]
+    rows = sum(n for _, n in spans[0])
+    vmem = pl.BlockSpec(memory_space=pltpu.VMEM)
+    return pl.pallas_call(
+        functools.partial(collect_kernel, spans),
+        out_shape=jax.ShapeDtypeStruct((len(spans), rows, flat[0].shape[2]), jnp.bfloat16),
+        in_specs=[pl.BlockSpec(memory_space=pltpu.SMEM)] + [vmem] * len(flat),
+        out_specs=vmem,
+        compiler_params=pltpu.CompilerParams(vmem_limit_bytes=16 * 1024 * 1024),
+    )(block, *flat)
+
+
+def page_copies(len_ref, kv_hbm, kv_ref, sem, r):
+    page = kv_ref.shape[1] // PAGES
+    out = []
+    for p in range(PAGES):
+        at = pl.ds(p * page, page)
+        copy = pltpu.make_async_copy(kv_hbm.at[r, at], kv_ref.at[r, at], sem.at[r, p])
+        out.append((copy, len_ref[r] > p * page))
+    return out
+
+
+def talker_kernel(spans, block_ref, len_ref, gain, w0, w1, w2, w3, *refs):
+    count = sum(map(len, spans))
+    pieces, (kv_hbm, new_kv, out_ref, kv_ref, sem, qkv, spreads, gathereds) = (
+        refs[:count],
+        refs[count:],
+    )
+    blocks = qkv.shape[0]
+    rows, cached, kv_width = kv_ref.shape
+    width = kv_width // 2
+    page = cached // PAGES
+    heads = out_ref.shape[1] // HEAD_DIM
+    group = heads // blocks
+    slot = LANES // ROW_STEP
+    sets = spreads.shape[0]
+    key, value = group * HEAD_DIM, (group + 1) * HEAD_DIM
+    inv = 1.0 / HEAD_DIM**0.5
+
+    @pl.loop(0, rows)
+    def _(r):
+        for p, (copy, needed) in enumerate(page_copies(len_ref, kv_hbm, kv_ref, sem, r)):
+            if p == 0:
+                copy.start()
+            else:
+                pl.when(needed)(copy.start)
+
     at = 0
     total = None
-    for e, span in enumerate(spans):
-        terms = []
-        for first, n in span:
-            home[e ^ block_ref[0], first : first + n, :] = pieces[at][0]
-            terms.append(pieces[at][1].astype(jnp.float32))
-            at += 1
+    for span in spans:
+        terms = [pieces[at + i][1].astype(jnp.float32) for i in range(len(span))]
+        at += len(span)
         term = jnp.concatenate(terms, axis=0) if len(terms) > 1 else terms[0]
         total = term if total is None else total + term
     scale = lax.rsqrt(jnp.mean(total * total, axis=1, keepdims=True) + 1e-06)
@@ -117,60 +158,20 @@
     for e, w in enumerate((w0, w1, w2, w3)):
         made = jnp.dot(normed, w[...], preferred_element_type=jnp.float32)
         qkv[e ^ block_ref[0]] = made.astype(jnp.bfloat16).astype(jnp.float32)
-    blocks = qkv.shape[0]
-    key, value = group * HEAD_DIM, (group + 1) * HEAD_DIM
     for g in range(blocks):
         for place, start in ((g, key), (blocks + g, value)):
             new_kv[:, place * HEAD_DIM : (place + 1) * HEAD_DIM] = qkv[
                 g, :, start : start + HEAD_DIM
             ].astype(jnp.bfloat16)
 
-
-def prepare(block, pieces, spans, talker_gain, weights):
-    flat = [p for piece in pieces for p in piece]
-    rows = sum(n for _, n in spans[0])
-    wide, columns = weights[0].shape
-    group = columns // HEAD_DIM - 2
-    vmem = pl.BlockSpec(memory_space=pltpu.VMEM)
-    return pl.pallas_call(
-        functools.partial(prepare_kernel, group, spans),
-        out_shape=(
-            jax.ShapeDtypeStruct((len(weights), rows, flat[0].shape[2]), jnp.bfloat16),
-            jax.ShapeDtypeStruct((rows, 2 * len(weights) * HEAD_DIM), jnp.bfloat16),
-            jax.ShapeDtypeStruct((len(weights), rows, columns), jnp.float32),
-        ),
-        in_specs=[pl.BlockSpec(memory_space=pltpu.SMEM)] + [vmem] * (5 + len(flat)),
-        out_specs=(vmem, vmem, vmem),
-        cost_estimate=pl.CostEstimate(
-            flops=2 * rows * wide * columns * len(weights),
-            bytes_accessed=2 * wide * columns * len(weights),
-            transcendentals=rows,
-        ),
-        compiler_params=pltpu.CompilerParams(vmem_limit_bytes=24 * 1024 * 1024),
-    )(block, talker_gain.reshape(1, wide), *weights, *flat)
-
-
-def attention_kernel(heads, len_ref, qkv, kv_ref, out_ref, spreads, gathereds):
-    step = pl.program_id(0)
-    blocks = qkv.shape[0]
-    group = heads // blocks
-    slot = LANES // ROW_STEP
-    rows, cached, _ = kv_ref.shape
-    width = blocks * HEAD_DIM
-    inv = 1.0 / HEAD_DIM**0.5
-
-    @pl.when(step == 0)
-    def _():
-        spreads[...] = jnp.zeros_like(spreads)
-
+    spreads[...] = jnp.zeros_like(spreads)
     lane = lax.broadcasted_iota(jnp.int32, (HEAD_DIM, LANES), 1)
     lane_row, lane_block = lane // slot, lane % slot // group
     row_block = lax.broadcasted_iota(jnp.int32, (slot, HEAD_DIM), 0) // group
     own_row = lax.broadcasted_iota(jnp.int32, (ROW_STEP, LANES), 0)
-    for part in range(rows // ROW_STEP):
-        at = part * ROW_STEP
-        here = slice(at, at + ROW_STEP)
-        spread, gathered = spreads.at[part], gathereds.at[part]
+
+    def one_set(at, spread, gathered):
+        here = pl.ds(at, ROW_STEP)
         for h in range(heads):
             g, j = h // group, h % group
             spread[pl.ds(h, ROW_STEP, stride=slot), :] = qkv[
@@ -192,15 +193,15 @@
             )
         own = jnp.zeros((ROW_STEP, LANES), jnp.float32)
         for g in range(blocks):
-            key = qkv[g, here, group * HEAD_DIM : (group + 1) * HEAD_DIM].astype(jnp.bfloat16)
-            own = own + jnp.dot(key, by_block[g], preferred_element_type=jnp.float32)
+            new_key = qkv[g, here, key:value].astype(jnp.bfloat16)
+            own = own + jnp.dot(new_key, by_block[g], preferred_element_type=jnp.float32)
         own = jnp.where(own_row == lane_row[:ROW_STEP], own, 0.0)
         own = jnp.sum(own, axis=0, keepdims=True)
 
         scores, own = scores * inv, own * inv
         lens = jnp.zeros((1, LANES), jnp.int32)
         for r in range(ROW_STEP):
-            lens = jnp.where(lane_row[:1] == r, len_ref[step * rows + at + r], lens)
+            lens = jnp.where(lane_row[:1] == r, len_ref[at + r], lens)
         valid = lax.broadcasted_iota(jnp.int32, scores.shape, 0) < lens
         scores = jnp.where(valid, scores, -jnp.inf)
         top = jnp.maximum(jnp.max(scores, axis=0, keepdims=True), own)
@@ -210,6 +211,7 @@
         probs = (expo / total).T.astype(jnp.bfloat16)
         own_prob = (own_expo / total).astype(jnp.bfloat16).astype(jnp.float32)
         own_prob = jnp.broadcast_to(own_prob, (LANES, LANES)).T
+        value_rows = qkv.at[:, here, value:]
 
         for r in range(ROW_STEP):
             lanes = slice(r * slot, (r + 1) * slot)
@@ -217,48 +219,72 @@
                 probs[lanes], kv_ref[at + r, :, width:], preferred_element_type=jnp.float32
             )
             ctx = jnp.zeros((slot, HEAD_DIM), jnp.float32)
-            value = jnp.zeros((slot, HEAD_DIM), jnp.float32)
+            new = jnp.zeros((slot, HEAD_DIM), jnp.float32)
             for g in range(blocks):
-                new = qkv[g, at + r : at + r + 1, (group + 1) * HEAD_DIM :]
                 block = made[:, g * HEAD_DIM : (g + 1) * HEAD_DIM]
                 ctx = jnp.where(row_block == g, block, ctx)
-                value = jnp.where(row_block == g, new, value)
-            gathered[lanes, :] = ctx + own_prob[lanes] * value
+                new = jnp.where(row_block == g, value_rows[g, r : r + 1, :], new)
+            gathered[lanes, :] = ctx + own_prob[lanes] * new
         for h in range(heads):
             out_ref[here, h * HEAD_DIM : (h + 1) * HEAD_DIM] = gathered[
                 pl.ds(h, ROW_STEP, stride=slot), :
             ]
 
-
-def attention(qkv, kv_len, kv_cache):
-    blocks, rows, columns = qkv.shape
-    _, cached, kv_width = kv_cache.shape
+    @pl.loop(0, rows // (sets * ROW_STEP))
+    def _(i):
+        first = pl.multiple_of(i * sets * ROW_STEP, sets * ROW_STEP)
+        for k in range(sets * ROW_STEP):
+            r = first + k
+            for p, (copy, needed) in enumerate(page_copies(len_ref, kv_hbm, kv_ref, sem, r)):
+                if p == 0:
+                    copy.wait()
+                    continue
+                pl.when(needed)(copy.wait)
+
+                @pl.when(jnp.logical_not(needed))
+                def _(p=p, r=r):
+                    kv_ref[r, p * page : (p + 1) * page, :] = jnp.zeros(
+                        (page, kv_width), kv_ref.dtype
+                    )
+
+        for k in range(sets):
+            at = pl.multiple_of(first + k * ROW_STEP, ROW_STEP)
+            one_set(at, spreads.at[k], gathereds.at[k])
+
+
+def talker(block, pieces, spans, talker_gain, weights, kv_len, kv_cache):
+    flat = [p for piece in pieces for p in piece]
+    rows, cached, kv_width = kv_cache.shape
+    wide, columns = weights[0].shape
+    blocks = len(weights)
     q_width = blocks * columns - kv_width
-    heads = q_width // HEAD_DIM
-    step = 2 * ROW_STEP
+    sets = 2
+    vmem = pl.BlockSpec(memory_space=pltpu.VMEM)
+    smem = pl.BlockSpec(memory_space=pltpu.SMEM)
     return pl.pallas_call(
-        functools.partial(attention_kernel, heads),
-        out_shape=jax.ShapeDtypeStruct((rows, q_width), jnp.float32),
-        grid_spec=pltpu.PrefetchScalarGridSpec(
-            num_scalar_prefetch=1,
-            grid=(rows // step,),
-            in_specs=[
-                pl.BlockSpec((blocks, step, columns), lambda i, *_: (0, i, 0)),
-                pl.BlockSpec((step, cached, kv_width), lambda i, *_: (i, 0, 0)),
-            ],
-            out_specs=pl.BlockSpec((step, q_width), lambda i, *_: (i, 0)),
-            scratch_shapes=[
-                pltpu.VMEM((step // ROW_STEP, LANES, HEAD_DIM), jnp.float32),
-                pltpu.VMEM((step // ROW_STEP, LANES, HEAD_DIM), jnp.float32),
-            ],
+        functools.partial(talker_kernel, spans),
+        out_shape=(
+            jax.ShapeDtypeStruct((rows, kv_width), jnp.bfloat16),
+            jax.ShapeDtypeStruct((rows, q_width), jnp.float32),
         ),
+        in_specs=[smem, smem]
+        + [vmem] * (1 + blocks + len(flat))
+        + [pl.BlockSpec(memory_space=pltpu.HBM)],
+        out_specs=(vmem, vmem),
+        scratch_shapes=[
+            pltpu.VMEM((rows, cached, kv_width), jnp.bfloat16),
+            pltpu.SemaphoreType.DMA((rows, PAGES)),
+            pltpu.VMEM((blocks, rows, columns), jnp.float32),
+            pltpu.VMEM((sets, LANES, HEAD_DIM), jnp.float32),
+            pltpu.VMEM((sets, LANES, HEAD_DIM), jnp.float32),
+        ],
         cost_estimate=pl.CostEstimate(
             flops=4 * rows * cached * q_width,
             bytes_accessed=2 * rows * cached * kv_width,
-            transcendentals=rows * cached * heads,
+            transcendentals=rows * cached * q_width // HEAD_DIM,
         ),
-        compiler_params=pltpu.CompilerParams(vmem_limit_bytes=40 * 1024 * 1024),
-    )(kv_len, qkv, kv_cache)
+        compiler_params=pltpu.CompilerParams(vmem_limit_bytes=46 * 1024 * 1024),
+    )(block, kv_len, talker_gain.reshape(1, wide), *weights, *flat, kv_cache)
 
 
 def rms_norm(talker_in, talker_gain):
@@ -404,8 +430,9 @@
 
     crossed = [over_section(sent[0])]
     near = down([*sent, *[over_core(x) for x in sent]], w_think, planes)
+    near_terms = lax.all_to_all(near, "mp", 0, 0)
+    crossed[0] = after(crossed[0], near)
     crossed.append(over_section(after(sent[1], near)))
-    near_terms = lax.all_to_all(near, "mp", 0, 0)
     far = [down([crossed[0], over_core(crossed[0])], w_think, planes)]
     late = after(crossed[1], far[0])
     far.append(down([late, over_core(late)], w_think, planes))
@@ -414,7 +441,6 @@
     block_w = feature_block(w_proj, g, m, c, near, far[0])
     mine = jnp.concatenate([w_query, w_key, w_value], axis=1)
     other = over_section(after(mine, late))
-    weights = [mine, over_core(mine), other, over_core(other)]
 
     own, next_core = finish(near_terms, block_w)
     pieces = [[own], [over_core(next_core)], [], []]
@@ -422,10 +448,11 @@
         across = finish(terms, block_w)
         pieces[2].append(over_plane(across[0], 2))
         pieces[3].append(over_plane(across[1], 3))
+    other = after(other, across[0])
+    weights = [mine, over_core(mine), other, over_core(other)]
     spans = [[(0, owned)], [(0, owned)], chunks, chunks]
-    home, new_kv, qkv = prepare(c.reshape(1), pieces, spans, talker_gain, weights)
-    home = lax.all_to_all(home, "mp", 0, 0)
-    ctx = attention(qkv, kv_len, kv_cache)
+    home = lax.all_to_all(collect(c.reshape(1), pieces, spans), "mp", 0, 0)
+    new_kv, ctx = talker(c.reshape(1), pieces, spans, talker_gain, weights, kv_len, kv_cache)
     pick = (slots[:, None] == jnp.arange(planes * owned)[None, :]).astype(jnp.bfloat16)
     thinker_out = jnp.dot(
         pick, home.reshape(planes * owned, -1), preferred_element_type=jnp.float32

time: 149 us -> 141 us (0.946)
  starting transfers between devices: 46.2 us -> 31.8 us
  blocking collectives: 0 us -> 14.1 us
  waiting for transfers between devices: 45.8 us -> 35.9 us
  Pallas kernels: 40.3 us -> 32.5 us
  local copies, waits for them, and re-layouts: 7.61 us -> 14.3 us
  other arithmetic: 4.13 us -> 6.44 us
    ppermute x3, waiting for transfers between devices: 40.1 us -> 10.7 us  [over_section(): return lax.ppermute(x, 'section', [(0, 1), (1, 0)])]
    all_to_all x0 -> x1, blocking collectives: none -> 14.1 us  [four_planes(): far_terms = [lax.all_to_all(x, 'mp', 0, 0) for x in far]]
    all_to_all x1, waiting for transfers between devices: 0.01 us -> 10.9 us  [four_planes(): home = lax.all_to_all(collect(c.reshape(1), pieces, spans), 'mp', 0, 0)]
    ppermute x3, starting transfers between devices: 12.9 us -> 4.59 us  [over_section(): return lax.ppermute(x, 'section', [(0, 1), (1, 0)])]
    unnamed x30 -> x32, local copies, waits for them, and re-layouts: 4.57 us -> 11.3 us
    pallas_call x3, Pallas kernels: 19.9 us -> 13.5 us  [down(): pl.pallas_call(functools.partial(down_kernel, counts, planes, list(zip(en...]
    ppermute x4, waiting for transfers between devices: 4.2 us -> 8.79 us  [over_plane(): return lax.ppermute(x, PLANE, [(b, b ^ e) for b in range(4)])]
    ppermute x7, starting transfers between devices: 5.7 us -> 1.34 us  [over_core(): return lax.ppermute(x, 'rows', [(0, 1), (1, 0)])]
  transfers between devices with their start and end apart: 21 -> 20, of which waited for: 5 -> 7; matrix products, arithmetic and copies ran while one was open for 7% -> 10% of each run, Pallas kernels for 24% -> 13%
where the time goes in v5:
time: 141 us; the launch traced here: 140 us
  waiting for transfers between devices  35.9 us (25%)
  Pallas kernels  32.5 us (23%)
  starting transfers between devices  31.8 us (23%)
  local copies, waits for them, and re-layouts  14.3 us (10%)
  blocking collectives  14.1 us (10%)
  other arithmetic  6.44 us (5%)
  matrix products  3.6 us (3%)
    pallas_call x1, Pallas kernels, talker(): pl.pallas_call(functools.partial(talker_kernel, spans), out_shape=(jax.Sh...  14.6 us
    all_to_all x1, blocking collectives, four_planes(): far_terms = [lax.all_to_all(x, 'mp', 0, 0) for x in far]  14.1 us
    pallas_call x3, Pallas kernels, down(): pl.pallas_call(functools.partial(down_kernel, counts, planes, list(zip(en...  13.5 us
    unnamed x32, local copies, waits for them, and re-layouts  11.3 us
    all_to_all x1, waiting for transfers between devices, four_planes(): home = lax.all_to_all(collect(c.reshape(1), pieces, spans), 'mp', 0, 0)  10.9 us
    ppermute x3, waiting for transfers between devices, over_section(): return lax.ppermute(x, 'section', [(0, 1), (1, 0)])  10.7 us
    ppermute x4, waiting for transfers between devices, over_plane(): return lax.ppermute(x, PLANE, [(b, b ^ e) for b in range(4)])  8.79 us
    ppermute x1, starting transfers between devices, feature_block(): lax.ppermute(piece, GROUP, [(b * 4 + b, (b ^ 2) * 4 + b) for b in range(4)])  5.37 us
  transfers between devices with their start and end apart: 20, of which 7 were waited for; matrix products, arithmetic and copies ran while one was open for 10% of the time, Pallas kernels for 13%

profile of v5, /device:TPU:0, one launch (start us, length us, event | category | flops | bytes accessed | tf_op | source)
XLA Modules:
  0.0 139.6 jit_solution(517074762983876020)
XLA Ops:
  3.9 2.6 %collective-permute-start.4 = (bf16[128,4736]{1,0:T(8,128)(2,1)S(1)}, bf16[128,4736]{1,0:T(8,128)(2,1)}, u32[]{:S(2)}, u32[]{:S(2)}) collective-permute-start(bf16[128,4736]{1,0:T(8,128)(2,1)S(1)} %convolution_convert_fusion.refs_0_), channel_id=1, source_target_pairs={{0,2},{2,0},{1,3},{3,1},{4,6},{6,4},{5,7},{7,5},{8,10},{10,8},{9,1... | collective-permute-start | bytes 3637256 | tf_op jit(solution)/shard_map/ppermute | solution.py:375
  8.1 2.1 %constant_dynamic-slice_fusion = bf16[448,896]{1,0:T(8,128)(2,1)} fusion(bf16[896,896]{1,0:T(8,128)(2,1)} %param.12, s32[]{:T(128)S(6)} %select_n.30), kind=kLoop, calls=%fused_computation.22 | loop fusion | bytes 1605636 | tf_op jit(solution)/shard_map/dynamic_slice | solution.py:392
  10.2 5.4 %collective-permute-start.2 = (bf16[448,896]{1,0:T(8,128)(2,1)}, bf16[448,896]{1,0:T(8,128)(2,1)}, u32[]{:S(2)}, u32[]{:S(2)}) collective-permute-start(bf16[448,896]{1,0:T(8,128)(2,1)} %constant_dynamic-slice_fusion), channel_id=1, source_target_pairs={{0,8},{5,13},{10,2},{15,7},{16,24},{21,29},{26,18},{31,23}} | collective-permute-start | bytes 2408456 | tf_op jit(solution)/shard_map/ppermute | solution.py:393
  15.6 3.4 %copy-done.1 = bf16[4736,896]{1,0:T(8,128)(2,1)S(1)} copy-done((bf16[4736,896]{1,0:T(8,128)(2,1)S(1)}, bf16[4736,896]{1,0:T(8,128)(2,1)}, u32[]{:S(2)}) %copy-start.1) | copy-done | bytes 8486936
  19.0 6.7 %shard_map.121 = bf16[4,96,896]{2,1,0:T(8,128)(2,1)} custom-call(bf16[128,4736]{1,0:T(8,128)(2,1)S(1)} %convolution_convert_fusion.refs_0_, bf16[64,4736]{1,0:T(8,128)(2,1)} %convolution_convert_fusion.1.refs_1_, bf16[128,4736]{1,0:T(8,128)(2,1)} %collective-permute-done.refs_2_, bf16[64,4736]{1,0:T(8,128)(2,1)} %collective-permute-done.1.refs_3_, ...), custom_call_target="tpu_custom_call" | custom-call | flops 3258974208 | bytes 12124160 | tf_op jit(solution)/shard_map/pallas_call | solution.py:43
  25.6 8.2 %collective-permute-done.4.refs_0_ = bf16[128,4736]{1,0:T(8,128)(2,1)} collective-permute-done((bf16[128,4736]{1,0:T(8,128)(2,1)S(1)}, bf16[128,4736]{1,0:T(8,128)(2,1)}, u32[]{:S(2)}, u32[]{:S(2)}) %collective-permute-start.4) | collective-permute-done | bytes 1212448 | tf_op jit(solution)/shard_map/ppermute | solution.py:375
  33.8 2.3 %broadcast_select_fusion = bf16[448,896]{1,0:T(8,128)(2,1)} fusion(bf16[448,896]{1,0:T(8,128)(2,1)} %collective-permute-done.2, pred[]{:T(512)S(6)} %eq.63, bf16[896,896]{1,0:T(8,128)(2,1)} %param.12, s32[]{:T(128)S(6)} %select_n.30), kind=kLoop, calls=%fused_computation.4 | loop fusion | flops 401408 | bytes 2408453 | tf_op jit(solution)/shard_map/jit(_where)/select_n | solution.py:394
  36.1 4.9 %collective-permute-start.3 = (bf16[448,896]{1,0:T(8,128)(2,1)}, bf16[448,896]{1,0:T(8,128)(2,1)}, u32[]{:S(2)}, u32[]{:S(2)}) collective-permute-start(bf16[448,896]{1,0:T(8,128)(2,1)} %broadcast_select_fusion), channel_id=1, source_target_pairs={{0,4},{5,1},{10,14},{15,11},{8,12},{13,9},{2,6},{7,3},{16,20},{21,... | collective-permute-start | bytes 2408456 | tf_op jit(solution)/shard_map/ppermute | solution.py:397
  43.5 3.9 %all-to-all-start = ((bf16[4,96,896]{2,1,0:T(8,128)(2,1)}), bf16[4,96,896]{2,1,0:T(8,128)(2,1)S(1)}, u32[]{:S(2)}, u32[]{:S(2)}) async-start(bf16[4,96,896]{2,1,0:T(8,128)(2,1)} %shard_map.121), calls=%async_computation | async-start | bytes 1376256 | tf_op jit(solution)/shard_map/all_to_all | solution.py:433
  47.3 3.4 %copy-done.2 = bf16[4736,896]{1,0:T(8,128)(2,1)S(1)} copy-done((bf16[4736,896]{1,0:T(8,128)(2,1)S(1)}, bf16[4736,896]{1,0:T(8,128)(2,1)}, u32[]{:S(2)}) %copy-start.2) | copy-done | bytes 8486936
  50.7 5.3 %shard_map.122 = bf16[4,64,896]{2,1,0:T(8,128)(2,1)} custom-call(bf16[128,4736]{1,0:T(8,128)(2,1)} %collective-permute-done.4.refs_0_, bf16[128,4736]{1,0:T(8,128)(2,1)} %collective-permute-done.5.refs_1_, bf16[4736,896]{1,0:T(8,128)(2,1)S(1)} %copy-done.2), custom_call_target="tpu_custom_call" | custom-call | flops 2172649472 | bytes 10911744 | tf_op jit(solution)/shard_map/pallas_call | solution.py:43
  56.1 2.3 %broadcast_select_fusion.1 = bf16[448,896]{1,0:T(8,128)(2,1)} fusion(bf16[448,896]{1,0:T(8,128)(2,1)} %broadcast_select_fusion, bf16[448,896]{1,0:T(8,128)(2,1)} %collective-permute-done.3, pred[]{:T(512)S(6)} %or.3), kind=kLoop, calls=%fused_computation.5 | loop fusion | flops 401408 | bytes 2408449 | tf_op jit(solution)/shard_map/jit(_where)/select_n | solution.py:398
  61.9 1.6 %shard_map.125 = bf16[4,32,896]{2,1,0:T(8,128)(2,1)S(1)} custom-call(bf16[64,4736]{1,0:T(8,128)(2,1)S(1)} %collective-permute-done.9.refs_0_, bf16[64,4736]{1,0:T(8,128)(2,1)S(1)} %collective-permute-done.10.refs_1_, bf16[4736,896]{1,0:T(8,128)(2,1)S(1)} %copy-done.2), custom_call_target="tpu_custom_call" | custom-call | flops 1086324736 | bytes 9699328 | tf_op jit(solution)/shard_map/pallas_call | solution.py:43
  63.5 1.8 %all-to-all-done.terms = bf16[4,96,896]{2,1,0:T(8,128)(2,1)S(1)} async-done(((bf16[4,96,896]{2,1,0:T(8,128)(2,1)}), bf16[4,96,896]{2,1,0:T(8,128)(2,1)S(1)}, u32[]{:S(2)}, u32[]{:S(2)}) %all-to-all-start) | async-done | bytes 688160 | tf_op jit(solution)/shard_map/all_to_all | solution.py:433
  65.2 14.1 %all_to_all.20.terms = bf16[4,32,896]{2,1,0:T(8,128)(2,1)} all-to-all(bf16[4,32,896]{2,1,0:T(8,128)(2,1)S(1)} %shard_map.125), channel_id=1, replica_groups=mesh['groups'=2,'mp'=4,'section'=2,'rows'=2] {'mp'}, dimensions={0} | all-to-all | bytes 458752 | tf_op jit(solution)/shard_map/all_to_all | solution.py:439
  79.4 4.1 %all-to-all-start.1 = ((bf16[4,64,896]{2,1,0:T(8,128)(2,1)}), bf16[4,64,896]{2,1,0:T(8,128)(2,1)}, u32[]{:S(2)}, u32[]{:S(2)}) async-start(bf16[4,64,896]{2,1,0:T(8,128)(2,1)} %shard_map.122), calls=%async_computation.1 | async-start | bytes 917504 | tf_op jit(solution)/shard_map/all_to_all | solution.py:439
  86.4 2.5 %collective-permute-done.15.w2 = bf16[896,640]{1,0:T(8,128)(2,1)} collective-permute-done((bf16[896,640]{1,0:T(8,128)(2,1)}, bf16[896,640]{1,0:T(8,128)(2,1)}, u32[]{:S(2)}, u32[]{:S(2)}) %collective-permute-start.15) | collective-permute-done | bytes 1146912 | tf_op jit(solution)/shard_map/ppermute | solution.py:375
  91.2 3.7 %all-to-all-done.1.terms = bf16[4,64,896]{2,1,0:T(8,128)(2,1)} async-done(((bf16[4,64,896]{2,1,0:T(8,128)(2,1)}), bf16[4,64,896]{2,1,0:T(8,128)(2,1)}, u32[]{:S(2)}, u32[]{:S(2)}) %all-to-all-start.1) | async-done | bytes 458784 | tf_op jit(solution)/shard_map/all_to_all | solution.py:439
  96.7 5.7 %collective-permute-done.8.refs_2_ = bf16[2,32,896]{2,1,0:T(8,128)(2,1)S(1)} collective-permute-done((bf16[2,32,896]{2,1,0:T(8,128)(2,1)S(1)}, bf16[2,32,896]{2,1,0:T(8,128)(2,1)S(1)}, u32[]{:S(2)}, u32[]{:S(2)}) %collective-permute-start.8) | collective-permute-done | bytes 114720 | tf_op jit(solution)/shard_map/ppermute | solution.py:383
  103.7 3.1 %collective-permute-done.11.refs_3_ = bf16[2,16,896]{2,1,0:T(8,128)(2,1)S(1)} collective-permute-done((bf16[2,16,896]{2,1,0:T(8,128)(2,1)S(1)}, bf16[2,16,896]{2,1,0:T(8,128)(2,1)S(1)}, u32[]{:S(2)}, u32[]{:S(2)}) %collective-permute-start.11) | collective-permute-done | bytes 57376 | tf_op jit(solution)/shard_map/ppermute | solution.py:383
  106.7 1.7 %shard_map.127 = bf16[4,48,896]{2,1,0:T(8,128)(2,1)} custom-call(s32[1]{0:T(128)} %bitcast.1.block_ref, bf16[2,48,896]{2,1,0:T(8,128)(2,1)S(1)} %copy-done.7, bf16[2,48,896]{2,1,0:T(8,128)(2,1)} %collective-permute-done.7.refs_1_, bf16[2,32,896]{2,1,0:T(8,128)(2,1)S(1)} %collective-permute-done.8.refs_2_, ...), custom_call_target="tpu_custom_call" | custom-call | tf_op jit(solution)/shard_map/pallas_call | solution.py:105
  108.4 4.5 %all-to-all-start.3 = ((bf16[4,48,896]{2,1,0:T(8,128)(2,1)}), bf16[4,48,896]{2,1,0:T(8,128)(2,1)S(1)}, u32[]{:S(2)}, u32[]{:S(2)}) async-start(bf16[4,48,896]{2,1,0:T(8,128)(2,1)} %shard_map.127), calls=%async_computation.3 | async-start | bytes 688128 | tf_op jit(solution)/shard_map/all_to_all | solution.py:454
  112.9 10.9 %all-to-all-done.3 = bf16[4,48,896]{2,1,0:T(8,128)(2,1)S(1)} async-done(((bf16[4,48,896]{2,1,0:T(8,128)(2,1)}), bf16[4,48,896]{2,1,0:T(8,128)(2,1)S(1)}, u32[]{:S(2)}, u32[]{:S(2)}) %all-to-all-start.3) | async-done | bytes 344096 | tf_op jit(solution)/shard_map/all_to_all | solution.py:454
  124.9 14.6 %shard_map.128 = (bf16[48,1024]{1,0:T(8,128)(2,1)}, f32[48,1536]{1,0:T(8,128)}) custom-call(s32[1]{0:T(128)} %bitcast.1.block_ref, s32[48]{0:T(128)S(1)} %copy-done.9, f32[1,896]{1,0:T(1,128)S(1)} %reshape.55.gain, bf16[896,640]{1,0:T(8,128)(2,1)} %constant_dynamic-update-slice_fusion.w0, bf16[896,640]{1,0:T(8,128)(2,1)} %collective-permute-done.14.w1, ...), custom_call_target="tpu_custom_call" | custom-call | flops 75497472 | bytes 25165824 | tf_op jit(solution)/shard_map/pallas_call | solution.py:264
  (73 shorter events, 20.1 us)
Async XLA Ops:
  3.3 12.2 %collective-permute-start = (bf16[128,4736]{1,0:T(8,128)(2,1)S(1)}, bf16[128,4736]{1,0:T(8,128)(2,1)}, u32[]{:S(2)}, u32[]{:S(2)}) collective-permute-start(bf16[128,4736]{1,0:T(8,128)(2,1)S(1)} %convolution_convert_fusion.refs_0_), channel_id=1, source_target_pairs={{0,1},{1,0},{2,3},{3,2},{4,5},{5,4},{6,7},{7,6},{8,9},{9,8},{10,11... | collective-permute-start | bytes 3637256 | tf_op jit(solution)/shard_map/ppermute | solution.py:371
  3.9 29.9 %collective-permute-start.4 = (bf16[128,4736]{1,0:T(8,128)(2,1)S(1)}, bf16[128,4736]{1,0:T(8,128)(2,1)}, u32[]{:S(2)}, u32[]{:S(2)}) collective-permute-start(bf16[128,4736]{1,0:T(8,128)(2,1)S(1)} %convolution_convert_fusion.refs_0_), channel_id=1, source_target_pairs={{0,2},{2,0},{1,3},{3,1},{4,6},{6,4},{5,7},{7,5},{8,10},{10,8},{9,1... | collective-permute-start | bytes 3637256 | tf_op jit(solution)/shard_map/ppermute | solution.py:375
  7.9 7.6 %collective-permute-start.1 = (bf16[64,4736]{1,0:T(8,128)(2,1)}, bf16[64,4736]{1,0:T(8,128)(2,1)}, u32[]{:S(2)}, u32[]{:S(2)}) collective-permute-start(bf16[64,4736]{1,0:T(8,128)(2,1)} %convolution_convert_fusion.1.refs_1_), channel_id=1, source_target_pairs={{0,1},{1,0},{2,3},{3,2},{4,5},{5,4},{6,7},{7,6},{8,9},{9,8},{10,11... | collective-permute-start | bytes 1818632 | tf_op jit(solution)/shard_map/ppermute | solution.py:371
  10.2 23.6 %collective-permute-start.2 = (bf16[448,896]{1,0:T(8,128)(2,1)}, bf16[448,896]{1,0:T(8,128)(2,1)}, u32[]{:S(2)}, u32[]{:S(2)}) collective-permute-start(bf16[448,896]{1,0:T(8,128)(2,1)} %constant_dynamic-slice_fusion), channel_id=1, source_target_pairs={{0,8},{5,13},{10,2},{15,7},{16,24},{21,29},{26,18},{31,23}} | collective-permute-start | bytes 2408456 | tf_op jit(solution)/shard_map/ppermute | solution.py:393
  33.8 13.5 %collective-permute-start.5 = (bf16[128,4736]{1,0:T(8,128)(2,1)}, bf16[128,4736]{1,0:T(8,128)(2,1)}, u32[]{:S(2)}, u32[]{:S(2)}) collective-permute-start(bf16[128,4736]{1,0:T(8,128)(2,1)} %collective-permute-done.4.refs_0_), channel_id=1, source_target_pairs={{0,1},{1,0},{2,3},{3,2},{4,5},{5,4},{6,7},{7,6},{8,9},{9,8},{10,11... | collective-permute-start | bytes 3637256 | tf_op jit(solution)/shard_map/ppermute | solution.py:371
  36.1 19.9 %collective-permute-start.3 = (bf16[448,896]{1,0:T(8,128)(2,1)}, bf16[448,896]{1,0:T(8,128)(2,1)}, u32[]{:S(2)}, u32[]{:S(2)}) collective-permute-start(bf16[448,896]{1,0:T(8,128)(2,1)} %broadcast_select_fusion), channel_id=1, source_target_pairs={{0,4},{5,1},{10,14},{15,11},{8,12},{13,9},{2,6},{7,3},{16,20},{21,... | collective-permute-start | bytes 2408456 | tf_op jit(solution)/shard_map/ppermute | solution.py:397
  41.0 15.0 %collective-permute-start.9 = (bf16[64,4736]{1,0:T(8,128)(2,1)}, bf16[64,4736]{1,0:T(8,128)(2,1)S(1)}, u32[]{:S(2)}, u32[]{:S(2)}) collective-permute-start(bf16[64,4736]{1,0:T(8,128)(2,1)} %convolution_convert_fusion.1.refs_1_), channel_id=1, source_target_pairs={{0,2},{2,0},{1,3},{3,1},{4,6},{6,4},{5,7},{7,5},{8,10},{10,8},{9,1... | collective-permute-start | bytes 1818632 | tf_op jit(solution)/shard_map/ppermute | solution.py:375
  43.5 21.8 %all-to-all-start = ((bf16[4,96,896]{2,1,0:T(8,128)(2,1)}), bf16[4,96,896]{2,1,0:T(8,128)(2,1)S(1)}, u32[]{:S(2)}, u32[]{:S(2)}) async-start(bf16[4,96,896]{2,1,0:T(8,128)(2,1)} %shard_map.121), calls=%async_computation | async-start | bytes 1376256 | tf_op jit(solution)/shard_map/all_to_all | solution.py:433
  56.0 5.9 %collective-permute-start.10 = (bf16[64,4736]{1,0:T(8,128)(2,1)S(1)}, bf16[64,4736]{1,0:T(8,128)(2,1)S(1)}, u32[]{:S(2)}, u32[]{:S(2)}) collective-permute-start(bf16[64,4736]{1,0:T(8,128)(2,1)S(1)} %collective-permute-done.9.refs_0_), channel_id=1, source_target_pairs={{0,1},{1,0},{2,3},{3,2},{4,5},{5,4},{6,7},{7,6},{8,9},{9,8},{10,11... | collective-permute-start | bytes 1818632 | tf_op jit(solution)/shard_map/ppermute | solution.py:371
  58.4 25.2 %collective-permute-start.6 = (bf16[448,896]{1,0:T(8,128)(2,1)}, bf16[448,896]{1,0:T(8,128)(2,1)}, u32[]{:S(2)}, u32[]{:S(2)}) collective-permute-start(bf16[448,896]{1,0:T(8,128)(2,1)} %broadcast_select_fusion.1), channel_id=1, source_target_pairs={{0,16},{16,0},{1,17},{17,1},{2,18},{18,2},{3,19},{19,3},{4,20},{20... | collective-permute-start | bytes 2408456 | tf_op jit(solution)/shard_map/ppermute | solution.py:379
  61.4 27.6 %collective-permute-start.15 = (bf16[896,640]{1,0:T(8,128)(2,1)}, bf16[896,640]{1,0:T(8,128)(2,1)}, u32[]{:S(2)}, u32[]{:S(2)}) collective-permute-start(bf16[896,640]{1,0:T(8,128)(2,1)} %constant_dynamic-update-slice_fusion.w0), channel_id=1, source_target_pairs={{0,2},{2,0},{1,3},{3,1},{4,6},{6,4},{5,7},{7,5},{8,10},{10,8},{9,1... | collective-permute-start | bytes 3440648 | tf_op jit(solution)/shard_map/ppermute | solution.py:375
  65.2 19.9 %copy-start.3 = (bf16[4,96,896]{2,1,0:T(8,128)(2,1)}, bf16[4,96,896]{2,1,0:T(8,128)(2,1)S(1)}, u32[]{:S(2)}) copy-start(bf16[4,96,896]{2,1,0:T(8,128)(2,1)S(1)} %all-to-all-done.terms) | copy-start | bytes 2064388
  79.4 15.5 %all-to-all-start.1 = ((bf16[4,64,896]{2,1,0:T(8,128)(2,1)}), bf16[4,64,896]{2,1,0:T(8,128)(2,1)}, u32[]{:S(2)}, u32[]{:S(2)}) async-start(bf16[4,64,896]{2,1,0:T(8,128)(2,1)} %shard_map.122), calls=%async_computation.1 | async-start | bytes 917504 | tf_op jit(solution)/shard_map/all_to_all | solution.py:439
  83.5 41.4 %collective-permute-start.14 = (bf16[896,640]{1,0:T(8,128)(2,1)}, bf16[896,640]{1,0:T(8,128)(2,1)}, u32[]{:S(2)}, u32[]{:S(2)}) collective-permute-start(bf16[896,640]{1,0:T(8,128)(2,1)} %constant_dynamic-update-slice_fusion.w0), channel_id=1, source_target_pairs={{0,1},{1,0},{2,3},{3,2},{4,5},{5,4},{6,7},{7,6},{8,9},{9,8},{10,11... | collective-permute-start | bytes 3440648 | tf_op jit(solution)/shard_map/ppermute | solution.py:371
  88.9 35.9 %collective-permute-start.16 = (bf16[896,640]{1,0:T(8,128)(2,1)}, bf16[896,640]{1,0:T(8,128)(2,1)}, u32[]{:S(2)}, u32[]{:S(2)}) collective-permute-start(bf16[896,640]{1,0:T(8,128)(2,1)} %collective-permute-done.15.w2), channel_id=1, source_target_pairs={{0,1},{1,0},{2,3},{3,2},{4,5},{5,4},{6,7},{7,6},{8,9},{9,8},{10,11... | collective-permute-start | bytes 3440648 | tf_op jit(solution)/shard_map/ppermute | solution.py:371
  90.7 22.2 %copy-start.14 = (f32[896]{0:T(1024)S(1)}, f32[896]{0:T(1024)}, u32[]{:S(2)}) copy-start(f32[896]{0:T(1024)} %param.13) | copy-start | bytes 10756
  90.7 12.9 %collective-permute-start.7 = (bf16[2,48,896]{2,1,0:T(8,128)(2,1)}, bf16[2,48,896]{2,1,0:T(8,128)(2,1)}, u32[]{:S(2)}, u32[]{:S(2)}) collective-permute-start(bf16[2,48,896]{2,1,0:T(8,128)(2,1)} %get-tuple-element.22), channel_id=1, source_target_pairs={{0,1},{1,0},{2,3},{3,2},{4,5},{5,4},{6,7},{7,6},{8,9},{9,8},{10,11... | collective-permute-start | bytes 516104 | tf_op jit(solution)/shard_map/ppermute | solution.py:371
  96.3 28.5 %copy-start.8 = (bf16[2,48,896]{2,1,0:T(8,128)(2,1)S(1)}, bf16[2,48,896]{2,1,0:T(8,128)(2,1)}, u32[]{:S(2)}) copy-start(bf16[2,48,896]{2,1,0:T(8,128)(2,1)} %copy-done.6) | copy-start | bytes 516100
  96.4 28.5 %copy-start.9 = (s32[48]{0:T(128)S(1)}, s32[48]{0:T(128)}, u32[]{:S(2)}) copy-start(s32[48]{0:T(128)} %len_ref.1) | copy-start | bytes 580
  96.4 6.1 %collective-permute-start.8 = (bf16[2,32,896]{2,1,0:T(8,128)(2,1)S(1)}, bf16[2,32,896]{2,1,0:T(8,128)(2,1)S(1)}, u32[]{:S(2)}, u32[]{:S(2)}) collective-permute-start(bf16[2,32,896]{2,1,0:T(8,128)(2,1)S(1)} %get-tuple-element.23), channel_id=1, source_target_pairs={{0,2},{1,3},{2,0},{3,1},{4,6},{5,7},{6,4},{7,5},{8,10},{9,11},{10,... | collective-permute-start | bytes 344072 | tf_op jit(solution)/shard_map/ppermute | solution.py:383
  96.7 5.7 %collective-permute-start.12 = (bf16[2,32,896]{2,1,0:T(8,128)(2,1)S(1)}, bf16[2,32,896]{2,1,0:T(8,128)(2,1)S(1)}, u32[]{:S(2)}, u32[]{:S(2)}) collective-permute-start(bf16[2,32,896]{2,1,0:T(8,128)(2,1)S(1)} %get-tuple-element.27), channel_id=1, source_target_pairs={{0,3},{1,2},{2,1},{3,0},{4,7},{5,6},{6,5},{7,4},{8,11},{9,10},{10,... | collective-permute-start | bytes 344072 | tf_op jit(solution)/shard_map/ppermute | solution.py:383
  102.5 4.3 %collective-permute-start.11 = (bf16[2,16,896]{2,1,0:T(8,128)(2,1)S(1)}, bf16[2,16,896]{2,1,0:T(8,128)(2,1)S(1)}, u32[]{:S(2)}, u32[]{:S(2)}) collective-permute-start(bf16[2,16,896]{2,1,0:T(8,128)(2,1)S(1)} %get-tuple-element.26), channel_id=1, source_target_pairs={{0,2},{1,3},{2,0},{3,1},{4,6},{5,7},{6,4},{7,5},{8,10},{9,11},{10,... | collective-permute-start | bytes 172040 | tf_op jit(solution)/shard_map/ppermute | solution.py:383
  102.5 4.2 %collective-permute-start.13 = (bf16[2,16,896]{2,1,0:T(8,128)(2,1)S(1)}, bf16[2,16,896]{2,1,0:T(8,128)(2,1)S(1)}, u32[]{:S(2)}, u32[]{:S(2)}) collective-permute-start(bf16[2,16,896]{2,1,0:T(8,128)(2,1)S(1)} %get-tuple-element.28), channel_id=1, source_target_pairs={{0,3},{1,2},{2,1},{3,0},{4,7},{5,6},{6,5},{7,4},{8,11},{9,10},{10,... | collective-permute-start | bytes 172040 | tf_op jit(solution)/shard_map/ppermute | solution.py:383
  108.4 15.5 %all-to-all-start.3 = ((bf16[4,48,896]{2,1,0:T(8,128)(2,1)}), bf16[4,48,896]{2,1,0:T(8,128)(2,1)S(1)}, u32[]{:S(2)}, u32[]{:S(2)}) async-start(bf16[4,48,896]{2,1,0:T(8,128)(2,1)} %shard_map.127), calls=%async_computation.3 | async-start | bytes 688128 | tf_op jit(solution)/shard_map/all_to_all | solution.py:454
  (11 other events, 47.8 us)

commit v6 on v5

--- a/solution.py
+++ b/solution.py
@@ -10,8 +10,9 @@
 HEAD_DIM = 128
 ROW_STEP = 8
 LANES = 128
-DOWN_LIMIT = 28
+DOWN_LIMIT = 20
 PAGES = 2
+SHORT = pl.CostEstimate(flops=1, bytes_accessed=1, transcendentals=0)
 
 
 def down_kernel(counts, planes, cuts, *refs):
@@ -49,44 +50,43 @@
             pltpu.VMEM((planes * rows, most), jnp.bfloat16),
             pltpu.VMEM((planes * rows, columns), jnp.float32),
         ],
-        cost_estimate=pl.CostEstimate(
-            flops=2 * planes * rows * depth * columns,
-            bytes_accessed=2 * depth * (columns + planes * rows),
-            transcendentals=0,
-        ),
+        cost_estimate=SHORT,
         compiler_params=pltpu.CompilerParams(vmem_limit_bytes=DOWN_LIMIT * 1024 * 1024),
     )(*xs, w)
 
 
-def finish_kernel(terms, w, near, far):
+def finish_kernel(turn_ref, terms, w_mine, w_other, *refs):
+    outs, w = refs[:-1], refs[-1]
+    half = w_mine.shape[0]
+    g = turn_ref[0]
+    w[pl.ds(pl.multiple_of(g * half, half), half), :] = w_mine[...]
+    w[pl.ds(pl.multiple_of((1 - g) * half, half), half), :] = w_other[...]
     total = terms[0].astype(jnp.float32)
     for k in range(1, terms.shape[0]):
         total = total + terms[k].astype(jnp.float32)
     features = total.astype(jnp.bfloat16)
     projected = jnp.dot(features, w[...], preferred_element_type=jnp.float32)
     projected = projected.astype(jnp.bfloat16)
-    n = features.shape[0] // 2
-    for out, at in ((near, 0), (far, n)):
-        out[0] = features[at : at + n]
-        out[1] = projected[at : at + n]
-
-
-def finish(terms, w_proj):
+    n = features.shape[0] // len(outs)
+    for i, out in enumerate(outs):
+        out[0] = features[i * n : (i + 1) * n]
+        out[1] = projected[i * n : (i + 1) * n]
+
+
+def finish(turn, terms, w_halves, parts):
     _, rows, columns = terms.shape
-    half = jax.ShapeDtypeStruct((2, rows // 2, columns), jnp.bfloat16)
+    wide = w_halves[0].shape[1]
+    part = jax.ShapeDtypeStruct((2, rows // parts, columns), jnp.bfloat16)
     vmem = pl.BlockSpec(memory_space=pltpu.VMEM)
     return pl.pallas_call(
         finish_kernel,
-        out_shape=(half, half),
-        in_specs=[vmem, vmem],
-        out_specs=(vmem, vmem),
-        cost_estimate=pl.CostEstimate(
-            flops=2 * rows * columns * columns,
-            bytes_accessed=2 * columns * (columns + 6 * rows),
-            transcendentals=0,
-        ),
+        out_shape=(part,) * parts,
+        in_specs=[pl.BlockSpec(memory_space=pltpu.SMEM), vmem, vmem, vmem],
+        out_specs=(vmem,) * parts,
+        scratch_shapes=[pltpu.VMEM((columns, wide), jnp.bfloat16)],
+        cost_estimate=SHORT,
         compiler_params=pltpu.CompilerParams(vmem_limit_bytes=16 * 1024 * 1024),
-    )(terms, w_proj)
+    )(turn, terms, *w_halves)
 
 
 def collect_kernel(spans, block_ref, *refs):
@@ -107,6 +107,7 @@
         out_shape=jax.ShapeDtypeStruct((len(spans), rows, flat[0].shape[2]), jnp.bfloat16),
         in_specs=[pl.BlockSpec(memory_space=pltpu.SMEM)] + [vmem] * len(flat),
         out_specs=vmem,
+        cost_estimate=SHORT,
         compiler_params=pltpu.CompilerParams(vmem_limit_bytes=16 * 1024 * 1024),
     )(block, *flat)
 
@@ -170,7 +171,7 @@
     row_block = lax.broadcasted_iota(jnp.int32, (slot, HEAD_DIM), 0) // group
     own_row = lax.broadcasted_iota(jnp.int32, (ROW_STEP, LANES), 0)
 
-    def one_set(at, spread, gathered):
+    def scores_of(at, spread):
         here = pl.ds(at, ROW_STEP)
         for h in range(heads):
             g, j = h // group, h % group
@@ -181,7 +182,6 @@
         by_block = [
             jnp.where(lane_block == g, query, 0.0).astype(jnp.bfloat16) for g in range(blocks)
         ]
-
         scores = jnp.zeros((cached, LANES), jnp.float32)
         for r in range(ROW_STEP):
             mine = lane_row == r
@@ -196,9 +196,9 @@
             new_key = qkv[g, here, key:value].astype(jnp.bfloat16)
             own = own + jnp.dot(new_key, by_block[g], preferred_element_type=jnp.float32)
         own = jnp.where(own_row == lane_row[:ROW_STEP], own, 0.0)
-        own = jnp.sum(own, axis=0, keepdims=True)
-
-        scores, own = scores * inv, own * inv
+        return scores * inv, jnp.sum(own, axis=0, keepdims=True) * inv
+
+    def softmax(at, scores, own):
         lens = jnp.zeros((1, LANES), jnp.int32)
         for r in range(ROW_STEP):
             lens = jnp.where(lane_row[:1] == r, len_ref[at + r], lens)
@@ -210,9 +210,11 @@
         total = jnp.sum(expo, axis=0, keepdims=True) + own_expo
         probs = (expo / total).T.astype(jnp.bfloat16)
         own_prob = (own_expo / total).astype(jnp.bfloat16).astype(jnp.float32)
-        own_prob = jnp.broadcast_to(own_prob, (LANES, LANES)).T
+        return probs, jnp.broadcast_to(own_prob, (LANES, LANES)).T
+
+    def context(at, probs, own_prob, gathered):
+        here = pl.ds(at, ROW_STEP)
         value_rows = qkv.at[:, here, value:]
-
         for r in range(ROW_STEP):
             lanes = slice(r * slot, (r + 1) * slot)
             made = jnp.dot(
@@ -247,9 +249,11 @@
                         (page, kv_width), kv_ref.dtype
                     )
 
-        for k in range(sets):
-            at = pl.multiple_of(first + k * ROW_STEP, ROW_STEP)
-            one_set(at, spreads.at[k], gathereds.at[k])
+        ats = [pl.multiple_of(first + k * ROW_STEP, ROW_STEP) for k in range(sets)]
+        scored = [scores_of(at, spreads.at[k]) for k, at in enumerate(ats)]
+        weighed = [softmax(at, *s) for at, s in zip(ats, scored)]
+        for k, at in enumerate(ats):
+            context(at, *weighed[k], gathereds.at[k])
 
 
 def talker(block, pieces, spans, talker_gain, weights, kv_len, kv_cache):
@@ -278,11 +282,7 @@
             pltpu.VMEM((sets, LANES, HEAD_DIM), jnp.float32),
             pltpu.VMEM((sets, LANES, HEAD_DIM), jnp.float32),
         ],
-        cost_estimate=pl.CostEstimate(
-            flops=4 * rows * cached * q_width,
-            bytes_accessed=2 * rows * cached * kv_width,
-            transcendentals=rows * cached * q_width // HEAD_DIM,
-        ),
+        cost_estimate=SHORT,
         compiler_params=pltpu.CompilerParams(vmem_limit_bytes=46 * 1024 * 1024),
     )(block, kv_len, talker_gain.reshape(1, wide), *weights, *flat, kv_cache)
 
@@ -387,19 +387,15 @@
     return lax.optimization_barrier((x, *others))[0]
 
 
-def feature_block(w_proj, g, m, c, first, second):
+def feature_block(w_proj, g, m, c, later):
     half = w_proj.shape[0] // 2
     piece = lax.dynamic_slice_in_dim(w_proj, g * half, half, axis=0)
-    got = lax.ppermute(piece, GROUP, [(b * 4 + b, (b ^ 2) * 4 + b) for b in range(4)])
-    piece = jnp.where(m == c, piece, after(got, first))
-    pairs = [(b * 4 + b, (b ^ 1) * 4 + b) for b in range(4)]
-    pairs += [((b ^ 2) * 4 + b, (b ^ 3) * 4 + b) for b in range(4)]
-    got = lax.ppermute(piece, GROUP, pairs)
-    piece = jnp.where((m == c) | (m == c ^ 2), piece, after(got, second))
-    other = over_groups(piece)
-    return jnp.concatenate(
-        [jnp.where(g == 0, piece, other), jnp.where(g == 0, other, piece)], axis=0
-    )
+    two = lax.ppermute(piece, GROUP, [(b * 4 + b, (b ^ 2) * 4 + b) for b in range(4)])
+    one = lax.ppermute(piece, GROUP, [(b * 4 + b, (b ^ 1) * 4 + b) for b in range(4)])
+    two, one, _ = lax.optimization_barrier((two, one, later))
+    three = lax.ppermute(two, GROUP, [((b ^ 2) * 4 + b, (b ^ 3) * 4 + b) for b in range(4)])
+    piece = jnp.where(m == c, piece, jnp.where(m == c ^ 2, two, jnp.where(m == c ^ 1, one, three)))
+    return piece, over_groups(piece)
 
 
 def four_planes(
@@ -418,41 +414,34 @@
     owned = kv_cache.shape[0]
     g, m, c = lax.axis_index("groups"), lax.axis_index("mp"), lax.axis_index(PLANE)
     slots = talker_slot[0]
-    chunks = [(0, 32), (32, 16)]
-
-    sent = []
-    for first, n in chunks:
-        plane = jnp.arange(planes, dtype=jnp.int32)[:, None] * owned
-        want = (plane + first + jnp.arange(n, dtype=jnp.int32)[None, :]).reshape(-1)
-        pick = (want[:, None] == slots[None, :]).astype(jnp.bfloat16)
-        rows = jnp.dot(pick, thinker_act, preferred_element_type=jnp.float32)
-        sent.append(rows.astype(jnp.bfloat16))
-
-    crossed = [over_section(sent[0])]
-    near = down([*sent, *[over_core(x) for x in sent]], w_think, planes)
+
+    pick = (jnp.arange(planes * owned)[:, None] == slots[None, :]).astype(jnp.bfloat16)
+    rows = jnp.dot(pick, thinker_act, preferred_element_type=jnp.float32).astype(jnp.bfloat16)
+
+    across = over_section(rows)
+    peer = over_core(rows)
+    near = down([rows, peer], w_think, planes)
     near_terms = lax.all_to_all(near, "mp", 0, 0)
-    crossed[0] = after(crossed[0], near)
-    crossed.append(over_section(after(sent[1], near)))
-    far = [down([crossed[0], over_core(crossed[0])], w_think, planes)]
-    late = after(crossed[1], far[0])
-    far.append(down([late, over_core(late)], w_think, planes))
+    block_w = feature_block(after(w_proj, peer), g, m, c, near)
+    across = after(across, near)
+    far = [down([x], w_think, planes) for x in (across, over_core(across))]
     far_terms = [lax.all_to_all(x, "mp", 0, 0) for x in far]
 
-    block_w = feature_block(w_proj, g, m, c, near, far[0])
     mine = jnp.concatenate([w_query, w_key, w_value], axis=1)
-    other = over_section(after(mine, late))
-
-    own, next_core = finish(near_terms, block_w)
+    other = over_section(after(mine, across))
+
+    turn = g.reshape(1)
+    own, next_core = finish(turn, near_terms, block_w, 2)
     pieces = [[own], [over_core(next_core)], [], []]
-    for terms in far_terms:
-        across = finish(terms, block_w)
-        pieces[2].append(over_plane(across[0], 2))
-        pieces[3].append(over_plane(across[1], 3))
-    other = after(other, across[0])
+    for e, terms in zip((2, 3), far_terms):
+        (made,) = finish(turn, terms, block_w, 1)
+        pieces[e].append(over_plane(made, e))
+    other = after(other, made)
     weights = [mine, over_core(mine), other, over_core(other)]
-    spans = [[(0, owned)], [(0, owned)], chunks, chunks]
+    spans = [[(0, owned)]] * 4
     home = lax.all_to_all(collect(c.reshape(1), pieces, spans), "mp", 0, 0)
     new_kv, ctx = talker(c.reshape(1), pieces, spans, talker_gain, weights, kv_len, kv_cache)
+    home = after(home, ctx)
     pick = (slots[:, None] == jnp.arange(planes * owned)[None, :]).astype(jnp.bfloat16)
     thinker_out = jnp.dot(
         pick, home.reshape(planes * owned, -1), preferred_element_type=jnp.float32

time: 141 us -> 140 us (level)
  starting transfers between devices: 31.8 us -> 50.3 us
  blocking collectives: 14.1 us -> 0 us
  other arithmetic: 6.44 us -> 1.78 us
  waiting for transfers between devices: 35.9 us -> 31.3 us
  local copies, waits for them, and re-layouts: 14.3 us -> 17.1 us
  Pallas kernels: 32.5 us -> 34.5 us
    all_to_all x1 -> x0, blocking collectives: 14.1 us -> none  [four_planes(): far_terms = [lax.all_to_all(x, 'mp', 0, 0) for x in far]]
    all_to_all x1 -> x2, starting transfers between devices: 4.12 us -> 16.9 us  [four_planes(): far_terms = [lax.all_to_all(x, 'mp', 0, 0) for x in far]]
    all_to_all x1, waiting for transfers between devices: 10.9 us -> 0.01 us  [four_planes(): home = lax.all_to_all(collect(c.reshape(1), pieces, spans), 'mp', 0, 0)]
    ppermute x3 -> x2, waiting for transfers between devices: 10.7 us -> 20.6 us  [over_section(): return lax.ppermute(x, 'section', [(0, 1), (1, 0)])]
    unnamed x32 -> x38, local copies, waits for them, and re-layouts: 11.3 us -> 16.3 us
    ppermute x4 -> x2, starting transfers between devices: 1.54 us -> 6.26 us  [over_plane(): return lax.ppermute(x, PLANE, [(b, b ^ e) for b in range(4)])]
    select_n x3 -> x1, other arithmetic: 6.15 us -> 1.78 us  [feature_block(): jnp.where(m == c, piece, jnp.where(m == c ^ 2, two, jnp.where(m == c ^ 1,...]
    all_to_all x1, starting transfers between devices: 3.86 us -> 6.93 us  [four_planes(): near_terms = lax.all_to_all(near, 'mp', 0, 0)]
  transfers between devices with their start and end apart: 20 -> 17, of which waited for: 7 -> 6; matrix products, arithmetic and copies ran while one was open for 10% -> 3% of each run, Pallas kernels for 13% -> 25%
where the time goes in v6:
time: 140 us
  starting transfers between devices  50.3 us (36%)
  Pallas kernels  34.5 us (25%)
  waiting for transfers between devices  31.3 us (22%)
  local copies, waits for them, and re-layouts  17.1 us (12%)
  matrix products  3.7 us (3%)
  other arithmetic  1.78 us (1%)
    ppermute x2, waiting for transfers between devices, over_section(): return lax.ppermute(x, 'section', [(0, 1), (1, 0)])  20.6 us
    all_to_all x2, starting transfers between devices, four_planes(): far_terms = [lax.all_to_all(x, 'mp', 0, 0) for x in far]  16.9 us
    unnamed x38, local copies, waits for them, and re-layouts  16.3 us
    pallas_call x3, Pallas kernels, down(): pl.pallas_call(functools.partial(down_kernel, counts, planes, list(zip(en...  14.5 us
    pallas_call x1, Pallas kernels, talker(): pl.pallas_call(functools.partial(talker_kernel, spans), out_shape=(jax.Sh...  13.1 us
    all_to_all x1, starting transfers between devices, four_planes(): near_terms = lax.all_to_all(near, 'mp', 0, 0)  6.93 us
    ppermute x2, waiting for transfers between devices, over_plane(): return lax.ppermute(x, PLANE, [(b, b ^ e) for b in range(4)])  6.75 us
    ppermute x2, starting transfers between devices, over_plane(): return lax.ppermute(x, PLANE, [(b, b ^ e) for b in range(4)])  6.26 us
  transfers between devices with their start and end apart: 17, of which 6 were waited for; matrix products, arithmetic and copies ran while one was open for 3% of the time, Pallas kernels for 25%

profile of v6, /device:TPU:0, one launch (start us, length us, event | category | flops | bytes accessed | tf_op | source)
XLA Modules:
  0.0 139.5 jit_solution(12368502715764417984)
XLA Ops:
  2.1 2.7 %convolution_convert_fusion.refs_0_ = bf16[192,4736]{1,0:T(8,128)(2,1)} fusion(bf16[192,4736]{1,0:T(8,128)(2,1)S(1)} %copy-done, s32[192]{0:T(256)} %bitcast.7), kind=kOutput, calls=%fused_computation | convolution fusion | flops 350121984 | bytes 3638016 | tf_op jit(solution)/shard_map/dot_general | solution.py:419
  5.3 2.5 %collective-permute-start.6 = (bf16[192,4736]{1,0:T(8,128)(2,1)}, bf16[192,4736]{1,0:T(8,128)(2,1)}, u32[]{:S(2)}, u32[]{:S(2)}) collective-permute-start(bf16[192,4736]{1,0:T(8,128)(2,1)} %convolution_convert_fusion.refs_0_), channel_id=1, source_target_pairs={{0,2},{2,0},{1,3},{3,1},{4,6},{6,4},{5,7},{7,5},{8,10},{10,8},{9,1... | collective-permute-start | bytes 5455880 | tf_op jit(solution)/shard_map/ppermute | solution.py:375
  9.1 5.9 %collective-permute-start.1 = (bf16[448,896]{1,0:T(8,128)(2,1)S(1)}, bf16[448,896]{1,0:T(8,128)(2,1)S(1)}, u32[]{:S(2)}, u32[]{:S(2)}) collective-permute-start(bf16[448,896]{1,0:T(8,128)(2,1)S(1)} %constant_dynamic-slice_fusion), channel_id=1, source_target_pairs={{0,8},{5,13},{10,2},{15,7},{16,24},{21,29},{26,18},{31,23}} | collective-permute-start | bytes 2408456 | tf_op jit(solution)/shard_map/ppermute | solution.py:393
  15.0 2.2 %collective-permute-start.2 = (bf16[448,896]{1,0:T(8,128)(2,1)S(1)}, bf16[448,896]{1,0:T(8,128)(2,1)}, u32[]{:S(2)}, u32[]{:S(2)}) collective-permute-start(bf16[448,896]{1,0:T(8,128)(2,1)S(1)} %constant_dynamic-slice_fusion), channel_id=1, source_target_pairs={{0,4},{5,1},{10,14},{15,11},{16,20},{21,17},{26,30},{31,27}} | collective-permute-start | bytes 2408456 | tf_op jit(solution)/shard_map/ppermute | solution.py:394
  17.2 3.4 %copy-done.1 = bf16[4736,896]{1,0:T(8,128)(2,1)S(1)} copy-done((bf16[4736,896]{1,0:T(8,128)(2,1)S(1)}, bf16[4736,896]{1,0:T(8,128)(2,1)}, u32[]{:S(2)}) %copy-start.1) | copy-done | bytes 8486936
  20.6 7.2 %shard_map.121 = bf16[4,96,896]{2,1,0:T(8,128)(2,1)} custom-call(bf16[192,4736]{1,0:T(8,128)(2,1)} %convolution_convert_fusion.refs_0_, bf16[192,4736]{1,0:T(8,128)(2,1)} %collective-permute-done.refs_1_, bf16[4736,896]{1,0:T(8,128)(2,1)S(1)} %copy-done.1), custom_call_target="tpu_custom_call" | custom-call | flops 1 | bytes 1 | tf_op jit(solution)/shard_map/pallas_call | solution.py:44
  27.8 20.6 %collective-permute-done.6.refs_0_ = bf16[192,4736]{1,0:T(8,128)(2,1)} collective-permute-done((bf16[192,4736]{1,0:T(8,128)(2,1)}, bf16[192,4736]{1,0:T(8,128)(2,1)}, u32[]{:S(2)}, u32[]{:S(2)}) %collective-permute-start.6) | collective-permute-done | bytes 1818656 | tf_op jit(solution)/shard_map/ppermute | solution.py:375
  50.0 6.9 %all-to-all-start = ((bf16[4,96,896]{2,1,0:T(8,128)(2,1)}), bf16[4,96,896]{2,1,0:T(8,128)(2,1)}, u32[]{:S(2)}, u32[]{:S(2)}) async-start(bf16[4,96,896]{2,1,0:T(8,128)(2,1)} %shard_map.121), calls=%async_computation | async-start | bytes 1376256 | tf_op jit(solution)/shard_map/all_to_all | solution.py:424
  59.4 1.9 %collective-permute-start.11 = (bf16[896,640]{1,0:T(8,128)(2,1)}, bf16[896,640]{1,0:T(8,128)(2,1)}, u32[]{:S(2)}, u32[]{:S(2)}) collective-permute-start(bf16[896,640]{1,0:T(8,128)(2,1)} %constant_dynamic-update-slice_fusion.w0), channel_id=1, source_target_pairs={{0,2},{2,0},{1,3},{3,1},{4,6},{6,4},{5,7},{7,5},{8,10},{10,8},{9,1... | collective-permute-start | bytes 3440648 | tf_op jit(solution)/shard_map/ppermute | solution.py:375
  61.2 1.8 %select_select_fusion.w_mine = bf16[448,896]{1,0:T(8,128)(2,1)S(1)} fusion(bf16[448,896]{1,0:T(8,128)(2,1)S(1)} %collective-permute-done.1, bf16[448,896]{1,0:T(8,128)(2,1)} %collective-permute-done.2, bf16[448,896]{1,0:T(8,128)(2,1)} %collective-permute-done.3, pred[]{:T(512)S(6)} %eq.46, pred[]{:T(512)S(6)} %eq.45, pred[]{:T(512)S(6)} %eq.44, ...), kind=kLoop, calls=%fused_computation.2 | loop fusion | flops 1204224 | bytes 4014087 | tf_op jit(solution)/shard_map/jit(_where)/select_n | solution.py:397
  64.6 3.4 %copy-done.2 = bf16[4736,896]{1,0:T(8,128)(2,1)S(1)} copy-done((bf16[4736,896]{1,0:T(8,128)(2,1)S(1)}, bf16[4736,896]{1,0:T(8,128)(2,1)}, u32[]{:S(2)}) %copy-start.2) | copy-done | bytes 8486936
  68.0 3.7 %shard_map.125 = bf16[4,48,896]{2,1,0:T(8,128)(2,1)S(1)} custom-call(bf16[192,4736]{1,0:T(8,128)(2,1)} %collective-permute-done.8.refs_0_, bf16[4736,896]{1,0:T(8,128)(2,1)S(1)} %copy-done.2), custom_call_target="tpu_custom_call" | custom-call | flops 1 | bytes 1 | tf_op jit(solution)/shard_map/pallas_call | solution.py:44
  73.2 11.8 %all-to-all-start.2 = ((bf16[4,48,896]{2,1,0:T(8,128)(2,1)}), bf16[4,48,896]{2,1,0:T(8,128)(2,1)}, u32[]{:S(2)}, u32[]{:S(2)}) async-start(bf16[4,48,896]{2,1,0:T(8,128)(2,1)} %copy-done.5), calls=%async_computation.2 | async-start | bytes 688128 | tf_op jit(solution)/shard_map/all_to_all | solution.py:428
  84.9 3.4 %copy-done.3 = bf16[4736,896]{1,0:T(8,128)(2,1)S(1)} copy-done((bf16[4736,896]{1,0:T(8,128)(2,1)S(1)}, bf16[4736,896]{1,0:T(8,128)(2,1)}, u32[]{:S(2)}) %copy-start.3) | copy-done | bytes 8486936
  88.4 3.7 %shard_map.123 = bf16[4,48,896]{2,1,0:T(8,128)(2,1)S(1)} custom-call(bf16[192,4736]{1,0:T(8,128)(2,1)} %collective-permute-done.6.refs_0_, bf16[4736,896]{1,0:T(8,128)(2,1)S(1)} %copy-done.3), custom_call_target="tpu_custom_call" | custom-call | flops 1 | bytes 1 | tf_op jit(solution)/shard_map/pallas_call | solution.py:44
  92.8 5.1 %all-to-all-start.1 = ((bf16[4,48,896]{2,1,0:T(8,128)(2,1)}), bf16[4,48,896]{2,1,0:T(8,128)(2,1)}, u32[]{:S(2)}, u32[]{:S(2)}) async-start(bf16[4,48,896]{2,1,0:T(8,128)(2,1)} %copy-done.4), calls=%async_computation.1 | async-start | bytes 688128 | tf_op jit(solution)/shard_map/all_to_all | solution.py:428
  100.5 2.3 %shard_map.122 = (bf16[2,48,896]{2,1,0:T(8,128)(2,1)S(1)}, bf16[2,48,896]{2,1,0:T(8,128)(2,1)}) custom-call(s32[1]{0:T(128)} %bitcast.2.turn_ref, bf16[4,96,896]{2,1,0:T(8,128)(2,1)} %all-to-all-done.terms, bf16[448,896]{1,0:T(8,128)(2,1)S(1)} %select_select_fusion.w_mine, bf16[448,896]{1,0:T(8,128)(2,1)S(1)} %collective-permute-done.4.w_other), custom_call_target="tpu_custom_call" | custom-call | flops 1 | bytes 1 | tf_op jit(solution)/shard_map/pallas_call | solution.py:81
  103.5 2.0 %all-to-all-done.1.terms = bf16[4,48,896]{2,1,0:T(8,128)(2,1)} async-done(((bf16[4,48,896]{2,1,0:T(8,128)(2,1)}), bf16[4,48,896]{2,1,0:T(8,128)(2,1)}, u32[]{:S(2)}, u32[]{:S(2)}) %all-to-all-start.1) | async-done | bytes 344096 | tf_op jit(solution)/shard_map/all_to_all | solution.py:428
  107.0 6.3 %collective-permute-start.7 = (bf16[2,48,896]{2,1,0:T(8,128)(2,1)S(1)}, bf16[2,48,896]{2,1,0:T(8,128)(2,1)S(1)}, u32[]{:S(2)}, u32[]{:S(2)}) collective-permute-start(bf16[2,48,896]{2,1,0:T(8,128)(2,1)S(1)} %shard_map.124), channel_id=1, source_target_pairs={{0,2},{1,3},{2,0},{3,1},{4,6},{5,7},{6,4},{7,5},{8,10},{9,11},{10,... | collective-permute-start | bytes 516104 | tf_op jit(solution)/shard_map/ppermute | solution.py:383
  113.2 4.8 %collective-permute-done.7.refs_2_ = bf16[2,48,896]{2,1,0:T(8,128)(2,1)S(1)} collective-permute-done((bf16[2,48,896]{2,1,0:T(8,128)(2,1)S(1)}, bf16[2,48,896]{2,1,0:T(8,128)(2,1)S(1)}, u32[]{:S(2)}, u32[]{:S(2)}) %collective-permute-start.7) | collective-permute-done | bytes 172064 | tf_op jit(solution)/shard_map/ppermute | solution.py:383
  118.0 1.9 %collective-permute-done.9.refs_3_ = bf16[2,48,896]{2,1,0:T(8,128)(2,1)S(1)} collective-permute-done((bf16[2,48,896]{2,1,0:T(8,128)(2,1)S(1)}, bf16[2,48,896]{2,1,0:T(8,128)(2,1)S(1)}, u32[]{:S(2)}, u32[]{:S(2)}) %collective-permute-start.9) | collective-permute-done | bytes 172064 | tf_op jit(solution)/shard_map/ppermute | solution.py:383
  120.0 1.7 %shard_map.127 = bf16[4,48,896]{2,1,0:T(8,128)(2,1)} custom-call(s32[1]{0:T(128)} %bitcast.1.block_ref, bf16[2,48,896]{2,1,0:T(8,128)(2,1)S(1)} %copy-done.7, bf16[2,48,896]{2,1,0:T(8,128)(2,1)} %collective-permute-done.5.refs_1_, bf16[2,48,896]{2,1,0:T(8,128)(2,1)S(1)} %collective-permute-done.7.refs_2_, bf16[2,48,896]{2,1,0:T(8,128)(2,1)S(1)} %collective-permute-done.9.refs_3_), custom_call_target="tpu_custom_call" | custom-call | flops 1 | bytes 1 | tf_op jit(solution)/shard_map/pallas_call | solution.py:105
  121.7 3.6 %all-to-all-start.3 = ((bf16[4,48,896]{2,1,0:T(8,128)(2,1)}), bf16[4,48,896]{2,1,0:T(8,128)(2,1)S(1)}, u32[]{:S(2)}, u32[]{:S(2)}) async-start(bf16[4,48,896]{2,1,0:T(8,128)(2,1)} %shard_map.127), calls=%async_computation.3 | async-start | bytes 688128 | tf_op jit(solution)/shard_map/all_to_all | solution.py:442
  125.4 13.1 %shard_map.128 = (bf16[48,1024]{1,0:T(8,128)(2,1)}, f32[48,1536]{1,0:T(8,128)}) custom-call(s32[1]{0:T(128)} %bitcast.1.block_ref, s32[48]{0:T(128)S(1)} %copy-done.11, f32[1,896]{1,0:T(1,128)S(1)} %reshape.22.gain, bf16[896,640]{1,0:T(8,128)(2,1)} %constant_dynamic-update-slice_fusion.w0, bf16[896,640]{1,0:T(8,128)(2,1)} %collective-permute-done.10.w1, ...), custom_call_target="tpu_custom_call" | custom-call | flops 1 | bytes 1 | tf_op jit(solution)/shard_map/pallas_call | solution.py:268
  (62 shorter events, 16.9 us)
Async XLA Ops:
  4.8 4.2 %collective-permute-start = (bf16[192,4736]{1,0:T(8,128)(2,1)}, bf16[192,4736]{1,0:T(8,128)(2,1)}, u32[]{:S(2)}, u32[]{:S(2)}) collective-permute-start(bf16[192,4736]{1,0:T(8,128)(2,1)} %convolution_convert_fusion.refs_0_), channel_id=1, source_target_pairs={{0,1},{1,0},{2,3},{3,2},{4,5},{5,4},{6,7},{7,6},{8,9},{9,8},{10,11... | collective-permute-start | bytes 5455880 | tf_op jit(solution)/shard_map/ppermute | solution.py:371
  5.3 43.1 %collective-permute-start.6 = (bf16[192,4736]{1,0:T(8,128)(2,1)}, bf16[192,4736]{1,0:T(8,128)(2,1)}, u32[]{:S(2)}, u32[]{:S(2)}) collective-permute-start(bf16[192,4736]{1,0:T(8,128)(2,1)} %convolution_convert_fusion.refs_0_), channel_id=1, source_target_pairs={{0,2},{2,0},{1,3},{3,1},{4,6},{6,4},{5,7},{7,5},{8,10},{10,8},{9,1... | collective-permute-start | bytes 5455880 | tf_op jit(solution)/shard_map/ppermute | solution.py:375
  9.1 39.3 %collective-permute-start.1 = (bf16[448,896]{1,0:T(8,128)(2,1)S(1)}, bf16[448,896]{1,0:T(8,128)(2,1)S(1)}, u32[]{:S(2)}, u32[]{:S(2)}) collective-permute-start(bf16[448,896]{1,0:T(8,128)(2,1)S(1)} %constant_dynamic-slice_fusion), channel_id=1, source_target_pairs={{0,8},{5,13},{10,2},{15,7},{16,24},{21,29},{26,18},{31,23}} | collective-permute-start | bytes 2408456 | tf_op jit(solution)/shard_map/ppermute | solution.py:393
  15.0 33.4 %collective-permute-start.2 = (bf16[448,896]{1,0:T(8,128)(2,1)S(1)}, bf16[448,896]{1,0:T(8,128)(2,1)}, u32[]{:S(2)}, u32[]{:S(2)}) collective-permute-start(bf16[448,896]{1,0:T(8,128)(2,1)S(1)} %constant_dynamic-slice_fusion), channel_id=1, source_target_pairs={{0,4},{5,1},{10,14},{15,11},{16,20},{21,17},{26,30},{31,27}} | collective-permute-start | bytes 2408456 | tf_op jit(solution)/shard_map/ppermute | solution.py:394
  27.8 29.1 %copy-start.13 = (bf16[896,384]{1,0:T(8,128)(2,1)S(1)}, bf16[896,384]{1,0:T(8,128)(2,1)}, u32[]{:S(2)}) copy-start(bf16[896,384]{1,0:T(8,128)(2,1)} %param.14) | copy-start | bytes 2064388
  27.8 30.1 %copy-start.14 = (bf16[896,128]{1,0:T(8,128)(2,1)S(1)}, bf16[896,128]{1,0:T(8,128)(2,1)}, u32[]{:S(2)}) copy-start(bf16[896,128]{1,0:T(8,128)(2,1)} %param.15) | copy-start | bytes 688132
  48.4 16.2 %collective-permute-start.8 = (bf16[192,4736]{1,0:T(8,128)(2,1)}, bf16[192,4736]{1,0:T(8,128)(2,1)}, u32[]{:S(2)}, u32[]{:S(2)}) collective-permute-start(bf16[192,4736]{1,0:T(8,128)(2,1)} %collective-permute-done.6.refs_0_), channel_id=1, source_target_pairs={{0,1},{1,0},{2,3},{3,2},{4,5},{5,4},{6,7},{7,6},{8,9},{9,8},{10,11... | collective-permute-start | bytes 5455880 | tf_op jit(solution)/shard_map/ppermute | solution.py:371
  48.4 12.8 %collective-permute-start.3 = (bf16[448,896]{1,0:T(8,128)(2,1)S(1)}, bf16[448,896]{1,0:T(8,128)(2,1)}, u32[]{:S(2)}, u32[]{:S(2)}) collective-permute-start(bf16[448,896]{1,0:T(8,128)(2,1)S(1)} %collective-permute-done.1), channel_id=1, source_target_pairs={{8,12},{13,9},{2,6},{7,3},{24,28},{29,25},{18,22},{23,19}} | collective-permute-start | bytes 2408456 | tf_op jit(solution)/shard_map/ppermute | solution.py:396
  50.0 23.2 %all-to-all-start = ((bf16[4,96,896]{2,1,0:T(8,128)(2,1)}), bf16[4,96,896]{2,1,0:T(8,128)(2,1)}, u32[]{:S(2)}, u32[]{:S(2)}) async-start(bf16[4,96,896]{2,1,0:T(8,128)(2,1)} %shard_map.121), calls=%async_computation | async-start | bytes 1376256 | tf_op jit(solution)/shard_map/all_to_all | solution.py:424
  59.4 40.7 %collective-permute-start.11 = (bf16[896,640]{1,0:T(8,128)(2,1)}, bf16[896,640]{1,0:T(8,128)(2,1)}, u32[]{:S(2)}, u32[]{:S(2)}) collective-permute-start(bf16[896,640]{1,0:T(8,128)(2,1)} %constant_dynamic-update-slice_fusion.w0), channel_id=1, source_target_pairs={{0,2},{2,0},{1,3},{3,1},{4,6},{6,4},{5,7},{7,5},{8,10},{10,8},{9,1... | collective-permute-start | bytes 3440648 | tf_op jit(solution)/shard_map/ppermute | solution.py:375
  63.0 34.9 %collective-permute-start.4 = (bf16[448,896]{1,0:T(8,128)(2,1)S(1)}, bf16[448,896]{1,0:T(8,128)(2,1)S(1)}, u32[]{:S(2)}, u32[]{:S(2)}) collective-permute-start(bf16[448,896]{1,0:T(8,128)(2,1)S(1)} %select_select_fusion.w_mine), channel_id=1, source_target_pairs={{0,16},{16,0},{1,17},{17,1},{2,18},{18,2},{3,19},{19,3},{4,20},{20... | collective-permute-start | bytes 2408456 | tf_op jit(solution)/shard_map/ppermute | solution.py:379
  73.2 19.6 %all-to-all-start.2 = ((bf16[4,48,896]{2,1,0:T(8,128)(2,1)}), bf16[4,48,896]{2,1,0:T(8,128)(2,1)}, u32[]{:S(2)}, u32[]{:S(2)}) async-start(bf16[4,48,896]{2,1,0:T(8,128)(2,1)} %copy-done.5), calls=%async_computation.2 | async-start | bytes 688128 | tf_op jit(solution)/shard_map/all_to_all | solution.py:428
  92.8 12.6 %all-to-all-start.1 = ((bf16[4,48,896]{2,1,0:T(8,128)(2,1)}), bf16[4,48,896]{2,1,0:T(8,128)(2,1)}, u32[]{:S(2)}, u32[]{:S(2)}) async-start(bf16[4,48,896]{2,1,0:T(8,128)(2,1)} %copy-done.4), calls=%async_computation.1 | async-start | bytes 688128 | tf_op jit(solution)/shard_map/all_to_all | solution.py:428
  97.9 27.5 %collective-permute-start.10 = (bf16[896,640]{1,0:T(8,128)(2,1)}, bf16[896,640]{1,0:T(8,128)(2,1)}, u32[]{:S(2)}, u32[]{:S(2)}) collective-permute-start(bf16[896,640]{1,0:T(8,128)(2,1)} %constant_dynamic-update-slice_fusion.w0), channel_id=1, source_target_pairs={{0,1},{1,0},{2,3},{3,2},{4,5},{5,4},{6,7},{7,6},{8,9},{9,8},{10,11... | collective-permute-start | bytes 3440648 | tf_op jit(solution)/shard_map/ppermute | solution.py:371
  100.0 25.3 %collective-permute-start.12 = (bf16[896,640]{1,0:T(8,128)(2,1)}, bf16[896,640]{1,0:T(8,128)(2,1)}, u32[]{:S(2)}, u32[]{:S(2)}) collective-permute-start(bf16[896,640]{1,0:T(8,128)(2,1)} %collective-permute-done.11.w2), channel_id=1, source_target_pairs={{0,1},{1,0},{2,3},{3,2},{4,5},{5,4},{6,7},{7,6},{8,9},{9,8},{10,11... | collective-permute-start | bytes 3440648 | tf_op jit(solution)/shard_map/ppermute | solution.py:371
  103.5 21.8 %copy-start.16 = (f32[896]{0:T(1024)S(1)}, f32[896]{0:T(1024)}, u32[]{:S(2)}) copy-start(f32[896]{0:T(1024)} %param.13) | copy-start | bytes 10756
  103.5 21.9 %copy-start.11 = (s32[48]{0:T(128)S(1)}, s32[48]{0:T(128)}, u32[]{:S(2)}) copy-start(s32[48]{0:T(128)} %len_ref.1) | copy-start | bytes 580
  103.5 9.8 %collective-permute-start.5 = (bf16[2,48,896]{2,1,0:T(8,128)(2,1)}, bf16[2,48,896]{2,1,0:T(8,128)(2,1)}, u32[]{:S(2)}, u32[]{:S(2)}) collective-permute-start(bf16[2,48,896]{2,1,0:T(8,128)(2,1)} %get-tuple-element.18), channel_id=1, source_target_pairs={{0,1},{1,0},{2,3},{3,2},{4,5},{5,4},{6,7},{7,6},{8,9},{9,8},{10,11... | collective-permute-start | bytes 516104 | tf_op jit(solution)/shard_map/ppermute | solution.py:371
  105.4 14.5 %copy-start.7 = (bf16[2,48,896]{2,1,0:T(8,128)(2,1)S(1)}, bf16[2,48,896]{2,1,0:T(8,128)(2,1)}, u32[]{:S(2)}) copy-start(bf16[2,48,896]{2,1,0:T(8,128)(2,1)} %copy-done.6) | copy-start | bytes 516100
  106.9 18.4 %copy-start.8 = (bf16[2,48,896]{2,1,0:T(8,128)(2,1)S(1)}, bf16[2,48,896]{2,1,0:T(8,128)(2,1)}, u32[]{:S(2)}) copy-start(bf16[2,48,896]{2,1,0:T(8,128)(2,1)} %copy-done.6) | copy-start | bytes 516100
  107.0 11.1 %collective-permute-start.7 = (bf16[2,48,896]{2,1,0:T(8,128)(2,1)S(1)}, bf16[2,48,896]{2,1,0:T(8,128)(2,1)S(1)}, u32[]{:S(2)}, u32[]{:S(2)}) collective-permute-start(bf16[2,48,896]{2,1,0:T(8,128)(2,1)S(1)} %shard_map.124), channel_id=1, source_target_pairs={{0,2},{1,3},{2,0},{3,1},{4,6},{5,7},{6,4},{7,5},{8,10},{9,11},{10,... | collective-permute-start | bytes 516104 | tf_op jit(solution)/shard_map/ppermute | solution.py:383
  113.2 6.8 %collective-permute-start.9 = (bf16[2,48,896]{2,1,0:T(8,128)(2,1)S(1)}, bf16[2,48,896]{2,1,0:T(8,128)(2,1)S(1)}, u32[]{:S(2)}, u32[]{:S(2)}) collective-permute-start(bf16[2,48,896]{2,1,0:T(8,128)(2,1)S(1)} %copy-done.10), channel_id=1, source_target_pairs={{0,3},{1,2},{2,1},{3,0},{4,7},{5,6},{6,5},{7,4},{8,11},{9,10},{10,... | collective-permute-start | bytes 516104 | tf_op jit(solution)/shard_map/ppermute | solution.py:383
  121.7 16.8 %all-to-all-start.3 = ((bf16[4,48,896]{2,1,0:T(8,128)(2,1)}), bf16[4,48,896]{2,1,0:T(8,128)(2,1)S(1)}, u32[]{:S(2)}, u32[]{:S(2)}) async-start(bf16[4,48,896]{2,1,0:T(8,128)(2,1)} %shard_map.127), calls=%async_computation.3 | async-start | bytes 688128 | tf_op jit(solution)/shard_map/all_to_all | solution.py:442
  125.3 13.2 %copy-start.17 = (s32[1,192]{1,0:T(1,128)S(1)}, s32[1,192]{1,0:T(1,128)}, u32[]{:S(2)}) copy-start(s32[1,192]{1,0:T(1,128)} %param.17) | copy-start | bytes 2308
  (11 other events, 30.9 us)

commit v7 on v6

--- a/solution.py
+++ b/solution.py
@@ -10,21 +10,40 @@
 HEAD_DIM = 128
 ROW_STEP = 8
 LANES = 128
-DOWN_LIMIT = 20
 PAGES = 2
 SHORT = pl.CostEstimate(flops=1, bytes_accessed=1, transcendentals=0)
-
-
-def down_kernel(counts, planes, cuts, *refs):
+LONG = pl.CostEstimate(flops=1 << 36, bytes_accessed=1 << 27, transcendentals=0)
+
+
+def down_kernel(counts, planes, cuts, fresh, *refs):
     groups = len(counts)
-    xs, (w, out, x_part, acc) = refs[:groups], refs[groups:]
+    xs, w, rest = refs[:groups], refs[groups], refs[groups + 1 :]
+    if fresh:
+        out, w_kept, x_all, acc, x_sem, w_sem = rest
+    else:
+        out, x_all, acc, x_sem = rest
+        w_kept = w
     first = [planes * sum(counts[:i]) for i in range(groups)]
+    loads = []
     for s, (lo, hi) in enumerate(cuts):
+        deep = pl.ds(lo, hi - lo)
+        copies = []
+        if fresh:
+            copies.append(pltpu.make_async_copy(w.at[deep], w_kept.at[deep], w_sem.at[s]))
         for i in range(groups):
-            x_part[first[i] : first[i] + planes * counts[i], : hi - lo] = xs[i][:, lo:hi]
-        part = jnp.dot(
-            x_part[:, : hi - lo], w[lo:hi, :], preferred_element_type=jnp.float32
-        )
+            here = pl.ds(first[i], planes * counts[i])
+            copies.append(
+                pltpu.make_async_copy(
+                    xs[i].at[:, deep], x_all.at[here, deep], x_sem.at[s, i]
+                )
+            )
+        for copy in copies:
+            copy.start()
+        loads.append(copies)
+    for s, (lo, hi) in enumerate(cuts):
+        for copy in loads[s]:
+            copy.wait()
+        part = jnp.dot(x_all[:, lo:hi], w_kept[lo:hi, :], preferred_element_type=jnp.float32)
         acc[...] = part if s == 0 else acc[...] + part
     for i, n in enumerate(counts):
         row = sum(counts[:i])
@@ -33,25 +52,28 @@
             out[p, row : row + n, :] = acc[at : at + n, :].astype(out.dtype)
 
 
-def down(xs, w, planes):
+def down(xs, w, planes, fresh, cost):
     depth, columns = w.shape
     counts = [x.shape[0] // planes for x in xs]
     rows = sum(counts)
-    tiles, parts = depth // LANES, 4
+    tiles, parts = depth // LANES, 6
     ends = [LANES * (tiles * i // parts) for i in range(parts)] + [depth]
-    most = max(hi - lo for lo, hi in zip(ends[:-1], ends[1:]))
     vmem = pl.BlockSpec(memory_space=pltpu.VMEM)
+    anywhere = pl.BlockSpec(memory_space=pl.ANY)
+    sums = jax.ShapeDtypeStruct((planes, rows, columns), jnp.bfloat16)
     return pl.pallas_call(
-        functools.partial(down_kernel, counts, planes, list(zip(ends[:-1], ends[1:]))),
-        out_shape=jax.ShapeDtypeStruct((planes, rows, columns), jnp.bfloat16),
-        in_specs=[vmem] * (len(xs) + 1),
-        out_specs=vmem,
+        functools.partial(down_kernel, counts, planes, list(zip(ends[:-1], ends[1:])), fresh),
+        out_shape=(sums, pltpu.VMEM(w.shape, w.dtype)) if fresh else sums,
+        in_specs=[anywhere] * len(xs) + [pl.BlockSpec(memory_space=pltpu.HBM) if fresh else vmem],
+        out_specs=(vmem, vmem) if fresh else vmem,
         scratch_shapes=[
-            pltpu.VMEM((planes * rows, most), jnp.bfloat16),
+            pltpu.VMEM((planes * rows, depth), jnp.bfloat16),
             pltpu.VMEM((planes * rows, columns), jnp.float32),
+            pltpu.SemaphoreType.DMA((parts, len(xs))),
+            *([pltpu.SemaphoreType.DMA((parts,))] if fresh else []),
         ],
-        cost_estimate=SHORT,
-        compiler_params=pltpu.CompilerParams(vmem_limit_bytes=DOWN_LIMIT * 1024 * 1024),
+        cost_estimate=cost,
+        compiler_params=pltpu.CompilerParams(vmem_limit_bytes=(48 if fresh else 14) * 1024 * 1024),
     )(*xs, w)
 
 
@@ -415,30 +437,43 @@
     g, m, c = lax.axis_index("groups"), lax.axis_index("mp"), lax.axis_index(PLANE)
     slots = talker_slot[0]
 
-    pick = (jnp.arange(planes * owned)[:, None] == slots[None, :]).astype(jnp.bfloat16)
-    rows = jnp.dot(pick, thinker_act, preferred_element_type=jnp.float32).astype(jnp.bfloat16)
-
-    across = over_section(rows)
-    peer = over_core(rows)
-    near = down([rows, peer], w_think, planes)
+    chunks = [(0, 32), (32, 16)]
+
+    sent = []
+    for first, n in chunks:
+        plane = jnp.arange(planes, dtype=jnp.int32)[:, None] * owned
+        want = (plane + first + jnp.arange(n, dtype=jnp.int32)[None, :]).reshape(-1)
+        pick = (want[:, None] == slots[None, :]).astype(jnp.bfloat16)
+        rows = jnp.dot(pick, thinker_act, preferred_element_type=jnp.float32)
+        sent.append(rows.astype(jnp.bfloat16))
+
+    crossed = [over_section(x) for x in sent]
+    peers = [over_core(x) for x in sent]
+    near, w_kept = down([*sent, *peers], w_think, planes, True, LONG)
     near_terms = lax.all_to_all(near, "mp", 0, 0)
-    block_w = feature_block(after(w_proj, peer), g, m, c, near)
-    across = after(across, near)
-    far = [down([x], w_think, planes) for x in (across, over_core(across))]
+    far = []
+    made = near_terms
+    for x in crossed:
+        x = after(x, made)
+        made = down([x, over_core(x)], w_kept, planes, False, SHORT)
+        far.append(made)
     far_terms = [lax.all_to_all(x, "mp", 0, 0) for x in far]
+    block_w = feature_block(after(w_proj, near), g, m, c, far[0])
 
     mine = jnp.concatenate([w_query, w_key, w_value], axis=1)
-    other = over_section(after(mine, across))
+    other = over_section(after(mine, x))
 
     turn = g.reshape(1)
-    own, next_core = finish(turn, near_terms, block_w, 2)
+    own, next_core = finish(turn, after(near_terms, made), block_w, 2)
     pieces = [[own], [over_core(next_core)], [], []]
-    for e, terms in zip((2, 3), far_terms):
-        (made,) = finish(turn, terms, block_w, 1)
-        pieces[e].append(over_plane(made, e))
-    other = after(other, made)
+    halves = [own]
+    for terms in far_terms:
+        halves = finish(turn, after(terms, halves[0]), block_w, 2)
+        for e in (2, 3):
+            pieces[e].append(over_plane(halves[e - 2], e))
+    other = after(other, halves[0])
     weights = [mine, over_core(mine), other, over_core(other)]
-    spans = [[(0, owned)]] * 4
+    spans = [[(0, owned)], [(0, owned)], chunks, chunks]
     home = lax.all_to_all(collect(c.reshape(1), pieces, spans), "mp", 0, 0)
     new_kv, ctx = talker(c.reshape(1), pieces, spans, talker_gain, weights, kv_len, kv_cache)
     home = after(home, ctx)

time: 140 us -> 153 us (1.093)
  waiting for transfers between devices: 31.3 us -> 54.8 us
  starting transfers between devices: 50.3 us -> 37.9 us
  local copies, waits for them, and re-layouts: 17.1 us -> 20.4 us
  Pallas kernels: 34.5 us -> 32.3 us
    all_to_all x2, starting transfers between devices: 16.9 us -> 7.67 us  [four_planes(): far_terms = [lax.all_to_all(x, 'mp', 0, 0) for x in far]]
    all_to_all x1, waiting for transfers between devices: 0.72 us -> 9.7 us  [four_planes(): near_terms = lax.all_to_all(near, 'mp', 0, 0)]
    ppermute x1, waiting for transfers between devices: 0.01 us -> 7.98 us  [feature_block(): lax.ppermute(piece, GROUP, [(b * 4 + b, (b ^ 1) * 4 + b) for b in range(4)])]
    ppermute x2 -> x3, starting transfers between devices: 4.34 us -> 9.03 us  [over_section(): return lax.ppermute(x, 'section', [(0, 1), (1, 0)])]
    ppermute x2 -> x4, starting transfers between devices: 6.26 us -> 2.52 us  [over_plane(): return lax.ppermute(x, PLANE, [(b, b ^ e) for b in range(4)])]
    ppermute x1, waiting for transfers between devices: 0.01 us -> 3.66 us  [over_groups(): return lax.ppermute(x, 'groups', [(0, 1), (1, 0)])]
    ppermute x1, starting transfers between devices: 5.91 us -> 2.45 us  [feature_block(): lax.ppermute(piece, GROUP, [(b * 4 + b, (b ^ 2) * 4 + b) for b in range(4)])]
    unnamed x38 -> x58, local copies, waits for them, and re-layouts: 16.3 us -> 18.8 us
  transfers between devices with their start and end apart: 17 -> 22, of which waited for: 6 -> 10; matrix products, arithmetic and copies ran while one was open for 3% -> 3% of each run, Pallas kernels for 25% -> 21%
where the time goes in v7:
time: 153 us; the launch traced here: 152 us
  waiting for transfers between devices  54.8 us (36%)
  starting transfers between devices  37.9 us (25%)
  Pallas kernels  32.3 us (21%)
  local copies, waits for them, and re-layouts  20.4 us (13%)
  matrix products  3.8 us (2%)
  other arithmetic  1.95 us (1%)
    ppermute x3, waiting for transfers between devices, over_section(): return lax.ppermute(x, 'section', [(0, 1), (1, 0)])  22.1 us
    unnamed x58, local copies, waits for them, and re-layouts  18.8 us
    pallas_call x3, Pallas kernels, down(): pl.pallas_call(functools.partial(down_kernel, counts, planes, list(zip(en...  16.2 us
    pallas_call x1, Pallas kernels, talker(): pl.pallas_call(functools.partial(talker_kernel, spans), out_shape=(jax.Sh...  12.3 us
    all_to_all x1, waiting for transfers between devices, four_planes(): near_terms = lax.all_to_all(near, 'mp', 0, 0)  9.7 us
    ppermute x3, starting transfers between devices, over_section(): return lax.ppermute(x, 'section', [(0, 1), (1, 0)])  9.03 us
    ppermute x1, waiting for transfers between devices, feature_block(): lax.ppermute(piece, GROUP, [(b * 4 + b, (b ^ 1) * 4 + b) for b in range(4)])  7.98 us
    ppermute x4, waiting for transfers between devices, over_plane(): return lax.ppermute(x, PLANE, [(b, b ^ e) for b in range(4)])  7.68 us
  transfers between devices with their start and end apart: 22, of which 10 were waited for; matrix products, arithmetic and copies ran while one was open for 3% of the time, Pallas kernels for 21%

profile of v7, /device:TPU:0, one launch (start us, length us, event | category | flops | bytes accessed | tf_op | source)
XLA Modules:
  0.0 152.2 jit_solution(4418997830034619264)
XLA Ops:
  4.7 2.9 %collective-permute-start.3 = (bf16[128,4736]{1,0:T(8,128)(2,1)S(1)}, bf16[128,4736]{1,0:T(8,128)(2,1)S(1)}, u32[]{:S(2)}, u32[]{:S(2)}) collective-permute-start(bf16[128,4736]{1,0:T(8,128)(2,1)S(1)} %convolution_convert_fusion.refs_0_), channel_id=1, source_target_pairs={{0,2},{2,0},{1,3},{3,1},{4,6},{6,4},{5,7},{7,5},{8,10},{10,8},{9,1... | collective-permute-start | bytes 3637256 | tf_op jit(solution)/shard_map/ppermute | solution.py:397
  8.5 8.2 %shard_map.121 = (bf16[4,96,896]{2,1,0:T(8,128)(2,1)}, bf16[4736,896]{1,0:T(8,128)(2,1)S(1)}) custom-call(bf16[128,4736]{1,0:T(8,128)(2,1)} %copy-done.17, bf16[64,4736]{1,0:T(8,128)(2,1)} %copy-done.21, bf16[128,4736]{1,0:T(8,128)(2,1)} %collective-permute-done.refs_2_, bf16[64,4736]{1,0:T(8,128)(2,1)} %copy-done.27, bf16[4736,896]{1,0:T(8,128)(2,1)} %refs_4_.1), custom_call_target="tpu_custom_call" | custom-call | flops 68719476736 | bytes 134217728 | tf_op jit(solution)/shard_map/pallas_call | solution.py:64
  16.8 3.3 %copy-done.2 = bf16[4736,896]{1,0:T(8,128)(2,1)} copy-done((bf16[4736,896]{1,0:T(8,128)(2,1)}, bf16[4736,896]{1,0:T(8,128)(2,1)S(1)}, u32[]{:S(2)}) %copy-start.2) | copy-done | bytes 8486936
  20.1 5.9 %all-to-all-start = ((bf16[4,96,896]{2,1,0:T(8,128)(2,1)}), bf16[4,96,896]{2,1,0:T(8,128)(2,1)S(1)}, u32[]{:S(2)}, u32[]{:S(2)}) async-start(bf16[4,96,896]{2,1,0:T(8,128)(2,1)} %get-tuple-element.24), calls=%async_computation | async-start | bytes 1376256 | tf_op jit(solution)/shard_map/all_to_all | solution.py:453
  26.0 8.6 %collective-permute-done.3.refs_0_ = bf16[128,4736]{1,0:T(8,128)(2,1)S(1)} collective-permute-done((bf16[128,4736]{1,0:T(8,128)(2,1)S(1)}, bf16[128,4736]{1,0:T(8,128)(2,1)S(1)}, u32[]{:S(2)}, u32[]{:S(2)}) %collective-permute-start.3) | collective-permute-done | bytes 1212448 | tf_op jit(solution)/shard_map/ppermute | solution.py:397
  34.6 9.7 %all-to-all-done.terms = bf16[4,96,896]{2,1,0:T(8,128)(2,1)S(1)} async-done(((bf16[4,96,896]{2,1,0:T(8,128)(2,1)}), bf16[4,96,896]{2,1,0:T(8,128)(2,1)S(1)}, u32[]{:S(2)}, u32[]{:S(2)}) %all-to-all-start) | async-done | bytes 688160 | tf_op jit(solution)/shard_map/all_to_all | solution.py:453
  45.8 2.4 %collective-permute-start.6 = (bf16[448,896]{1,0:T(8,128)(2,1)S(1)}, bf16[448,896]{1,0:T(8,128)(2,1)}, u32[]{:S(2)}, u32[]{:S(2)}) collective-permute-start(bf16[448,896]{1,0:T(8,128)(2,1)S(1)} %constant_dynamic-slice_fusion), channel_id=1, source_target_pairs={{0,8},{5,13},{10,2},{15,7},{16,24},{21,29},{26,18},{31,23}} | collective-permute-start | bytes 2408456 | tf_op jit(solution)/shard_map/ppermute | solution.py:415
  49.6 3.4 %copy-done.3 = bf16[4736,896]{1,0:T(8,128)(2,1)S(1)} copy-done((bf16[4736,896]{1,0:T(8,128)(2,1)S(1)}, bf16[4736,896]{1,0:T(8,128)(2,1)}, u32[]{:S(2)}) %copy-start.3) | copy-done | bytes 8486936
  53.0 4.6 %shard_map.122 = bf16[4,64,896]{2,1,0:T(8,128)(2,1)} custom-call(bf16[128,4736]{1,0:T(8,128)(2,1)S(1)} %collective-permute-done.3.refs_0_, bf16[128,4736]{1,0:T(8,128)(2,1)S(1)} %collective-permute-done.4.refs_1_, bf16[4736,896]{1,0:T(8,128)(2,1)S(1)} %copy-done.3), custom_call_target="tpu_custom_call" | custom-call | flops 1 | bytes 1 | tf_op jit(solution)/shard_map/pallas_call | solution.py:64
  57.7 8.0 %collective-permute-done.7 = bf16[448,896]{1,0:T(8,128)(2,1)S(1)} collective-permute-done((bf16[448,896]{1,0:T(8,128)(2,1)S(1)}, bf16[448,896]{1,0:T(8,128)(2,1)S(1)}, u32[]{:S(2)}, u32[]{:S(2)}) %collective-permute-start.7) | collective-permute-done | bytes 802848 | tf_op jit(solution)/shard_map/ppermute | solution.py:416
  67.2 3.5 %collective-permute-start.2 = (bf16[64,4736]{1,0:T(8,128)(2,1)S(1)}, bf16[64,4736]{1,0:T(8,128)(2,1)}, u32[]{:S(2)}, u32[]{:S(2)}) collective-permute-start(bf16[64,4736]{1,0:T(8,128)(2,1)S(1)} %copy-done.22), channel_id=1, source_target_pairs={{0,2},{2,0},{1,3},{3,1},{4,6},{6,4},{5,7},{7,5},{8,10},{10,8},{9,1... | collective-permute-start | bytes 1818632 | tf_op jit(solution)/shard_map/ppermute | solution.py:397
  70.9 13.5 %collective-permute-done.2.refs_0_ = bf16[64,4736]{1,0:T(8,128)(2,1)} collective-permute-done((bf16[64,4736]{1,0:T(8,128)(2,1)S(1)}, bf16[64,4736]{1,0:T(8,128)(2,1)}, u32[]{:S(2)}, u32[]{:S(2)}) %collective-permute-start.2) | collective-permute-done | bytes 606240 | tf_op jit(solution)/shard_map/ppermute | solution.py:397
  84.5 2.6 %collective-permute-start.16 = (bf16[896,640]{1,0:T(8,128)(2,1)S(1)}, bf16[896,640]{1,0:T(8,128)(2,1)}, u32[]{:S(2)}, u32[]{:S(2)}) collective-permute-start(bf16[896,640]{1,0:T(8,128)(2,1)S(1)} %constant_dynamic-update-slice_fusion.w0), channel_id=1, source_target_pairs={{0,2},{2,0},{1,3},{3,1},{4,6},{6,4},{5,7},{7,5},{8,10},{10,8},{9,1... | collective-permute-start | bytes 3440648 | tf_op jit(solution)/shard_map/ppermute | solution.py:397
  87.1 3.5 %all-to-all-start.1 = ((bf16[4,64,896]{2,1,0:T(8,128)(2,1)}), bf16[4,64,896]{2,1,0:T(8,128)(2,1)S(1)}, u32[]{:S(2)}, u32[]{:S(2)}) async-start(bf16[4,64,896]{2,1,0:T(8,128)(2,1)} %shard_map.122), calls=%async_computation.1 | async-start | bytes 917504 | tf_op jit(solution)/shard_map/all_to_all | solution.py:460
  94.0 3.4 %copy-done.4 = bf16[4736,896]{1,0:T(8,128)(2,1)S(1)} copy-done((bf16[4736,896]{1,0:T(8,128)(2,1)S(1)}, bf16[4736,896]{1,0:T(8,128)(2,1)}, u32[]{:S(2)}) %copy-start.4) | copy-done | bytes 8486936
  97.4 3.3 %shard_map.123 = bf16[4,32,896]{2,1,0:T(8,128)(2,1)S(1)} custom-call(bf16[64,4736]{1,0:T(8,128)(2,1)} %collective-permute-done.2.refs_0_, bf16[64,4736]{1,0:T(8,128)(2,1)} %collective-permute-done.5.refs_1_, bf16[4736,896]{1,0:T(8,128)(2,1)S(1)} %copy-done.4), custom_call_target="tpu_custom_call" | custom-call | flops 1 | bytes 1 | tf_op jit(solution)/shard_map/pallas_call | solution.py:64
  101.4 3.2 %all-to-all-done.1.terms = bf16[4,64,896]{2,1,0:T(8,128)(2,1)S(1)} async-done(((bf16[4,64,896]{2,1,0:T(8,128)(2,1)}), bf16[4,64,896]{2,1,0:T(8,128)(2,1)S(1)}, u32[]{:S(2)}, u32[]{:S(2)}) %all-to-all-start.1) | async-done | bytes 458784 | tf_op jit(solution)/shard_map/all_to_all | solution.py:460
  104.6 4.2 %all-to-all-start.2 = ((bf16[4,32,896]{2,1,0:T(8,128)(2,1)}), bf16[4,32,896]{2,1,0:T(8,128)(2,1)}, u32[]{:S(2)}, u32[]{:S(2)}) async-start(bf16[4,32,896]{2,1,0:T(8,128)(2,1)} %copy-done.9), calls=%async_computation.2 | async-start | bytes 458752 | tf_op jit(solution)/shard_map/all_to_all | solution.py:460
  108.8 3.7 %collective-permute-done.9.w_other = bf16[448,896]{1,0:T(8,128)(2,1)S(1)} collective-permute-done((bf16[448,896]{1,0:T(8,128)(2,1)S(1)}, bf16[448,896]{1,0:T(8,128)(2,1)S(1)}, u32[]{:S(2)}, u32[]{:S(2)}) %collective-permute-start.9) | collective-permute-done | bytes 802848 | tf_op jit(solution)/shard_map/ppermute | solution.py:401
  120.8 2.6 %collective-permute-done.12.refs_3_ = bf16[2,16,896]{2,1,0:T(8,128)(2,1)S(1)} collective-permute-done((bf16[2,16,896]{2,1,0:T(8,128)(2,1)S(1)}, bf16[2,16,896]{2,1,0:T(8,128)(2,1)S(1)}, u32[]{:S(2)}, u32[]{:S(2)}) %collective-permute-start.12) | collective-permute-done | bytes 57376 | tf_op jit(solution)/shard_map/ppermute | solution.py:405
  124.4 4.8 %collective-permute-done.11.refs_2_ = bf16[2,32,896]{2,1,0:T(8,128)(2,1)S(1)} collective-permute-done((bf16[2,32,896]{2,1,0:T(8,128)(2,1)S(1)}, bf16[2,32,896]{2,1,0:T(8,128)(2,1)S(1)}, u32[]{:S(2)}, u32[]{:S(2)}) %collective-permute-start.11) | collective-permute-done | bytes 114720 | tf_op jit(solution)/shard_map/ppermute | solution.py:405
  129.9 4.8 %all-to-all-start.3 = ((bf16[4,48,896]{2,1,0:T(8,128)(2,1)}), bf16[4,48,896]{2,1,0:T(8,128)(2,1)}, u32[]{:S(2)}, u32[]{:S(2)}) async-start(bf16[4,48,896]{2,1,0:T(8,128)(2,1)} %shard_map.127), calls=%async_computation.3 | async-start | bytes 688128 | tf_op jit(solution)/shard_map/all_to_all | solution.py:477
  138.0 12.3 %shard_map.128 = (bf16[48,1024]{1,0:T(8,128)(2,1)}, f32[48,1536]{1,0:T(8,128)}) custom-call(s32[1]{0:T(128)} %bitcast.1.block_ref, s32[48]{0:T(128)S(1)} %copy-done.12, f32[1,896]{1,0:T(1,128)S(1)} %reshape.58.gain, bf16[896,640]{1,0:T(8,128)(2,1)S(1)} %constant_dynamic-update-slice_fusion.w0, bf16[896,640]{1,0:T(8,128)(2,1)} %collective-permute-done.15.w1, ...), custom_call_target="tpu_custom_call" | custom-call | flops 1 | bytes 1 | tf_op jit(solution)/shard_map/pallas_call | solution.py:290
  150.2 2.0 %convolution_convert_fusion.2 = bf16[192,896]{1,0:T(8,128)(2,1)} fusion(bf16[192,896]{1,0:T(8,128)(2,1)} %bitcast.3, s32[192]{0:T(256)S(1)} %bitcast.9), kind=kOutput, calls=%fused_computation.2 | convolution fusion | flops 66269184 | bytes 688896 | tf_op jit(solution)/shard_map/dot_general | solution.py:481
  (99 shorter events, 26.8 us)
Async XLA Ops:
  3.4 4.3 %collective-permute-start = (bf16[128,4736]{1,0:T(8,128)(2,1)S(1)}, bf16[128,4736]{1,0:T(8,128)(2,1)}, u32[]{:S(2)}, u32[]{:S(2)}) collective-permute-start(bf16[128,4736]{1,0:T(8,128)(2,1)S(1)} %convolution_convert_fusion.refs_0_), channel_id=1, source_target_pairs={{0,1},{1,0},{2,3},{3,2},{4,5},{5,4},{6,7},{7,6},{8,9},{9,8},{10,11... | collective-permute-start | bytes 3637256 | tf_op jit(solution)/shard_map/ppermute | solution.py:393
  4.6 3.1 %collective-permute-start.1 = (bf16[64,4736]{1,0:T(8,128)(2,1)S(1)}, bf16[64,4736]{1,0:T(8,128)(2,1)S(1)}, u32[]{:S(2)}, u32[]{:S(2)}) collective-permute-start(bf16[64,4736]{1,0:T(8,128)(2,1)S(1)} %convolution_convert_fusion.1.refs_1_), channel_id=1, source_target_pairs={{0,1},{1,0},{2,3},{3,2},{4,5},{5,4},{6,7},{7,6},{8,9},{9,8},{10,11... | collective-permute-start | bytes 1818632 | tf_op jit(solution)/shard_map/ppermute | solution.py:393
  4.7 29.9 %collective-permute-start.3 = (bf16[128,4736]{1,0:T(8,128)(2,1)S(1)}, bf16[128,4736]{1,0:T(8,128)(2,1)S(1)}, u32[]{:S(2)}, u32[]{:S(2)}) collective-permute-start(bf16[128,4736]{1,0:T(8,128)(2,1)S(1)} %convolution_convert_fusion.refs_0_), channel_id=1, source_target_pairs={{0,2},{2,0},{1,3},{3,1},{4,6},{6,4},{5,7},{7,5},{8,10},{10,8},{9,1... | collective-permute-start | bytes 3637256 | tf_op jit(solution)/shard_map/ppermute | solution.py:397
  20.1 24.2 %all-to-all-start = ((bf16[4,96,896]{2,1,0:T(8,128)(2,1)}), bf16[4,96,896]{2,1,0:T(8,128)(2,1)S(1)}, u32[]{:S(2)}, u32[]{:S(2)}) async-start(bf16[4,96,896]{2,1,0:T(8,128)(2,1)} %get-tuple-element.24), calls=%async_computation | async-start | bytes 1376256 | tf_op jit(solution)/shard_map/all_to_all | solution.py:453
  44.3 5.2 %collective-permute-start.4 = (bf16[128,4736]{1,0:T(8,128)(2,1)S(1)}, bf16[128,4736]{1,0:T(8,128)(2,1)S(1)}, u32[]{:S(2)}, u32[]{:S(2)}) collective-permute-start(bf16[128,4736]{1,0:T(8,128)(2,1)S(1)} %collective-permute-done.3.refs_0_), channel_id=1, source_target_pairs={{0,1},{1,0},{2,3},{3,2},{4,5},{5,4},{6,7},{7,6},{8,9},{9,8},{10,11... | collective-permute-start | bytes 3637256 | tf_op jit(solution)/shard_map/ppermute | solution.py:393
  45.8 11.9 %collective-permute-start.6 = (bf16[448,896]{1,0:T(8,128)(2,1)S(1)}, bf16[448,896]{1,0:T(8,128)(2,1)}, u32[]{:S(2)}, u32[]{:S(2)}) collective-permute-start(bf16[448,896]{1,0:T(8,128)(2,1)S(1)} %constant_dynamic-slice_fusion), channel_id=1, source_target_pairs={{0,8},{5,13},{10,2},{15,7},{16,24},{21,29},{26,18},{31,23}} | collective-permute-start | bytes 2408456 | tf_op jit(solution)/shard_map/ppermute | solution.py:415
  48.2 17.4 %collective-permute-start.7 = (bf16[448,896]{1,0:T(8,128)(2,1)S(1)}, bf16[448,896]{1,0:T(8,128)(2,1)S(1)}, u32[]{:S(2)}, u32[]{:S(2)}) collective-permute-start(bf16[448,896]{1,0:T(8,128)(2,1)S(1)} %constant_dynamic-slice_fusion), channel_id=1, source_target_pairs={{0,4},{5,1},{10,14},{15,11},{16,20},{21,17},{26,30},{31,27}} | collective-permute-start | bytes 2408456 | tf_op jit(solution)/shard_map/ppermute | solution.py:416
  53.0 17.7 %copy-start.20 = (bf16[896,384]{1,0:T(8,128)(2,1)S(1)}, bf16[896,384]{1,0:T(8,128)(2,1)}, u32[]{:S(2)}) copy-start(bf16[896,384]{1,0:T(8,128)(2,1)} %param.14) | copy-start | bytes 2064388
  65.6 24.9 %collective-permute-start.8 = (bf16[448,896]{1,0:T(8,128)(2,1)}, bf16[448,896]{1,0:T(8,128)(2,1)}, u32[]{:S(2)}, u32[]{:S(2)}) collective-permute-start(bf16[448,896]{1,0:T(8,128)(2,1)} %collective-permute-done.6), channel_id=1, source_target_pairs={{8,12},{13,9},{2,6},{7,3},{24,28},{29,25},{18,22},{23,19}} | collective-permute-start | bytes 2408456 | tf_op jit(solution)/shard_map/ppermute | solution.py:418
  67.2 17.3 %collective-permute-start.2 = (bf16[64,4736]{1,0:T(8,128)(2,1)S(1)}, bf16[64,4736]{1,0:T(8,128)(2,1)}, u32[]{:S(2)}, u32[]{:S(2)}) collective-permute-start(bf16[64,4736]{1,0:T(8,128)(2,1)S(1)} %copy-done.22), channel_id=1, source_target_pairs={{0,2},{2,0},{1,3},{3,1},{4,6},{6,4},{5,7},{7,5},{8,10},{10,8},{9,1... | collective-permute-start | bytes 1818632 | tf_op jit(solution)/shard_map/ppermute | solution.py:397
  84.5 34.0 %collective-permute-start.16 = (bf16[896,640]{1,0:T(8,128)(2,1)S(1)}, bf16[896,640]{1,0:T(8,128)(2,1)}, u32[]{:S(2)}, u32[]{:S(2)}) collective-permute-start(bf16[896,640]{1,0:T(8,128)(2,1)S(1)} %constant_dynamic-update-slice_fusion.w0), channel_id=1, source_target_pairs={{0,2},{2,0},{1,3},{3,1},{4,6},{6,4},{5,7},{7,5},{8,10},{10,8},{9,1... | collective-permute-start | bytes 3440648 | tf_op jit(solution)/shard_map/ppermute | solution.py:397
  87.1 6.9 %collective-permute-start.5 = (bf16[64,4736]{1,0:T(8,128)(2,1)}, bf16[64,4736]{1,0:T(8,128)(2,1)}, u32[]{:S(2)}, u32[]{:S(2)}) collective-permute-start(bf16[64,4736]{1,0:T(8,128)(2,1)} %collective-permute-done.2.refs_0_), channel_id=1, source_target_pairs={{0,1},{1,0},{2,3},{3,2},{4,5},{5,4},{6,7},{7,6},{8,9},{9,8},{10,11... | collective-permute-start | bytes 1818632 | tf_op jit(solution)/shard_map/ppermute | solution.py:393
  87.1 17.5 %all-to-all-start.1 = ((bf16[4,64,896]{2,1,0:T(8,128)(2,1)}), bf16[4,64,896]{2,1,0:T(8,128)(2,1)S(1)}, u32[]{:S(2)}, u32[]{:S(2)}) async-start(bf16[4,64,896]{2,1,0:T(8,128)(2,1)} %shard_map.122), calls=%async_computation.1 | async-start | bytes 917504 | tf_op jit(solution)/shard_map/all_to_all | solution.py:460
  92.4 20.1 %collective-permute-start.9 = (bf16[448,896]{1,0:T(8,128)(2,1)S(1)}, bf16[448,896]{1,0:T(8,128)(2,1)S(1)}, u32[]{:S(2)}, u32[]{:S(2)}) collective-permute-start(bf16[448,896]{1,0:T(8,128)(2,1)S(1)} %select_select_fusion.w_mine), channel_id=1, source_target_pairs={{0,16},{16,0},{1,17},{17,1},{2,18},{18,2},{3,19},{19,3},{4,20},{20... | collective-permute-start | bytes 2408456 | tf_op jit(solution)/shard_map/ppermute | solution.py:401
  104.6 12.5 %all-to-all-start.2 = ((bf16[4,32,896]{2,1,0:T(8,128)(2,1)}), bf16[4,32,896]{2,1,0:T(8,128)(2,1)}, u32[]{:S(2)}, u32[]{:S(2)}) async-start(bf16[4,32,896]{2,1,0:T(8,128)(2,1)} %copy-done.9), calls=%async_computation.2 | async-start | bytes 458752 | tf_op jit(solution)/shard_map/all_to_all | solution.py:460
  108.8 26.0 %collective-permute-start.15 = (bf16[896,640]{1,0:T(8,128)(2,1)S(1)}, bf16[896,640]{1,0:T(8,128)(2,1)}, u32[]{:S(2)}, u32[]{:S(2)}) collective-permute-start(bf16[896,640]{1,0:T(8,128)(2,1)S(1)} %constant_dynamic-update-slice_fusion.w0), channel_id=1, source_target_pairs={{0,1},{1,0},{2,3},{3,2},{4,5},{5,4},{6,7},{7,6},{8,9},{9,8},{10,11... | collective-permute-start | bytes 3440648 | tf_op jit(solution)/shard_map/ppermute | solution.py:393
  118.5 17.3 %copy-start.12 = (s32[48]{0:T(128)S(1)}, s32[48]{0:T(128)}, u32[]{:S(2)}) copy-start(s32[48]{0:T(128)} %len_ref.1) | copy-start | bytes 580
  118.5 16.2 %collective-permute-start.17 = (bf16[896,640]{1,0:T(8,128)(2,1)}, bf16[896,640]{1,0:T(8,128)(2,1)S(1)}, u32[]{:S(2)}, u32[]{:S(2)}) collective-permute-start(bf16[896,640]{1,0:T(8,128)(2,1)} %collective-permute-done.16.w2), channel_id=1, source_target_pairs={{0,1},{1,0},{2,3},{3,2},{4,5},{5,4},{6,7},{7,6},{8,9},{9,8},{10,11... | collective-permute-start | bytes 3440648 | tf_op jit(solution)/shard_map/ppermute | solution.py:393
  118.6 4.8 %collective-permute-start.12 = (bf16[2,16,896]{2,1,0:T(8,128)(2,1)S(1)}, bf16[2,16,896]{2,1,0:T(8,128)(2,1)S(1)}, u32[]{:S(2)}, u32[]{:S(2)}) collective-permute-start(bf16[2,16,896]{2,1,0:T(8,128)(2,1)S(1)} %get-tuple-element.37), channel_id=1, source_target_pairs={{0,2},{1,3},{2,0},{3,1},{4,6},{5,7},{6,4},{7,5},{8,10},{9,11},{10,... | collective-permute-start | bytes 172040 | tf_op jit(solution)/shard_map/ppermute | solution.py:405
  118.7 5.0 %collective-permute-start.14 = (bf16[2,16,896]{2,1,0:T(8,128)(2,1)S(1)}, bf16[2,16,896]{2,1,0:T(8,128)(2,1)S(1)}, u32[]{:S(2)}, u32[]{:S(2)}) collective-permute-start(bf16[2,16,896]{2,1,0:T(8,128)(2,1)S(1)} %get-tuple-element.39), channel_id=1, source_target_pairs={{0,3},{1,2},{2,1},{3,0},{4,7},{5,6},{6,5},{7,4},{8,11},{9,10},{10,... | collective-permute-start | bytes 172040 | tf_op jit(solution)/shard_map/ppermute | solution.py:405
  120.5 8.7 %collective-permute-start.10 = (bf16[2,48,896]{2,1,0:T(8,128)(2,1)}, bf16[2,48,896]{2,1,0:T(8,128)(2,1)S(1)}, u32[]{:S(2)}, u32[]{:S(2)}) collective-permute-start(bf16[2,48,896]{2,1,0:T(8,128)(2,1)} %get-tuple-element.33), channel_id=1, source_target_pairs={{0,1},{1,0},{2,3},{3,2},{4,5},{5,4},{6,7},{7,6},{8,9},{9,8},{10,11... | collective-permute-start | bytes 516104 | tf_op jit(solution)/shard_map/ppermute | solution.py:393
  123.4 5.8 %collective-permute-start.11 = (bf16[2,32,896]{2,1,0:T(8,128)(2,1)S(1)}, bf16[2,32,896]{2,1,0:T(8,128)(2,1)S(1)}, u32[]{:S(2)}, u32[]{:S(2)}) collective-permute-start(bf16[2,32,896]{2,1,0:T(8,128)(2,1)S(1)} %copy-done.16), channel_id=1, source_target_pairs={{0,2},{1,3},{2,0},{3,1},{4,6},{5,7},{6,4},{7,5},{8,10},{9,11},{10,... | collective-permute-start | bytes 344072 | tf_op jit(solution)/shard_map/ppermute | solution.py:405
  123.7 5.5 %collective-permute-start.13 = (bf16[2,32,896]{2,1,0:T(8,128)(2,1)S(1)}, bf16[2,32,896]{2,1,0:T(8,128)(2,1)S(1)}, u32[]{:S(2)}, u32[]{:S(2)}) collective-permute-start(bf16[2,32,896]{2,1,0:T(8,128)(2,1)S(1)} %copy-done.14), channel_id=1, source_target_pairs={{0,3},{1,2},{2,1},{3,0},{4,7},{5,6},{6,5},{7,4},{8,11},{9,10},{10,... | collective-permute-start | bytes 344072 | tf_op jit(solution)/shard_map/ppermute | solution.py:405
  129.9 20.3 %all-to-all-start.3 = ((bf16[4,48,896]{2,1,0:T(8,128)(2,1)}), bf16[4,48,896]{2,1,0:T(8,128)(2,1)}, u32[]{:S(2)}, u32[]{:S(2)}) async-start(bf16[4,48,896]{2,1,0:T(8,128)(2,1)} %shard_map.127), calls=%async_computation.3 | async-start | bytes 688128 | tf_op jit(solution)/shard_map/all_to_all | solution.py:477
  (26 other events, 148.4 us)

commit v8 on v6

--- a/solution.py
+++ b/solution.py
@@ -10,21 +10,33 @@
 HEAD_DIM = 128
 ROW_STEP = 8
 LANES = 128
-DOWN_LIMIT = 20
 PAGES = 2
 SHORT = pl.CostEstimate(flops=1, bytes_accessed=1, transcendentals=0)
+MOST_VMEM = 56 * 1024 * 1024
 
 
 def down_kernel(counts, planes, cuts, *refs):
     groups = len(counts)
-    xs, (w, out, x_part, acc) = refs[:groups], refs[groups:]
+    xs, (w, out, x_all, w_all, acc, x_sem, w_sem) = refs[:groups], refs[groups:]
     first = [planes * sum(counts[:i]) for i in range(groups)]
+    loads = []
     for s, (lo, hi) in enumerate(cuts):
+        deep = pl.ds(lo, hi - lo)
+        copies = [pltpu.make_async_copy(w.at[deep], w_all.at[deep], w_sem.at[s])]
         for i in range(groups):
-            x_part[first[i] : first[i] + planes * counts[i], : hi - lo] = xs[i][:, lo:hi]
-        part = jnp.dot(
-            x_part[:, : hi - lo], w[lo:hi, :], preferred_element_type=jnp.float32
-        )
+            here = pl.ds(first[i], planes * counts[i])
+            copies.append(
+                pltpu.make_async_copy(
+                    xs[i].at[:, deep], x_all.at[here, deep], x_sem.at[s, i]
+                )
+            )
+        for copy in copies:
+            copy.start()
+        loads.append(copies)
+    for s, (lo, hi) in enumerate(cuts):
+        for copy in loads[s]:
+            copy.wait()
+        part = jnp.dot(x_all[:, lo:hi], w_all[lo:hi, :], preferred_element_type=jnp.float32)
         acc[...] = part if s == 0 else acc[...] + part
     for i, n in enumerate(counts):
         row = sum(counts[:i])
@@ -37,21 +49,23 @@
     depth, columns = w.shape
     counts = [x.shape[0] // planes for x in xs]
     rows = sum(counts)
-    tiles, parts = depth // LANES, 4
+    tiles, parts = depth // LANES, 6
     ends = [LANES * (tiles * i // parts) for i in range(parts)] + [depth]
-    most = max(hi - lo for lo, hi in zip(ends[:-1], ends[1:]))
-    vmem = pl.BlockSpec(memory_space=pltpu.VMEM)
+    anywhere = pl.BlockSpec(memory_space=pl.ANY)
     return pl.pallas_call(
         functools.partial(down_kernel, counts, planes, list(zip(ends[:-1], ends[1:]))),
         out_shape=jax.ShapeDtypeStruct((planes, rows, columns), jnp.bfloat16),
-        in_specs=[vmem] * (len(xs) + 1),
-        out_specs=vmem,
+        in_specs=[anywhere] * (len(xs) + 1),
+        out_specs=pl.BlockSpec(memory_space=pltpu.VMEM),
         scratch_shapes=[
-            pltpu.VMEM((planes * rows, most), jnp.bfloat16),
+            pltpu.VMEM((planes * rows, depth), jnp.bfloat16),
+            pltpu.VMEM((depth, columns), jnp.bfloat16),
             pltpu.VMEM((planes * rows, columns), jnp.float32),
+            pltpu.SemaphoreType.DMA((parts, len(xs))),
+            pltpu.SemaphoreType.DMA((parts,)),
         ],
         cost_estimate=SHORT,
-        compiler_params=pltpu.CompilerParams(vmem_limit_bytes=DOWN_LIMIT * 1024 * 1024),
+        compiler_params=pltpu.CompilerParams(vmem_limit_bytes=MOST_VMEM),
     )(*xs, w)
 
 
@@ -122,13 +136,12 @@
     return out
 
 
-def talker_kernel(spans, block_ref, len_ref, gain, w0, w1, w2, w3, *refs):
+def talker_kernel(spans, blocks, block_ref, len_ref, gain, *refs):
     count = sum(map(len, spans))
-    pieces, (kv_hbm, new_kv, out_ref, kv_ref, sem, qkv, spreads, gathereds) = (
-        refs[:count],
-        refs[count:],
-    )
-    blocks = qkv.shape[0]
+    w_hbm, pieces = refs[:blocks], refs[blocks : blocks + count]
+    kv_hbm, new_kv, out_ref, kv_ref, sem, w_ref, w_sem, qkv, spreads, gathereds = refs[
+        blocks + count :
+    ]
     rows, cached, kv_width = kv_ref.shape
     width = kv_width // 2
     page = cached // PAGES
@@ -139,6 +152,12 @@
     key, value = group * HEAD_DIM, (group + 1) * HEAD_DIM
     inv = 1.0 / HEAD_DIM**0.5
 
+    w_copies = [
+        pltpu.make_async_copy(w_hbm[e], w_ref.at[e], w_sem.at[e]) for e in range(blocks)
+    ]
+    for copy in w_copies:
+        copy.start()
+
     @pl.loop(0, rows)
     def _(r):
         for p, (copy, needed) in enumerate(page_copies(len_ref, kv_hbm, kv_ref, sem, r)):
@@ -156,8 +175,9 @@
         total = term if total is None else total + term
     scale = lax.rsqrt(jnp.mean(total * total, axis=1, keepdims=True) + 1e-06)
     normed = (total * scale * gain[...]).astype(jnp.bfloat16)
-    for e, w in enumerate((w0, w1, w2, w3)):
-        made = jnp.dot(normed, w[...], preferred_element_type=jnp.float32)
+    for e in range(blocks):
+        w_copies[e].wait()
+        made = jnp.dot(normed, w_ref[e], preferred_element_type=jnp.float32)
         qkv[e ^ block_ref[0]] = made.astype(jnp.bfloat16).astype(jnp.float32)
     for g in range(blocks):
         for place, start in ((g, key), (blocks + g, value)):
@@ -266,24 +286,27 @@
     vmem = pl.BlockSpec(memory_space=pltpu.VMEM)
     smem = pl.BlockSpec(memory_space=pltpu.SMEM)
     return pl.pallas_call(
-        functools.partial(talker_kernel, spans),
+        functools.partial(talker_kernel, spans, blocks),
         out_shape=(
             jax.ShapeDtypeStruct((rows, kv_width), jnp.bfloat16),
             jax.ShapeDtypeStruct((rows, q_width), jnp.float32),
         ),
-        in_specs=[smem, smem]
-        + [vmem] * (1 + blocks + len(flat))
-        + [pl.BlockSpec(memory_space=pltpu.HBM)],
+        in_specs=[smem, smem, vmem]
+        + [pl.BlockSpec(memory_space=pl.ANY)] * blocks
+        + [vmem] * len(flat)
+        + [pl.BlockSpec(memory_space=pl.ANY)],
         out_specs=(vmem, vmem),
         scratch_shapes=[
             pltpu.VMEM((rows, cached, kv_width), jnp.bfloat16),
             pltpu.SemaphoreType.DMA((rows, PAGES)),
+            pltpu.VMEM((blocks, wide, columns), jnp.bfloat16),
+            pltpu.SemaphoreType.DMA((blocks,)),
             pltpu.VMEM((blocks, rows, columns), jnp.float32),
             pltpu.VMEM((sets, LANES, HEAD_DIM), jnp.float32),
             pltpu.VMEM((sets, LANES, HEAD_DIM), jnp.float32),
         ],
         cost_estimate=SHORT,
-        compiler_params=pltpu.CompilerParams(vmem_limit_bytes=46 * 1024 * 1024),
+        compiler_params=pltpu.CompilerParams(vmem_limit_bytes=48 * 1024 * 1024),
     )(block, kv_len, talker_gain.reshape(1, wide), *weights, *flat, kv_cache)
 
 
@@ -387,13 +410,17 @@
     return lax.optimization_barrier((x, *others))[0]
 
 
-def feature_block(w_proj, g, m, c, later):
+def feature_block_first(w_proj, g):
     half = w_proj.shape[0] // 2
     piece = lax.dynamic_slice_in_dim(w_proj, g * half, half, axis=0)
     two = lax.ppermute(piece, GROUP, [(b * 4 + b, (b ^ 2) * 4 + b) for b in range(4)])
     one = lax.ppermute(piece, GROUP, [(b * 4 + b, (b ^ 1) * 4 + b) for b in range(4)])
-    two, one, _ = lax.optimization_barrier((two, one, later))
+    return piece, one, two
+
+
+def feature_block(piece, one, two, m, c, later):
     three = lax.ppermute(two, GROUP, [((b ^ 2) * 4 + b, (b ^ 3) * 4 + b) for b in range(4)])
+    three = after(three, later)
     piece = jnp.where(m == c, piece, jnp.where(m == c ^ 2, two, jnp.where(m == c ^ 1, one, three)))
     return piece, over_groups(piece)
 
@@ -422,19 +449,24 @@
     peer = over_core(rows)
     near = down([rows, peer], w_think, planes)
     near_terms = lax.all_to_all(near, "mp", 0, 0)
-    block_w = feature_block(after(w_proj, peer), g, m, c, near)
-    across = after(across, near)
-    far = [down([x], w_think, planes) for x in (across, over_core(across))]
+    early_w = feature_block_first(after(w_proj, peer), g)
+    mine = jnp.concatenate([w_query, w_key, w_value], axis=1)
+
+    across, near_terms, mine, *early_w = lax.optimization_barrier(
+        (across, near_terms, mine, *early_w)
+    )
+    far = [down([across], w_think, planes)]
+    far.append(down([after(over_core(across), far[0])], w_think, planes))
     far_terms = [lax.all_to_all(x, "mp", 0, 0) for x in far]
-
-    mine = jnp.concatenate([w_query, w_key, w_value], axis=1)
     other = over_section(after(mine, across))
+    block_w = feature_block(*early_w, m, c, far[1])
 
     turn = g.reshape(1)
-    own, next_core = finish(turn, near_terms, block_w, 2)
+    own, next_core = finish(turn, after(near_terms, far[1]), block_w, 2)
     pieces = [[own], [over_core(next_core)], [], []]
+    made = own
     for e, terms in zip((2, 3), far_terms):
-        (made,) = finish(turn, terms, block_w, 1)
+        (made,) = finish(turn, after(terms, made), block_w, 1)
         pieces[e].append(over_plane(made, e))
     other = after(other, made)
     weights = [mine, over_core(mine), other, over_core(other)]

time: 140 us -> 138 us (0.986)
  local copies, waits for them, and re-layouts: 17.1 us -> 9.57 us
  waiting for transfers between devices: 31.3 us -> 38.8 us
  starting transfers between devices: 50.3 us -> 44.5 us
  other arithmetic: 1.78 us -> 3.76 us
    ppermute x1, waiting for transfers between devices: 0.01 us -> 9.91 us  [over_groups(): return lax.ppermute(x, 'groups', [(0, 1), (1, 0)])]
    all_to_all x2, starting transfers between devices: 16.9 us -> 8.41 us  [four_planes(): far_terms = [lax.all_to_all(x, 'mp', 0, 0) for x in far]]
    unnamed x38 -> x36, local copies, waits for them, and re-layouts: 16.3 us -> 8.37 us
    ppermute x2, starting transfers between devices: 4.34 us -> 11.4 us  [over_section(): return lax.ppermute(x, 'section', [(0, 1), (1, 0)])]
    ppermute x2, waiting for transfers between devices: 20.6 us -> 14.1 us  [over_section(): return lax.ppermute(x, 'section', [(0, 1), (1, 0)])]
    ppermute x2, starting transfers between devices: 6.26 us -> 1.45 us  [over_plane(): return lax.ppermute(x, PLANE, [(b, b ^ e) for b in range(4)])]
    pallas_call x3, Pallas kernels: 14.5 us -> 18.5 us  [down(): pl.pallas_call(functools.partial(down_kernel, counts, planes, list(zip(en...]
    ppermute x2, waiting for transfers between devices: 0.01 us -> 3.68 us  [the longest x1 3.68 us: feature_block_first(): lax.ppermute(piece, GROUP, [(b * 4 + b, (b ^ 2) * 4 + b) for b in range(4)])]
  transfers between devices with their start and end apart: 17 -> 17, of which waited for: 6 -> 8; matrix products, arithmetic and copies ran while one was open for 3% -> 4% of each run, Pallas kernels for 25% -> 25%
where the time goes in v8:
time: 138 us; the launch traced here: 137 us
  starting transfers between devices  44.5 us (32%)
  waiting for transfers between devices  38.8 us (28%)
  Pallas kernels  34.7 us (25%)
  local copies, waits for them, and re-layouts  9.57 us (7%)
  matrix products  4.56 us (3%)
  other arithmetic  3.76 us (3%)
    pallas_call x3, Pallas kernels, down(): pl.pallas_call(functools.partial(down_kernel, counts, planes, list(zip(en...  18.5 us
    ppermute x2, waiting for transfers between devices, over_section(): return lax.ppermute(x, 'section', [(0, 1), (1, 0)])  14.1 us
    pallas_call x1, Pallas kernels, talker(): pl.pallas_call(functools.partial(talker_kernel, spans, blocks), out_shape...  12 us
    ppermute x2, starting transfers between devices, over_section(): return lax.ppermute(x, 'section', [(0, 1), (1, 0)])  11.4 us
    ppermute x1, waiting for transfers between devices, over_groups(): return lax.ppermute(x, 'groups', [(0, 1), (1, 0)])  9.91 us
    all_to_all x2, starting transfers between devices, four_planes(): far_terms = [lax.all_to_all(x, 'mp', 0, 0) for x in far]  8.41 us
    unnamed x36, local copies, waits for them, and re-layouts  8.37 us
    ppermute x2, waiting for transfers between devices, over_plane(): return lax.ppermute(x, PLANE, [(b, b ^ e) for b in range(4)])  7.02 us
  transfers between devices with their start and end apart: 17, of which 8 were waited for; matrix products, arithmetic and copies ran while one was open for 4% of the time, Pallas kernels for 25%

profile of v8, /device:TPU:0, one launch (start us, length us, event | category | flops | bytes accessed | tf_op | source)
XLA Modules:
  0.0 136.9 jit_solution(3413934436201636494)
XLA Ops:
  2.1 2.5 %convolution_convert_fusion.refs_0_ = bf16[192,4736]{1,0:T(8,128)(2,1)} fusion(bf16[192,4736]{1,0:T(8,128)(2,1)S(1)} %copy-done, s32[192]{0:T(256)} %bitcast.6), kind=kOutput, calls=%fused_computation | convolution fusion | flops 350121984 | bytes 3638016 | tf_op jit(solution)/shard_map/dot_general | solution.py:446
  5.1 2.5 %collective-permute-start = (bf16[192,4736]{1,0:T(8,128)(2,1)}, bf16[192,4736]{1,0:T(8,128)(2,1)}, u32[]{:S(2)}, u32[]{:S(2)}) collective-permute-start(bf16[192,4736]{1,0:T(8,128)(2,1)} %convolution_convert_fusion.refs_0_), channel_id=1, source_target_pairs={{0,2},{2,0},{1,3},{3,1},{4,6},{6,4},{5,7},{7,5},{8,10},{10,8},{9,1... | collective-permute-start | bytes 5455880 | tf_op jit(solution)/shard_map/ppermute | solution.py:398
  10.0 7.8 %shard_map.121 = bf16[4,96,896]{2,1,0:T(8,128)(2,1)} custom-call(bf16[192,4736]{1,0:T(8,128)(2,1)} %convolution_convert_fusion.refs_0_, bf16[192,4736]{1,0:T(8,128)(2,1)} %copy-done.13, bf16[4736,896]{1,0:T(8,128)(2,1)} %refs_1_.3), custom_call_target="tpu_custom_call" | custom-call | flops 1 | bytes 1 | tf_op jit(solution)/shard_map/pallas_call | solution.py:55
  17.8 6.3 %all-to-all-start = ((bf16[4,96,896]{2,1,0:T(8,128)(2,1)}), bf16[4,96,896]{2,1,0:T(8,128)(2,1)S(1)}, u32[]{:S(2)}, u32[]{:S(2)}) async-start(bf16[4,96,896]{2,1,0:T(8,128)(2,1)} %shard_map.121), calls=%async_computation | async-start | bytes 1376256 | tf_op jit(solution)/shard_map/all_to_all | solution.py:451
  25.3 4.0 %collective-permute-start.2 = (bf16[448,896]{1,0:T(8,128)(2,1)S(1)}, bf16[448,896]{1,0:T(8,128)(2,1)S(1)}, u32[]{:S(2)}, u32[]{:S(2)}) collective-permute-start(bf16[448,896]{1,0:T(8,128)(2,1)S(1)} %constant_dynamic-slice_fusion), channel_id=1, source_target_pairs={{0,4},{5,1},{10,14},{15,11},{16,20},{21,17},{26,30},{31,27}} | collective-permute-start | bytes 2408456 | tf_op jit(solution)/shard_map/ppermute | solution.py:417
  29.2 2.5 %collective-permute-start.3 = (bf16[448,896]{1,0:T(8,128)(2,1)S(1)}, bf16[448,896]{1,0:T(8,128)(2,1)}, u32[]{:S(2)}, u32[]{:S(2)}) collective-permute-start(bf16[448,896]{1,0:T(8,128)(2,1)S(1)} %constant_dynamic-slice_fusion), channel_id=1, source_target_pairs={{0,8},{5,13},{10,2},{15,7},{16,24},{21,29},{26,18},{31,23}} | collective-permute-start | bytes 2408456 | tf_op jit(solution)/shard_map/ppermute | solution.py:416
  31.7 2.4 %pad_maximum_fusion.refs_0_ = bf16[896,640]{1,0:T(8,128)(2,1)} fusion(bf16[896,128]{1,0:T(8,128)(2,1)} %param.16, bf16[896,128]{1,0:T(8,128)(2,1)} %param.15, bf16[896,384]{1,0:T(8,128)(2,1)} %param.14), kind=kLoop, calls=%fused_computation.2 | loop fusion | flops 3440640 | bytes 2293760 | tf_op jit(solution)/shard_map/concatenate | solution.py:453
  34.2 14.1 %collective-permute-done.refs_0_ = bf16[192,4736]{1,0:T(8,128)(2,1)} collective-permute-done((bf16[192,4736]{1,0:T(8,128)(2,1)}, bf16[192,4736]{1,0:T(8,128)(2,1)}, u32[]{:S(2)}, u32[]{:S(2)}) %collective-permute-start) | collective-permute-done | bytes 1818656 | tf_op jit(solution)/shard_map/ppermute | solution.py:398
  49.2 3.7 %collective-permute-done.3 = bf16[448,896]{1,0:T(8,128)(2,1)} collective-permute-done((bf16[448,896]{1,0:T(8,128)(2,1)S(1)}, bf16[448,896]{1,0:T(8,128)(2,1)}, u32[]{:S(2)}, u32[]{:S(2)}) %collective-permute-start.3) | collective-permute-done | bytes 802848 | tf_op jit(solution)/shard_map/ppermute | solution.py:416
  52.9 1.6 %collective-permute-start.5 = (bf16[448,896]{1,0:T(8,128)(2,1)}, bf16[448,896]{1,0:T(8,128)(2,1)}, u32[]{:S(2)}, u32[]{:S(2)}) collective-permute-start(bf16[448,896]{1,0:T(8,128)(2,1)} %collective-permute-done.3), channel_id=1, source_target_pairs={{8,12},{13,9},{2,6},{7,3},{24,28},{29,25},{18,22},{23,19}} | collective-permute-start | bytes 2408456 | tf_op jit(solution)/shard_map/ppermute | solution.py:422
  54.5 8.9 %collective-permute-start.11 = (bf16[896,640]{1,0:T(8,128)(2,1)}, bf16[896,640]{1,0:T(8,128)(2,1)}, u32[]{:S(2)}, u32[]{:S(2)}) collective-permute-start(bf16[896,640]{1,0:T(8,128)(2,1)} %pad_maximum_fusion.refs_0_), channel_id=1, source_target_pairs={{0,2},{2,0},{1,3},{3,1},{4,6},{6,4},{5,7},{7,5},{8,10},{10,8},{9,1... | collective-permute-start | bytes 3440648 | tf_op jit(solution)/shard_map/ppermute | solution.py:398
  63.4 5.3 %shard_map.122 = bf16[4,48,896]{2,1,0:T(8,128)(2,1)} custom-call(bf16[192,4736]{1,0:T(8,128)(2,1)} %collective-permute-done.refs_0_, bf16[4736,896]{1,0:T(8,128)(2,1)} %refs_1_.3), custom_call_target="tpu_custom_call" | custom-call | flops 1 | bytes 1 | tf_op jit(solution)/shard_map/pallas_call | solution.py:55
  68.8 4.1 %all-to-all-start.1 = ((bf16[4,48,896]{2,1,0:T(8,128)(2,1)}), bf16[4,48,896]{2,1,0:T(8,128)(2,1)}, u32[]{:S(2)}, u32[]{:S(2)}) async-start(bf16[4,48,896]{2,1,0:T(8,128)(2,1)} %shard_map.122), calls=%async_computation.1 | async-start | bytes 688128 | tf_op jit(solution)/shard_map/all_to_all | solution.py:460
  72.9 5.4 %shard_map.123 = bf16[4,48,896]{2,1,0:T(8,128)(2,1)} custom-call(bf16[192,4736]{1,0:T(8,128)(2,1)} %collective-permute-done.4.refs_0_, bf16[4736,896]{1,0:T(8,128)(2,1)} %refs_1_.3), custom_call_target="tpu_custom_call" | custom-call | flops 1 | bytes 1 | tf_op jit(solution)/shard_map/pallas_call | solution.py:55
  79.7 1.6 %collective-permute-start.6 = (bf16[448,896]{1,0:T(8,128)(2,1)S(1)}, bf16[448,896]{1,0:T(8,128)(2,1)S(1)}, u32[]{:S(2)}, u32[]{:S(2)}) collective-permute-start(bf16[448,896]{1,0:T(8,128)(2,1)S(1)} %select_select_fusion.w_mine), channel_id=1, source_target_pairs={{0,16},{16,0},{1,17},{17,1},{2,18},{18,2},{3,19},{19,3},{4,20},{20... | collective-permute-start | bytes 2408456 | tf_op jit(solution)/shard_map/ppermute | solution.py:402
  81.2 2.3 %all-to-all-done.1.terms = bf16[4,48,896]{2,1,0:T(8,128)(2,1)} async-done(((bf16[4,48,896]{2,1,0:T(8,128)(2,1)}), bf16[4,48,896]{2,1,0:T(8,128)(2,1)}, u32[]{:S(2)}, u32[]{:S(2)}) %all-to-all-start.1) | async-done | bytes 344096 | tf_op jit(solution)/shard_map/all_to_all | solution.py:460
  83.5 4.3 %all-to-all-start.2 = ((bf16[4,48,896]{2,1,0:T(8,128)(2,1)}), bf16[4,48,896]{2,1,0:T(8,128)(2,1)}, u32[]{:S(2)}, u32[]{:S(2)}) async-start(bf16[4,48,896]{2,1,0:T(8,128)(2,1)} %shard_map.123), calls=%async_computation.2 | async-start | bytes 688128 | tf_op jit(solution)/shard_map/all_to_all | solution.py:460
  87.9 9.9 %collective-permute-done.6.w_other = bf16[448,896]{1,0:T(8,128)(2,1)S(1)} collective-permute-done((bf16[448,896]{1,0:T(8,128)(2,1)S(1)}, bf16[448,896]{1,0:T(8,128)(2,1)S(1)}, u32[]{:S(2)}, u32[]{:S(2)}) %collective-permute-start.6) | collective-permute-done | bytes 802848 | tf_op jit(solution)/shard_map/ppermute | solution.py:402
  102.9 1.5 %shard_map.126 = bf16[2,48,896]{2,1,0:T(8,128)(2,1)S(1)} custom-call(s32[1]{0:T(128)} %bitcast.2.turn_ref, bf16[4,48,896]{2,1,0:T(8,128)(2,1)} %all-to-all-done.2.terms, bf16[448,896]{1,0:T(8,128)(2,1)S(1)} %select_select_fusion.w_mine, bf16[448,896]{1,0:T(8,128)(2,1)S(1)} %collective-permute-done.6.w_other), custom_call_target="tpu_custom_call" | custom-call | flops 1 | bytes 1 | tf_op jit(solution)/shard_map/pallas_call | solution.py:95
  107.2 5.1 %collective-permute-done.8.refs_2_.refs_6_ = bf16[2,48,896]{2,1,0:T(8,128)(2,1)S(1)} collective-permute-done((bf16[2,48,896]{2,1,0:T(8,128)(2,1)S(1)}, bf16[2,48,896]{2,1,0:T(8,128)(2,1)S(1)}, u32[]{:S(2)}, u32[]{:S(2)}) %collective-permute-start.8) | collective-permute-done | bytes 172064 | tf_op jit(solution)/shard_map/ppermute | solution.py:406
  112.3 1.9 %collective-permute-done.9.refs_3_.refs_7_ = bf16[2,48,896]{2,1,0:T(8,128)(2,1)S(1)} collective-permute-done((bf16[2,48,896]{2,1,0:T(8,128)(2,1)S(1)}, bf16[2,48,896]{2,1,0:T(8,128)(2,1)S(1)}, u32[]{:S(2)}, u32[]{:S(2)}) %collective-permute-start.9) | collective-permute-done | bytes 172064 | tf_op jit(solution)/shard_map/ppermute | solution.py:406
  115.7 6.2 %all-to-all-start.3 = ((bf16[4,48,896]{2,1,0:T(8,128)(2,1)}), bf16[4,48,896]{2,1,0:T(8,128)(2,1)}, u32[]{:S(2)}, u32[]{:S(2)}) async-start(bf16[4,48,896]{2,1,0:T(8,128)(2,1)} %shard_map.127), calls=%async_computation.3 | async-start | bytes 688128 | tf_op jit(solution)/shard_map/all_to_all | solution.py:474
  122.8 12.0 %shard_map.128 = (bf16[48,1024]{1,0:T(8,128)(2,1)}, f32[48,1536]{1,0:T(8,128)}) custom-call(s32[1]{0:T(128)} %bitcast.1.block_ref, s32[48]{0:T(128)S(1)} %copy-done.10, f32[1,896]{1,0:T(1,128)S(1)} %reshape.22.gain, bf16[896,640]{1,0:T(8,128)(2,1)} %pad_maximum_fusion.refs_0_, bf16[896,640]{1,0:T(8,128)(2,1)} %collective-permute-done.10.refs_1_, ...), custom_call_target="tpu_custom_call" | custom-call | flops 1 | bytes 1 | tf_op jit(solution)/shard_map/pallas_call | solution.py:288
  134.8 2.0 %convolution_convert_fusion.1 = bf16[192,896]{1,0:T(8,128)(2,1)} fusion(bf16[192,896]{1,0:T(8,128)(2,1)} %bitcast.3, s32[192]{0:T(256)S(1)} %bitcast.7), kind=kOutput, calls=%fused_computation.1 | convolution fusion | flops 66269184 | bytes 688896 | tf_op jit(solution)/shard_map/dot_general | solution.py:478
  (60 shorter events, 18.0 us)
Async XLA Ops:
  4.7 4.1 %collective-permute-start.1 = (bf16[192,4736]{1,0:T(8,128)(2,1)}, bf16[192,4736]{1,0:T(8,128)(2,1)S(1)}, u32[]{:S(2)}, u32[]{:S(2)}) collective-permute-start(bf16[192,4736]{1,0:T(8,128)(2,1)} %convolution_convert_fusion.refs_0_), channel_id=1, source_target_pairs={{0,1},{1,0},{2,3},{3,2},{4,5},{5,4},{6,7},{7,6},{8,9},{9,8},{10,11... | collective-permute-start | bytes 5455880 | tf_op jit(solution)/shard_map/ppermute | solution.py:394
  5.1 43.1 %collective-permute-start = (bf16[192,4736]{1,0:T(8,128)(2,1)}, bf16[192,4736]{1,0:T(8,128)(2,1)}, u32[]{:S(2)}, u32[]{:S(2)}) collective-permute-start(bf16[192,4736]{1,0:T(8,128)(2,1)} %convolution_convert_fusion.refs_0_), channel_id=1, source_target_pairs={{0,2},{2,0},{1,3},{3,1},{4,6},{6,4},{5,7},{7,5},{8,10},{10,8},{9,1... | collective-permute-start | bytes 5455880 | tf_op jit(solution)/shard_map/ppermute | solution.py:398
  17.8 35.1 %all-to-all-start = ((bf16[4,96,896]{2,1,0:T(8,128)(2,1)}), bf16[4,96,896]{2,1,0:T(8,128)(2,1)S(1)}, u32[]{:S(2)}, u32[]{:S(2)}) async-start(bf16[4,96,896]{2,1,0:T(8,128)(2,1)} %shard_map.121), calls=%async_computation | async-start | bytes 1376256 | tf_op jit(solution)/shard_map/all_to_all | solution.py:451
  25.3 23.0 %collective-permute-start.2 = (bf16[448,896]{1,0:T(8,128)(2,1)S(1)}, bf16[448,896]{1,0:T(8,128)(2,1)S(1)}, u32[]{:S(2)}, u32[]{:S(2)}) collective-permute-start(bf16[448,896]{1,0:T(8,128)(2,1)S(1)} %constant_dynamic-slice_fusion), channel_id=1, source_target_pairs={{0,4},{5,1},{10,14},{15,11},{16,20},{21,17},{26,30},{31,27}} | collective-permute-start | bytes 2408456 | tf_op jit(solution)/shard_map/ppermute | solution.py:417
  29.2 23.6 %collective-permute-start.3 = (bf16[448,896]{1,0:T(8,128)(2,1)S(1)}, bf16[448,896]{1,0:T(8,128)(2,1)}, u32[]{:S(2)}, u32[]{:S(2)}) collective-permute-start(bf16[448,896]{1,0:T(8,128)(2,1)S(1)} %constant_dynamic-slice_fusion), channel_id=1, source_target_pairs={{0,8},{5,13},{10,2},{15,7},{16,24},{21,29},{26,18},{31,23}} | collective-permute-start | bytes 2408456 | tf_op jit(solution)/shard_map/ppermute | solution.py:416
  52.9 15.9 %copy-start.1 = (bf16[4,96,896]{2,1,0:T(8,128)(2,1)}, bf16[4,96,896]{2,1,0:T(8,128)(2,1)S(1)}, u32[]{:S(2)}) copy-start(bf16[4,96,896]{2,1,0:T(8,128)(2,1)S(1)} %all-to-all-done.terms) | copy-start | bytes 2064388
  52.9 20.1 %collective-permute-start.4 = (bf16[192,4736]{1,0:T(8,128)(2,1)}, bf16[192,4736]{1,0:T(8,128)(2,1)}, u32[]{:S(2)}, u32[]{:S(2)}) collective-permute-start(bf16[192,4736]{1,0:T(8,128)(2,1)} %collective-permute-done.refs_0_), channel_id=1, source_target_pairs={{0,1},{1,0},{2,3},{3,2},{4,5},{5,4},{6,7},{7,6},{8,9},{9,8},{10,11... | collective-permute-start | bytes 5455880 | tf_op jit(solution)/shard_map/ppermute | solution.py:394
  52.9 25.5 %collective-permute-start.5 = (bf16[448,896]{1,0:T(8,128)(2,1)}, bf16[448,896]{1,0:T(8,128)(2,1)}, u32[]{:S(2)}, u32[]{:S(2)}) collective-permute-start(bf16[448,896]{1,0:T(8,128)(2,1)} %collective-permute-done.3), channel_id=1, source_target_pairs={{8,12},{13,9},{2,6},{7,3},{24,28},{29,25},{18,22},{23,19}} | collective-permute-start | bytes 2408456 | tf_op jit(solution)/shard_map/ppermute | solution.py:422
  54.5 50.0 %collective-permute-start.11 = (bf16[896,640]{1,0:T(8,128)(2,1)}, bf16[896,640]{1,0:T(8,128)(2,1)}, u32[]{:S(2)}, u32[]{:S(2)}) collective-permute-start(bf16[896,640]{1,0:T(8,128)(2,1)} %pad_maximum_fusion.refs_0_), channel_id=1, source_target_pairs={{0,2},{2,0},{1,3},{3,1},{4,6},{6,4},{5,7},{7,5},{8,10},{10,8},{9,1... | collective-permute-start | bytes 3440648 | tf_op jit(solution)/shard_map/ppermute | solution.py:398
  68.8 14.8 %all-to-all-start.1 = ((bf16[4,48,896]{2,1,0:T(8,128)(2,1)}), bf16[4,48,896]{2,1,0:T(8,128)(2,1)}, u32[]{:S(2)}, u32[]{:S(2)}) async-start(bf16[4,48,896]{2,1,0:T(8,128)(2,1)} %shard_map.122), calls=%async_computation.1 | async-start | bytes 688128 | tf_op jit(solution)/shard_map/all_to_all | solution.py:460
  72.9 5.4 %copy-start.15 = (bf16[448,896]{1,0:T(8,128)(2,1)S(1)}, bf16[448,896]{1,0:T(8,128)(2,1)}, u32[]{:S(2)}) copy-start(bf16[448,896]{1,0:T(8,128)(2,1)} %copy-done.14) | copy-start | bytes 2408452
  79.7 18.2 %collective-permute-start.6 = (bf16[448,896]{1,0:T(8,128)(2,1)S(1)}, bf16[448,896]{1,0:T(8,128)(2,1)S(1)}, u32[]{:S(2)}, u32[]{:S(2)}) collective-permute-start(bf16[448,896]{1,0:T(8,128)(2,1)S(1)} %select_select_fusion.w_mine), channel_id=1, source_target_pairs={{0,16},{16,0},{1,17},{17,1},{2,18},{18,2},{3,19},{19,3},{4,20},{20... | collective-permute-start | bytes 2408456 | tf_op jit(solution)/shard_map/ppermute | solution.py:402
  83.5 19.4 %all-to-all-start.2 = ((bf16[4,48,896]{2,1,0:T(8,128)(2,1)}), bf16[4,48,896]{2,1,0:T(8,128)(2,1)}, u32[]{:S(2)}, u32[]{:S(2)}) async-start(bf16[4,48,896]{2,1,0:T(8,128)(2,1)} %shard_map.123), calls=%async_computation.2 | async-start | bytes 688128 | tf_op jit(solution)/shard_map/all_to_all | solution.py:460
  87.8 34.0 %collective-permute-start.10 = (bf16[896,640]{1,0:T(8,128)(2,1)}, bf16[896,640]{1,0:T(8,128)(2,1)}, u32[]{:S(2)}, u32[]{:S(2)}) collective-permute-start(bf16[896,640]{1,0:T(8,128)(2,1)} %pad_maximum_fusion.refs_0_), channel_id=1, source_target_pairs={{0,1},{1,0},{2,3},{3,2},{4,5},{5,4},{6,7},{7,6},{8,9},{9,8},{10,11... | collective-permute-start | bytes 3440648 | tf_op jit(solution)/shard_map/ppermute | solution.py:394
  102.9 19.0 %copy-start.16 = (f32[896]{0:T(1024)S(1)}, f32[896]{0:T(1024)}, u32[]{:S(2)}) copy-start(f32[896]{0:T(1024)} %param.13) | copy-start | bytes 10756
  102.9 19.0 %copy-start.10 = (s32[48]{0:T(128)S(1)}, s32[48]{0:T(128)}, u32[]{:S(2)}) copy-start(s32[48]{0:T(128)} %len_ref.1) | copy-start | bytes 580
  102.9 11.3 %copy-start.4 = (bf16[2,48,896]{2,1,0:T(8,128)(2,1)S(1)}, bf16[2,48,896]{2,1,0:T(8,128)(2,1)}, u32[]{:S(2)}) copy-start(bf16[2,48,896]{2,1,0:T(8,128)(2,1)} %copy-done.3) | copy-start | bytes 516100
  104.5 17.4 %copy-start.5 = (bf16[2,48,896]{2,1,0:T(8,128)(2,1)S(1)}, bf16[2,48,896]{2,1,0:T(8,128)(2,1)}, u32[]{:S(2)}) copy-start(bf16[2,48,896]{2,1,0:T(8,128)(2,1)} %copy-done.3) | copy-start | bytes 516100
  104.5 17.4 %collective-permute-start.12 = (bf16[896,640]{1,0:T(8,128)(2,1)}, bf16[896,640]{1,0:T(8,128)(2,1)S(1)}, u32[]{:S(2)}, u32[]{:S(2)}) collective-permute-start(bf16[896,640]{1,0:T(8,128)(2,1)} %collective-permute-done.11.refs_2_), channel_id=1, source_target_pairs={{0,1},{1,0},{2,3},{3,2},{4,5},{5,4},{6,7},{7,6},{8,9},{9,8},{10,11... | collective-permute-start | bytes 3440648 | tf_op jit(solution)/shard_map/ppermute | solution.py:394
  104.6 2.7 %collective-permute-start.7 = (bf16[2,48,896]{2,1,0:T(8,128)(2,1)S(1)}, bf16[2,48,896]{2,1,0:T(8,128)(2,1)S(1)}, u32[]{:S(2)}, u32[]{:S(2)}) collective-permute-start(bf16[2,48,896]{2,1,0:T(8,128)(2,1)S(1)} %copy-done.12), channel_id=1, source_target_pairs={{0,1},{1,0},{2,3},{3,2},{4,5},{5,4},{6,7},{7,6},{8,9},{9,8},{10,11... | collective-permute-start | bytes 516104 | tf_op jit(solution)/shard_map/ppermute | solution.py:394
  105.1 7.2 %collective-permute-start.8 = (bf16[2,48,896]{2,1,0:T(8,128)(2,1)S(1)}, bf16[2,48,896]{2,1,0:T(8,128)(2,1)S(1)}, u32[]{:S(2)}, u32[]{:S(2)}) collective-permute-start(bf16[2,48,896]{2,1,0:T(8,128)(2,1)S(1)} %copy-done.9), channel_id=1, source_target_pairs={{0,2},{1,3},{2,0},{3,1},{4,6},{5,7},{6,4},{7,5},{8,10},{9,11},{10,... | collective-permute-start | bytes 516104 | tf_op jit(solution)/shard_map/ppermute | solution.py:406
  106.5 7.8 %collective-permute-start.9 = (bf16[2,48,896]{2,1,0:T(8,128)(2,1)S(1)}, bf16[2,48,896]{2,1,0:T(8,128)(2,1)S(1)}, u32[]{:S(2)}, u32[]{:S(2)}) collective-permute-start(bf16[2,48,896]{2,1,0:T(8,128)(2,1)S(1)} %shard_map.126), channel_id=1, source_target_pairs={{0,3},{1,2},{2,1},{3,0},{4,7},{5,6},{6,5},{7,4},{8,11},{9,10},{10,... | collective-permute-start | bytes 516104 | tf_op jit(solution)/shard_map/ppermute | solution.py:406
  115.7 19.1 %all-to-all-start.3 = ((bf16[4,48,896]{2,1,0:T(8,128)(2,1)}), bf16[4,48,896]{2,1,0:T(8,128)(2,1)}, u32[]{:S(2)}, u32[]{:S(2)}) async-start(bf16[4,48,896]{2,1,0:T(8,128)(2,1)} %shard_map.127), calls=%async_computation.3 | async-start | bytes 688128 | tf_op jit(solution)/shard_map/all_to_all | solution.py:474
  121.9 13.0 %copy-start.17 = (s32[1,192]{1,0:T(1,128)S(1)}, s32[1,192]{1,0:T(1,128)}, u32[]{:S(2)}) copy-start(s32[1,192]{1,0:T(1,128)} %param.17) | copy-start | bytes 2308
  (11 other events, 12.2 us)

commit v9 on v8

--- a/solution.py
+++ b/solution.py
@@ -69,61 +69,44 @@
     )(*xs, w)
 
 
-def finish_kernel(turn_ref, terms, w_mine, w_other, *refs):
-    outs, w = refs[:-1], refs[-1]
-    half = w_mine.shape[0]
-    g = turn_ref[0]
-    w[pl.ds(pl.multiple_of(g * half, half), half), :] = w_mine[...]
-    w[pl.ds(pl.multiple_of((1 - g) * half, half), half), :] = w_other[...]
+def add_kernel(terms, *outs):
     total = terms[0].astype(jnp.float32)
     for k in range(1, terms.shape[0]):
         total = total + terms[k].astype(jnp.float32)
-    features = total.astype(jnp.bfloat16)
-    projected = jnp.dot(features, w[...], preferred_element_type=jnp.float32)
-    projected = projected.astype(jnp.bfloat16)
-    n = features.shape[0] // len(outs)
+    n = outs[0].shape[0]
     for i, out in enumerate(outs):
-        out[0] = features[i * n : (i + 1) * n]
-        out[1] = projected[i * n : (i + 1) * n]
-
-
-def finish(turn, terms, w_halves, parts):
+        out[...] = total[i * n : (i + 1) * n].astype(out.dtype)
+
+
+def add(terms, parts):
     _, rows, columns = terms.shape
-    wide = w_halves[0].shape[1]
-    part = jax.ShapeDtypeStruct((2, rows // parts, columns), jnp.bfloat16)
+    part = jax.ShapeDtypeStruct((rows // parts, columns), jnp.bfloat16)
     vmem = pl.BlockSpec(memory_space=pltpu.VMEM)
     return pl.pallas_call(
-        finish_kernel,
+        add_kernel,
         out_shape=(part,) * parts,
-        in_specs=[pl.BlockSpec(memory_space=pltpu.SMEM), vmem, vmem, vmem],
+        in_specs=[vmem],
         out_specs=(vmem,) * parts,
-        scratch_shapes=[pltpu.VMEM((columns, wide), jnp.bfloat16)],
         cost_estimate=SHORT,
         compiler_params=pltpu.CompilerParams(vmem_limit_bytes=16 * 1024 * 1024),
-    )(turn, terms, *w_halves)
-
-
-def collect_kernel(spans, block_ref, *refs):
-    pieces, home = refs[:-1], refs[-1]
-    at = 0
-    for e, span in enumerate(spans):
-        for first, n in span:
-            home[e ^ block_ref[0], first : first + n, :] = pieces[at][0]
-            at += 1
-
-
-def collect(block, pieces, spans):
-    flat = [p for piece in pieces for p in piece]
-    rows = sum(n for _, n in spans[0])
+    )(terms)
+
+
+def collect_kernel(block_ref, *refs):
+    for e, piece in enumerate(refs[:-1]):
+        refs[-1][e ^ block_ref[0]] = piece[...]
+
+
+def collect(block, pieces):
     vmem = pl.BlockSpec(memory_space=pltpu.VMEM)
     return pl.pallas_call(
-        functools.partial(collect_kernel, spans),
-        out_shape=jax.ShapeDtypeStruct((len(spans), rows, flat[0].shape[2]), jnp.bfloat16),
-        in_specs=[pl.BlockSpec(memory_space=pltpu.SMEM)] + [vmem] * len(flat),
+        collect_kernel,
+        out_shape=jax.ShapeDtypeStruct((len(pieces), *pieces[0].shape), jnp.bfloat16),
+        in_specs=[pl.BlockSpec(memory_space=pltpu.SMEM)] + [vmem] * len(pieces),
         out_specs=vmem,
         cost_estimate=SHORT,
         compiler_params=pltpu.CompilerParams(vmem_limit_bytes=16 * 1024 * 1024),
-    )(block, *flat)
+    )(block, *pieces)
 
 
 def page_copies(len_ref, kv_hbm, kv_ref, sem, r):
@@ -136,12 +119,9 @@
     return out
 
 
-def talker_kernel(spans, blocks, block_ref, len_ref, gain, *refs):
-    count = sum(map(len, spans))
-    w_hbm, pieces = refs[:blocks], refs[blocks : blocks + count]
-    kv_hbm, new_kv, out_ref, kv_ref, sem, w_ref, w_sem, qkv, spreads, gathereds = refs[
-        blocks + count :
-    ]
+def talker_kernel(blocks, block_ref, len_ref, gain, *refs):
+    w_hbm, refs = refs[:blocks], refs[blocks:]
+    terms, kv_hbm, new_kv, out_ref, kv_ref, sem, w_ref, w_sem, qkv, spreads, gathereds = refs
     rows, cached, kv_width = kv_ref.shape
     width = kv_width // 2
     page = cached // PAGES
@@ -166,13 +146,9 @@
             else:
                 pl.when(needed)(copy.start)
 
-    at = 0
-    total = None
-    for span in spans:
-        terms = [pieces[at + i][1].astype(jnp.float32) for i in range(len(span))]
-        at += len(span)
-        term = jnp.concatenate(terms, axis=0) if len(terms) > 1 else terms[0]
-        total = term if total is None else total + term
+    total = terms[0].astype(jnp.float32)
+    for k in range(1, terms.shape[0]):
+        total = total + terms[k].astype(jnp.float32)
     scale = lax.rsqrt(jnp.mean(total * total, axis=1, keepdims=True) + 1e-06)
     normed = (total * scale * gain[...]).astype(jnp.bfloat16)
     for e in range(blocks):
@@ -276,8 +252,7 @@
             context(at, *weighed[k], gathereds.at[k])
 
 
-def talker(block, pieces, spans, talker_gain, weights, kv_len, kv_cache):
-    flat = [p for piece in pieces for p in piece]
+def talker(block, terms, talker_gain, weights, kv_len, kv_cache):
     rows, cached, kv_width = kv_cache.shape
     wide, columns = weights[0].shape
     blocks = len(weights)
@@ -286,15 +261,14 @@
     vmem = pl.BlockSpec(memory_space=pltpu.VMEM)
     smem = pl.BlockSpec(memory_space=pltpu.SMEM)
     return pl.pallas_call(
-        functools.partial(talker_kernel, spans, blocks),
+        functools.partial(talker_kernel, blocks),
         out_shape=(
             jax.ShapeDtypeStruct((rows, kv_width), jnp.bfloat16),
             jax.ShapeDtypeStruct((rows, q_width), jnp.float32),
         ),
         in_specs=[smem, smem, vmem]
         + [pl.BlockSpec(memory_space=pl.ANY)] * blocks
-        + [vmem] * len(flat)
-        + [pl.BlockSpec(memory_space=pl.ANY)],
+        + [vmem, pl.BlockSpec(memory_space=pl.ANY)],
         out_specs=(vmem, vmem),
         scratch_shapes=[
             pltpu.VMEM((rows, cached, kv_width), jnp.bfloat16),
@@ -307,7 +281,7 @@
         ],
         cost_estimate=SHORT,
         compiler_params=pltpu.CompilerParams(vmem_limit_bytes=48 * 1024 * 1024),
-    )(block, kv_len, talker_gain.reshape(1, wide), *weights, *flat, kv_cache)
+    )(block, kv_len, talker_gain.reshape(1, wide), *weights, terms, kv_cache)
 
 
 def rms_norm(talker_in, talker_gain):
@@ -398,31 +372,12 @@
     return lax.ppermute(x, "section", [(0, 1), (1, 0)])
 
 
-def over_groups(x):
-    return lax.ppermute(x, "groups", [(0, 1), (1, 0)])
-
-
 def over_plane(x, e):
     return lax.ppermute(x, PLANE, [(b, b ^ e) for b in range(4)])
 
 
 def after(x, *others):
     return lax.optimization_barrier((x, *others))[0]
-
-
-def feature_block_first(w_proj, g):
-    half = w_proj.shape[0] // 2
-    piece = lax.dynamic_slice_in_dim(w_proj, g * half, half, axis=0)
-    two = lax.ppermute(piece, GROUP, [(b * 4 + b, (b ^ 2) * 4 + b) for b in range(4)])
-    one = lax.ppermute(piece, GROUP, [(b * 4 + b, (b ^ 1) * 4 + b) for b in range(4)])
-    return piece, one, two
-
-
-def feature_block(piece, one, two, m, c, later):
-    three = lax.ppermute(two, GROUP, [((b ^ 2) * 4 + b, (b ^ 3) * 4 + b) for b in range(4)])
-    three = after(three, later)
-    piece = jnp.where(m == c, piece, jnp.where(m == c ^ 2, two, jnp.where(m == c ^ 1, one, three)))
-    return piece, over_groups(piece)
 
 
 def four_planes(
@@ -439,7 +394,7 @@
 ):
     planes = 4
     owned = kv_cache.shape[0]
-    g, m, c = lax.axis_index("groups"), lax.axis_index("mp"), lax.axis_index(PLANE)
+    block = lax.axis_index(PLANE).reshape(1)
     slots = talker_slot[0]
 
     pick = (jnp.arange(planes * owned)[:, None] == slots[None, :]).astype(jnp.bfloat16)
@@ -449,31 +404,29 @@
     peer = over_core(rows)
     near = down([rows, peer], w_think, planes)
     near_terms = lax.all_to_all(near, "mp", 0, 0)
-    early_w = feature_block_first(after(w_proj, peer), g)
     mine = jnp.concatenate([w_query, w_key, w_value], axis=1)
 
-    across, near_terms, mine, *early_w = lax.optimization_barrier(
-        (across, near_terms, mine, *early_w)
-    )
+    own, next_core = add(near_terms, 2)
+    across, own, next_core, mine = lax.optimization_barrier((across, own, next_core, mine))
     far = [down([across], w_think, planes)]
     far.append(down([after(over_core(across), far[0])], w_think, planes))
-    far_terms = [lax.all_to_all(x, "mp", 0, 0) for x in far]
-    other = over_section(after(mine, across))
-    block_w = feature_block(*early_w, m, c, far[1])
-
-    turn = g.reshape(1)
-    own, next_core = finish(turn, after(near_terms, far[1]), block_w, 2)
-    pieces = [[own], [over_core(next_core)], [], []]
+    pieces = [own, over_core(next_core)]
     made = own
-    for e, terms in zip((2, 3), far_terms):
-        (made,) = finish(turn, after(terms, made), block_w, 1)
-        pieces[e].append(over_plane(made, e))
+    for e, x in zip((2, 3), far):
+        (made,) = add(after(lax.all_to_all(x, "mp", 0, 0), made, far[1]), 1)
+        pieces.append(over_plane(made, e))
+    other = over_section(after(mine, far[0]))
+
+    home = lax.all_to_all(collect(block, pieces), "mp", 0, 0)
+    projected = jnp.dot(
+        home.reshape(planes * owned, -1), w_proj, preferred_element_type=jnp.float32
+    )
+    projected = projected.astype(jnp.bfloat16).reshape(planes, owned, -1)
+    terms = lax.all_to_all(projected, "mp", 0, 0)
     other = after(other, made)
     weights = [mine, over_core(mine), other, over_core(other)]
-    spans = [[(0, owned)]] * 4
-    home = lax.all_to_all(collect(c.reshape(1), pieces, spans), "mp", 0, 0)
-    new_kv, ctx = talker(c.reshape(1), pieces, spans, talker_gain, weights, kv_len, kv_cache)
-    home = after(home, ctx)
+    new_kv, ctx = talker(block, terms, talker_gain, weights, kv_len, kv_cache)
+    home = after(home, projected)
     pick = (slots[:, None] == jnp.arange(planes * owned)[None, :]).astype(jnp.bfloat16)
     thinker_out = jnp.dot(
         pick, home.reshape(planes * owned, -1), preferred_element_type=jnp.float32

time: 138 us -> 136 us (0.986)
  waiting for transfers between devices: 38.8 us -> 58.6 us
  starting transfers between devices: 44.5 us -> 29.4 us
  local copies, waits for them, and re-layouts: 9.57 us -> 3.4 us
  matrix products: 4.56 us -> 7.41 us
  other arithmetic: 3.76 us -> 1.22 us
    all_to_all x3 -> x4, waiting for transfers between devices: 2.3 us -> 31.5 us  [the longest x2 12.8 us: four_planes(): made, = add(after(lax.all_to_all(x, 'mp', 0, 0), made, far[1]), 1)]
    all_to_all x1, waiting for transfers between devices: 0.01 us -> 17.2 us  [four_planes(): near_terms = lax.all_to_all(near, 'mp', 0, 0)]
    ppermute x4 -> x0, waiting for transfers between devices: 13.6 us -> none  [the longest x1 9.91 us: over_groups(): return lax.ppermute(x, 'groups', [(0, 1), (1, 0)])]
    ppermute x2, waiting for transfers between devices: 14.1 us -> 4.06 us  [over_section(): return lax.ppermute(x, 'section', [(0, 1), (1, 0)])]
    ppermute x4 -> x0, starting transfers between devices: 9.67 us -> none  [the longest x1 3.98 us: feature_block_first(): lax.ppermute(piece, GROUP, [(b * 4 + b, (b ^ 1) * 4 + b) for b in range(4)])]
    ppermute x2, starting transfers between devices: 11.4 us -> 4.04 us  [over_section(): return lax.ppermute(x, 'section', [(0, 1), (1, 0)])]
    unnamed x36 -> x18, local copies, waits for them, and re-layouts: 8.37 us -> 3.39 us
    dot_general x0 -> x1, matrix products: none -> 2.86 us  [four_planes(): jnp.dot(home.reshape(planes * owned, -1), w_proj, preferred_element_type=...]
  transfers between devices with their start and end apart: 17 -> 14, of which waited for: 8 -> 9; matrix products, arithmetic and copies ran while one was open for 4% -> 5% of each run, Pallas kernels for 25% -> 16%
where the time goes in v9:
time: 136 us; the launch traced here: 135 us
  waiting for transfers between devices  58.6 us (43%)
  Pallas kernels  34.3 us (25%)
  starting transfers between devices  29.4 us (22%)
  matrix products  7.41 us (5%)
  local copies, waits for them, and re-layouts  3.4 us (2%)
    pallas_call x3, Pallas kernels, down(): pl.pallas_call(functools.partial(down_kernel, counts, planes, list(zip(en...  18.4 us
    all_to_all x1, waiting for transfers between devices, four_planes(): near_terms = lax.all_to_all(near, 'mp', 0, 0)  17.2 us
    all_to_all x2, waiting for transfers between devices, four_planes(): made, = add(after(lax.all_to_all(x, 'mp', 0, 0), made, far[1]), 1)  12.8 us
    pallas_call x1, Pallas kernels, talker(): pl.pallas_call(functools.partial(talker_kernel, blocks), out_shape=(jax.S...  12.3 us
    all_to_all x1, waiting for transfers between devices, four_planes(): home = lax.all_to_all(collect(block, pieces), 'mp', 0, 0)  10.6 us
    all_to_all x2, starting transfers between devices, four_planes(): made, = add(after(lax.all_to_all(x, 'mp', 0, 0), made, far[1]), 1)  9.25 us
    all_to_all x1, waiting for transfers between devices, four_planes(): terms = lax.all_to_all(projected, 'mp', 0, 0)  8.14 us
    all_to_all x1, starting transfers between devices, four_planes(): near_terms = lax.all_to_all(near, 'mp', 0, 0)  6.25 us
  transfers between devices with their start and end apart: 14, of which 9 were waited for; matrix products, arithmetic and copies ran while one was open for 5% of the time, Pallas kernels for 16%

profile of v9, /device:TPU:0, one launch (start us, length us, event | category | flops | bytes accessed | tf_op | source)
XLA Modules:
  0.0 135.3 jit_solution(13574750532341651430)
XLA Ops:
  0.6 1.5 %copy-done = bf16[192,4736]{1,0:T(8,128)(2,1)S(1)} copy-done((bf16[192,4736]{1,0:T(8,128)(2,1)S(1)}, bf16[192,4736]{1,0:T(8,128)(2,1)}, u32[]{:S(2)}) %copy-start) | copy-done | bytes 1818648
  2.1 2.5 %convolution_convert_fusion.refs_0_ = bf16[192,4736]{1,0:T(8,128)(2,1)} fusion(bf16[192,4736]{1,0:T(8,128)(2,1)S(1)} %copy-done, s32[192]{0:T(256)} %bitcast.12), kind=kOutput, calls=%fused_computation | convolution fusion | flops 350121984 | bytes 3638016 | tf_op jit(solution)/shard_map/dot_general | solution.py:401
  5.1 2.5 %collective-permute-start = (bf16[192,4736]{1,0:T(8,128)(2,1)}, bf16[192,4736]{1,0:T(8,128)(2,1)}, u32[]{:S(2)}, u32[]{:S(2)}) collective-permute-start(bf16[192,4736]{1,0:T(8,128)(2,1)} %convolution_convert_fusion.refs_0_), channel_id=1, source_target_pairs={{0,2},{2,0},{1,3},{3,1},{4,6},{6,4},{5,7},{7,5},{8,10},{10,8},{9,1... | collective-permute-start | bytes 5455880 | tf_op jit(solution)/shard_map/ppermute | solution.py:372
  10.0 7.7 %shard_map.121 = bf16[4,96,896]{2,1,0:T(8,128)(2,1)} custom-call(bf16[192,4736]{1,0:T(8,128)(2,1)} %convolution_convert_fusion.refs_0_, bf16[192,4736]{1,0:T(8,128)(2,1)} %copy-done.4, bf16[4736,896]{1,0:T(8,128)(2,1)} %refs_1_.3), custom_call_target="tpu_custom_call" | custom-call | flops 1 | bytes 1 | tf_op jit(solution)/shard_map/pallas_call | solution.py:55
  17.7 6.2 %all-to-all-start = ((bf16[4,96,896]{2,1,0:T(8,128)(2,1)}), bf16[4,96,896]{2,1,0:T(8,128)(2,1)}, u32[]{:S(2)}, u32[]{:S(2)}) async-start(bf16[4,96,896]{2,1,0:T(8,128)(2,1)} %shard_map.121), calls=%async_computation | async-start | bytes 1376256 | tf_op jit(solution)/shard_map/all_to_all | solution.py:406
  25.2 17.2 %all-to-all-done.terms = bf16[4,96,896]{2,1,0:T(8,128)(2,1)} async-done(((bf16[4,96,896]{2,1,0:T(8,128)(2,1)}), bf16[4,96,896]{2,1,0:T(8,128)(2,1)}, u32[]{:S(2)}, u32[]{:S(2)}) %all-to-all-start) | async-done | bytes 688160 | tf_op jit(solution)/shard_map/all_to_all | solution.py:406
  44.2 4.1 %collective-permute-done.refs_0_ = bf16[192,4736]{1,0:T(8,128)(2,1)} collective-permute-done((bf16[192,4736]{1,0:T(8,128)(2,1)}, bf16[192,4736]{1,0:T(8,128)(2,1)}, u32[]{:S(2)}, u32[]{:S(2)}) %collective-permute-start) | collective-permute-done | bytes 1818656 | tf_op jit(solution)/shard_map/ppermute | solution.py:372
  48.3 5.3 %shard_map.123 = bf16[4,48,896]{2,1,0:T(8,128)(2,1)} custom-call(bf16[192,4736]{1,0:T(8,128)(2,1)} %collective-permute-done.refs_0_, bf16[4736,896]{1,0:T(8,128)(2,1)} %refs_1_.3), custom_call_target="tpu_custom_call" | custom-call | flops 1 | bytes 1 | tf_op jit(solution)/shard_map/pallas_call | solution.py:55
  53.6 5.1 %all-to-all-start.1 = ((bf16[4,48,896]{2,1,0:T(8,128)(2,1)}), bf16[4,48,896]{2,1,0:T(8,128)(2,1)S(1)}, u32[]{:S(2)}, u32[]{:S(2)}) async-start(bf16[4,48,896]{2,1,0:T(8,128)(2,1)} %shard_map.123), calls=%async_computation.1 | async-start | bytes 688128 | tf_op jit(solution)/shard_map/all_to_all | solution.py:416
  58.7 1.5 %collective-permute-start.7 = (bf16[896,640]{1,0:T(8,128)(2,1)S(1)}, bf16[896,640]{1,0:T(8,128)(2,1)}, u32[]{:S(2)}, u32[]{:S(2)}) collective-permute-start(bf16[896,640]{1,0:T(8,128)(2,1)S(1)} %pad_maximum_fusion.refs_0_), channel_id=1, source_target_pairs={{0,2},{2,0},{1,3},{3,1},{4,6},{6,4},{5,7},{7,5},{8,10},{10,8},{9,1... | collective-permute-start | bytes 3440648 | tf_op jit(solution)/shard_map/ppermute | solution.py:372
  60.2 5.3 %shard_map.124 = bf16[4,48,896]{2,1,0:T(8,128)(2,1)} custom-call(bf16[192,4736]{1,0:T(8,128)(2,1)} %collective-permute-done.3.refs_0_, bf16[4736,896]{1,0:T(8,128)(2,1)} %refs_1_.3), custom_call_target="tpu_custom_call" | custom-call | flops 1 | bytes 1 | tf_op jit(solution)/shard_map/pallas_call | solution.py:55
  65.6 4.5 %all-to-all-done.1.terms = bf16[4,48,896]{2,1,0:T(8,128)(2,1)S(1)} async-done(((bf16[4,48,896]{2,1,0:T(8,128)(2,1)}), bf16[4,48,896]{2,1,0:T(8,128)(2,1)S(1)}, u32[]{:S(2)}, u32[]{:S(2)}) %all-to-all-start.1) | async-done | bytes 344096 | tf_op jit(solution)/shard_map/all_to_all | solution.py:416
  70.0 4.1 %all-to-all-start.2 = ((bf16[4,48,896]{2,1,0:T(8,128)(2,1)}), bf16[4,48,896]{2,1,0:T(8,128)(2,1)}, u32[]{:S(2)}, u32[]{:S(2)}) async-start(bf16[4,48,896]{2,1,0:T(8,128)(2,1)} %shard_map.124), calls=%async_computation.2 | async-start | bytes 688128 | tf_op jit(solution)/shard_map/all_to_all | solution.py:416
  74.9 1.5 %collective-permute-start.4 = (bf16[48,896]{1,0:T(8,128)(2,1)}, bf16[48,896]{1,0:T(8,128)(2,1)S(1)}, u32[]{:S(2)}, u32[]{:S(2)}) collective-permute-start(bf16[48,896]{1,0:T(8,128)(2,1)} %shard_map.125), channel_id=1, source_target_pairs={{0,2},{1,3},{2,0},{3,1},{4,6},{5,7},{6,4},{7,5},{8,10},{9,11},{10,... | collective-permute-start | bytes 258056 | tf_op jit(solution)/shard_map/ppermute | solution.py:376
  76.4 8.3 %all-to-all-done.2.terms = bf16[4,48,896]{2,1,0:T(8,128)(2,1)} async-done(((bf16[4,48,896]{2,1,0:T(8,128)(2,1)}), bf16[4,48,896]{2,1,0:T(8,128)(2,1)}, u32[]{:S(2)}, u32[]{:S(2)}) %all-to-all-start.2) | async-done | bytes 344096 | tf_op jit(solution)/shard_map/all_to_all | solution.py:416
  85.8 2.1 %collective-permute-done.4.refs_2_ = bf16[48,896]{1,0:T(8,128)(2,1)S(1)} collective-permute-done((bf16[48,896]{1,0:T(8,128)(2,1)}, bf16[48,896]{1,0:T(8,128)(2,1)S(1)}, u32[]{:S(2)}, u32[]{:S(2)}) %collective-permute-start.4) | collective-permute-done | bytes 86048 | tf_op jit(solution)/shard_map/ppermute | solution.py:376
  88.0 2.6 %collective-permute-done.5.refs_3_ = bf16[48,896]{1,0:T(8,128)(2,1)S(1)} collective-permute-done((bf16[48,896]{1,0:T(8,128)(2,1)S(1)}, bf16[48,896]{1,0:T(8,128)(2,1)S(1)}, u32[]{:S(2)}, u32[]{:S(2)}) %collective-permute-start.5) | collective-permute-done | bytes 86048 | tf_op jit(solution)/shard_map/ppermute | solution.py:376
  91.4 3.6 %all-to-all-start.3 = ((bf16[4,48,896]{2,1,0:T(8,128)(2,1)}), bf16[4,48,896]{2,1,0:T(8,128)(2,1)S(1)}, u32[]{:S(2)}, u32[]{:S(2)}) async-start(bf16[4,48,896]{2,1,0:T(8,128)(2,1)} %shard_map.127), calls=%async_computation.3 | async-start | bytes 688128 | tf_op jit(solution)/shard_map/all_to_all | solution.py:420
  95.5 10.6 %all-to-all-done.3 = bf16[4,48,896]{2,1,0:T(8,128)(2,1)S(1)} async-done(((bf16[4,48,896]{2,1,0:T(8,128)(2,1)}), bf16[4,48,896]{2,1,0:T(8,128)(2,1)S(1)}, u32[]{:S(2)}, u32[]{:S(2)}) %all-to-all-start.3) | async-done | bytes 344096 | tf_op jit(solution)/shard_map/all_to_all | solution.py:420
  106.1 2.9 %convolution_convert_fusion.2 = bf16[192,896]{1,0:T(8,128)(2,1)} fusion(bf16[192,896]{1,0:T(8,128)(2,1)S(1)} %bitcast.9, bf16[896,896]{1,0:T(8,128)(2,1)} %param.12), kind=kOutput, calls=%fused_computation.2 | convolution fusion | flops 308453376 | bytes 2293760 | tf_op jit(solution)/shard_map/dot_general | solution.py:421
  109.0 3.6 %all-to-all-start.4 = ((bf16[4,48,896]{2,1,0:T(8,128)(2,1)}), bf16[4,48,896]{2,1,0:T(8,128)(2,1)S(1)}, u32[]{:S(2)}, u32[]{:S(2)}) async-start(bf16[4,48,896]{2,1,0:T(8,128)(2,1)} %bitcast.11), calls=%async_computation.4 | async-start | bytes 688128 | tf_op jit(solution)/shard_map/all_to_all | solution.py:425
  112.7 2.0 %convolution_convert_fusion.1 = bf16[192,896]{1,0:T(8,128)(2,1)} fusion(bf16[192,896]{1,0:T(8,128)(2,1)} %bitcast.10, s32[192]{0:T(256)S(1)} %bitcast.13), kind=kOutput, calls=%fused_computation.1 | convolution fusion | flops 66269184 | bytes 688896 | tf_op jit(solution)/shard_map/dot_general | solution.py:431
  114.7 8.1 %all-to-all-done.4.refs_4_ = bf16[4,48,896]{2,1,0:T(8,128)(2,1)S(1)} async-done(((bf16[4,48,896]{2,1,0:T(8,128)(2,1)}), bf16[4,48,896]{2,1,0:T(8,128)(2,1)S(1)}, u32[]{:S(2)}, u32[]{:S(2)}) %all-to-all-start.4) | async-done | bytes 344096 | tf_op jit(solution)/shard_map/all_to_all | solution.py:425
  122.8 12.3 %shard_map.128 = (bf16[48,1024]{1,0:T(8,128)(2,1)}, f32[48,1536]{1,0:T(8,128)}) custom-call(s32[1]{0:T(128)} %bitcast.1.block_ref, s32[48]{0:T(128)S(1)} %copy-done.1, f32[1,896]{1,0:T(1,128)S(1)} %reshape.26.gain, bf16[896,640]{1,0:T(8,128)(2,1)S(1)} %pad_maximum_fusion.refs_0_, bf16[896,640]{1,0:T(8,128)(2,1)} %collective-permute-done.6.refs_1_, ...), custom_call_target="tpu_custom_call" | custom-call | flops 1 | bytes 1 | tf_op jit(solution)/shard_map/pallas_call | solution.py:263
  (35 shorter events, 9.0 us)
Async XLA Ops:
  0.6 1.5 %copy-start = (bf16[192,4736]{1,0:T(8,128)(2,1)S(1)}, bf16[192,4736]{1,0:T(8,128)(2,1)}, u32[]{:S(2)}) copy-start(bf16[192,4736]{1,0:T(8,128)(2,1)} %param.10) | copy-start | bytes 5455876
  4.7 19.3 %copy-start.5 = (bf16[896,128]{1,0:T(8,128)(2,1)S(1)}, bf16[896,128]{1,0:T(8,128)(2,1)}, u32[]{:S(2)}) copy-start(bf16[896,128]{1,0:T(8,128)(2,1)} %param.16) | copy-start | bytes 688132
  4.7 19.3 %copy-start.6 = (bf16[896,128]{1,0:T(8,128)(2,1)S(1)}, bf16[896,128]{1,0:T(8,128)(2,1)}, u32[]{:S(2)}) copy-start(bf16[896,128]{1,0:T(8,128)(2,1)} %param.15) | copy-start | bytes 688132
  4.7 4.1 %collective-permute-start.1 = (bf16[192,4736]{1,0:T(8,128)(2,1)}, bf16[192,4736]{1,0:T(8,128)(2,1)S(1)}, u32[]{:S(2)}, u32[]{:S(2)}) collective-permute-start(bf16[192,4736]{1,0:T(8,128)(2,1)} %convolution_convert_fusion.refs_0_), channel_id=1, source_target_pairs={{0,1},{1,0},{2,3},{3,2},{4,5},{5,4},{6,7},{7,6},{8,9},{9,8},{10,11... | collective-permute-start | bytes 5455880 | tf_op jit(solution)/shard_map/ppermute | solution.py:368
  5.1 43.1 %collective-permute-start = (bf16[192,4736]{1,0:T(8,128)(2,1)}, bf16[192,4736]{1,0:T(8,128)(2,1)}, u32[]{:S(2)}, u32[]{:S(2)}) collective-permute-start(bf16[192,4736]{1,0:T(8,128)(2,1)} %convolution_convert_fusion.refs_0_), channel_id=1, source_target_pairs={{0,2},{2,0},{1,3},{3,1},{4,6},{6,4},{5,7},{7,5},{8,10},{10,8},{9,1... | collective-permute-start | bytes 5455880 | tf_op jit(solution)/shard_map/ppermute | solution.py:372
  8.7 1.2 copy-start.4
  17.7 24.7 %all-to-all-start = ((bf16[4,96,896]{2,1,0:T(8,128)(2,1)}), bf16[4,96,896]{2,1,0:T(8,128)(2,1)}, u32[]{:S(2)}, u32[]{:S(2)}) async-start(bf16[4,96,896]{2,1,0:T(8,128)(2,1)} %shard_map.121), calls=%async_computation | async-start | bytes 1376256 | tf_op jit(solution)/shard_map/all_to_all | solution.py:406
  43.6 0.6 copy-start.2
  48.3 12.0 %collective-permute-start.3 = (bf16[192,4736]{1,0:T(8,128)(2,1)}, bf16[192,4736]{1,0:T(8,128)(2,1)}, u32[]{:S(2)}, u32[]{:S(2)}) collective-permute-start(bf16[192,4736]{1,0:T(8,128)(2,1)} %collective-permute-done.refs_0_), channel_id=1, source_target_pairs={{0,1},{1,0},{2,3},{3,2},{4,5},{5,4},{6,7},{7,6},{8,9},{9,8},{10,11... | collective-permute-start | bytes 5455880 | tf_op jit(solution)/shard_map/ppermute | solution.py:368
  53.6 16.4 %all-to-all-start.1 = ((bf16[4,48,896]{2,1,0:T(8,128)(2,1)}), bf16[4,48,896]{2,1,0:T(8,128)(2,1)S(1)}, u32[]{:S(2)}, u32[]{:S(2)}) async-start(bf16[4,48,896]{2,1,0:T(8,128)(2,1)} %shard_map.123), calls=%async_computation.1 | async-start | bytes 688128 | tf_op jit(solution)/shard_map/all_to_all | solution.py:416
  58.7 36.4 %collective-permute-start.7 = (bf16[896,640]{1,0:T(8,128)(2,1)S(1)}, bf16[896,640]{1,0:T(8,128)(2,1)}, u32[]{:S(2)}, u32[]{:S(2)}) collective-permute-start(bf16[896,640]{1,0:T(8,128)(2,1)S(1)} %pad_maximum_fusion.refs_0_), channel_id=1, source_target_pairs={{0,2},{2,0},{1,3},{3,1},{4,6},{6,4},{5,7},{7,5},{8,10},{10,8},{9,1... | collective-permute-start | bytes 3440648 | tf_op jit(solution)/shard_map/ppermute | solution.py:372
  70.0 14.7 %all-to-all-start.2 = ((bf16[4,48,896]{2,1,0:T(8,128)(2,1)}), bf16[4,48,896]{2,1,0:T(8,128)(2,1)}, u32[]{:S(2)}, u32[]{:S(2)}) async-start(bf16[4,48,896]{2,1,0:T(8,128)(2,1)} %shard_map.124), calls=%async_computation.2 | async-start | bytes 688128 | tf_op jit(solution)/shard_map/all_to_all | solution.py:416
  74.2 11.7 %collective-permute-start.2 = (bf16[48,896]{1,0:T(8,128)(2,1)}, bf16[48,896]{1,0:T(8,128)(2,1)S(1)}, u32[]{:S(2)}, u32[]{:S(2)}) collective-permute-start(bf16[48,896]{1,0:T(8,128)(2,1)} %copy-done.2), channel_id=1, source_target_pairs={{0,1},{1,0},{2,3},{3,2},{4,5},{5,4},{6,7},{7,6},{8,9},{9,8},{10,11... | collective-permute-start | bytes 258056 | tf_op jit(solution)/shard_map/ppermute | solution.py:368
  74.9 13.1 %collective-permute-start.4 = (bf16[48,896]{1,0:T(8,128)(2,1)}, bf16[48,896]{1,0:T(8,128)(2,1)S(1)}, u32[]{:S(2)}, u32[]{:S(2)}) collective-permute-start(bf16[48,896]{1,0:T(8,128)(2,1)} %shard_map.125), channel_id=1, source_target_pairs={{0,2},{1,3},{2,0},{3,1},{4,6},{5,7},{6,4},{7,5},{8,10},{9,11},{10,... | collective-permute-start | bytes 258056 | tf_op jit(solution)/shard_map/ppermute | solution.py:376
  85.7 4.8 %collective-permute-start.5 = (bf16[48,896]{1,0:T(8,128)(2,1)S(1)}, bf16[48,896]{1,0:T(8,128)(2,1)S(1)}, u32[]{:S(2)}, u32[]{:S(2)}) collective-permute-start(bf16[48,896]{1,0:T(8,128)(2,1)S(1)} %shard_map.126), channel_id=1, source_target_pairs={{0,3},{1,2},{2,1},{3,0},{4,7},{5,6},{6,5},{7,4},{8,11},{9,10},{10,... | collective-permute-start | bytes 258056 | tf_op jit(solution)/shard_map/ppermute | solution.py:376
  91.4 21.3 %copy-start.7 = (f32[896]{0:T(1024)S(1)}, f32[896]{0:T(1024)}, u32[]{:S(2)}) copy-start(f32[896]{0:T(1024)} %param.13) | copy-start | bytes 10756
  91.4 21.3 %copy-start.8 = (s32[1,192]{1,0:T(1,128)S(1)}, s32[1,192]{1,0:T(1,128)}, u32[]{:S(2)}) copy-start(s32[1,192]{1,0:T(1,128)} %param.17) | copy-start | bytes 2308
  91.4 14.8 %all-to-all-start.3 = ((bf16[4,48,896]{2,1,0:T(8,128)(2,1)}), bf16[4,48,896]{2,1,0:T(8,128)(2,1)S(1)}, u32[]{:S(2)}, u32[]{:S(2)}) async-start(bf16[4,48,896]{2,1,0:T(8,128)(2,1)} %shard_map.127), calls=%async_computation.3 | async-start | bytes 688128 | tf_op jit(solution)/shard_map/all_to_all | solution.py:420
  95.0 19.7 %collective-permute-start.6 = (bf16[896,640]{1,0:T(8,128)(2,1)S(1)}, bf16[896,640]{1,0:T(8,128)(2,1)}, u32[]{:S(2)}, u32[]{:S(2)}) collective-permute-start(bf16[896,640]{1,0:T(8,128)(2,1)S(1)} %pad_maximum_fusion.refs_0_), channel_id=1, source_target_pairs={{0,1},{1,0},{2,3},{3,2},{4,5},{5,4},{6,7},{7,6},{8,9},{9,8},{10,11... | collective-permute-start | bytes 3440648 | tf_op jit(solution)/shard_map/ppermute | solution.py:368
  95.1 27.7 %collective-permute-start.8 = (bf16[896,640]{1,0:T(8,128)(2,1)}, bf16[896,640]{1,0:T(8,128)(2,1)}, u32[]{:S(2)}, u32[]{:S(2)}) collective-permute-start(bf16[896,640]{1,0:T(8,128)(2,1)} %collective-permute-done.7.refs_2_), channel_id=1, source_target_pairs={{0,1},{1,0},{2,3},{3,2},{4,5},{5,4},{6,7},{7,6},{8,9},{9,8},{10,11... | collective-permute-start | bytes 3440648 | tf_op jit(solution)/shard_map/ppermute | solution.py:368
  106.1 2.9 %copy-start.3 = (bf16[4,48,896]{2,1,0:T(8,128)(2,1)}, bf16[4,48,896]{2,1,0:T(8,128)(2,1)S(1)}, u32[]{:S(2)}) copy-start(bf16[4,48,896]{2,1,0:T(8,128)(2,1)S(1)} %all-to-all-done.3) | copy-start | bytes 1032196
  106.1 16.7 %copy-start.1 = (s32[48]{0:T(128)S(1)}, s32[48]{0:T(128)}, u32[]{:S(2)}) copy-start(s32[48]{0:T(128)} %len_ref.1) | copy-start | bytes 580
  109.0 13.8 %all-to-all-start.4 = ((bf16[4,48,896]{2,1,0:T(8,128)(2,1)}), bf16[4,48,896]{2,1,0:T(8,128)(2,1)S(1)}, u32[]{:S(2)}, u32[]{:S(2)}) async-start(bf16[4,48,896]{2,1,0:T(8,128)(2,1)} %bitcast.11), calls=%async_computation.4 | async-start | bytes 688128 | tf_op jit(solution)/shard_map/all_to_all | solution.py:425

commit v10 on v9

--- a/solution.py
+++ b/solution.py
@@ -15,19 +15,18 @@
 MOST_VMEM = 56 * 1024 * 1024
 
 
-def down_kernel(counts, planes, cuts, *refs):
-    groups = len(counts)
-    xs, (w, out, x_all, w_all, acc, x_sem, w_sem) = refs[:groups], refs[groups:]
-    first = [planes * sum(counts[:i]) for i in range(groups)]
+def down_kernel(owned, cuts, groups, *refs):
+    slots, xs, refs = refs[:groups], refs[groups : 2 * groups], refs[2 * groups :]
+    w, out, x_all, w_all, acc, x_sem, w_sem = refs
+    n = xs[0].shape[0]
     loads = []
     for s, (lo, hi) in enumerate(cuts):
         deep = pl.ds(lo, hi - lo)
         copies = [pltpu.make_async_copy(w.at[deep], w_all.at[deep], w_sem.at[s])]
         for i in range(groups):
-            here = pl.ds(first[i], planes * counts[i])
             copies.append(
                 pltpu.make_async_copy(
-                    xs[i].at[:, deep], x_all.at[here, deep], x_sem.at[s, i]
+                    xs[i].at[:, deep], x_all.at[pl.ds(i * n, n), deep], x_sem.at[s, i]
                 )
             )
         for copy in copies:
@@ -38,70 +37,83 @@
             copy.wait()
         part = jnp.dot(x_all[:, lo:hi], w_all[lo:hi, :], preferred_element_type=jnp.float32)
         acc[...] = part if s == 0 else acc[...] + part
-    for i, n in enumerate(counts):
-        row = sum(counts[:i])
-        for p in range(planes):
-            at = first[i] + p * n
-            out[p, row : row + n, :] = acc[at : at + n, :].astype(out.dtype)
-
-
-def down(xs, w, planes):
+    place = lax.broadcasted_iota(jnp.int32, (n, n), 0)
+    for i in range(groups):
+        pick = (place == slots[i][...]).astype(jnp.float32).astype(jnp.bfloat16)
+        sums = acc[i * n : (i + 1) * n, :].astype(jnp.bfloat16)
+        ordered = jnp.dot(pick, sums, preferred_element_type=jnp.float32).astype(out.dtype)
+        for p in range(n // owned):
+            out[p, i * owned : (i + 1) * owned, :] = ordered[p * owned : (p + 1) * owned, :]
+
+
+def down(xs, slots, w, owned):
     depth, columns = w.shape
-    counts = [x.shape[0] // planes for x in xs]
-    rows = sum(counts)
+    groups, n = len(xs), xs[0].shape[0]
     tiles, parts = depth // LANES, 6
     ends = [LANES * (tiles * i // parts) for i in range(parts)] + [depth]
     anywhere = pl.BlockSpec(memory_space=pl.ANY)
+    vmem = pl.BlockSpec(memory_space=pltpu.VMEM)
     return pl.pallas_call(
-        functools.partial(down_kernel, counts, planes, list(zip(ends[:-1], ends[1:]))),
-        out_shape=jax.ShapeDtypeStruct((planes, rows, columns), jnp.bfloat16),
-        in_specs=[anywhere] * (len(xs) + 1),
-        out_specs=pl.BlockSpec(memory_space=pltpu.VMEM),
+        functools.partial(down_kernel, owned, list(zip(ends[:-1], ends[1:])), groups),
+        out_shape=jax.ShapeDtypeStruct((n // owned, groups * owned, columns), jnp.bfloat16),
+        in_specs=[vmem] * groups + [anywhere] * (groups + 1),
+        out_specs=vmem,
         scratch_shapes=[
-            pltpu.VMEM((planes * rows, depth), jnp.bfloat16),
+            pltpu.VMEM((groups * n, depth), jnp.bfloat16),
             pltpu.VMEM((depth, columns), jnp.bfloat16),
-            pltpu.VMEM((planes * rows, columns), jnp.float32),
-            pltpu.SemaphoreType.DMA((parts, len(xs))),
+            pltpu.VMEM((groups * n, columns), jnp.float32),
+            pltpu.SemaphoreType.DMA((parts, groups)),
             pltpu.SemaphoreType.DMA((parts,)),
         ],
         cost_estimate=SHORT,
         compiler_params=pltpu.CompilerParams(vmem_limit_bytes=MOST_VMEM),
-    )(*xs, w)
-
-
-def add_kernel(terms, *outs):
+    )(*slots, *xs, w)
+
+
+def finish_kernel(turn_ref, terms, w_mine, w_other, *refs):
+    outs, w = refs[:-1], refs[-1]
+    half = w_mine.shape[0]
+    g = turn_ref[0]
+    w[pl.ds(pl.multiple_of(g * half, half), half), :] = w_mine[...]
+    w[pl.ds(pl.multiple_of((1 - g) * half, half), half), :] = w_other[...]
     total = terms[0].astype(jnp.float32)
     for k in range(1, terms.shape[0]):
         total = total + terms[k].astype(jnp.float32)
-    n = outs[0].shape[0]
+    features = total.astype(jnp.bfloat16)
+    projected = jnp.dot(features, w[...], preferred_element_type=jnp.float32)
+    projected = projected.astype(jnp.bfloat16)
+    n = features.shape[0] // len(outs)
     for i, out in enumerate(outs):
-        out[...] = total[i * n : (i + 1) * n].astype(out.dtype)
-
-
-def add(terms, parts):
+        out[0] = features[i * n : (i + 1) * n]
+        out[1] = projected[i * n : (i + 1) * n]
+
+
+def finish(turn, terms, w_halves, parts):
     _, rows, columns = terms.shape
-    part = jax.ShapeDtypeStruct((rows // parts, columns), jnp.bfloat16)
+    wide = w_halves[0].shape[1]
+    part = jax.ShapeDtypeStruct((2, rows // parts, columns), jnp.bfloat16)
     vmem = pl.BlockSpec(memory_space=pltpu.VMEM)
     return pl.pallas_call(
-        add_kernel,
+        finish_kernel,
         out_shape=(part,) * parts,
-        in_specs=[vmem],
+        in_specs=[pl.BlockSpec(memory_space=pltpu.SMEM), vmem, vmem, vmem],
         out_specs=(vmem,) * parts,
+        scratch_shapes=[pltpu.VMEM((columns, wide), jnp.bfloat16)],
         cost_estimate=SHORT,
         compiler_params=pltpu.CompilerParams(vmem_limit_bytes=16 * 1024 * 1024),
-    )(terms)
+    )(turn, terms, *w_halves)
 
 
 def collect_kernel(block_ref, *refs):
     for e, piece in enumerate(refs[:-1]):
-        refs[-1][e ^ block_ref[0]] = piece[...]
+        refs[-1][e ^ block_ref[0]] = piece[0]
 
 
 def collect(block, pieces):
     vmem = pl.BlockSpec(memory_space=pltpu.VMEM)
     return pl.pallas_call(
         collect_kernel,
-        out_shape=jax.ShapeDtypeStruct((len(pieces), *pieces[0].shape), jnp.bfloat16),
+        out_shape=jax.ShapeDtypeStruct((len(pieces), *pieces[0].shape[1:]), jnp.bfloat16),
         in_specs=[pl.BlockSpec(memory_space=pltpu.SMEM)] + [vmem] * len(pieces),
         out_specs=vmem,
         cost_estimate=SHORT,
@@ -121,7 +133,8 @@
 
 def talker_kernel(blocks, block_ref, len_ref, gain, *refs):
     w_hbm, refs = refs[:blocks], refs[blocks:]
-    terms, kv_hbm, new_kv, out_ref, kv_ref, sem, w_ref, w_sem, qkv, spreads, gathereds = refs
+    terms, refs = refs[:blocks], refs[blocks:]
+    kv_hbm, new_kv, out_ref, kv_ref, sem, w_ref, w_sem, qkv, spreads, gathereds = refs
     rows, cached, kv_width = kv_ref.shape
     width = kv_width // 2
     page = cached // PAGES
@@ -146,9 +159,9 @@
             else:
                 pl.when(needed)(copy.start)
 
-    total = terms[0].astype(jnp.float32)
-    for k in range(1, terms.shape[0]):
-        total = total + terms[k].astype(jnp.float32)
+    total = terms[0][1].astype(jnp.float32)
+    for term in terms[1:]:
+        total = total + term[1].astype(jnp.float32)
     scale = lax.rsqrt(jnp.mean(total * total, axis=1, keepdims=True) + 1e-06)
     normed = (total * scale * gain[...]).astype(jnp.bfloat16)
     for e in range(blocks):
@@ -252,7 +265,7 @@
             context(at, *weighed[k], gathereds.at[k])
 
 
-def talker(block, terms, talker_gain, weights, kv_len, kv_cache):
+def talker(block, pieces, talker_gain, weights, kv_len, kv_cache):
     rows, cached, kv_width = kv_cache.shape
     wide, columns = weights[0].shape
     blocks = len(weights)
@@ -268,7 +281,8 @@
         ),
         in_specs=[smem, smem, vmem]
         + [pl.BlockSpec(memory_space=pl.ANY)] * blocks
-        + [vmem, pl.BlockSpec(memory_space=pl.ANY)],
+        + [vmem] * len(pieces)
+        + [pl.BlockSpec(memory_space=pl.ANY)],
         out_specs=(vmem, vmem),
         scratch_shapes=[
             pltpu.VMEM((rows, cached, kv_width), jnp.bfloat16),
@@ -281,7 +295,7 @@
         ],
         cost_estimate=SHORT,
         compiler_params=pltpu.CompilerParams(vmem_limit_bytes=48 * 1024 * 1024),
-    )(block, kv_len, talker_gain.reshape(1, wide), *weights, terms, kv_cache)
+    )(block, kv_len, talker_gain.reshape(1, wide), *weights, *pieces, kv_cache)
 
 
 def rms_norm(talker_in, talker_gain):
@@ -376,6 +390,10 @@
     return lax.ppermute(x, PLANE, [(b, b ^ e) for b in range(4)])
 
 
+def over_groups(x):
+    return lax.ppermute(x, "groups", [(0, 1), (1, 0)])
+
+
 def after(x, *others):
     return lax.optimization_barrier((x, *others))[0]
 
@@ -394,39 +412,41 @@
 ):
     planes = 4
     owned = kv_cache.shape[0]
-    block = lax.axis_index(PLANE).reshape(1)
+    g, m, c = lax.axis_index("groups"), lax.axis_index("mp"), lax.axis_index(PLANE)
+    block, turn = c.reshape(1), g.reshape(1)
     slots = talker_slot[0]
 
-    pick = (jnp.arange(planes * owned)[:, None] == slots[None, :]).astype(jnp.bfloat16)
-    rows = jnp.dot(pick, thinker_act, preferred_element_type=jnp.float32).astype(jnp.bfloat16)
-
-    across = over_section(rows)
-    peer = over_core(rows)
-    near = down([rows, peer], w_think, planes)
+    across, peer = over_section(thinker_act), over_core(thinker_act)
+    peer_slots, across_slots = over_core(talker_slot), over_section(talker_slot)
+    far_slots = over_core(across_slots)
+    near = down([thinker_act, peer], [talker_slot, peer_slots], w_think, owned)
     near_terms = lax.all_to_all(near, "mp", 0, 0)
     mine = jnp.concatenate([w_query, w_key, w_value], axis=1)
 
-    own, next_core = add(near_terms, 2)
-    across, own, next_core, mine = lax.optimization_barrier((across, own, next_core, mine))
-    far = [down([across], w_think, planes)]
-    far.append(down([after(over_core(across), far[0])], w_think, planes))
+    half = w_proj.shape[0] // 2
+    half_w = lax.dynamic_slice_in_dim(w_proj, g * half, half, axis=0)
+    half_w = lax.psum(jnp.where(m == c, half_w, jnp.zeros_like(half_w)), "mp")
+
+    across, near_terms, mine, far_slots, half_w = lax.optimization_barrier(
+        (across, near_terms, mine, far_slots, half_w)
+    )
+    far = [down([across], [across_slots], w_think, owned)]
+    far.append(down([after(over_core(across), far[0])], [far_slots], w_think, owned))
+    block_w = (half_w, over_groups(half_w))
+    other = over_section(after(mine, far[0]))
+
+    own, next_core = finish(turn, after(near_terms, far[1]), block_w, 2)
     pieces = [own, over_core(next_core)]
     made = own
     for e, x in zip((2, 3), far):
-        (made,) = add(after(lax.all_to_all(x, "mp", 0, 0), made, far[1]), 1)
+        (made,) = finish(turn, after(lax.all_to_all(x, "mp", 0, 0), made), block_w, 1)
         pieces.append(over_plane(made, e))
-    other = over_section(after(mine, far[0]))
-
-    home = lax.all_to_all(collect(block, pieces), "mp", 0, 0)
-    projected = jnp.dot(
-        home.reshape(planes * owned, -1), w_proj, preferred_element_type=jnp.float32
-    )
-    projected = projected.astype(jnp.bfloat16).reshape(planes, owned, -1)
-    terms = lax.all_to_all(projected, "mp", 0, 0)
     other = after(other, made)
     weights = [mine, over_core(mine), other, over_core(other)]
-    new_kv, ctx = talker(block, terms, talker_gain, weights, kv_len, kv_cache)
-    home = after(home, projected)
+
+    home = lax.all_to_all(collect(block, pieces), "mp", 0, 0)
+    new_kv, ctx = talker(block, pieces, talker_gain, weights, kv_len, kv_cache)
+    home = after(home, ctx)
     pick = (slots[:, None] == jnp.arange(planes * owned)[None, :]).astype(jnp.bfloat16)
     thinker_out = jnp.dot(
         pick, home.reshape(planes * owned, -1), preferred_element_type=jnp.float32

time: 136 us -> 160 us (1.18)
  between operations: 0.94 us -> 14.3 us
  waiting for transfers between devices: 58.6 us -> 71 us
  matrix products: 7.41 us -> 2.01 us
  Pallas kernels: 34.3 us -> 37.8 us
    psum x0 -> x1, waiting for transfers between devices: none -> 31.5 us  [four_planes(): half_w = lax.psum(jnp.where(m == c, half_w, jnp.zeros_like(half_w)), 'mp')]
    all_to_all x1, waiting for transfers between devices: 17.2 us -> 0.01 us  [four_planes(): near_terms = lax.all_to_all(near, 'mp', 0, 0)]
    ppermute x2 -> x3, waiting for transfers between devices: 4.06 us -> 20 us  [over_section(): return lax.ppermute(x, 'section', [(0, 1), (1, 0)])]
    all_to_all x3 -> x2, waiting for transfers between devices: 20.9 us -> 6 us  [four_planes(): made, = finish(turn, after(lax.all_to_all(x, 'mp', 0, 0), made), block_w, 1)]
    all_to_all x1, waiting for transfers between devices: 10.6 us -> 0.01 us  [four_planes(): home = lax.all_to_all(collect(block, pieces), 'mp', 0, 0)]
    dot_general x2 -> x0, matrix products: 5.39 us -> none  [the longest x1 2.86 us: four_planes(): jnp.dot(home.reshape(planes * owned, -1), w_proj, preferred_element_type=...]
    all_to_all x3 -> x2, starting transfers between devices: 12.9 us -> 8.21 us  [four_planes(): made, = finish(turn, after(lax.all_to_all(x, 'mp', 0, 0), made), block_w, 1)]
    ppermute x0 -> x1, waiting for transfers between devices: none -> 4.55 us  [over_groups(): return lax.ppermute(x, 'groups', [(0, 1), (1, 0)])]
  transfers between devices with their start and end apart: 14 -> 18, of which waited for: 9 -> 9; matrix products, arithmetic and copies ran while one was open for 5% -> 1% of each run, Pallas kernels for 16% -> 24%
where the time goes in v10:
time: 160 us; the launch traced here: 159 us
  waiting for transfers between devices  71 us (44%)
  Pallas kernels  37.8 us (24%)
  starting transfers between devices  28.6 us (18%)
  between operations  14.3 us (9%)
  local copies, waits for them, and re-layouts  3.16 us (2%)
  other arithmetic  2.21 us (1%)
  matrix products  2.01 us (1%)
    psum x1, waiting for transfers between devices, four_planes(): half_w = lax.psum(jnp.where(m == c, half_w, jnp.zeros_like(half_w)), 'mp')  31.5 us
    pallas_call x3, Pallas kernels, down(): pl.pallas_call(functools.partial(down_kernel, owned, list(zip(ends[:-1],...  21.2 us
    ppermute x3, waiting for transfers between devices, over_section(): return lax.ppermute(x, 'section', [(0, 1), (1, 0)])  20 us
    pallas_call x1, Pallas kernels, talker(): pl.pallas_call(functools.partial(talker_kernel, blocks), out_shape=(jax.S...  12.4 us
    all_to_all x2, starting transfers between devices, four_planes(): made, = finish(turn, after(lax.all_to_all(x, 'mp', 0, 0), made), block_w, 1)  8.21 us
    ppermute x2, waiting for transfers between devices, over_plane(): return lax.ppermute(x, PLANE, [(b, b ^ e) for b in range(4)])  7 us
    all_to_all x1, starting transfers between devices, four_planes(): near_terms = lax.all_to_all(near, 'mp', 0, 0)  6.06 us
    all_to_all x2, waiting for transfers between devices, four_planes(): made, = finish(turn, after(lax.all_to_all(x, 'mp', 0, 0), made), block_w, 1)  6 us
  transfers between devices with their start and end apart: 18, of which 9 were waited for; matrix products, arithmetic and copies ran while one was open for 1% of the time, Pallas kernels for 24%

profile of v10, /device:TPU:0, one launch (start us, length us, event | category | flops | bytes accessed | tf_op | source)
XLA Modules:
  0.0 159.0 jit_solution(8948695823274753365)
XLA Ops:
  7.7 2.6 %collective-permute-start = (bf16[192,4736]{1,0:T(8,128)(2,1)}, bf16[192,4736]{1,0:T(8,128)(2,1)}, u32[]{:S(2)}, u32[]{:S(2)}) collective-permute-start(bf16[192,4736]{1,0:T(8,128)(2,1)} %refs_2_.3), channel_id=1, source_target_pairs={{0,2},{2,0},{1,3},{3,1},{4,6},{6,4},{5,7},{7,5},{8,10},{10,8},{9,1... | collective-permute-start | bytes 5455880 | tf_op jit(solution)/shard_map/ppermute | solution.py:386
  10.4 1.2 collective-permute-done.1.refs_1_
  12.2 1.2 copy-done.6
  13.4 8.8 %shard_map.121 = bf16[4,96,896]{2,1,0:T(8,128)(2,1)} custom-call(s32[1,192]{1,0:T(1,128)} %refs_0_.1, s32[1,192]{1,0:T(1,128)} %copy-done.13, bf16[192,4736]{1,0:T(8,128)(2,1)} %refs_2_.3, bf16[192,4736]{1,0:T(8,128)(2,1)} %copy-done.6, bf16[4736,896]{1,0:T(8,128)(2,1)} %refs_2_.5), custom_call_target="tpu_custom_call" | custom-call | flops 1 | bytes 1 | tf_op jit(solution)/shard_map/pallas_call | solution.py:56
  22.2 6.1 %all-to-all-start = ((bf16[4,96,896]{2,1,0:T(8,128)(2,1)}), bf16[4,96,896]{2,1,0:T(8,128)(2,1)S(1)}, u32[]{:S(2)}, u32[]{:S(2)}) async-start(bf16[4,96,896]{2,1,0:T(8,128)(2,1)} %shard_map.121), calls=%async_computation | async-start | bytes 1376256 | tf_op jit(solution)/shard_map/all_to_all | solution.py:423
  29.3 1.6 collective-permute-start.3
  30.9 20.0 %collective-permute-done.3.refs_0_ = s32[1,192]{1,0:T(1,128)S(1)} collective-permute-done((s32[1,192]{1,0:T(1,128)S(1)}, s32[1,192]{1,0:T(1,128)S(1)}, u32[]{:S(2)}, u32[]{:S(2)}) %collective-permute-start.3) | collective-permute-done | bytes 800 | tf_op jit(solution)/shard_map/ppermute | solution.py:386
  52.0 31.5 %all-reduce.2.cloned.1.call-done.w_mine = bf16[448,896]{1,0:T(8,128)(2,1)} async-done(((bf16[448,896]{1,0:T(8,128)(2,1)}), bf16[448,896]{1,0:T(8,128)(2,1)}) %all-reduce.2.cloned.1.call-update) | async-done | bytes 802832 | tf_op jit(solution)/shard_map/psum | solution.py:428
  83.6 6.2 %shard_map.122 = bf16[4,48,896]{2,1,0:T(8,128)(2,1)} custom-call(s32[1,192]{1,0:T(1,128)} %copy-done.12, bf16[192,4736]{1,0:T(8,128)(2,1)} %collective-permute-done.refs_1_, bf16[4736,896]{1,0:T(8,128)(2,1)} %refs_2_.5), custom_call_target="tpu_custom_call" | custom-call | flops 1 | bytes 1 | tf_op jit(solution)/shard_map/pallas_call | solution.py:56
  89.9 1.5 collective-permute-start.11
  91.4 4.1 %all-to-all-start.1 = ((bf16[4,48,896]{2,1,0:T(8,128)(2,1)}), bf16[4,48,896]{2,1,0:T(8,128)(2,1)}, u32[]{:S(2)}, u32[]{:S(2)}) async-start(bf16[4,48,896]{2,1,0:T(8,128)(2,1)} %shard_map.122), calls=%async_computation.1 | async-start | bytes 688128 | tf_op jit(solution)/shard_map/all_to_all | solution.py:442
  95.6 1.5 collective-permute-start.6
  97.1 6.2 %shard_map.123 = bf16[4,48,896]{2,1,0:T(8,128)(2,1)} custom-call(s32[1,192]{1,0:T(1,128)} %copy-done.11, bf16[192,4736]{1,0:T(8,128)(2,1)} %collective-permute-done.5.refs_1_, bf16[4736,896]{1,0:T(8,128)(2,1)} %refs_2_.5), custom_call_target="tpu_custom_call" | custom-call | flops 1 | bytes 1 | tf_op jit(solution)/shard_map/pallas_call | solution.py:56
  103.3 3.5 %all-to-all-done.1.terms = bf16[4,48,896]{2,1,0:T(8,128)(2,1)} async-done(((bf16[4,48,896]{2,1,0:T(8,128)(2,1)}), bf16[4,48,896]{2,1,0:T(8,128)(2,1)}, u32[]{:S(2)}, u32[]{:S(2)}) %all-to-all-start.1) | async-done | bytes 344096 | tf_op jit(solution)/shard_map/all_to_all | solution.py:442
  106.8 4.1 %all-to-all-start.2 = ((bf16[4,48,896]{2,1,0:T(8,128)(2,1)}), bf16[4,48,896]{2,1,0:T(8,128)(2,1)}, u32[]{:S(2)}, u32[]{:S(2)}) async-start(bf16[4,48,896]{2,1,0:T(8,128)(2,1)} %shard_map.123), calls=%async_computation.2 | async-start | bytes 688128 | tf_op jit(solution)/shard_map/all_to_all | solution.py:442
  111.0 4.6 %collective-permute-done.6.w_other = bf16[448,896]{1,0:T(8,128)(2,1)S(1)} collective-permute-done((bf16[448,896]{1,0:T(8,128)(2,1)S(1)}, bf16[448,896]{1,0:T(8,128)(2,1)S(1)}, u32[]{:S(2)}, u32[]{:S(2)}) %collective-permute-start.6) | collective-permute-done | bytes 802848 | tf_op jit(solution)/shard_map/ppermute | solution.py:394
  117.4 1.5 shard_map.125
  119.0 2.5 %all-to-all-done.2.terms = bf16[4,48,896]{2,1,0:T(8,128)(2,1)} async-done(((bf16[4,48,896]{2,1,0:T(8,128)(2,1)}), bf16[4,48,896]{2,1,0:T(8,128)(2,1)}, u32[]{:S(2)}, u32[]{:S(2)}) %all-to-all-start.2) | async-done | bytes 344096 | tf_op jit(solution)/shard_map/all_to_all | solution.py:442
  121.4 1.5 shard_map.126
  125.7 5.1 %collective-permute-done.8.refs_2_.refs_6_ = bf16[2,48,896]{2,1,0:T(8,128)(2,1)S(1)} collective-permute-done((bf16[2,48,896]{2,1,0:T(8,128)(2,1)S(1)}, bf16[2,48,896]{2,1,0:T(8,128)(2,1)S(1)}, u32[]{:S(2)}, u32[]{:S(2)}) %collective-permute-start.8) | collective-permute-done | bytes 172064 | tf_op jit(solution)/shard_map/ppermute | solution.py:390
  130.7 1.9 %collective-permute-done.9.refs_3_.refs_7_ = bf16[2,48,896]{2,1,0:T(8,128)(2,1)S(1)} collective-permute-done((bf16[2,48,896]{2,1,0:T(8,128)(2,1)S(1)}, bf16[2,48,896]{2,1,0:T(8,128)(2,1)S(1)}, u32[]{:S(2)}, u32[]{:S(2)}) %collective-permute-start.9) | collective-permute-done | bytes 172064 | tf_op jit(solution)/shard_map/ppermute | solution.py:390
  133.4 4.3 %all-to-all-start.3 = ((bf16[4,48,896]{2,1,0:T(8,128)(2,1)}), bf16[4,48,896]{2,1,0:T(8,128)(2,1)}, u32[]{:S(2)}, u32[]{:S(2)}) async-start(bf16[4,48,896]{2,1,0:T(8,128)(2,1)} %shard_map.127), calls=%async_computation.3 | async-start | bytes 688128 | tf_op jit(solution)/shard_map/all_to_all | solution.py:447
  137.8 12.4 %shard_map.128 = (bf16[48,1024]{1,0:T(8,128)(2,1)}, f32[48,1536]{1,0:T(8,128)}) custom-call(s32[1]{0:T(128)} %bitcast.1.block_ref, s32[48]{0:T(128)S(1)} %copy-done.3, f32[1,896]{1,0:T(1,128)S(1)} %reshape.21.gain, bf16[896,640]{1,0:T(8,128)(2,1)S(1)} %pad_maximum_fusion.refs_0_, bf16[896,640]{1,0:T(8,128)(2,1)} %collective-permute-done.10.refs_1_, ...), custom_call_target="tpu_custom_call" | custom-call | flops 1 | bytes 1 | tf_op jit(solution)/shard_map/pallas_call | solution.py:276
  150.1 2.0 %convolution_convert_fusion = bf16[192,896]{1,0:T(8,128)(2,1)} fusion(bf16[192,896]{1,0:T(8,128)(2,1)} %bitcast.3, s32[192]{0:T(256)S(1)} %bitcast.5), kind=kOutput, calls=%fused_computation | convolution fusion | flops 66269184 | bytes 688896 | tf_op jit(solution)/shard_map/dot_general | solution.py:451
  (53 shorter events, 9.0 us)
Async XLA Ops:
  7.2 4.4 %collective-permute-start.2 = (bf16[192,4736]{1,0:T(8,128)(2,1)}, bf16[192,4736]{1,0:T(8,128)(2,1)S(1)}, u32[]{:S(2)}, u32[]{:S(2)}) collective-permute-start(bf16[192,4736]{1,0:T(8,128)(2,1)} %refs_2_.3), channel_id=1, source_target_pairs={{0,1},{1,0},{2,3},{3,2},{4,5},{5,4},{6,7},{7,6},{8,9},{9,8},{10,11... | collective-permute-start | bytes 5455880 | tf_op jit(solution)/shard_map/ppermute | solution.py:382
  7.7 75.9 %collective-permute-start = (bf16[192,4736]{1,0:T(8,128)(2,1)}, bf16[192,4736]{1,0:T(8,128)(2,1)}, u32[]{:S(2)}, u32[]{:S(2)}) collective-permute-start(bf16[192,4736]{1,0:T(8,128)(2,1)} %refs_2_.3), channel_id=1, source_target_pairs={{0,2},{2,0},{1,3},{3,1},{4,6},{6,4},{5,7},{7,5},{8,10},{10,8},{9,1... | collective-permute-start | bytes 5455880 | tf_op jit(solution)/shard_map/ppermute | solution.py:386
  10.2 1.4 collective-permute-start.1
  22.2 28.7 %copy-start.7 = (bf16[896,384]{1,0:T(8,128)(2,1)S(1)}, bf16[896,384]{1,0:T(8,128)(2,1)}, u32[]{:S(2)}) copy-start(bf16[896,384]{1,0:T(8,128)(2,1)} %param.14) | copy-start | bytes 2064388
  22.2 61.4 %all-to-all-start = ((bf16[4,96,896]{2,1,0:T(8,128)(2,1)}), bf16[4,96,896]{2,1,0:T(8,128)(2,1)S(1)}, u32[]{:S(2)}, u32[]{:S(2)}) async-start(bf16[4,96,896]{2,1,0:T(8,128)(2,1)} %shard_map.121), calls=%async_computation | async-start | bytes 1376256 | tf_op jit(solution)/shard_map/all_to_all | solution.py:423
  28.2 55.3 %all-reduce.2.cloned.1.call-start = ((), (), s32[]{:S(2)}) async-start(), calls=%async_computation.4 | async-start | bytes 1605632 | tf_op jit(solution)/shard_map/psum | solution.py:428
  29.3 21.5 %collective-permute-start.3 = (s32[1,192]{1,0:T(1,128)S(1)}, s32[1,192]{1,0:T(1,128)S(1)}, u32[]{:S(2)}, u32[]{:S(2)}) collective-permute-start(s32[1,192]{1,0:T(1,128)S(1)} %copy-done.10), channel_id=1, source_target_pairs={{0,2},{2,0},{1,3},{3,1},{4,6},{6,4},{5,7},{7,5},{8,10},{10,8},{9,1... | collective-permute-start | bytes 2312 | tf_op jit(solution)/shard_map/ppermute | solution.py:386
  50.8 32.8 %copy-start.12 = (s32[1,192]{1,0:T(1,128)}, s32[1,192]{1,0:T(1,128)S(1)}, u32[]{:S(2)}) copy-start(s32[1,192]{1,0:T(1,128)S(1)} %collective-permute-done.3.refs_0_) | copy-start | bytes 2308
  50.8 1.2 collective-permute-start.4
  52.0 37.9 %copy-start.11 = (s32[1,192]{1,0:T(1,128)}, s32[1,192]{1,0:T(1,128)S(1)}, u32[]{:S(2)}) copy-start(s32[1,192]{1,0:T(1,128)S(1)} %collective-permute-done.4.refs_0_) | copy-start | bytes 2308
  83.6 13.6 %collective-permute-start.5 = (bf16[192,4736]{1,0:T(8,128)(2,1)}, bf16[192,4736]{1,0:T(8,128)(2,1)}, u32[]{:S(2)}, u32[]{:S(2)}) collective-permute-start(bf16[192,4736]{1,0:T(8,128)(2,1)} %collective-permute-done.refs_1_), channel_id=1, source_target_pairs={{0,1},{1,0},{2,3},{3,2},{4,5},{5,4},{6,7},{7,6},{8,9},{9,8},{10,11... | collective-permute-start | bytes 5455880 | tf_op jit(solution)/shard_map/ppermute | solution.py:382
  89.9 33.0 %collective-permute-start.11 = (bf16[896,640]{1,0:T(8,128)(2,1)S(1)}, bf16[896,640]{1,0:T(8,128)(2,1)}, u32[]{:S(2)}, u32[]{:S(2)}) collective-permute-start(bf16[896,640]{1,0:T(8,128)(2,1)S(1)} %pad_maximum_fusion.refs_0_), channel_id=1, source_target_pairs={{0,2},{2,0},{1,3},{3,1},{4,6},{6,4},{5,7},{7,5},{8,10},{10,8},{9,1... | collective-permute-start | bytes 3440648 | tf_op jit(solution)/shard_map/ppermute | solution.py:386
  91.4 15.4 %all-to-all-start.1 = ((bf16[4,48,896]{2,1,0:T(8,128)(2,1)}), bf16[4,48,896]{2,1,0:T(8,128)(2,1)}, u32[]{:S(2)}, u32[]{:S(2)}) async-start(bf16[4,48,896]{2,1,0:T(8,128)(2,1)} %shard_map.122), calls=%async_computation.1 | async-start | bytes 688128 | tf_op jit(solution)/shard_map/all_to_all | solution.py:442
  95.6 20.0 %collective-permute-start.6 = (bf16[448,896]{1,0:T(8,128)(2,1)S(1)}, bf16[448,896]{1,0:T(8,128)(2,1)S(1)}, u32[]{:S(2)}, u32[]{:S(2)}) collective-permute-start(bf16[448,896]{1,0:T(8,128)(2,1)S(1)} %copy-done), channel_id=1, source_target_pairs={{0,16},{16,0},{1,17},{17,1},{2,18},{18,2},{3,19},{19,3},{4,20},{20... | collective-permute-start | bytes 2408456 | tf_op jit(solution)/shard_map/ppermute | solution.py:394
  106.8 14.6 %all-to-all-start.2 = ((bf16[4,48,896]{2,1,0:T(8,128)(2,1)}), bf16[4,48,896]{2,1,0:T(8,128)(2,1)}, u32[]{:S(2)}, u32[]{:S(2)}) async-start(bf16[4,48,896]{2,1,0:T(8,128)(2,1)} %shard_map.123), calls=%async_computation.2 | async-start | bytes 688128 | tf_op jit(solution)/shard_map/all_to_all | solution.py:442
  111.0 26.8 %collective-permute-start.10 = (bf16[896,640]{1,0:T(8,128)(2,1)S(1)}, bf16[896,640]{1,0:T(8,128)(2,1)}, u32[]{:S(2)}, u32[]{:S(2)}) collective-permute-start(bf16[896,640]{1,0:T(8,128)(2,1)S(1)} %pad_maximum_fusion.refs_0_), channel_id=1, source_target_pairs={{0,1},{1,0},{2,3},{3,2},{4,5},{5,4},{6,7},{7,6},{8,9},{9,8},{10,11... | collective-permute-start | bytes 3440648 | tf_op jit(solution)/shard_map/ppermute | solution.py:382
  117.4 15.2 %copy-start.2 = (bf16[2,48,896]{2,1,0:T(8,128)(2,1)S(1)}, bf16[2,48,896]{2,1,0:T(8,128)(2,1)}, u32[]{:S(2)}) copy-start(bf16[2,48,896]{2,1,0:T(8,128)(2,1)} %copy-done.1) | copy-start | bytes 516100
  118.9 18.8 %copy-start.9 = (f32[896]{0:T(1024)S(1)}, f32[896]{0:T(1024)}, u32[]{:S(2)}) copy-start(f32[896]{0:T(1024)} %param.13) | copy-start | bytes 10756
  119.0 18.8 %copy-start.3 = (s32[48]{0:T(128)S(1)}, s32[48]{0:T(128)}, u32[]{:S(2)}) copy-start(s32[48]{0:T(128)} %len_ref.1) | copy-start | bytes 580
  122.9 14.8 %collective-permute-start.12 = (bf16[896,640]{1,0:T(8,128)(2,1)}, bf16[896,640]{1,0:T(8,128)(2,1)S(1)}, u32[]{:S(2)}, u32[]{:S(2)}) collective-permute-start(bf16[896,640]{1,0:T(8,128)(2,1)} %collective-permute-done.11.refs_2_), channel_id=1, source_target_pairs={{0,1},{1,0},{2,3},{3,2},{4,5},{5,4},{6,7},{7,6},{8,9},{9,8},{10,11... | collective-permute-start | bytes 3440648 | tf_op jit(solution)/shard_map/ppermute | solution.py:382
  123.0 2.7 %collective-permute-start.7 = (bf16[2,48,896]{2,1,0:T(8,128)(2,1)S(1)}, bf16[2,48,896]{2,1,0:T(8,128)(2,1)S(1)}, u32[]{:S(2)}, u32[]{:S(2)}) collective-permute-start(bf16[2,48,896]{2,1,0:T(8,128)(2,1)S(1)} %copy-done.5), channel_id=1, source_target_pairs={{0,1},{1,0},{2,3},{3,2},{4,5},{5,4},{6,7},{7,6},{8,9},{9,8},{10,11... | collective-permute-start | bytes 516104 | tf_op jit(solution)/shard_map/ppermute | solution.py:382
  123.5 7.2 %collective-permute-start.8 = (bf16[2,48,896]{2,1,0:T(8,128)(2,1)S(1)}, bf16[2,48,896]{2,1,0:T(8,128)(2,1)S(1)}, u32[]{:S(2)}, u32[]{:S(2)}) collective-permute-start(bf16[2,48,896]{2,1,0:T(8,128)(2,1)S(1)} %shard_map.125), channel_id=1, source_target_pairs={{0,2},{1,3},{2,0},{3,1},{4,6},{5,7},{6,4},{7,5},{8,10},{9,11},{10,... | collective-permute-start | bytes 516104 | tf_op jit(solution)/shard_map/ppermute | solution.py:390
  124.1 8.6 %collective-permute-start.9 = (bf16[2,48,896]{2,1,0:T(8,128)(2,1)S(1)}, bf16[2,48,896]{2,1,0:T(8,128)(2,1)S(1)}, u32[]{:S(2)}, u32[]{:S(2)}) collective-permute-start(bf16[2,48,896]{2,1,0:T(8,128)(2,1)S(1)} %shard_map.126), channel_id=1, source_target_pairs={{0,3},{1,2},{2,1},{3,0},{4,7},{5,6},{6,5},{7,4},{8,11},{9,10},{10,... | collective-permute-start | bytes 516104 | tf_op jit(solution)/shard_map/ppermute | solution.py:390
  133.4 16.7 %all-to-all-start.3 = ((bf16[4,48,896]{2,1,0:T(8,128)(2,1)}), bf16[4,48,896]{2,1,0:T(8,128)(2,1)}, u32[]{:S(2)}, u32[]{:S(2)}) async-start(bf16[4,48,896]{2,1,0:T(8,128)(2,1)} %shard_map.127), calls=%async_computation.3 | async-start | bytes 688128 | tf_op jit(solution)/shard_map/all_to_all | solution.py:447
  (8 other events, 42.7 us)
Sparse Core Ops, SparseCore 0:
  31.4 52.0 all-reduce.1

commit v11 on v10

--- a/solution.py
+++ b/solution.py
@@ -417,30 +417,32 @@
     slots = talker_slot[0]
 
     across, peer = over_section(thinker_act), over_core(thinker_act)
-    peer_slots, across_slots = over_core(talker_slot), over_section(talker_slot)
-    far_slots = over_core(across_slots)
+    peer_slots = over_core(talker_slot)
     near = down([thinker_act, peer], [talker_slot, peer_slots], w_think, owned)
     near_terms = lax.all_to_all(near, "mp", 0, 0)
     mine = jnp.concatenate([w_query, w_key, w_value], axis=1)
 
     half = w_proj.shape[0] // 2
-    half_w = lax.dynamic_slice_in_dim(w_proj, g * half, half, axis=0)
-    half_w = lax.psum(jnp.where(m == c, half_w, jnp.zeros_like(half_w)), "mp")
-
-    across, near_terms, mine, far_slots, half_w = lax.optimization_barrier(
-        (across, near_terms, mine, far_slots, half_w)
-    )
-    far = [down([across], [across_slots], w_think, owned)]
-    far.append(down([after(over_core(across), far[0])], [far_slots], w_think, owned))
-    block_w = (half_w, over_groups(half_w))
-    other = over_section(after(mine, far[0]))
-
-    own, next_core = finish(turn, after(near_terms, far[1]), block_w, 2)
-    pieces = [own, over_core(next_core)]
-    made = own
-    for e, x in zip((2, 3), far):
-        (made,) = finish(turn, after(lax.all_to_all(x, "mp", 0, 0), made), block_w, 1)
-        pieces.append(over_plane(made, e))
+    plane_w = lax.dynamic_slice_in_dim(after(w_proj, peer), g * half, half, axis=0)
+    two = lax.ppermute(plane_w, GROUP, [(b * 4 + b, (b ^ 2) * 4 + b) for b in range(4)])
+    one = lax.ppermute(plane_w, GROUP, [(b * 4 + b, (b ^ 1) * 4 + b) for b in range(4)])
+
+    across, near_terms, mine, plane_w, one, two = lax.optimization_barrier(
+        (across, near_terms, mine, plane_w, one, two)
+    )
+    far_slots = [over_plane(talker_slot, e) for e in (2, 3)]
+    far = down([across, over_core(across)], far_slots, w_think, owned)
+    far_terms = lax.all_to_all(far, "mp", 0, 0)
+    three = lax.ppermute(two, GROUP, [((b ^ 2) * 4 + b, (b ^ 3) * 4 + b) for b in range(4)])
+    three = after(three, far)
+    mine_w = jnp.where(m == c ^ 1, one, jnp.where(m == c ^ 3, three, two))
+    mine_w = jnp.where(m == c, plane_w, mine_w)
+    block_w = (mine_w, over_groups(mine_w))
+    other = over_section(after(mine, far))
+
+    own, next_core = finish(turn, after(near_terms, far), block_w, 2)
+    made, last = finish(turn, after(far_terms, own), block_w, 2)
+    pieces = [own, over_core(next_core), over_plane(made, 2), over_plane(last, 3)]
     other = after(other, made)
     weights = [mine, over_core(mine), other, over_core(other)]
 

time: 160 us -> 138 us (0.86)
  waiting for transfers between devices: 71 us -> 49.9 us
  between operations: 14.3 us -> 0.85 us
  starting transfers between devices: 28.6 us -> 39.1 us
  local copies, waits for them, and re-layouts: 3.16 us -> 9.35 us
  Pallas kernels: 37.8 us -> 32.8 us
    psum x1 -> x0, waiting for transfers between devices: 31.5 us -> none  [four_planes(): half_w = lax.psum(jnp.where(m == c, half_w, jnp.zeros_like(half_w)), 'mp')]
    ppermute x1, waiting for transfers between devices: 4.55 us -> 18.1 us  [over_groups(): return lax.ppermute(x, 'groups', [(0, 1), (1, 0)])]
    ppermute x2 -> x4, starting transfers between devices: 1.44 us -> 10.4 us  [over_plane(): return lax.ppermute(x, PLANE, [(b, b ^ e) for b in range(4)])]
    ppermute x0 -> x3, starting transfers between devices: none -> 8.01 us  [the longest x1 3.98 us: four_planes(): lax.ppermute(plane_w, GROUP, [(b * 4 + b, (b ^ 1) * 4 + b) for b in range...]
    all_to_all x2 -> x1, waiting for transfers between devices: 6 us -> 0.01 us  [four_planes(): far_terms = lax.all_to_all(far, 'mp', 0, 0)]
    unnamed x28 -> x40, local copies, waits for them, and re-layouts: 3.16 us -> 8.58 us
    ppermute x3 -> x2, waiting for transfers between devices: 20 us -> 14.8 us  [over_section(): return lax.ppermute(x, 'section', [(0, 1), (1, 0)])]
    ppermute x0 -> x3, waiting for transfers between devices: none -> 5.06 us  [the longest x1 5.05 us: four_planes(): lax.ppermute(plane_w, GROUP, [(b * 4 + b, (b ^ 2) * 4 + b) for b in range...]
  transfers between devices with their start and end apart: 18 -> 19, of which waited for: 9 -> 9; matrix products, arithmetic and copies ran while one was open for 1% -> 3% of each run, Pallas kernels for 24% -> 24%
where the time goes in v11:
time: 138 us; the launch traced here: 137 us
  waiting for transfers between devices  49.9 us (36%)
  starting transfers between devices  39.1 us (28%)
  Pallas kernels  32.8 us (24%)
  local copies, waits for them, and re-layouts  9.35 us (7%)
  other arithmetic  3.06 us (2%)
  matrix products  2.01 us (1%)
    ppermute x1, waiting for transfers between devices, over_groups(): return lax.ppermute(x, 'groups', [(0, 1), (1, 0)])  18.1 us
    pallas_call x2, Pallas kernels, down(): pl.pallas_call(functools.partial(down_kernel, owned, list(zip(ends[:-1],...  17.4 us
    ppermute x2, waiting for transfers between devices, over_section(): return lax.ppermute(x, 'section', [(0, 1), (1, 0)])  14.8 us
    pallas_call x1, Pallas kernels, talker(): pl.pallas_call(functools.partial(talker_kernel, blocks), out_shape=(jax.S...  12.5 us
    ppermute x4, starting transfers between devices, over_plane(): return lax.ppermute(x, PLANE, [(b, b ^ e) for b in range(4)])  10.4 us
    ppermute x4, waiting for transfers between devices, over_plane(): return lax.ppermute(x, PLANE, [(b, b ^ e) for b in range(4)])  10 us
    unnamed x40, local copies, waits for them, and re-layouts  8.58 us
    all_to_all x1, starting transfers between devices, four_planes(): near_terms = lax.all_to_all(near, 'mp', 0, 0)  5.94 us
  transfers between devices with their start and end apart: 19, of which 9 were waited for; matrix products, arithmetic and copies ran while one was open for 3% of the time, Pallas kernels for 24%

profile of v11, /device:TPU:0, one launch (start us, length us, event | category | flops | bytes accessed | tf_op | source)
XLA Modules:
  0.0 137.0 jit_solution(15043521742324619369)
XLA Ops:
  1.2 2.6 %collective-permute-start = (bf16[192,4736]{1,0:T(8,128)(2,1)}, bf16[192,4736]{1,0:T(8,128)(2,1)}, u32[]{:S(2)}, u32[]{:S(2)}) collective-permute-start(bf16[192,4736]{1,0:T(8,128)(2,1)} %refs_2_.1), channel_id=1, source_target_pairs={{0,2},{2,0},{1,3},{3,1},{4,6},{6,4},{5,7},{7,5},{8,10},{10,8},{9,1... | collective-permute-start | bytes 5455880 | tf_op jit(solution)/shard_map/ppermute | solution.py:386
  5.6 1.2 copy-done.13
  6.9 8.6 %shard_map.121 = bf16[4,96,896]{2,1,0:T(8,128)(2,1)} custom-call(s32[1,192]{1,0:T(1,128)} %refs_0_.1, s32[1,192]{1,0:T(1,128)} %copy-done.19, bf16[192,4736]{1,0:T(8,128)(2,1)} %refs_2_.1, bf16[192,4736]{1,0:T(8,128)(2,1)} %copy-done.13, bf16[4736,896]{1,0:T(8,128)(2,1)} %refs_4_.3), custom_call_target="tpu_custom_call" | custom-call | flops 1 | bytes 1 | tf_op jit(solution)/shard_map/pallas_call | solution.py:56
  15.5 5.9 %all-to-all-start = ((bf16[4,96,896]{2,1,0:T(8,128)(2,1)}), bf16[4,96,896]{2,1,0:T(8,128)(2,1)S(1)}, u32[]{:S(2)}, u32[]{:S(2)}) async-start(bf16[4,96,896]{2,1,0:T(8,128)(2,1)} %shard_map.121), calls=%async_computation | async-start | bytes 1376256 | tf_op jit(solution)/shard_map/all_to_all | solution.py:422
  21.6 4.0 %collective-permute-start.3 = (bf16[448,896]{1,0:T(8,128)(2,1)S(1)}, bf16[448,896]{1,0:T(8,128)(2,1)S(1)}, u32[]{:S(2)}, u32[]{:S(2)}) collective-permute-start(bf16[448,896]{1,0:T(8,128)(2,1)S(1)} %constant_dynamic-slice_fusion), channel_id=1, source_target_pairs={{0,4},{5,1},{10,14},{15,11},{16,20},{21,17},{26,30},{31,27}} | collective-permute-start | bytes 2408456 | tf_op jit(solution)/shard_map/ppermute | solution.py:428
  25.5 2.5 %collective-permute-start.4 = (bf16[448,896]{1,0:T(8,128)(2,1)S(1)}, bf16[448,896]{1,0:T(8,128)(2,1)}, u32[]{:S(2)}, u32[]{:S(2)}) collective-permute-start(bf16[448,896]{1,0:T(8,128)(2,1)S(1)} %constant_dynamic-slice_fusion), channel_id=1, source_target_pairs={{0,8},{5,13},{10,2},{15,7},{16,24},{21,29},{26,18},{31,23}} | collective-permute-start | bytes 2408456 | tf_op jit(solution)/shard_map/ppermute | solution.py:427
  28.0 1.5 %pad_maximum_fusion.refs_0_ = bf16[896,640]{1,0:T(8,128)(2,1)S(1)} fusion(bf16[896,128]{1,0:T(8,128)(2,1)} %param.16, bf16[896,128]{1,0:T(8,128)(2,1)} %param.15, bf16[896,384]{1,0:T(8,128)(2,1)} %param.14), kind=kLoop, calls=%fused_computation.1 | loop fusion | flops 3440640 | bytes 2293760 | tf_op jit(solution)/shard_map/concatenate | solution.py:423
  29.5 14.8 %collective-permute-done.refs_2_ = bf16[192,4736]{1,0:T(8,128)(2,1)} collective-permute-done((bf16[192,4736]{1,0:T(8,128)(2,1)}, bf16[192,4736]{1,0:T(8,128)(2,1)}, u32[]{:S(2)}, u32[]{:S(2)}) %collective-permute-start) | collective-permute-done | bytes 1818656 | tf_op jit(solution)/shard_map/ppermute | solution.py:386
  45.2 5.1 %collective-permute-done.4 = bf16[448,896]{1,0:T(8,128)(2,1)} collective-permute-done((bf16[448,896]{1,0:T(8,128)(2,1)S(1)}, bf16[448,896]{1,0:T(8,128)(2,1)}, u32[]{:S(2)}, u32[]{:S(2)}) %collective-permute-start.4) | collective-permute-done | bytes 802848 | tf_op jit(solution)/shard_map/ppermute | solution.py:427
  50.3 1.6 %collective-permute-start.8 = (bf16[448,896]{1,0:T(8,128)(2,1)}, bf16[448,896]{1,0:T(8,128)(2,1)}, u32[]{:S(2)}, u32[]{:S(2)}) collective-permute-start(bf16[448,896]{1,0:T(8,128)(2,1)} %collective-permute-done.4), channel_id=1, source_target_pairs={{8,12},{13,9},{2,6},{7,3},{24,28},{29,25},{18,22},{23,19}} | collective-permute-start | bytes 2408456 | tf_op jit(solution)/shard_map/ppermute | solution.py:436
  51.9 8.9 %collective-permute-start.5 = (s32[1,192]{1,0:T(1,128)S(1)}, s32[1,192]{1,0:T(1,128)S(1)}, u32[]{:S(2)}, u32[]{:S(2)}) collective-permute-start(s32[1,192]{1,0:T(1,128)S(1)} %copy-done.15), channel_id=1, source_target_pairs={{0,2},{1,3},{2,0},{3,1},{4,6},{5,7},{6,4},{7,5},{8,10},{9,11},{10,... | collective-permute-start | bytes 2312 | tf_op jit(solution)/shard_map/ppermute | solution.py:390
  60.8 1.5 %collective-permute-done.5.refs_0_ = s32[1,192]{1,0:T(1,128)S(1)} collective-permute-done((s32[1,192]{1,0:T(1,128)S(1)}, s32[1,192]{1,0:T(1,128)S(1)}, u32[]{:S(2)}, u32[]{:S(2)}) %collective-permute-start.5) | collective-permute-done | bytes 800 | tf_op jit(solution)/shard_map/ppermute | solution.py:390
  62.3 1.4 %collective-permute-done.6.refs_1_ = s32[1,192]{1,0:T(1,128)S(1)} collective-permute-done((s32[1,192]{1,0:T(1,128)S(1)}, s32[1,192]{1,0:T(1,128)S(1)}, u32[]{:S(2)}, u32[]{:S(2)}) %collective-permute-start.6) | collective-permute-done | bytes 800 | tf_op jit(solution)/shard_map/ppermute | solution.py:390
  65.6 8.7 %shard_map.122 = bf16[4,96,896]{2,1,0:T(8,128)(2,1)} custom-call(s32[1,192]{1,0:T(1,128)} %copy-done.17, s32[1,192]{1,0:T(1,128)} %copy-done.18, bf16[192,4736]{1,0:T(8,128)(2,1)} %collective-permute-done.refs_2_, bf16[192,4736]{1,0:T(8,128)(2,1)} %copy-done.12, bf16[4736,896]{1,0:T(8,128)(2,1)} %refs_4_.3), custom_call_target="tpu_custom_call" | custom-call | flops 1 | bytes 1 | tf_op jit(solution)/shard_map/pallas_call | solution.py:56
  75.0 4.2 %all-to-all-start.1 = ((bf16[4,96,896]{2,1,0:T(8,128)(2,1)}), bf16[4,96,896]{2,1,0:T(8,128)(2,1)}, u32[]{:S(2)}, u32[]{:S(2)}) async-start(bf16[4,96,896]{2,1,0:T(8,128)(2,1)} %shard_map.122), calls=%async_computation.1 | async-start | bytes 1376256 | tf_op jit(solution)/shard_map/all_to_all | solution.py:435
  79.2 1.6 %select_select_fusion.w_mine = bf16[448,896]{1,0:T(8,128)(2,1)S(1)} fusion(bf16[448,896]{1,0:T(8,128)(2,1)} %copy-done.11, bf16[448,896]{1,0:T(8,128)(2,1)} %copy-done.14, bf16[448,896]{1,0:T(8,128)(2,1)} %collective-permute-done.8, bf16[448,896]{1,0:T(8,128)(2,1)} %collective-permute-done.4, pred[]{:T(512)S(6)} %eq.30, pred[]{:T(512)S(6)} %eq.29, pred[]{:T(512)S(6)} %eq.28), kind=kLoop, calls=%fused_computation.2 | loop fusion | flops 1204224 | bytes 4014083 | tf_op jit(solution)/shard_map/jit(_where)/select_n | solution.py:439
  80.8 1.6 %collective-permute-start.9 = (bf16[448,896]{1,0:T(8,128)(2,1)S(1)}, bf16[448,896]{1,0:T(8,128)(2,1)S(1)}, u32[]{:S(2)}, u32[]{:S(2)}) collective-permute-start(bf16[448,896]{1,0:T(8,128)(2,1)S(1)} %select_select_fusion.w_mine), channel_id=1, source_target_pairs={{0,16},{16,0},{1,17},{17,1},{2,18},{18,2},{3,19},{19,3},{4,20},{20... | collective-permute-start | bytes 2408456 | tf_op jit(solution)/shard_map/ppermute | solution.py:394
  82.4 18.1 %collective-permute-done.9.w_other = bf16[448,896]{1,0:T(8,128)(2,1)S(1)} collective-permute-done((bf16[448,896]{1,0:T(8,128)(2,1)S(1)}, bf16[448,896]{1,0:T(8,128)(2,1)S(1)}, u32[]{:S(2)}, u32[]{:S(2)}) %collective-permute-start.9) | collective-permute-done | bytes 802848 | tf_op jit(solution)/shard_map/ppermute | solution.py:394
  104.4 1.6 %shard_map.124 = (bf16[2,48,896]{2,1,0:T(8,128)(2,1)S(1)}, bf16[2,48,896]{2,1,0:T(8,128)(2,1)S(1)}) custom-call(s32[1]{0:T(128)} %bitcast.2.turn_ref, bf16[4,96,896]{2,1,0:T(8,128)(2,1)} %all-to-all-done.1.terms, bf16[448,896]{1,0:T(8,128)(2,1)S(1)} %select_select_fusion.w_mine, bf16[448,896]{1,0:T(8,128)(2,1)S(1)} %copy-done.2), custom_call_target="tpu_custom_call" | custom-call | flops 1 | bytes 1 | tf_op jit(solution)/shard_map/pallas_call | solution.py:96
  108.8 5.1 %collective-permute-done.11.refs_2_.refs_6_ = bf16[2,48,896]{2,1,0:T(8,128)(2,1)S(1)} collective-permute-done((bf16[2,48,896]{2,1,0:T(8,128)(2,1)S(1)}, bf16[2,48,896]{2,1,0:T(8,128)(2,1)S(1)}, u32[]{:S(2)}, u32[]{:S(2)}) %collective-permute-start.11) | collective-permute-done | bytes 172064 | tf_op jit(solution)/shard_map/ppermute | solution.py:390
  113.9 2.0 %collective-permute-done.12.refs_3_.refs_7_ = bf16[2,48,896]{2,1,0:T(8,128)(2,1)S(1)} collective-permute-done((bf16[2,48,896]{2,1,0:T(8,128)(2,1)S(1)}, bf16[2,48,896]{2,1,0:T(8,128)(2,1)S(1)}, u32[]{:S(2)}, u32[]{:S(2)}) %collective-permute-start.12) | collective-permute-done | bytes 172064 | tf_op jit(solution)/shard_map/ppermute | solution.py:390
  116.6 4.5 %all-to-all-start.2 = ((bf16[4,48,896]{2,1,0:T(8,128)(2,1)}), bf16[4,48,896]{2,1,0:T(8,128)(2,1)}, u32[]{:S(2)}, u32[]{:S(2)}) async-start(bf16[4,48,896]{2,1,0:T(8,128)(2,1)} %shard_map.125), calls=%async_computation.2 | async-start | bytes 688128 | tf_op jit(solution)/shard_map/all_to_all | solution.py:449
  122.5 12.5 %shard_map.126 = (bf16[48,1024]{1,0:T(8,128)(2,1)}, f32[48,1536]{1,0:T(8,128)}) custom-call(s32[1]{0:T(128)} %bitcast.1.block_ref, s32[48]{0:T(128)S(1)} %copy-done.8, f32[1,896]{1,0:T(1,128)S(1)} %reshape.21.gain, bf16[896,640]{1,0:T(8,128)(2,1)S(1)} %pad_maximum_fusion.refs_0_, bf16[896,640]{1,0:T(8,128)(2,1)} %collective-permute-done.13.refs_1_, ...), custom_call_target="tpu_custom_call" | custom-call | flops 1 | bytes 1 | tf_op jit(solution)/shard_map/pallas_call | solution.py:276
  135.0 2.0 %convolution_convert_fusion = bf16[192,896]{1,0:T(8,128)(2,1)} fusion(bf16[192,896]{1,0:T(8,128)(2,1)} %bitcast.3, s32[192]{0:T(256)S(1)} %bitcast.5), kind=kOutput, calls=%fused_computation | convolution fusion | flops 66269184 | bytes 688896 | tf_op jit(solution)/shard_map/dot_general | solution.py:453
  (65 shorter events, 14.7 us)
Async XLA Ops:
  0.6 20.9 %copy-start = (bf16[896,896]{1,0:T(8,128)(2,1)S(1)}, bf16[896,896]{1,0:T(8,128)(2,1)}, u32[]{:S(2)}) copy-start(bf16[896,896]{1,0:T(8,128)(2,1)} %param.12) | copy-start | bytes 4816900
  0.6 4.4 %collective-permute-start.2 = (bf16[192,4736]{1,0:T(8,128)(2,1)}, bf16[192,4736]{1,0:T(8,128)(2,1)S(1)}, u32[]{:S(2)}, u32[]{:S(2)}) collective-permute-start(bf16[192,4736]{1,0:T(8,128)(2,1)} %refs_2_.1), channel_id=1, source_target_pairs={{0,1},{1,0},{2,3},{3,2},{4,5},{5,4},{6,7},{7,6},{8,9},{9,8},{10,11... | collective-permute-start | bytes 5455880 | tf_op jit(solution)/shard_map/ppermute | solution.py:382
  1.2 43.1 %collective-permute-start = (bf16[192,4736]{1,0:T(8,128)(2,1)}, bf16[192,4736]{1,0:T(8,128)(2,1)}, u32[]{:S(2)}, u32[]{:S(2)}) collective-permute-start(bf16[192,4736]{1,0:T(8,128)(2,1)} %refs_2_.1), channel_id=1, source_target_pairs={{0,2},{2,0},{1,3},{3,1},{4,6},{6,4},{5,7},{7,5},{8,10},{10,8},{9,1... | collective-permute-start | bytes 5455880 | tf_op jit(solution)/shard_map/ppermute | solution.py:386
  3.7 1.4 collective-permute-start.1
  15.5 34.8 %all-to-all-start = ((bf16[4,96,896]{2,1,0:T(8,128)(2,1)}), bf16[4,96,896]{2,1,0:T(8,128)(2,1)S(1)}, u32[]{:S(2)}, u32[]{:S(2)}) async-start(bf16[4,96,896]{2,1,0:T(8,128)(2,1)} %shard_map.121), calls=%async_computation | async-start | bytes 1376256 | tf_op jit(solution)/shard_map/all_to_all | solution.py:422
  21.5 30.4 %copy-start.15 = (s32[1,192]{1,0:T(1,128)S(1)}, s32[1,192]{1,0:T(1,128)}, u32[]{:S(2)}) copy-start(s32[1,192]{1,0:T(1,128)} %refs_0_.1) | copy-start | bytes 2308
  21.6 22.8 %copy-start.11 = (bf16[448,896]{1,0:T(8,128)(2,1)}, bf16[448,896]{1,0:T(8,128)(2,1)S(1)}, u32[]{:S(2)}) copy-start(bf16[448,896]{1,0:T(8,128)(2,1)S(1)} %constant_dynamic-slice_fusion) | copy-start | bytes 2408452
  21.6 22.7 %collective-permute-start.3 = (bf16[448,896]{1,0:T(8,128)(2,1)S(1)}, bf16[448,896]{1,0:T(8,128)(2,1)S(1)}, u32[]{:S(2)}, u32[]{:S(2)}) collective-permute-start(bf16[448,896]{1,0:T(8,128)(2,1)S(1)} %constant_dynamic-slice_fusion), channel_id=1, source_target_pairs={{0,4},{5,1},{10,14},{15,11},{16,20},{21,17},{26,30},{31,27}} | collective-permute-start | bytes 2408456 | tf_op jit(solution)/shard_map/ppermute | solution.py:428
  25.5 24.7 %collective-permute-start.4 = (bf16[448,896]{1,0:T(8,128)(2,1)S(1)}, bf16[448,896]{1,0:T(8,128)(2,1)}, u32[]{:S(2)}, u32[]{:S(2)}) collective-permute-start(bf16[448,896]{1,0:T(8,128)(2,1)S(1)} %constant_dynamic-slice_fusion), channel_id=1, source_target_pairs={{0,8},{5,13},{10,2},{15,7},{16,24},{21,29},{26,18},{31,23}} | collective-permute-start | bytes 2408456 | tf_op jit(solution)/shard_map/ppermute | solution.py:427
  50.3 24.0 %copy-start.3 = (bf16[4,96,896]{2,1,0:T(8,128)(2,1)}, bf16[4,96,896]{2,1,0:T(8,128)(2,1)S(1)}, u32[]{:S(2)}) copy-start(bf16[4,96,896]{2,1,0:T(8,128)(2,1)S(1)} %all-to-all-done.terms) | copy-start | bytes 2064388
  50.3 13.5 %collective-permute-start.7 = (bf16[192,4736]{1,0:T(8,128)(2,1)}, bf16[192,4736]{1,0:T(8,128)(2,1)S(1)}, u32[]{:S(2)}, u32[]{:S(2)}) collective-permute-start(bf16[192,4736]{1,0:T(8,128)(2,1)} %collective-permute-done.refs_2_), channel_id=1, source_target_pairs={{0,1},{1,0},{2,3},{3,2},{4,5},{5,4},{6,7},{7,6},{8,9},{9,8},{10,11... | collective-permute-start | bytes 5455880 | tf_op jit(solution)/shard_map/ppermute | solution.py:382
  50.3 28.9 %collective-permute-start.8 = (bf16[448,896]{1,0:T(8,128)(2,1)}, bf16[448,896]{1,0:T(8,128)(2,1)}, u32[]{:S(2)}, u32[]{:S(2)}) collective-permute-start(bf16[448,896]{1,0:T(8,128)(2,1)} %collective-permute-done.4), channel_id=1, source_target_pairs={{8,12},{13,9},{2,6},{7,3},{24,28},{29,25},{18,22},{23,19}} | collective-permute-start | bytes 2408456 | tf_op jit(solution)/shard_map/ppermute | solution.py:436
  51.9 10.5 %collective-permute-start.5 = (s32[1,192]{1,0:T(1,128)S(1)}, s32[1,192]{1,0:T(1,128)S(1)}, u32[]{:S(2)}, u32[]{:S(2)}) collective-permute-start(s32[1,192]{1,0:T(1,128)S(1)} %copy-done.15), channel_id=1, source_target_pairs={{0,2},{1,3},{2,0},{3,1},{4,6},{5,7},{6,4},{7,5},{8,10},{9,11},{10,... | collective-permute-start | bytes 2312 | tf_op jit(solution)/shard_map/ppermute | solution.py:390
  60.8 3.0 %collective-permute-start.6 = (s32[1,192]{1,0:T(1,128)S(1)}, s32[1,192]{1,0:T(1,128)S(1)}, u32[]{:S(2)}, u32[]{:S(2)}) collective-permute-start(s32[1,192]{1,0:T(1,128)S(1)} %copy-done.15), channel_id=1, source_target_pairs={{0,3},{1,2},{2,1},{3,0},{4,7},{5,6},{6,5},{7,4},{8,11},{9,10},{10,... | collective-permute-start | bytes 2312 | tf_op jit(solution)/shard_map/ppermute | solution.py:390
  74.3 31.7 %collective-permute-start.14 = (bf16[896,640]{1,0:T(8,128)(2,1)S(1)}, bf16[896,640]{1,0:T(8,128)(2,1)}, u32[]{:S(2)}, u32[]{:S(2)}) collective-permute-start(bf16[896,640]{1,0:T(8,128)(2,1)S(1)} %pad_maximum_fusion.refs_0_), channel_id=1, source_target_pairs={{0,2},{2,0},{1,3},{3,1},{4,6},{6,4},{5,7},{7,5},{8,10},{10,8},{9,1... | collective-permute-start | bytes 3440648 | tf_op jit(solution)/shard_map/ppermute | solution.py:386
  75.0 28.3 %all-to-all-start.1 = ((bf16[4,96,896]{2,1,0:T(8,128)(2,1)}), bf16[4,96,896]{2,1,0:T(8,128)(2,1)}, u32[]{:S(2)}, u32[]{:S(2)}) async-start(bf16[4,96,896]{2,1,0:T(8,128)(2,1)} %shard_map.122), calls=%async_computation.1 | async-start | bytes 1376256 | tf_op jit(solution)/shard_map/all_to_all | solution.py:435
  79.1 21.3 %copy-start.4 = (bf16[4,96,896]{2,1,0:T(8,128)(2,1)S(1)}, bf16[4,96,896]{2,1,0:T(8,128)(2,1)}, u32[]{:S(2)}) copy-start(bf16[4,96,896]{2,1,0:T(8,128)(2,1)} %copy-done.3) | copy-start | bytes 2064388
  80.8 19.7 %collective-permute-start.9 = (bf16[448,896]{1,0:T(8,128)(2,1)S(1)}, bf16[448,896]{1,0:T(8,128)(2,1)S(1)}, u32[]{:S(2)}, u32[]{:S(2)}) collective-permute-start(bf16[448,896]{1,0:T(8,128)(2,1)S(1)} %select_select_fusion.w_mine), channel_id=1, source_target_pairs={{0,16},{16,0},{1,17},{17,1},{2,18},{18,2},{3,19},{19,3},{4,20},{20... | collective-permute-start | bytes 2408456 | tf_op jit(solution)/shard_map/ppermute | solution.py:394
  82.4 39.5 %collective-permute-start.13 = (bf16[896,640]{1,0:T(8,128)(2,1)S(1)}, bf16[896,640]{1,0:T(8,128)(2,1)}, u32[]{:S(2)}, u32[]{:S(2)}) collective-permute-start(bf16[896,640]{1,0:T(8,128)(2,1)S(1)} %pad_maximum_fusion.refs_0_), channel_id=1, source_target_pairs={{0,1},{1,0},{2,3},{3,2},{4,5},{5,4},{6,7},{7,6},{8,9},{9,8},{10,11... | collective-permute-start | bytes 3440648 | tf_op jit(solution)/shard_map/ppermute | solution.py:382
  106.1 15.8 %collective-permute-start.15 = (bf16[896,640]{1,0:T(8,128)(2,1)}, bf16[896,640]{1,0:T(8,128)(2,1)}, u32[]{:S(2)}, u32[]{:S(2)}) collective-permute-start(bf16[896,640]{1,0:T(8,128)(2,1)} %collective-permute-done.14.refs_2_), channel_id=1, source_target_pairs={{0,1},{1,0},{2,3},{3,2},{4,5},{5,4},{6,7},{7,6},{8,9},{9,8},{10,11... | collective-permute-start | bytes 3440648 | tf_op jit(solution)/shard_map/ppermute | solution.py:382
  106.2 2.7 %collective-permute-start.10 = (bf16[2,48,896]{2,1,0:T(8,128)(2,1)S(1)}, bf16[2,48,896]{2,1,0:T(8,128)(2,1)S(1)}, u32[]{:S(2)}, u32[]{:S(2)}) collective-permute-start(bf16[2,48,896]{2,1,0:T(8,128)(2,1)S(1)} %copy-done.10), channel_id=1, source_target_pairs={{0,1},{1,0},{2,3},{3,2},{4,5},{5,4},{6,7},{7,6},{8,9},{9,8},{10,11... | collective-permute-start | bytes 516104 | tf_op jit(solution)/shard_map/ppermute | solution.py:382
  106.6 7.2 %collective-permute-start.11 = (bf16[2,48,896]{2,1,0:T(8,128)(2,1)S(1)}, bf16[2,48,896]{2,1,0:T(8,128)(2,1)S(1)}, u32[]{:S(2)}, u32[]{:S(2)}) collective-permute-start(bf16[2,48,896]{2,1,0:T(8,128)(2,1)S(1)} %get-tuple-element.33), channel_id=1, source_target_pairs={{0,2},{1,3},{2,0},{3,1},{4,6},{5,7},{6,4},{7,5},{8,10},{9,11},{10,... | collective-permute-start | bytes 516104 | tf_op jit(solution)/shard_map/ppermute | solution.py:390
  107.1 8.7 %collective-permute-start.12 = (bf16[2,48,896]{2,1,0:T(8,128)(2,1)S(1)}, bf16[2,48,896]{2,1,0:T(8,128)(2,1)S(1)}, u32[]{:S(2)}, u32[]{:S(2)}) collective-permute-start(bf16[2,48,896]{2,1,0:T(8,128)(2,1)S(1)} %get-tuple-element.34), channel_id=1, source_target_pairs={{0,3},{1,2},{2,1},{3,0},{4,7},{5,6},{6,5},{7,4},{8,11},{9,10},{10,... | collective-permute-start | bytes 516104 | tf_op jit(solution)/shard_map/ppermute | solution.py:390
  116.6 18.4 %all-to-all-start.2 = ((bf16[4,48,896]{2,1,0:T(8,128)(2,1)}), bf16[4,48,896]{2,1,0:T(8,128)(2,1)}, u32[]{:S(2)}, u32[]{:S(2)}) async-start(bf16[4,48,896]{2,1,0:T(8,128)(2,1)} %shard_map.125), calls=%async_computation.2 | async-start | bytes 688128 | tf_op jit(solution)/shard_map/all_to_all | solution.py:449
  (15 other events, 52.9 us)

commit v12 on v11

--- a/solution.py
+++ b/solution.py
@@ -70,55 +70,54 @@
     )(*slots, *xs, w)
 
 
-def finish_kernel(turn_ref, terms, w_mine, w_other, *refs):
-    outs, w = refs[:-1], refs[-1]
-    half = w_mine.shape[0]
-    g = turn_ref[0]
-    w[pl.ds(pl.multiple_of(g * half, half), half), :] = w_mine[...]
-    w[pl.ds(pl.multiple_of((1 - g) * half, half), half), :] = w_other[...]
+def add_kernel(odd_ref, terms, even_out, odd_out):
     total = terms[0].astype(jnp.float32)
     for k in range(1, terms.shape[0]):
         total = total + terms[k].astype(jnp.float32)
-    features = total.astype(jnp.bfloat16)
-    projected = jnp.dot(features, w[...], preferred_element_type=jnp.float32)
-    projected = projected.astype(jnp.bfloat16)
-    n = features.shape[0] // len(outs)
-    for i, out in enumerate(outs):
-        out[0] = features[i * n : (i + 1) * n]
-        out[1] = projected[i * n : (i + 1) * n]
-
-
-def finish(turn, terms, w_halves, parts):
+    n = even_out.shape[0]
+    first, second = total[:n].astype(jnp.bfloat16), total[n:].astype(jnp.bfloat16)
+    odd = odd_ref[0] != 0
+    even_out[...] = jnp.where(odd, second, first)
+    odd_out[...] = jnp.where(odd, first, second)
+
+
+def add(odd, terms):
     _, rows, columns = terms.shape
-    wide = w_halves[0].shape[1]
-    part = jax.ShapeDtypeStruct((2, rows // parts, columns), jnp.bfloat16)
+    part = jax.ShapeDtypeStruct((rows // 2, columns), jnp.bfloat16)
     vmem = pl.BlockSpec(memory_space=pltpu.VMEM)
     return pl.pallas_call(
-        finish_kernel,
-        out_shape=(part,) * parts,
-        in_specs=[pl.BlockSpec(memory_space=pltpu.SMEM), vmem, vmem, vmem],
-        out_specs=(vmem,) * parts,
-        scratch_shapes=[pltpu.VMEM((columns, wide), jnp.bfloat16)],
+        add_kernel,
+        out_shape=(part, part),
+        in_specs=[pl.BlockSpec(memory_space=pltpu.SMEM), vmem],
+        out_specs=(vmem, vmem),
         cost_estimate=SHORT,
         compiler_params=pltpu.CompilerParams(vmem_limit_bytes=16 * 1024 * 1024),
-    )(turn, terms, *w_halves)
-
-
-def collect_kernel(block_ref, *refs):
-    for e, piece in enumerate(refs[:-1]):
-        refs[-1][e ^ block_ref[0]] = piece[0]
-
-
-def collect(block, pieces):
+    )(odd, terms)
+
+
+def project_kernel(block_ref, w, *refs):
+    planes = (len(refs) - 1) // 3
+    near, far, home, outs = refs[:planes], refs[planes : 2 * planes], refs[2 * planes], refs[-planes:]
+    for k in range(planes):
+        home[k ^ block_ref[0]] = near[k][...] + far[k][...]
+    for d in range(planes):
+        made = jnp.dot(home[d], w[...], preferred_element_type=jnp.float32)
+        outs[d][...] = made.astype(jnp.bfloat16)
+
+
+def project(block, w_proj, near, far):
+    planes = len(near)
+    rows, columns = near[0].shape
     vmem = pl.BlockSpec(memory_space=pltpu.VMEM)
+    made = jax.ShapeDtypeStruct((rows, w_proj.shape[1]), jnp.bfloat16)
     return pl.pallas_call(
-        collect_kernel,
-        out_shape=jax.ShapeDtypeStruct((len(pieces), *pieces[0].shape[1:]), jnp.bfloat16),
-        in_specs=[pl.BlockSpec(memory_space=pltpu.SMEM)] + [vmem] * len(pieces),
-        out_specs=vmem,
+        project_kernel,
+        out_shape=(jax.ShapeDtypeStruct((planes, rows, columns), jnp.bfloat16), *[made] * planes),
+        in_specs=[pl.BlockSpec(memory_space=pltpu.SMEM)] + [vmem] * (1 + 2 * planes),
+        out_specs=(vmem,) * (1 + planes),
         cost_estimate=SHORT,
         compiler_params=pltpu.CompilerParams(vmem_limit_bytes=16 * 1024 * 1024),
-    )(block, *pieces)
+    )(block, w_proj, *near, *far)
 
 
 def page_copies(len_ref, kv_hbm, kv_ref, sem, r):
@@ -133,7 +132,7 @@
 
 def talker_kernel(blocks, block_ref, len_ref, gain, *refs):
     w_hbm, refs = refs[:blocks], refs[blocks:]
-    terms, refs = refs[:blocks], refs[blocks:]
+    terms, refs = refs[:-10], refs[-10:]
     kv_hbm, new_kv, out_ref, kv_ref, sem, w_ref, w_sem, qkv, spreads, gathereds = refs
     rows, cached, kv_width = kv_ref.shape
     width = kv_width // 2
@@ -159,9 +158,9 @@
             else:
                 pl.when(needed)(copy.start)
 
-    total = terms[0][1].astype(jnp.float32)
+    total = terms[0][...].astype(jnp.float32)
     for term in terms[1:]:
-        total = total + term[1].astype(jnp.float32)
+        total = total + term[...].astype(jnp.float32)
     scale = lax.rsqrt(jnp.mean(total * total, axis=1, keepdims=True) + 1e-06)
     normed = (total * scale * gain[...]).astype(jnp.bfloat16)
     for e in range(blocks):
@@ -265,7 +264,7 @@
             context(at, *weighed[k], gathereds.at[k])
 
 
-def talker(block, pieces, talker_gain, weights, kv_len, kv_cache):
+def talker(block, terms, talker_gain, weights, kv_len, kv_cache):
     rows, cached, kv_width = kv_cache.shape
     wide, columns = weights[0].shape
     blocks = len(weights)
@@ -281,7 +280,7 @@
         ),
         in_specs=[smem, smem, vmem]
         + [pl.BlockSpec(memory_space=pl.ANY)] * blocks
-        + [vmem] * len(pieces)
+        + [vmem] * len(terms)
         + [pl.BlockSpec(memory_space=pl.ANY)],
         out_specs=(vmem, vmem),
         scratch_shapes=[
@@ -295,7 +294,7 @@
         ],
         cost_estimate=SHORT,
         compiler_params=pltpu.CompilerParams(vmem_limit_bytes=48 * 1024 * 1024),
-    )(block, kv_len, talker_gain.reshape(1, wide), *weights, *pieces, kv_cache)
+    )(block, kv_len, talker_gain.reshape(1, wide), *weights, *terms, kv_cache)
 
 
 def rms_norm(talker_in, talker_gain):
@@ -390,8 +389,17 @@
     return lax.ppermute(x, PLANE, [(b, b ^ e) for b in range(4)])
 
 
-def over_groups(x):
-    return lax.ppermute(x, "groups", [(0, 1), (1, 0)])
+def sent_home(even, odd, upper):
+    out = []
+    for k in range(4):
+        pairs = [
+            (p * 4 + c, c * 4 + (c ^ p ^ k))
+            for p in range(4)
+            for c in range(4)
+            if (p ^ k) // 2 == upper
+        ]
+        out.append(lax.ppermute(odd if k % 2 else even, GROUP, pairs))
+    return out
 
 
 def after(x, *others):
@@ -412,44 +420,33 @@
 ):
     planes = 4
     owned = kv_cache.shape[0]
-    g, m, c = lax.axis_index("groups"), lax.axis_index("mp"), lax.axis_index(PLANE)
-    block, turn = c.reshape(1), g.reshape(1)
+    m, c = lax.axis_index("mp"), lax.axis_index(PLANE)
+    block, odd = c.reshape(1), (m & 1).reshape(1)
     slots = talker_slot[0]
 
     across, peer = over_section(thinker_act), over_core(thinker_act)
-    peer_slots = over_core(talker_slot)
-    near = down([thinker_act, peer], [talker_slot, peer_slots], w_think, owned)
+    near = down([thinker_act, peer], [talker_slot, over_core(talker_slot)], w_think, owned)
     near_terms = lax.all_to_all(near, "mp", 0, 0)
     mine = jnp.concatenate([w_query, w_key, w_value], axis=1)
 
-    half = w_proj.shape[0] // 2
-    plane_w = lax.dynamic_slice_in_dim(after(w_proj, peer), g * half, half, axis=0)
-    two = lax.ppermute(plane_w, GROUP, [(b * 4 + b, (b ^ 2) * 4 + b) for b in range(4)])
-    one = lax.ppermute(plane_w, GROUP, [(b * 4 + b, (b ^ 1) * 4 + b) for b in range(4)])
-
-    across, near_terms, mine, plane_w, one, two = lax.optimization_barrier(
-        (across, near_terms, mine, plane_w, one, two)
-    )
+    across, near_terms, mine = lax.optimization_barrier((across, near_terms, mine))
     far_slots = [over_plane(talker_slot, e) for e in (2, 3)]
     far = down([across, over_core(across)], far_slots, w_think, owned)
     far_terms = lax.all_to_all(far, "mp", 0, 0)
-    three = lax.ppermute(two, GROUP, [((b ^ 2) * 4 + b, (b ^ 3) * 4 + b) for b in range(4)])
-    three = after(three, far)
-    mine_w = jnp.where(m == c ^ 1, one, jnp.where(m == c ^ 3, three, two))
-    mine_w = jnp.where(m == c, plane_w, mine_w)
-    block_w = (mine_w, over_groups(mine_w))
     other = over_section(after(mine, far))
 
-    own, next_core = finish(turn, after(near_terms, far), block_w, 2)
-    made, last = finish(turn, after(far_terms, own), block_w, 2)
-    pieces = [own, over_core(next_core), over_plane(made, 2), over_plane(last, 3)]
-    other = after(other, made)
+    near_home = sent_home(*add(odd, after(near_terms, far)), 0)
+    far_home = sent_home(*add(odd, after(far_terms, *near_home)), 1)
+    home, *projected = project(block, w_proj, near_home, far_home)
+    terms = projected[:1]
+    for d in range(1, planes):
+        terms.append(lax.ppermute(projected[d], "mp", [(p, p ^ d) for p in range(planes)]))
+    other = after(other, *far_home)
     weights = [mine, over_core(mine), other, over_core(other)]
-
-    home = lax.all_to_all(collect(block, pieces), "mp", 0, 0)
-    new_kv, ctx = talker(block, pieces, talker_gain, weights, kv_len, kv_cache)
-    home = after(home, ctx)
-    pick = (slots[:, None] == jnp.arange(planes * owned)[None, :]).astype(jnp.bfloat16)
+    new_kv, ctx = talker(block, terms, talker_gain, weights, kv_len, kv_cache)
+
+    place = (jnp.arange(planes)[:, None] ^ m) * owned + jnp.arange(owned)[None, :]
+    pick = (slots[:, None] == place.reshape(-1)[None, :]).astype(jnp.bfloat16)
     thinker_out = jnp.dot(
         pick, home.reshape(planes * owned, -1), preferred_element_type=jnp.float32
     )

time: 138 us -> 139 us (level)
  local copies, waits for them, and re-layouts: 9.35 us -> 13.9 us
  other arithmetic: 3.06 us -> 0.2 us
  starting transfers between devices: 39.1 us -> 41 us
  Pallas kernels: 32.8 us -> 31 us
    ppermute x4 -> x11, starting transfers between devices: 9.6 us -> 24.2 us  [the longest x8 19 us: sent_home(): out.append(lax.ppermute(odd if k % 2 else even, GROUP, pairs))]
    ppermute x4 -> x2, starting transfers between devices: 10.4 us -> 1.9 us  [over_plane(): return lax.ppermute(x, PLANE, [(b, b ^ e) for b in range(4)])]
    ppermute x2, waiting for transfers between devices: 14.8 us -> 22.5 us  [over_section(): return lax.ppermute(x, 'section', [(0, 1), (1, 0)])]
    ppermute x4 -> x2, waiting for transfers between devices: 10 us -> 2.91 us  [over_plane(): return lax.ppermute(x, PLANE, [(b, b ^ e) for b in range(4)])]
    unnamed x40 -> x52, local copies, waits for them, and re-layouts: 8.58 us -> 13.8 us
    all_to_all x1 -> x0, starting transfers between devices: 4.52 us -> none  [four_planes(): home = lax.all_to_all(collect(block, pieces), 'mp', 0, 0)]
    select_n x1 -> x0, other arithmetic: 1.61 us -> none  [four_planes(): mine_w = jnp.where(m == c, plane_w, mine_w)]
    pallas_call x3, Pallas kernels: 2.93 us -> 1.33 us  [the longest x1 1.12 us: project(): pl.pallas_call(project_kernel, out_shape=(jax.ShapeDtypeStruct((planes, r...]
  transfers between devices with their start and end apart: 19 -> 22, of which waited for: 9 -> 9; matrix products, arithmetic and copies ran while one was open for 3% -> 1% of each run, Pallas kernels for 24% -> 7%
where the time goes in v12:
time: 139 us; the launch traced here: 138 us
  waiting for transfers between devices  50 us (36%)
  starting transfers between devices  41 us (29%)
  Pallas kernels  31 us (22%)
  local copies, waits for them, and re-layouts  13.9 us (10%)
    ppermute x2, waiting for transfers between devices, over_section(): return lax.ppermute(x, 'section', [(0, 1), (1, 0)])  22.5 us
    ppermute x8, starting transfers between devices, sent_home(): out.append(lax.ppermute(odd if k % 2 else even, GROUP, pairs))  19 us
    ppermute x8, waiting for transfers between devices, sent_home(): out.append(lax.ppermute(odd if k % 2 else even, GROUP, pairs))  17.7 us
    pallas_call x2, Pallas kernels, down(): pl.pallas_call(functools.partial(down_kernel, owned, list(zip(ends[:-1],...  17.3 us
    unnamed x52, local copies, waits for them, and re-layouts  13.8 us
    pallas_call x1, Pallas kernels, talker(): pl.pallas_call(functools.partial(talker_kernel, blocks), out_shape=(jax.S...  12.4 us
    all_to_all x1, starting transfers between devices, four_planes(): near_terms = lax.all_to_all(near, 'mp', 0, 0)  6.06 us
    ppermute x3, waiting for transfers between devices, four_planes(): lax.ppermute(projected[d], 'mp', [(p, p ^ d) for p in range(planes)])  5.65 us
  transfers between devices with their start and end apart: 22, of which 9 were waited for; matrix products, arithmetic and copies ran while one was open for 1% of the time, Pallas kernels for 7%

profile of v12, /device:TPU:0, one launch (start us, length us, event | category | flops | bytes accessed | tf_op | source)
XLA Modules:
  0.0 138.1 jit_solution(12177197767039666414)
XLA Ops:
  1.2 2.6 %collective-permute-start = (bf16[192,4736]{1,0:T(8,128)(2,1)}, bf16[192,4736]{1,0:T(8,128)(2,1)}, u32[]{:S(2)}, u32[]{:S(2)}) collective-permute-start(bf16[192,4736]{1,0:T(8,128)(2,1)} %refs_2_.1), channel_id=1, source_target_pairs={{0,2},{2,0},{1,3},{3,1},{4,6},{6,4},{5,7},{7,5},{8,10},{10,8},{9,1... | collective-permute-start | bytes 5455880 | tf_op jit(solution)/shard_map/ppermute | solution.py:385
  3.9 1.2 collective-permute-done.1.refs_1_
  5.6 1.2 copy-done.17
  6.9 8.7 %shard_map.121 = bf16[4,96,896]{2,1,0:T(8,128)(2,1)} custom-call(s32[1,192]{1,0:T(1,128)} %refs_0_.1, s32[1,192]{1,0:T(1,128)} %copy-done.25, bf16[192,4736]{1,0:T(8,128)(2,1)} %refs_2_.1, bf16[192,4736]{1,0:T(8,128)(2,1)} %copy-done.17, bf16[4736,896]{1,0:T(8,128)(2,1)} %refs_4_.3), custom_call_target="tpu_custom_call" | custom-call | flops 1 | bytes 1 | tf_op jit(solution)/shard_map/pallas_call | solution.py:56
  15.6 6.1 %all-to-all-start = ((bf16[4,96,896]{2,1,0:T(8,128)(2,1)}), bf16[4,96,896]{2,1,0:T(8,128)(2,1)S(1)}, u32[]{:S(2)}, u32[]{:S(2)}) async-start(bf16[4,96,896]{2,1,0:T(8,128)(2,1)} %shard_map.121), calls=%async_computation | async-start | bytes 1376256 | tf_op jit(solution)/shard_map/all_to_all | solution.py:429
  21.8 22.5 %collective-permute-done.refs_2_ = bf16[192,4736]{1,0:T(8,128)(2,1)} collective-permute-done((bf16[192,4736]{1,0:T(8,128)(2,1)}, bf16[192,4736]{1,0:T(8,128)(2,1)}, u32[]{:S(2)}, u32[]{:S(2)}) %collective-permute-start) | collective-permute-done | bytes 1818656 | tf_op jit(solution)/shard_map/ppermute | solution.py:385
  44.3 1.8 %collective-permute-start.3 = (s32[1,192]{1,0:T(1,128)S(1)}, s32[1,192]{1,0:T(1,128)S(1)}, u32[]{:S(2)}, u32[]{:S(2)}) collective-permute-start(s32[1,192]{1,0:T(1,128)S(1)} %copy-done.22), channel_id=1, source_target_pairs={{0,2},{1,3},{2,0},{3,1},{4,6},{5,7},{6,4},{7,5},{8,10},{9,11},{10,... | collective-permute-start | bytes 2312 | tf_op jit(solution)/shard_map/ppermute | solution.py:389
  46.2 1.7 %collective-permute-done.3.refs_0_ = s32[1,192]{1,0:T(1,128)S(1)} collective-permute-done((s32[1,192]{1,0:T(1,128)S(1)}, s32[1,192]{1,0:T(1,128)S(1)}, u32[]{:S(2)}, u32[]{:S(2)}) %collective-permute-start.3) | collective-permute-done | bytes 800 | tf_op jit(solution)/shard_map/ppermute | solution.py:389
  48.0 1.2 collective-permute-done.4.refs_1_
  49.7 1.2 copy-done.16
  50.9 8.7 %shard_map.122 = bf16[4,96,896]{2,1,0:T(8,128)(2,1)} custom-call(s32[1,192]{1,0:T(1,128)} %copy-done.23, s32[1,192]{1,0:T(1,128)} %copy-done.24, bf16[192,4736]{1,0:T(8,128)(2,1)} %collective-permute-done.refs_2_, bf16[192,4736]{1,0:T(8,128)(2,1)} %copy-done.16, bf16[4736,896]{1,0:T(8,128)(2,1)} %refs_4_.3), custom_call_target="tpu_custom_call" | custom-call | flops 1 | bytes 1 | tf_op jit(solution)/shard_map/pallas_call | solution.py:56
  60.3 4.9 %all-to-all-start.1 = ((bf16[4,96,896]{2,1,0:T(8,128)(2,1)}), bf16[4,96,896]{2,1,0:T(8,128)(2,1)S(1)}, u32[]{:S(2)}, u32[]{:S(2)}) async-start(bf16[4,96,896]{2,1,0:T(8,128)(2,1)} %shard_map.122), calls=%async_computation.1 | async-start | bytes 1376256 | tf_op jit(solution)/shard_map/all_to_all | solution.py:435
  65.9 4.2 %collective-permute-start.7 = (bf16[48,896]{1,0:T(8,128)(2,1)S(1)}, bf16[48,896]{1,0:T(8,128)(2,1)S(1)}, u32[]{:S(2)}, u32[]{:S(2)}) collective-permute-start(bf16[48,896]{1,0:T(8,128)(2,1)S(1)} %get-tuple-element.25), channel_id=1, source_target_pairs={{0,1},{1,4},{2,11},{3,14},{4,0},{5,5},{6,10},{7,15},{16,17},{17,20... | collective-permute-start | bytes 258056 | tf_op jit(solution)/shard_map/ppermute | solution.py:401
  70.1 1.3 collective-permute-start.8
  71.4 1.3 collective-permute-start.9
  72.7 4.8 %collective-permute-done.7.refs_1_ = bf16[48,896]{1,0:T(8,128)(2,1)S(1)} collective-permute-done((bf16[48,896]{1,0:T(8,128)(2,1)S(1)}, bf16[48,896]{1,0:T(8,128)(2,1)S(1)}, u32[]{:S(2)}, u32[]{:S(2)}) %collective-permute-start.7) | collective-permute-done | bytes 86048 | tf_op jit(solution)/shard_map/ppermute | solution.py:401
  77.5 12.0 %collective-permute-done.8.refs_2_ = bf16[48,896]{1,0:T(8,128)(2,1)S(1)} collective-permute-done((bf16[48,896]{1,0:T(8,128)(2,1)S(1)}, bf16[48,896]{1,0:T(8,128)(2,1)S(1)}, u32[]{:S(2)}, u32[]{:S(2)}) %collective-permute-start.8) | collective-permute-done | bytes 86048 | tf_op jit(solution)/shard_map/ppermute | solution.py:401
  91.0 1.3 collective-permute-start.12
  92.3 9.0 %collective-permute-start.13 = (bf16[48,896]{1,0:T(8,128)(2,1)S(1)}, bf16[48,896]{1,0:T(8,128)(2,1)S(1)}, u32[]{:S(2)}, u32[]{:S(2)}) collective-permute-start(bf16[48,896]{1,0:T(8,128)(2,1)S(1)} %get-tuple-element.28), channel_id=1, source_target_pairs={{0,3},{1,6},{2,9},{3,12},{4,2},{5,7},{6,8},{7,13},{16,19},{17,22},... | collective-permute-start | bytes 258056 | tf_op jit(solution)/shard_map/ppermute | solution.py:401
  104.9 1.4 %copy-done = bf16[896,896]{1,0:T(8,128)(2,1)S(1)} copy-done((bf16[896,896]{1,0:T(8,128)(2,1)S(1)}, bf16[896,896]{1,0:T(8,128)(2,1)}, u32[]{:S(2)}) %copy-start) | copy-done | bytes 1605656
  114.0 4.7 %collective-permute-start.18 = (bf16[48,896]{1,0:T(8,128)(2,1)S(1)}, bf16[48,896]{1,0:T(8,128)(2,1)S(1)}, u32[]{:S(2)}, u32[]{:S(2)}) collective-permute-start(bf16[48,896]{1,0:T(8,128)(2,1)S(1)} %get-tuple-element.35), channel_id=1, source_target_pairs={{0,8},{4,12},{8,0},{12,4},{1,9},{5,13},{9,1},{13,5},{2,10},{6,14},... | collective-permute-start | bytes 258056 | tf_op jit(solution)/shard_map/ppermute | solution.py:443
  119.9 1.5 %collective-permute-done.18.refs_6_ = bf16[48,896]{1,0:T(8,128)(2,1)S(1)} collective-permute-done((bf16[48,896]{1,0:T(8,128)(2,1)S(1)}, bf16[48,896]{1,0:T(8,128)(2,1)S(1)}, u32[]{:S(2)}, u32[]{:S(2)}) %collective-permute-start.18) | collective-permute-done | bytes 86048 | tf_op jit(solution)/shard_map/ppermute | solution.py:443
  121.3 4.2 %collective-permute-done.19.refs_7_ = bf16[48,896]{1,0:T(8,128)(2,1)S(1)} collective-permute-done((bf16[48,896]{1,0:T(8,128)(2,1)S(1)}, bf16[48,896]{1,0:T(8,128)(2,1)S(1)}, u32[]{:S(2)}, u32[]{:S(2)}) %collective-permute-start.19) | collective-permute-done | bytes 86048 | tf_op jit(solution)/shard_map/ppermute | solution.py:443
  125.5 12.4 %shard_map.126 = (bf16[48,1024]{1,0:T(8,128)(2,1)}, f32[48,1536]{1,0:T(8,128)}) custom-call(s32[1]{0:T(128)} %bitcast.1.block_ref, s32[48]{0:T(128)S(1)} %copy-done.15, f32[1,896]{1,0:T(1,128)S(1)} %reshape.43.gain, bf16[896,640]{1,0:T(8,128)(2,1)S(1)} %pad_maximum_fusion.refs_0_, bf16[896,640]{1,0:T(8,128)(2,1)S(1)} %collective-permute-done.14.refs_1_, ...), custom_call_target="tpu_custom_call" | custom-call | flops 1 | bytes 1 | tf_op jit(solution)/shard_map/pallas_call | solution.py:275
  (84 shorter events, 17.3 us)
Async XLA Ops:
  0.7 4.4 %collective-permute-start.2 = (bf16[192,4736]{1,0:T(8,128)(2,1)}, bf16[192,4736]{1,0:T(8,128)(2,1)S(1)}, u32[]{:S(2)}, u32[]{:S(2)}) collective-permute-start(bf16[192,4736]{1,0:T(8,128)(2,1)} %refs_2_.1), channel_id=1, source_target_pairs={{0,1},{1,0},{2,3},{3,2},{4,5},{5,4},{6,7},{7,6},{8,9},{9,8},{10,11... | collective-permute-start | bytes 5455880 | tf_op jit(solution)/shard_map/ppermute | solution.py:381
  1.2 43.1 %collective-permute-start = (bf16[192,4736]{1,0:T(8,128)(2,1)}, bf16[192,4736]{1,0:T(8,128)(2,1)}, u32[]{:S(2)}, u32[]{:S(2)}) collective-permute-start(bf16[192,4736]{1,0:T(8,128)(2,1)} %refs_2_.1), channel_id=1, source_target_pairs={{0,2},{2,0},{1,3},{3,1},{4,6},{6,4},{5,7},{7,5},{8,10},{10,8},{9,1... | collective-permute-start | bytes 5455880 | tf_op jit(solution)/shard_map/ppermute | solution.py:385
  3.7 1.4 collective-permute-start.1
  15.6 28.7 %all-to-all-start = ((bf16[4,96,896]{2,1,0:T(8,128)(2,1)}), bf16[4,96,896]{2,1,0:T(8,128)(2,1)S(1)}, u32[]{:S(2)}, u32[]{:S(2)}) async-start(bf16[4,96,896]{2,1,0:T(8,128)(2,1)} %shard_map.121), calls=%async_computation | async-start | bytes 1376256 | tf_op jit(solution)/shard_map/all_to_all | solution.py:429
  44.3 4.8 %collective-permute-start.5 = (bf16[192,4736]{1,0:T(8,128)(2,1)}, bf16[192,4736]{1,0:T(8,128)(2,1)S(1)}, u32[]{:S(2)}, u32[]{:S(2)}) collective-permute-start(bf16[192,4736]{1,0:T(8,128)(2,1)} %collective-permute-done.refs_2_), channel_id=1, source_target_pairs={{0,1},{1,0},{2,3},{3,2},{4,5},{5,4},{6,7},{7,6},{8,9},{9,8},{10,11... | collective-permute-start | bytes 5455880 | tf_op jit(solution)/shard_map/ppermute | solution.py:381
  44.3 3.6 %collective-permute-start.3 = (s32[1,192]{1,0:T(1,128)S(1)}, s32[1,192]{1,0:T(1,128)S(1)}, u32[]{:S(2)}, u32[]{:S(2)}) collective-permute-start(s32[1,192]{1,0:T(1,128)S(1)} %copy-done.22), channel_id=1, source_target_pairs={{0,2},{1,3},{2,0},{3,1},{4,6},{5,7},{6,4},{7,5},{8,10},{9,11},{10,... | collective-permute-start | bytes 2312 | tf_op jit(solution)/shard_map/ppermute | solution.py:389
  46.1 3.0 %collective-permute-start.4 = (s32[1,192]{1,0:T(1,128)S(1)}, s32[1,192]{1,0:T(1,128)S(1)}, u32[]{:S(2)}, u32[]{:S(2)}) collective-permute-start(s32[1,192]{1,0:T(1,128)S(1)} %copy-done.22), channel_id=1, source_target_pairs={{0,3},{1,2},{2,1},{3,0},{4,7},{5,6},{6,5},{7,4},{8,11},{9,10},{10,... | collective-permute-start | bytes 2312 | tf_op jit(solution)/shard_map/ppermute | solution.py:389
  59.6 45.1 %copy-start.21 = (f32[896]{0:T(1024)S(1)}, f32[896]{0:T(1024)}, u32[]{:S(2)}) copy-start(f32[896]{0:T(1024)} %param.13) | copy-start | bytes 10756
  59.6 45.1 %collective-permute-start.15 = (bf16[896,640]{1,0:T(8,128)(2,1)S(1)}, bf16[896,640]{1,0:T(8,128)(2,1)}, u32[]{:S(2)}, u32[]{:S(2)}) collective-permute-start(bf16[896,640]{1,0:T(8,128)(2,1)S(1)} %pad_maximum_fusion.refs_0_), channel_id=1, source_target_pairs={{0,2},{2,0},{1,3},{3,1},{4,6},{6,4},{5,7},{7,5},{8,10},{10,8},{9,1... | collective-permute-start | bytes 3440648 | tf_op jit(solution)/shard_map/ppermute | solution.py:385
  60.3 29.3 %all-to-all-start.1 = ((bf16[4,96,896]{2,1,0:T(8,128)(2,1)}), bf16[4,96,896]{2,1,0:T(8,128)(2,1)S(1)}, u32[]{:S(2)}, u32[]{:S(2)}) async-start(bf16[4,96,896]{2,1,0:T(8,128)(2,1)} %shard_map.122), calls=%async_computation.1 | async-start | bytes 1376256 | tf_op jit(solution)/shard_map/all_to_all | solution.py:435
  65.2 7.5 %collective-permute-start.6 = (bf16[48,896]{1,0:T(8,128)(2,1)S(1)}, bf16[48,896]{1,0:T(8,128)(2,1)S(1)}, u32[]{:S(2)}, u32[]{:S(2)}) collective-permute-start(bf16[48,896]{1,0:T(8,128)(2,1)S(1)} %get-tuple-element.24), channel_id=1, source_target_pairs={{0,0},{1,5},{2,10},{3,15},{4,1},{5,4},{6,11},{7,14},{16,16},{17,21... | collective-permute-start | bytes 258056 | tf_op jit(solution)/shard_map/ppermute | solution.py:401
  65.9 59.6 %copy-start.15 = (s32[48]{0:T(128)S(1)}, s32[48]{0:T(128)}, u32[]{:S(2)}) copy-start(s32[48]{0:T(128)} %len_ref.1) | copy-start | bytes 580
  65.9 11.6 %collective-permute-start.7 = (bf16[48,896]{1,0:T(8,128)(2,1)S(1)}, bf16[48,896]{1,0:T(8,128)(2,1)S(1)}, u32[]{:S(2)}, u32[]{:S(2)}) collective-permute-start(bf16[48,896]{1,0:T(8,128)(2,1)S(1)} %get-tuple-element.25), channel_id=1, source_target_pairs={{0,1},{1,4},{2,11},{3,14},{4,0},{5,5},{6,10},{7,15},{16,17},{17,20... | collective-permute-start | bytes 258056 | tf_op jit(solution)/shard_map/ppermute | solution.py:401
  70.1 19.5 %collective-permute-start.8 = (bf16[48,896]{1,0:T(8,128)(2,1)S(1)}, bf16[48,896]{1,0:T(8,128)(2,1)S(1)}, u32[]{:S(2)}, u32[]{:S(2)}) collective-permute-start(bf16[48,896]{1,0:T(8,128)(2,1)S(1)} %get-tuple-element.24), channel_id=1, source_target_pairs={{8,0},{9,5},{10,10},{11,15},{12,1},{13,4},{14,11},{15,14},{24,16},... | collective-permute-start | bytes 258056 | tf_op jit(solution)/shard_map/ppermute | solution.py:401
  71.4 18.2 %collective-permute-start.9 = (bf16[48,896]{1,0:T(8,128)(2,1)S(1)}, bf16[48,896]{1,0:T(8,128)(2,1)S(1)}, u32[]{:S(2)}, u32[]{:S(2)}) collective-permute-start(bf16[48,896]{1,0:T(8,128)(2,1)S(1)} %get-tuple-element.25), channel_id=1, source_target_pairs={{8,1},{9,4},{10,11},{11,14},{12,0},{13,5},{14,10},{15,15},{24,17},... | collective-permute-start | bytes 258056 | tf_op jit(solution)/shard_map/ppermute | solution.py:401
  89.7 11.7 %collective-permute-start.10 = (bf16[48,896]{1,0:T(8,128)(2,1)S(1)}, bf16[48,896]{1,0:T(8,128)(2,1)S(1)}, u32[]{:S(2)}, u32[]{:S(2)}) collective-permute-start(bf16[48,896]{1,0:T(8,128)(2,1)S(1)} %get-tuple-element.27), channel_id=1, source_target_pairs={{8,2},{9,7},{10,8},{11,13},{12,3},{13,6},{14,9},{15,12},{24,18},{2... | collective-permute-start | bytes 258056 | tf_op jit(solution)/shard_map/ppermute | solution.py:401
  90.4 11.6 %collective-permute-start.11 = (bf16[48,896]{1,0:T(8,128)(2,1)S(1)}, bf16[48,896]{1,0:T(8,128)(2,1)S(1)}, u32[]{:S(2)}, u32[]{:S(2)}) collective-permute-start(bf16[48,896]{1,0:T(8,128)(2,1)S(1)} %get-tuple-element.28), channel_id=1, source_target_pairs={{8,3},{9,6},{10,9},{11,12},{12,2},{13,7},{14,8},{15,13},{24,19},{2... | collective-permute-start | bytes 258056 | tf_op jit(solution)/shard_map/ppermute | solution.py:401
  91.0 11.6 %collective-permute-start.12 = (bf16[48,896]{1,0:T(8,128)(2,1)S(1)}, bf16[48,896]{1,0:T(8,128)(2,1)S(1)}, u32[]{:S(2)}, u32[]{:S(2)}) collective-permute-start(bf16[48,896]{1,0:T(8,128)(2,1)S(1)} %get-tuple-element.27), channel_id=1, source_target_pairs={{0,2},{1,7},{2,8},{3,13},{4,3},{5,6},{6,9},{7,12},{16,18},{17,23},... | collective-permute-start | bytes 258056 | tf_op jit(solution)/shard_map/ppermute | solution.py:401
  92.3 11.7 %collective-permute-start.13 = (bf16[48,896]{1,0:T(8,128)(2,1)S(1)}, bf16[48,896]{1,0:T(8,128)(2,1)S(1)}, u32[]{:S(2)}, u32[]{:S(2)}) collective-permute-start(bf16[48,896]{1,0:T(8,128)(2,1)S(1)} %get-tuple-element.28), channel_id=1, source_target_pairs={{0,3},{1,6},{2,9},{3,12},{4,2},{5,7},{6,8},{7,13},{16,19},{17,22},... | collective-permute-start | bytes 258056 | tf_op jit(solution)/shard_map/ppermute | solution.py:401
  102.0 17.9 %collective-permute-start.14 = (bf16[896,640]{1,0:T(8,128)(2,1)S(1)}, bf16[896,640]{1,0:T(8,128)(2,1)S(1)}, u32[]{:S(2)}, u32[]{:S(2)}) collective-permute-start(bf16[896,640]{1,0:T(8,128)(2,1)S(1)} %pad_maximum_fusion.refs_0_), channel_id=1, source_target_pairs={{0,1},{1,0},{2,3},{3,2},{4,5},{5,4},{6,7},{7,6},{8,9},{9,8},{10,11... | collective-permute-start | bytes 3440648 | tf_op jit(solution)/shard_map/ppermute | solution.py:381
  104.7 20.9 %collective-permute-start.16 = (bf16[896,640]{1,0:T(8,128)(2,1)}, bf16[896,640]{1,0:T(8,128)(2,1)S(1)}, u32[]{:S(2)}, u32[]{:S(2)}) collective-permute-start(bf16[896,640]{1,0:T(8,128)(2,1)} %collective-permute-done.15.refs_2_), channel_id=1, source_target_pairs={{0,1},{1,0},{2,3},{3,2},{4,5},{5,4},{6,7},{7,6},{8,9},{9,8},{10,11... | collective-permute-start | bytes 3440648 | tf_op jit(solution)/shard_map/ppermute | solution.py:381
  113.7 6.2 %collective-permute-start.17 = (bf16[48,896]{1,0:T(8,128)(2,1)S(1)}, bf16[48,896]{1,0:T(8,128)(2,1)S(1)}, u32[]{:S(2)}, u32[]{:S(2)}) collective-permute-start(bf16[48,896]{1,0:T(8,128)(2,1)S(1)} %get-tuple-element.34), channel_id=1, source_target_pairs={{0,4},{4,0},{8,12},{12,8},{1,5},{5,1},{9,13},{13,9},{2,6},{6,2},{1... | collective-permute-start | bytes 258056 | tf_op jit(solution)/shard_map/ppermute | solution.py:443
  114.0 7.3 %collective-permute-start.18 = (bf16[48,896]{1,0:T(8,128)(2,1)S(1)}, bf16[48,896]{1,0:T(8,128)(2,1)S(1)}, u32[]{:S(2)}, u32[]{:S(2)}) collective-permute-start(bf16[48,896]{1,0:T(8,128)(2,1)S(1)} %get-tuple-element.35), channel_id=1, source_target_pairs={{0,8},{4,12},{8,0},{12,4},{1,9},{5,13},{9,1},{13,5},{2,10},{6,14},... | collective-permute-start | bytes 258056 | tf_op jit(solution)/shard_map/ppermute | solution.py:443
  118.7 6.9 %collective-permute-start.19 = (bf16[48,896]{1,0:T(8,128)(2,1)S(1)}, bf16[48,896]{1,0:T(8,128)(2,1)S(1)}, u32[]{:S(2)}, u32[]{:S(2)}) collective-permute-start(bf16[48,896]{1,0:T(8,128)(2,1)S(1)} %get-tuple-element.36), channel_id=1, source_target_pairs={{0,12},{4,8},{8,4},{12,0},{1,13},{5,9},{9,5},{13,1},{2,14},{6,10},... | collective-permute-start | bytes 258056 | tf_op jit(solution)/shard_map/ppermute | solution.py:443
  (24 other events, 139.2 us)

commit v13 on v12

--- a/solution.py
+++ b/solution.py
@@ -56,7 +56,7 @@
     return pl.pallas_call(
         functools.partial(down_kernel, owned, list(zip(ends[:-1], ends[1:])), groups),
         out_shape=jax.ShapeDtypeStruct((n // owned, groups * owned, columns), jnp.bfloat16),
-        in_specs=[vmem] * groups + [anywhere] * (groups + 1),
+        in_specs=[vmem] * groups + [anywhere] * (groups - 1) + [vmem, anywhere],
         out_specs=vmem,
         scratch_shapes=[
             pltpu.VMEM((groups * n, depth), jnp.bfloat16),
@@ -70,54 +70,92 @@
     )(*slots, *xs, w)
 
 
-def add_kernel(odd_ref, terms, even_out, odd_out):
+def add_kernel(terms, out):
     total = terms[0].astype(jnp.float32)
     for k in range(1, terms.shape[0]):
         total = total + terms[k].astype(jnp.float32)
-    n = even_out.shape[0]
-    first, second = total[:n].astype(jnp.bfloat16), total[n:].astype(jnp.bfloat16)
-    odd = odd_ref[0] != 0
-    even_out[...] = jnp.where(odd, second, first)
-    odd_out[...] = jnp.where(odd, first, second)
-
-
-def add(odd, terms):
-    _, rows, columns = terms.shape
-    part = jax.ShapeDtypeStruct((rows // 2, columns), jnp.bfloat16)
+    out[...] = total.astype(jnp.bfloat16)
+
+
+def add(terms):
     vmem = pl.BlockSpec(memory_space=pltpu.VMEM)
     return pl.pallas_call(
         add_kernel,
-        out_shape=(part, part),
-        in_specs=[pl.BlockSpec(memory_space=pltpu.SMEM), vmem],
-        out_specs=(vmem, vmem),
+        out_shape=jax.ShapeDtypeStruct(terms.shape[1:], jnp.bfloat16),
+        in_specs=[vmem],
+        out_specs=vmem,
         cost_estimate=SHORT,
         compiler_params=pltpu.CompilerParams(vmem_limit_bytes=16 * 1024 * 1024),
-    )(odd, terms)
-
-
-def project_kernel(block_ref, w, *refs):
-    planes = (len(refs) - 1) // 3
-    near, far, home, outs = refs[:planes], refs[planes : 2 * planes], refs[2 * planes], refs[-planes:]
-    for k in range(planes):
-        home[k ^ block_ref[0]] = near[k][...] + far[k][...]
+    )(terms)
+
+
+def add_and_deal_kernel(plane_ref, near, terms, *refs):
+    outs, sums = refs[:-1], refs[-1]
+    total = terms[0].astype(jnp.float32)
+    for k in range(1, terms.shape[0]):
+        total = total + terms[k].astype(jnp.float32)
+    rows = sums.shape[1]
+    half = len(outs) // 2
+    for e in range(half):
+        sums[e] = near[e * rows : (e + 1) * rows, :]
+        sums[half + e] = total[e * rows : (e + 1) * rows].astype(jnp.bfloat16)
+    for k, out in enumerate(outs):
+        out[...] = sums[plane_ref[0] ^ k]
+
+
+def add_and_deal(plane, near, terms):
+    rows, columns = near.shape
+    blocks = 4
+    part = jax.ShapeDtypeStruct((2 * rows // blocks, columns), jnp.bfloat16)
+    vmem = pl.BlockSpec(memory_space=pltpu.VMEM)
+    return pl.pallas_call(
+        add_and_deal_kernel,
+        out_shape=(part,) * blocks,
+        in_specs=[pl.BlockSpec(memory_space=pltpu.SMEM), vmem, vmem],
+        out_specs=(vmem,) * blocks,
+        scratch_shapes=[pltpu.VMEM((blocks, *part.shape), jnp.bfloat16)],
+        cost_estimate=SHORT,
+        compiler_params=pltpu.CompilerParams(vmem_limit_bytes=16 * 1024 * 1024),
+    )(plane, near, terms)
+
+
+def project_kernel(block_ref, w_hbm, *refs):
+    planes = (len(refs) - 4) // 2
+    came, home, outs = refs[:planes], refs[planes], refs[planes + 1 : 2 * planes + 1]
+    w, sem, w_sem = refs[-3:]
+    copies = [
+        pltpu.make_async_copy(came[k], home.at[k ^ block_ref[0]], sem.at[k])
+        for k in range(planes)
+    ]
+    copies.append(pltpu.make_async_copy(w_hbm, w, w_sem))
+    for copy in copies:
+        copy.start()
+    for copy in copies:
+        copy.wait()
     for d in range(planes):
         made = jnp.dot(home[d], w[...], preferred_element_type=jnp.float32)
         outs[d][...] = made.astype(jnp.bfloat16)
 
 
-def project(block, w_proj, near, far):
-    planes = len(near)
-    rows, columns = near[0].shape
+def project(block, w_proj, came):
+    planes = len(came)
+    rows, columns = came[0].shape
     vmem = pl.BlockSpec(memory_space=pltpu.VMEM)
     made = jax.ShapeDtypeStruct((rows, w_proj.shape[1]), jnp.bfloat16)
     return pl.pallas_call(
         project_kernel,
         out_shape=(jax.ShapeDtypeStruct((planes, rows, columns), jnp.bfloat16), *[made] * planes),
-        in_specs=[pl.BlockSpec(memory_space=pltpu.SMEM)] + [vmem] * (1 + 2 * planes),
+        in_specs=[pl.BlockSpec(memory_space=pltpu.SMEM)]
+        + [pl.BlockSpec(memory_space=pl.ANY)] * (1 + planes),
         out_specs=(vmem,) * (1 + planes),
+        scratch_shapes=[
+            pltpu.VMEM(w_proj.shape, w_proj.dtype),
+            pltpu.SemaphoreType.DMA((planes,)),
+            pltpu.SemaphoreType.DMA,
+        ],
         cost_estimate=SHORT,
         compiler_params=pltpu.CompilerParams(vmem_limit_bytes=16 * 1024 * 1024),
-    )(block, w_proj, *near, *far)
+    )(block, w_proj, *came)
 
 
 def page_copies(len_ref, kv_hbm, kv_ref, sem, r):
@@ -389,17 +427,8 @@
     return lax.ppermute(x, PLANE, [(b, b ^ e) for b in range(4)])
 
 
-def sent_home(even, odd, upper):
-    out = []
-    for k in range(4):
-        pairs = [
-            (p * 4 + c, c * 4 + (c ^ p ^ k))
-            for p in range(4)
-            for c in range(4)
-            if (p ^ k) // 2 == upper
-        ]
-        out.append(lax.ppermute(odd if k % 2 else even, GROUP, pairs))
-    return out
+def over_groups(x):
+    return lax.ppermute(x, "groups", [(0, 1), (1, 0)])
 
 
 def after(x, *others):
@@ -420,28 +449,43 @@
 ):
     planes = 4
     owned = kv_cache.shape[0]
-    m, c = lax.axis_index("mp"), lax.axis_index(PLANE)
-    block, odd = c.reshape(1), (m & 1).reshape(1)
+    g, m, c = lax.axis_index("groups"), lax.axis_index("mp"), lax.axis_index(PLANE)
+    block, plane = c.reshape(1), m.reshape(1)
     slots = talker_slot[0]
 
     across, peer = over_section(thinker_act), over_core(thinker_act)
-    near = down([thinker_act, peer], [talker_slot, over_core(talker_slot)], w_think, owned)
+    peer_slots = over_core(talker_slot)
+    far_slots = over_section(jnp.concatenate([talker_slot, peer_slots], axis=0))
+    near = down([thinker_act, peer], [talker_slot, peer_slots], w_think, owned)
     near_terms = lax.all_to_all(near, "mp", 0, 0)
     mine = jnp.concatenate([w_query, w_key, w_value], axis=1)
-
-    across, near_terms, mine = lax.optimization_barrier((across, near_terms, mine))
-    far_slots = [over_plane(talker_slot, e) for e in (2, 3)]
-    far = down([across, over_core(across)], far_slots, w_think, owned)
+    half = mine.shape[0] // 2
+    my_half = lax.dynamic_slice_in_dim(mine, g * half, half, axis=0)
+
+    across, near_terms, far_slots, mine, my_half = lax.optimization_barrier(
+        (across, near_terms, far_slots, mine, my_half)
+    )
+    far = down([across, over_core(across)], [far_slots[:1], far_slots[1:]], w_think, owned)
     far_terms = lax.all_to_all(far, "mp", 0, 0)
-    other = over_section(after(mine, far))
-
-    near_home = sent_home(*add(odd, after(near_terms, far)), 0)
-    far_home = sent_home(*add(odd, after(far_terms, *near_home)), 1)
-    home, *projected = project(block, w_proj, near_home, far_home)
+
+    my_half = over_section(after(my_half, far))
+    near_sums = add(after(near_terms, far))
+
+    dealt = add_and_deal(plane, near_sums, far_terms)
+    came = [
+        lax.ppermute(x, GROUP, [(p * 4 + b, b * 4 + (b ^ p ^ k)) for p in range(4) for b in range(4)])
+        for k, x in enumerate(dealt)
+    ]
+    my_half = after(my_half, near_sums)
+    came[0], other_half = lax.optimization_barrier((came[0], over_groups(my_half)))
+    home, *projected = project(block, w_proj, came)
     terms = projected[:1]
     for d in range(1, planes):
         terms.append(lax.ppermute(projected[d], "mp", [(p, p ^ d) for p in range(planes)]))
-    other = after(other, *far_home)
+    halves = [my_half, after(other_half, projected[0])]
+    other = jnp.concatenate(
+        [jnp.where(g == 0, *halves), jnp.where(g == 0, *halves[::-1])], axis=0
+    )
     weights = [mine, over_core(mine), other, over_core(other)]
     new_kv, ctx = talker(block, terms, talker_gain, weights, kv_len, kv_cache)
 

time: 139 us -> 131 us (0.942)
  local copies, waits for them, and re-layouts: 13.9 us -> 6.58 us
  starting transfers between devices: 41 us -> 34 us
  waiting for transfers between devices: 50 us -> 52.9 us
  other arithmetic: 0.2 us -> 1.72 us
    ppermute x10 -> x5, waiting for transfers between devices: 20.6 us -> 8.54 us  [the longest x4 8.54 us: four_planes(): lax.ppermute(x, GROUP, [(p * 4 + b, b * 4 + (b ^ p ^ k)) for p in range(4...]
    ppermute x10 -> x5, starting transfers between devices: 20.9 us -> 11.9 us  [the longest x4 10.1 us: four_planes(): lax.ppermute(x, GROUP, [(p * 4 + b, b * 4 + (b ^ p ^ k)) for p in range(4...]
    unnamed x52 -> x32, local copies, waits for them, and re-layouts: 13.8 us -> 5.82 us
    all_to_all x1, waiting for transfers between devices: 0.01 us -> 7.74 us  [four_planes(): far_terms = lax.all_to_all(far, 'mp', 0, 0)]
    ppermute x2 -> x3, waiting for transfers between devices: 22.5 us -> 28.2 us  [over_section(): return lax.ppermute(x, 'section', [(0, 1), (1, 0)])]
    ppermute x5, waiting for transfers between devices: 1.19 us -> 4.58 us  [over_core(): return lax.ppermute(x, 'rows', [(0, 1), (1, 0)])]
    ppermute x2 -> x3, starting transfers between devices: 3.21 us -> 5.94 us  [over_section(): return lax.ppermute(x, 'section', [(0, 1), (1, 0)])]
    ppermute x3, waiting for transfers between devices: 5.65 us -> 3.79 us  [four_planes(): lax.ppermute(projected[d], 'mp', [(p, p ^ d) for p in range(planes)])]
  transfers between devices with their start and end apart: 22 -> 18, of which waited for: 9 -> 8; matrix products, arithmetic and copies ran while one was open for 1% -> 4% of each run, Pallas kernels for 7% -> 8%
where the time goes in v13:
time: 131 us; the launch traced here: 130 us
  waiting for transfers between devices  52.9 us (40%)
  starting transfers between devices  34 us (26%)
  Pallas kernels  31.8 us (24%)
  local copies, waits for them, and re-layouts  6.58 us (5%)
  matrix products  2.01 us (2%)
  other arithmetic  1.72 us (1%)
    ppermute x3, waiting for transfers between devices, over_section(): return lax.ppermute(x, 'section', [(0, 1), (1, 0)])  28.2 us
    pallas_call x2, Pallas kernels, down(): pl.pallas_call(functools.partial(down_kernel, owned, list(zip(ends[:-1],...  17.9 us
    pallas_call x1, Pallas kernels, talker(): pl.pallas_call(functools.partial(talker_kernel, blocks), out_shape=(jax.S...  11.9 us
    ppermute x4, starting transfers between devices, four_planes(): lax.ppermute(x, GROUP, [(p * 4 + b, b * 4 + (b ^ p ^ k)) for p in range(4...  10.1 us
    ppermute x4, waiting for transfers between devices, four_planes(): lax.ppermute(x, GROUP, [(p * 4 + b, b * 4 + (b ^ p ^ k)) for p in range(4...  8.54 us
    all_to_all x1, waiting for transfers between devices, four_planes(): far_terms = lax.all_to_all(far, 'mp', 0, 0)  7.74 us
    all_to_all x1, starting transfers between devices, four_planes(): near_terms = lax.all_to_all(near, 'mp', 0, 0)  6.06 us
    ppermute x3, starting transfers between devices, over_section(): return lax.ppermute(x, 'section', [(0, 1), (1, 0)])  5.94 us
  transfers between devices with their start and end apart: 18, of which 8 were waited for; matrix products, arithmetic and copies ran while one was open for 4% of the time, Pallas kernels for 8%

profile of v13, /device:TPU:0, one launch (start us, length us, event | category | flops | bytes accessed | tf_op | source)
XLA Modules:
  0.0 130.1 jit_solution(5034803173784411401)
XLA Ops:
  1.1 2.6 %collective-permute-start = (bf16[192,4736]{1,0:T(8,128)(2,1)}, bf16[192,4736]{1,0:T(8,128)(2,1)}, u32[]{:S(2)}, u32[]{:S(2)}) collective-permute-start(bf16[192,4736]{1,0:T(8,128)(2,1)} %refs_2_.1), channel_id=1, source_target_pairs={{0,2},{2,0},{1,3},{3,1},{4,6},{6,4},{5,7},{7,5},{8,10},{10,8},{9,1... | collective-permute-start | bytes 5455880 | tf_op jit(solution)/shard_map/ppermute | solution.py:423
  6.8 9.0 %shard_map.121 = bf16[4,96,896]{2,1,0:T(8,128)(2,1)} custom-call(s32[1,192]{1,0:T(1,128)} %refs_0_.1, s32[1,192]{1,0:T(1,128)} %copy-done.13, bf16[192,4736]{1,0:T(8,128)(2,1)} %refs_2_.1, bf16[192,4736]{1,0:T(8,128)(2,1)} %copy-done.6, bf16[4736,896]{1,0:T(8,128)(2,1)} %refs_4_.3), custom_call_target="tpu_custom_call" | custom-call | flops 1 | bytes 1 | tf_op jit(solution)/shard_map/pallas_call | solution.py:56
  15.8 6.1 %all-to-all-start = ((bf16[4,96,896]{2,1,0:T(8,128)(2,1)}), bf16[4,96,896]{2,1,0:T(8,128)(2,1)S(1)}, u32[]{:S(2)}, u32[]{:S(2)}) async-start(bf16[4,96,896]{2,1,0:T(8,128)(2,1)} %shard_map.121), calls=%async_computation | async-start | bytes 1376256 | tf_op jit(solution)/shard_map/all_to_all | solution.py:460
  22.9 1.6 %collective-permute-start.3 = (s32[2,192]{1,0:T(2,128)S(1)}, s32[2,192]{1,0:T(2,128)S(1)}, u32[]{:S(2)}, u32[]{:S(2)}) collective-permute-start(s32[2,192]{1,0:T(2,128)S(1)} %pad_add_fusion), channel_id=1, source_target_pairs={{0,2},{2,0},{1,3},{3,1},{4,6},{6,4},{5,7},{7,5},{8,10},{10,8},{9,1... | collective-permute-start | bytes 4616 | tf_op jit(solution)/shard_map/ppermute | solution.py:423
  24.5 19.8 %collective-permute-done.3 = s32[2,192]{1,0:T(2,128)S(1)} collective-permute-done((s32[2,192]{1,0:T(2,128)S(1)}, s32[2,192]{1,0:T(2,128)S(1)}, u32[]{:S(2)}, u32[]{:S(2)}) %collective-permute-start.3) | collective-permute-done | bytes 1568 | tf_op jit(solution)/shard_map/ppermute | solution.py:423
  44.9 3.4 %collective-permute-done.4.refs_3_ = bf16[192,4736]{1,0:T(8,128)(2,1)S(1)} collective-permute-done((bf16[192,4736]{1,0:T(8,128)(2,1)}, bf16[192,4736]{1,0:T(8,128)(2,1)S(1)}, u32[]{:S(2)}, u32[]{:S(2)}) %collective-permute-start.4) | collective-permute-done | bytes 1818656 | tf_op jit(solution)/shard_map/ppermute | solution.py:419
  49.5 9.0 %shard_map.122 = bf16[4,96,896]{2,1,0:T(8,128)(2,1)} custom-call(s32[1,192]{1,0:T(1,128)} %get-tuple-element.50.refs_0_, s32[1,192]{1,0:T(1,128)} %get-tuple-element.49.refs_1_, bf16[192,4736]{1,0:T(8,128)(2,1)} %collective-permute-done.refs_2_, bf16[192,4736]{1,0:T(8,128)(2,1)} %copy-done.7, bf16[4736,896]{1,0:T(8,128)(2,1)} %refs_4_.3), custom_call_target="tpu_custom_call" | custom-call | flops 1 | bytes 1 | tf_op jit(solution)/shard_map/pallas_call | solution.py:56
  58.5 1.8 %collective-permute-start.6 = (bf16[448,640]{1,0:T(8,128)(2,1)S(1)}, bf16[448,640]{1,0:T(8,128)(2,1)}, u32[]{:S(2)}, u32[]{:S(2)}) collective-permute-start(bf16[448,640]{1,0:T(8,128)(2,1)S(1)} %constant_dynamic-slice_fusion), channel_id=1, source_target_pairs={{0,2},{2,0},{1,3},{3,1},{4,6},{6,4},{5,7},{7,5},{8,10},{10,8},{9,1... | collective-permute-start | bytes 1720328 | tf_op jit(solution)/shard_map/ppermute | solution.py:423
  60.3 4.9 %all-to-all-start.1 = ((bf16[4,96,896]{2,1,0:T(8,128)(2,1)}), bf16[4,96,896]{2,1,0:T(8,128)(2,1)S(1)}, u32[]{:S(2)}, u32[]{:S(2)}) async-start(bf16[4,96,896]{2,1,0:T(8,128)(2,1)} %shard_map.122), calls=%async_computation.1 | async-start | bytes 1376256 | tf_op jit(solution)/shard_map/all_to_all | solution.py:469
  65.2 8.4 %collective-permute-done.6 = bf16[448,640]{1,0:T(8,128)(2,1)} collective-permute-done((bf16[448,640]{1,0:T(8,128)(2,1)S(1)}, bf16[448,640]{1,0:T(8,128)(2,1)}, u32[]{:S(2)}, u32[]{:S(2)}) %collective-permute-start.6) | collective-permute-done | bytes 573472 | tf_op jit(solution)/shard_map/ppermute | solution.py:423
  73.7 1.8 %collective-permute-start.7 = (bf16[448,640]{1,0:T(8,128)(2,1)}, bf16[448,640]{1,0:T(8,128)(2,1)}, u32[]{:S(2)}, u32[]{:S(2)}) collective-permute-start(bf16[448,640]{1,0:T(8,128)(2,1)} %collective-permute-done.6), channel_id=1, source_target_pairs={{0,16},{16,0},{1,17},{17,1},{2,18},{18,2},{3,19},{19,3},{4,20},{20... | collective-permute-start | bytes 1720328 | tf_op jit(solution)/shard_map/ppermute | solution.py:431
  75.4 7.7 %all-to-all-done.1.terms = bf16[4,96,896]{2,1,0:T(8,128)(2,1)S(1)} async-done(((bf16[4,96,896]{2,1,0:T(8,128)(2,1)}), bf16[4,96,896]{2,1,0:T(8,128)(2,1)S(1)}, u32[]{:S(2)}, u32[]{:S(2)}) %all-to-all-start.1) | async-done | bytes 688160 | tf_op jit(solution)/shard_map/all_to_all | solution.py:469
  84.0 3.1 %collective-permute-start.10 = (bf16[48,896]{1,0:T(8,128)(2,1)S(1)}, bf16[48,896]{1,0:T(8,128)(2,1)S(1)}, u32[]{:S(2)}, u32[]{:S(2)}) collective-permute-start(bf16[48,896]{1,0:T(8,128)(2,1)S(1)} %get-tuple-element.36), channel_id=1, source_target_pairs={{0,3},{1,6},{2,9},{3,12},{4,2},{5,7},{6,8},{7,13},{8,1},{9,4},{10,... | collective-permute-start | bytes 258056 | tf_op jit(solution)/shard_map/ppermute | solution.py:476
  87.2 1.9 %collective-permute-start.8 = (bf16[48,896]{1,0:T(8,128)(2,1)S(1)}, bf16[48,896]{1,0:T(8,128)(2,1)S(1)}, u32[]{:S(2)}, u32[]{:S(2)}) collective-permute-start(bf16[48,896]{1,0:T(8,128)(2,1)S(1)} %get-tuple-element.34), channel_id=1, source_target_pairs={{0,1},{1,4},{2,11},{3,14},{4,0},{5,5},{6,10},{7,15},{8,3},{9,6},{1... | collective-permute-start | bytes 258056 | tf_op jit(solution)/shard_map/ppermute | solution.py:476
  89.1 4.4 %collective-permute-start.9 = (bf16[48,896]{1,0:T(8,128)(2,1)S(1)}, bf16[48,896]{1,0:T(8,128)(2,1)S(1)}, u32[]{:S(2)}, u32[]{:S(2)}) collective-permute-start(bf16[48,896]{1,0:T(8,128)(2,1)S(1)} %get-tuple-element.35), channel_id=1, source_target_pairs={{0,2},{1,7},{2,8},{3,13},{4,3},{5,6},{6,9},{7,12},{8,0},{9,5},{10,... | collective-permute-start | bytes 258056 | tf_op jit(solution)/shard_map/ppermute | solution.py:476
  93.6 2.1 %collective-permute-done.8.refs_1_ = bf16[48,896]{1,0:T(8,128)(2,1)S(1)} collective-permute-done((bf16[48,896]{1,0:T(8,128)(2,1)S(1)}, bf16[48,896]{1,0:T(8,128)(2,1)S(1)}, u32[]{:S(2)}, u32[]{:S(2)}) %collective-permute-start.8) | collective-permute-done | bytes 86048 | tf_op jit(solution)/shard_map/ppermute | solution.py:476
  95.7 6.4 %collective-permute-done.9.refs_2_ = bf16[48,896]{1,0:T(8,128)(2,1)S(1)} collective-permute-done((bf16[48,896]{1,0:T(8,128)(2,1)S(1)}, bf16[48,896]{1,0:T(8,128)(2,1)S(1)}, u32[]{:S(2)}, u32[]{:S(2)}) %collective-permute-start.9) | collective-permute-done | bytes 86048 | tf_op jit(solution)/shard_map/ppermute | solution.py:476
  102.2 1.4 %copy-done = bf16[896,896]{1,0:T(8,128)(2,1)S(1)} copy-done((bf16[896,896]{1,0:T(8,128)(2,1)S(1)}, bf16[896,896]{1,0:T(8,128)(2,1)}, u32[]{:S(2)}) %copy-start) | copy-done | bytes 1605656
  103.6 1.7 %shard_map.125 = (bf16[4,48,896]{2,1,0:T(8,128)(2,1)S(1)}, bf16[48,896]{1,0:T(8,128)(2,1)S(1)}, bf16[48,896]{1,0:T(8,128)(2,1)S(1)}, bf16[48,896]{1,0:T(8,128)(2,1)S(1)}, bf16[48,896]{1,0:T(8,128)(2,1)S(1)}) custom-call(s32[1]{0:T(128)} %bitcast.1.block_ref, bf16[896,896]{1,0:T(8,128)(2,1)S(1)} %copy-done, ...), custom_call_target="tpu_custom_call" | custom-call | flops 1 | bytes 1 | tf_op jit(solution)/shard_map/pallas_call | solution.py:145
  105.3 1.5 %broadcast_select_fusion.1 = (bf16[448,640]{1,0:T(8,128)(2,1)S(1)}, bf16[448,640]{1,0:T(8,128)(2,1)S(1)}) fusion(bf16[448,640]{1,0:T(8,128)(2,1)} %collective-permute-done.6, bf16[448,640]{1,0:T(8,128)(2,1)} %collective-permute-done.7, pred[]{:T(512)S(6)} %eq.23), kind=kLoop, calls=%fused_computation.3 | loop fusion | flops 573440 | bytes 2293761 | tf_op jit(solution)/shard_map/jit(_where)/select_n | solution.py:487
  109.0 3.2 %collective-permute-start.15 = (bf16[48,896]{1,0:T(8,128)(2,1)}, bf16[48,896]{1,0:T(8,128)(2,1)S(1)}, u32[]{:S(2)}, u32[]{:S(2)}) collective-permute-start(bf16[48,896]{1,0:T(8,128)(2,1)} %copy-done.3), channel_id=1, source_target_pairs={{0,12},{4,8},{8,4},{12,0},{1,13},{5,9},{9,5},{13,1},{2,14},{6,10},... | collective-permute-start | bytes 258056 | tf_op jit(solution)/shard_map/ppermute | solution.py:484
  112.1 2.0 %convolution_convert_fusion = bf16[192,896]{1,0:T(8,128)(2,1)} fusion(bf16[192,896]{1,0:T(8,128)(2,1)} %bitcast.5, s32[192]{0:T(256)S(1)} %add.29, s32[192]{0:T(256)S(1)} %bitcast.6), kind=kOutput, calls=%fused_computation | convolution fusion | flops 66269184 | bytes 689664 | tf_op jit(solution)/shard_map/dot_general | solution.py:494
  114.2 3.8 %collective-permute-done.14.refs_6_ = bf16[48,896]{1,0:T(8,128)(2,1)S(1)} collective-permute-done((bf16[48,896]{1,0:T(8,128)(2,1)}, bf16[48,896]{1,0:T(8,128)(2,1)S(1)}, u32[]{:S(2)}, u32[]{:S(2)}) %collective-permute-start.14) | collective-permute-done | bytes 86048 | tf_op jit(solution)/shard_map/ppermute | solution.py:484
  118.0 11.9 %shard_map.126 = (bf16[48,1024]{1,0:T(8,128)(2,1)}, f32[48,1536]{1,0:T(8,128)}) custom-call(s32[1]{0:T(128)} %bitcast.1.block_ref, s32[48]{0:T(128)S(1)} %copy-done.2, f32[1,896]{1,0:T(1,128)S(1)} %reshape.43.gain, bf16[896,640]{1,0:T(8,128)(2,1)S(1)} %constant_dynamic-update-slice_fusion.refs_0_, bf16[896,640]{1,0:T(8,128)(2,1)S(1)} %collective-permute-done.11.refs_1_, ...), custom_call_target="tpu_custom_call" | custom-call | flops 1 | bytes 1 | tf_op jit(solution)/shard_map/pallas_call | solution.py:313
  (61 shorter events, 9.5 us)
Async XLA Ops:
  0.6 4.4 %collective-permute-start.2 = (bf16[192,4736]{1,0:T(8,128)(2,1)}, bf16[192,4736]{1,0:T(8,128)(2,1)S(1)}, u32[]{:S(2)}, u32[]{:S(2)}) collective-permute-start(bf16[192,4736]{1,0:T(8,128)(2,1)} %refs_2_.1), channel_id=1, source_target_pairs={{0,1},{1,0},{2,3},{3,2},{4,5},{5,4},{6,7},{7,6},{8,9},{9,8},{10,11... | collective-permute-start | bytes 5455880 | tf_op jit(solution)/shard_map/ppermute | solution.py:419
  1.1 43.2 %collective-permute-start = (bf16[192,4736]{1,0:T(8,128)(2,1)}, bf16[192,4736]{1,0:T(8,128)(2,1)}, u32[]{:S(2)}, u32[]{:S(2)}) collective-permute-start(bf16[192,4736]{1,0:T(8,128)(2,1)} %refs_2_.1), channel_id=1, source_target_pairs={{0,2},{2,0},{1,3},{3,1},{4,6},{6,4},{5,7},{7,5},{8,10},{10,8},{9,1... | collective-permute-start | bytes 5455880 | tf_op jit(solution)/shard_map/ppermute | solution.py:423
  3.7 1.4 %collective-permute-start.1 = (s32[1,192]{1,0:T(1,128)}, s32[1,192]{1,0:T(1,128)S(1)}, u32[]{:S(2)}, u32[]{:S(2)}) collective-permute-start(s32[1,192]{1,0:T(1,128)} %refs_0_.1), channel_id=1, source_target_pairs={{0,1},{1,0},{2,3},{3,2},{4,5},{5,4},{6,7},{7,6},{8,9},{9,8},{10,11... | collective-permute-start | bytes 2312 | tf_op jit(solution)/shard_map/ppermute | solution.py:419
  15.8 6.1 %copy-start.8 = (bf16[896,384]{1,0:T(8,128)(2,1)S(1)}, bf16[896,384]{1,0:T(8,128)(2,1)}, u32[]{:S(2)}) copy-start(bf16[896,384]{1,0:T(8,128)(2,1)} %param.14) | copy-start | bytes 2064388
  15.8 6.2 %copy-start.9 = (bf16[896,128]{1,0:T(8,128)(2,1)S(1)}, bf16[896,128]{1,0:T(8,128)(2,1)}, u32[]{:S(2)}) copy-start(bf16[896,128]{1,0:T(8,128)(2,1)} %param.15) | copy-start | bytes 688132
  15.8 28.5 %all-to-all-start = ((bf16[4,96,896]{2,1,0:T(8,128)(2,1)}), bf16[4,96,896]{2,1,0:T(8,128)(2,1)S(1)}, u32[]{:S(2)}, u32[]{:S(2)}) async-start(bf16[4,96,896]{2,1,0:T(8,128)(2,1)} %shard_map.121), calls=%async_computation | async-start | bytes 1376256 | tf_op jit(solution)/shard_map/all_to_all | solution.py:460
  22.9 21.4 %collective-permute-start.3 = (s32[2,192]{1,0:T(2,128)S(1)}, s32[2,192]{1,0:T(2,128)S(1)}, u32[]{:S(2)}, u32[]{:S(2)}) collective-permute-start(s32[2,192]{1,0:T(2,128)S(1)} %pad_add_fusion), channel_id=1, source_target_pairs={{0,2},{2,0},{1,3},{3,1},{4,6},{6,4},{5,7},{7,5},{8,10},{10,8},{9,1... | collective-permute-start | bytes 4616 | tf_op jit(solution)/shard_map/ppermute | solution.py:423
  44.3 4.0 %collective-permute-start.4 = (bf16[192,4736]{1,0:T(8,128)(2,1)}, bf16[192,4736]{1,0:T(8,128)(2,1)S(1)}, u32[]{:S(2)}, u32[]{:S(2)}) collective-permute-start(bf16[192,4736]{1,0:T(8,128)(2,1)} %collective-permute-done.refs_2_), channel_id=1, source_target_pairs={{0,1},{1,0},{2,3},{3,2},{4,5},{5,4},{6,7},{7,6},{8,9},{9,8},{10,11... | collective-permute-start | bytes 5455880 | tf_op jit(solution)/shard_map/ppermute | solution.py:419
  58.5 15.2 %collective-permute-start.6 = (bf16[448,640]{1,0:T(8,128)(2,1)S(1)}, bf16[448,640]{1,0:T(8,128)(2,1)}, u32[]{:S(2)}, u32[]{:S(2)}) collective-permute-start(bf16[448,640]{1,0:T(8,128)(2,1)S(1)} %constant_dynamic-slice_fusion), channel_id=1, source_target_pairs={{0,2},{2,0},{1,3},{3,1},{4,6},{6,4},{5,7},{7,5},{8,10},{10,8},{9,1... | collective-permute-start | bytes 1720328 | tf_op jit(solution)/shard_map/ppermute | solution.py:423
  60.3 22.9 %all-to-all-start.1 = ((bf16[4,96,896]{2,1,0:T(8,128)(2,1)}), bf16[4,96,896]{2,1,0:T(8,128)(2,1)S(1)}, u32[]{:S(2)}, u32[]{:S(2)}) async-start(bf16[4,96,896]{2,1,0:T(8,128)(2,1)} %shard_map.122), calls=%async_computation.1 | async-start | bytes 1376256 | tf_op jit(solution)/shard_map/all_to_all | solution.py:469
  73.7 19.9 %collective-permute-start.7 = (bf16[448,640]{1,0:T(8,128)(2,1)}, bf16[448,640]{1,0:T(8,128)(2,1)}, u32[]{:S(2)}, u32[]{:S(2)}) collective-permute-start(bf16[448,640]{1,0:T(8,128)(2,1)} %collective-permute-done.6), channel_id=1, source_target_pairs={{0,16},{16,0},{1,17},{17,1},{2,18},{18,2},{3,19},{19,3},{4,20},{20... | collective-permute-start | bytes 1720328 | tf_op jit(solution)/shard_map/ppermute | solution.py:431
  83.4 10.1 %collective-permute-start.5 = (bf16[48,896]{1,0:T(8,128)(2,1)S(1)}, bf16[48,896]{1,0:T(8,128)(2,1)S(1)}, u32[]{:S(2)}, u32[]{:S(2)}) collective-permute-start(bf16[48,896]{1,0:T(8,128)(2,1)S(1)} %get-tuple-element.29), channel_id=1, source_target_pairs={{0,0},{1,5},{2,10},{3,15},{4,1},{5,4},{6,11},{7,14},{8,2},{9,7},{1... | collective-permute-start | bytes 258056 | tf_op jit(solution)/shard_map/ppermute | solution.py:476
  84.0 9.6 %collective-permute-start.10 = (bf16[48,896]{1,0:T(8,128)(2,1)S(1)}, bf16[48,896]{1,0:T(8,128)(2,1)S(1)}, u32[]{:S(2)}, u32[]{:S(2)}) collective-permute-start(bf16[48,896]{1,0:T(8,128)(2,1)S(1)} %get-tuple-element.36), channel_id=1, source_target_pairs={{0,3},{1,6},{2,9},{3,12},{4,2},{5,7},{6,8},{7,13},{8,1},{9,4},{10,... | collective-permute-start | bytes 258056 | tf_op jit(solution)/shard_map/ppermute | solution.py:476
  87.2 8.6 %collective-permute-start.8 = (bf16[48,896]{1,0:T(8,128)(2,1)S(1)}, bf16[48,896]{1,0:T(8,128)(2,1)S(1)}, u32[]{:S(2)}, u32[]{:S(2)}) collective-permute-start(bf16[48,896]{1,0:T(8,128)(2,1)S(1)} %get-tuple-element.34), channel_id=1, source_target_pairs={{0,1},{1,4},{2,11},{3,14},{4,0},{5,5},{6,10},{7,15},{8,3},{9,6},{1... | collective-permute-start | bytes 258056 | tf_op jit(solution)/shard_map/ppermute | solution.py:476
  89.1 13.1 %collective-permute-start.9 = (bf16[48,896]{1,0:T(8,128)(2,1)S(1)}, bf16[48,896]{1,0:T(8,128)(2,1)S(1)}, u32[]{:S(2)}, u32[]{:S(2)}) collective-permute-start(bf16[48,896]{1,0:T(8,128)(2,1)S(1)} %get-tuple-element.35), channel_id=1, source_target_pairs={{0,2},{1,7},{2,8},{3,13},{4,3},{5,6},{6,9},{7,12},{8,0},{9,5},{10,... | collective-permute-start | bytes 258056 | tf_op jit(solution)/shard_map/ppermute | solution.py:476
  93.5 20.6 %collective-permute-start.11 = (bf16[896,640]{1,0:T(8,128)(2,1)S(1)}, bf16[896,640]{1,0:T(8,128)(2,1)S(1)}, u32[]{:S(2)}, u32[]{:S(2)}) collective-permute-start(bf16[896,640]{1,0:T(8,128)(2,1)S(1)} %constant_dynamic-update-slice_fusion.refs_0_), channel_id=1, source_target_pairs={{0,1},{1,0},{2,3},{3,2},{4,5},{5,4},{6,7},{7,6},{8,9},{9,8},{10,11... | collective-permute-start | bytes 3440648 | tf_op jit(solution)/shard_map/ppermute | solution.py:419
  105.3 1.6 %copy-start.1 = (bf16[4,48,896]{2,1,0:T(8,128)(2,1)}, bf16[4,48,896]{2,1,0:T(8,128)(2,1)S(1)}, u32[]{:S(2)}) copy-start(bf16[4,48,896]{2,1,0:T(8,128)(2,1)S(1)} %get-tuple-element.37) | copy-start | bytes 1032196
  105.3 1.6 %copy-start.3 = (bf16[48,896]{1,0:T(8,128)(2,1)}, bf16[48,896]{1,0:T(8,128)(2,1)S(1)}, u32[]{:S(2)}) copy-start(bf16[48,896]{1,0:T(8,128)(2,1)S(1)} %get-tuple-element.44) | copy-start | bytes 258052
  105.3 1.6 %copy-start.4 = (bf16[48,896]{1,0:T(8,128)(2,1)}, bf16[48,896]{1,0:T(8,128)(2,1)S(1)}, u32[]{:S(2)}) copy-start(bf16[48,896]{1,0:T(8,128)(2,1)S(1)} %get-tuple-element.43) | copy-start | bytes 258052
  106.9 11.0 %copy-start.2 = (s32[48]{0:T(128)S(1)}, s32[48]{0:T(128)}, u32[]{:S(2)}) copy-start(s32[48]{0:T(128)} %len_ref.1) | copy-start | bytes 580
  107.0 10.9 %collective-permute-start.12 = (bf16[896,640]{1,0:T(8,128)(2,1)S(1)}, bf16[896,640]{1,0:T(8,128)(2,1)}, u32[]{:S(2)}, u32[]{:S(2)}) collective-permute-start(bf16[896,640]{1,0:T(8,128)(2,1)S(1)} %pad_maximum_fusion.refs_2_), channel_id=1, source_target_pairs={{0,1},{1,0},{2,3},{3,2},{4,5},{5,4},{6,7},{7,6},{8,9},{9,8},{10,11... | collective-permute-start | bytes 3440648 | tf_op jit(solution)/shard_map/ppermute | solution.py:419
  107.8 6.4 %collective-permute-start.13 = (bf16[48,896]{1,0:T(8,128)(2,1)}, bf16[48,896]{1,0:T(8,128)(2,1)S(1)}, u32[]{:S(2)}, u32[]{:S(2)}) collective-permute-start(bf16[48,896]{1,0:T(8,128)(2,1)} %copy-done.5), channel_id=1, source_target_pairs={{0,4},{4,0},{8,12},{12,8},{1,5},{5,1},{9,13},{13,9},{2,6},{6,2},{1... | collective-permute-start | bytes 258056 | tf_op jit(solution)/shard_map/ppermute | solution.py:484
  107.8 10.2 %collective-permute-start.14 = (bf16[48,896]{1,0:T(8,128)(2,1)}, bf16[48,896]{1,0:T(8,128)(2,1)S(1)}, u32[]{:S(2)}, u32[]{:S(2)}) collective-permute-start(bf16[48,896]{1,0:T(8,128)(2,1)} %copy-done.4), channel_id=1, source_target_pairs={{0,8},{4,12},{8,0},{12,4},{1,9},{5,13},{9,1},{13,5},{2,10},{6,14},... | collective-permute-start | bytes 258056 | tf_op jit(solution)/shard_map/ppermute | solution.py:484
  109.0 9.0 %collective-permute-start.15 = (bf16[48,896]{1,0:T(8,128)(2,1)}, bf16[48,896]{1,0:T(8,128)(2,1)S(1)}, u32[]{:S(2)}, u32[]{:S(2)}) collective-permute-start(bf16[48,896]{1,0:T(8,128)(2,1)} %copy-done.3), channel_id=1, source_target_pairs={{0,12},{4,8},{8,4},{12,0},{1,13},{5,9},{9,5},{13,1},{2,14},{6,10},... | collective-permute-start | bytes 258056 | tf_op jit(solution)/shard_map/ppermute | solution.py:484
  (9 other events, 9.6 us)

commit v14 on v12

--- a/solution.py
+++ b/solution.py
@@ -15,9 +15,8 @@
 MOST_VMEM = 56 * 1024 * 1024
 
 
-def down_kernel(owned, cuts, groups, *refs):
-    slots, xs, refs = refs[:groups], refs[groups : 2 * groups], refs[2 * groups :]
-    w, out, x_all, w_all, acc, x_sem, w_sem = refs
+def down_kernel(planes, cuts, groups, *refs):
+    xs, (w, out, x_all, w_all, acc, x_sem, w_sem) = refs[:groups], refs[groups:]
     n = xs[0].shape[0]
     loads = []
     for s, (lo, hi) in enumerate(cuts):
@@ -37,27 +36,23 @@
             copy.wait()
         part = jnp.dot(x_all[:, lo:hi], w_all[lo:hi, :], preferred_element_type=jnp.float32)
         acc[...] = part if s == 0 else acc[...] + part
-    place = lax.broadcasted_iota(jnp.int32, (n, n), 0)
+    part = n // planes
     for i in range(groups):
-        pick = (place == slots[i][...]).astype(jnp.float32).astype(jnp.bfloat16)
-        sums = acc[i * n : (i + 1) * n, :].astype(jnp.bfloat16)
-        ordered = jnp.dot(pick, sums, preferred_element_type=jnp.float32).astype(out.dtype)
-        for p in range(n // owned):
-            out[p, i * owned : (i + 1) * owned, :] = ordered[p * owned : (p + 1) * owned, :]
-
-
-def down(xs, slots, w, owned):
+        for p in range(planes):
+            at = i * n + p * part
+            out[p, i * part : (i + 1) * part, :] = acc[at : at + part, :].astype(out.dtype)
+
+
+def down(xs, w, planes):
     depth, columns = w.shape
     groups, n = len(xs), xs[0].shape[0]
     tiles, parts = depth // LANES, 6
     ends = [LANES * (tiles * i // parts) for i in range(parts)] + [depth]
-    anywhere = pl.BlockSpec(memory_space=pl.ANY)
-    vmem = pl.BlockSpec(memory_space=pltpu.VMEM)
     return pl.pallas_call(
-        functools.partial(down_kernel, owned, list(zip(ends[:-1], ends[1:])), groups),
-        out_shape=jax.ShapeDtypeStruct((n // owned, groups * owned, columns), jnp.bfloat16),
-        in_specs=[vmem] * groups + [anywhere] * (groups + 1),
-        out_specs=vmem,
+        functools.partial(down_kernel, planes, list(zip(ends[:-1], ends[1:])), groups),
+        out_shape=jax.ShapeDtypeStruct((planes, groups * n // planes, columns), jnp.bfloat16),
+        in_specs=[pl.BlockSpec(memory_space=pl.ANY)] * (groups + 1),
+        out_specs=pl.BlockSpec(memory_space=pltpu.VMEM),
         scratch_shapes=[
             pltpu.VMEM((groups * n, depth), jnp.bfloat16),
             pltpu.VMEM((depth, columns), jnp.bfloat16),
@@ -67,7 +62,7 @@
         ],
         cost_estimate=SHORT,
         compiler_params=pltpu.CompilerParams(vmem_limit_bytes=MOST_VMEM),
-    )(*slots, *xs, w)
+    )(*xs, w)
 
 
 def add_kernel(odd_ref, terms, even_out, odd_out):
@@ -95,29 +90,50 @@
     )(odd, terms)
 
 
-def project_kernel(block_ref, w, *refs):
-    planes = (len(refs) - 1) // 3
-    near, far, home, outs = refs[:planes], refs[planes : 2 * planes], refs[2 * planes], refs[-planes:]
-    for k in range(planes):
-        home[k ^ block_ref[0]] = near[k][...] + far[k][...]
+def project_kernel(planes, here_ref, slots, w_hbm, *refs):
+    came, refs = refs[: 2 * planes], refs[2 * planes :]
+    home, outs, (two, w, sem, w_sem) = refs[0], refs[1 : planes + 1], refs[planes + 1 :]
+    plane, block = here_ref[0], here_ref[1]
+    copies = [pltpu.make_async_copy(w_hbm, w, w_sem)]
+    for i in range(2 * planes):
+        to = two.at[i // planes, plane ^ block ^ (i % planes)]
+        copies.append(pltpu.make_async_copy(came[i], to, sem.at[i]))
+    for copy in copies:
+        copy.start()
+    for copy in copies:
+        copy.wait()
+    rows = two.shape[2]
+    home[...] = (two[0] + two[1]).reshape(home.shape)
+    n = home.shape[0]
+    place = lax.broadcasted_iota(jnp.int32, (n, n), 0)
+    place = ((place // rows) ^ plane) * rows + place % rows
+    pick = (place == slots[...]).astype(jnp.float32).astype(jnp.bfloat16)
+    ordered = jnp.dot(pick, home[...], preferred_element_type=jnp.float32).astype(jnp.bfloat16)
+    made = jnp.dot(ordered, w[...], preferred_element_type=jnp.float32).astype(jnp.bfloat16)
     for d in range(planes):
-        made = jnp.dot(home[d], w[...], preferred_element_type=jnp.float32)
-        outs[d][...] = made.astype(jnp.bfloat16)
-
-
-def project(block, w_proj, near, far):
+        outs[d][...] = made[d * rows : (d + 1) * rows]
+
+
+def project(here, slots, w_proj, near, far):
     planes = len(near)
     rows, columns = near[0].shape
     vmem = pl.BlockSpec(memory_space=pltpu.VMEM)
     made = jax.ShapeDtypeStruct((rows, w_proj.shape[1]), jnp.bfloat16)
     return pl.pallas_call(
-        project_kernel,
-        out_shape=(jax.ShapeDtypeStruct((planes, rows, columns), jnp.bfloat16), *[made] * planes),
-        in_specs=[pl.BlockSpec(memory_space=pltpu.SMEM)] + [vmem] * (1 + 2 * planes),
+        functools.partial(project_kernel, planes),
+        out_shape=(jax.ShapeDtypeStruct((planes * rows, columns), jnp.bfloat16), *[made] * planes),
+        in_specs=[pl.BlockSpec(memory_space=pltpu.SMEM), vmem]
+        + [pl.BlockSpec(memory_space=pl.ANY)] * (1 + 2 * planes),
         out_specs=(vmem,) * (1 + planes),
+        scratch_shapes=[
+            pltpu.VMEM((2, planes, rows, columns), jnp.bfloat16),
+            pltpu.VMEM(w_proj.shape, w_proj.dtype),
+            pltpu.SemaphoreType.DMA((2 * planes,)),
+            pltpu.SemaphoreType.DMA,
+        ],
         cost_estimate=SHORT,
         compiler_params=pltpu.CompilerParams(vmem_limit_bytes=16 * 1024 * 1024),
-    )(block, w_proj, *near, *far)
+    )(here, slots, w_proj, *near, *far)
 
 
 def page_copies(len_ref, kv_hbm, kv_ref, sem, r):
@@ -130,10 +146,11 @@
     return out
 
 
-def talker_kernel(blocks, block_ref, len_ref, gain, *refs):
-    w_hbm, refs = refs[:blocks], refs[blocks:]
-    terms, refs = refs[:-10], refs[-10:]
+def talker_kernel(here_ref, len_ref, gain, *refs):
+    w_hbm, terms, refs = refs[:6], refs[6:-10], refs[-10:]
     kv_hbm, new_kv, out_ref, kv_ref, sem, w_ref, w_sem, qkv, spreads, gathereds = refs
+    block, turn = here_ref[1], here_ref[2]
+    blocks = qkv.shape[0]
     rows, cached, kv_width = kv_ref.shape
     width = kv_width // 2
     page = cached // PAGES
@@ -144,11 +161,22 @@
     key, value = group * HEAD_DIM, (group + 1) * HEAD_DIM
     inv = 1.0 / HEAD_DIM**0.5
 
-    w_copies = [
-        pltpu.make_async_copy(w_hbm[e], w_ref.at[e], w_sem.at[e]) for e in range(blocks)
-    ]
-    for copy in w_copies:
-        copy.start()
+    half = w_ref.shape[1] // 2
+    w_parts = [(w_ref.at[0],), (w_ref.at[1],)]
+    for e in (2, 3):
+        w_parts.append(
+            [
+                w_ref.at[e, pl.ds(pl.multiple_of(which * half, half), half)]
+                for which in (turn, 1 - turn)
+            ]
+        )
+    w_copies, at = [], 0
+    for parts in w_parts:
+        w_copies.append([])
+        for part in parts:
+            w_copies[-1].append(pltpu.make_async_copy(w_hbm[at], part, w_sem.at[at]))
+            w_copies[-1][-1].start()
+            at += 1
 
     @pl.loop(0, rows)
     def _(r):
@@ -164,9 +192,10 @@
     scale = lax.rsqrt(jnp.mean(total * total, axis=1, keepdims=True) + 1e-06)
     normed = (total * scale * gain[...]).astype(jnp.bfloat16)
     for e in range(blocks):
-        w_copies[e].wait()
+        for copy in w_copies[e]:
+            copy.wait()
         made = jnp.dot(normed, w_ref[e], preferred_element_type=jnp.float32)
-        qkv[e ^ block_ref[0]] = made.astype(jnp.bfloat16).astype(jnp.float32)
+        qkv[e ^ block] = made.astype(jnp.bfloat16).astype(jnp.float32)
     for g in range(blocks):
         for place, start in ((g, key), (blocks + g, value)):
             new_kv[:, place * HEAD_DIM : (place + 1) * HEAD_DIM] = qkv[
@@ -264,22 +293,22 @@
             context(at, *weighed[k], gathereds.at[k])
 
 
-def talker(block, terms, talker_gain, weights, kv_len, kv_cache):
+def talker(here, terms, talker_gain, weights, kv_len, kv_cache):
     rows, cached, kv_width = kv_cache.shape
     wide, columns = weights[0].shape
-    blocks = len(weights)
+    blocks = 4
     q_width = blocks * columns - kv_width
     sets = 2
     vmem = pl.BlockSpec(memory_space=pltpu.VMEM)
     smem = pl.BlockSpec(memory_space=pltpu.SMEM)
     return pl.pallas_call(
-        functools.partial(talker_kernel, blocks),
+        talker_kernel,
         out_shape=(
             jax.ShapeDtypeStruct((rows, kv_width), jnp.bfloat16),
             jax.ShapeDtypeStruct((rows, q_width), jnp.float32),
         ),
         in_specs=[smem, smem, vmem]
-        + [pl.BlockSpec(memory_space=pl.ANY)] * blocks
+        + [pl.BlockSpec(memory_space=pl.ANY)] * len(weights)
         + [vmem] * len(terms)
         + [pl.BlockSpec(memory_space=pl.ANY)],
         out_specs=(vmem, vmem),
@@ -287,14 +316,14 @@
             pltpu.VMEM((rows, cached, kv_width), jnp.bfloat16),
             pltpu.SemaphoreType.DMA((rows, PAGES)),
             pltpu.VMEM((blocks, wide, columns), jnp.bfloat16),
-            pltpu.SemaphoreType.DMA((blocks,)),
+            pltpu.SemaphoreType.DMA((len(weights),)),
             pltpu.VMEM((blocks, rows, columns), jnp.float32),
             pltpu.VMEM((sets, LANES, HEAD_DIM), jnp.float32),
             pltpu.VMEM((sets, LANES, HEAD_DIM), jnp.float32),
         ],
         cost_estimate=SHORT,
         compiler_params=pltpu.CompilerParams(vmem_limit_bytes=48 * 1024 * 1024),
-    )(block, kv_len, talker_gain.reshape(1, wide), *weights, *terms, kv_cache)
+    )(here, kv_len, talker_gain.reshape(1, wide), *weights, *terms, kv_cache)
 
 
 def rms_norm(talker_in, talker_gain):
@@ -389,6 +418,10 @@
     return lax.ppermute(x, PLANE, [(b, b ^ e) for b in range(4)])
 
 
+def over_groups(x):
+    return lax.ppermute(x, "groups", [(0, 1), (1, 0)])
+
+
 def sent_home(even, odd, upper):
     out = []
     for k in range(4):
@@ -419,38 +452,36 @@
     kv_cache,
 ):
     planes = 4
-    owned = kv_cache.shape[0]
-    m, c = lax.axis_index("mp"), lax.axis_index(PLANE)
-    block, odd = c.reshape(1), (m & 1).reshape(1)
-    slots = talker_slot[0]
+    g, m, c = lax.axis_index("groups"), lax.axis_index("mp"), lax.axis_index(PLANE)
+    here, odd = jnp.stack([m, c, g]), (m & 1).reshape(1)
 
     across, peer = over_section(thinker_act), over_core(thinker_act)
-    near = down([thinker_act, peer], [talker_slot, over_core(talker_slot)], w_think, owned)
-    near_terms = lax.all_to_all(near, "mp", 0, 0)
+    near = down([thinker_act, peer], w_think, planes)
+    near_even, near_odd = add(odd, lax.all_to_all(near, "mp", 0, 0))
     mine = jnp.concatenate([w_query, w_key, w_value], axis=1)
-
-    across, near_terms, mine = lax.optimization_barrier((across, near_terms, mine))
-    far_slots = [over_plane(talker_slot, e) for e in (2, 3)]
-    far = down([across, over_core(across)], far_slots, w_think, owned)
-    far_terms = lax.all_to_all(far, "mp", 0, 0)
-    other = over_section(after(mine, far))
-
-    near_home = sent_home(*add(odd, after(near_terms, far)), 0)
-    far_home = sent_home(*add(odd, after(far_terms, *near_home)), 1)
-    home, *projected = project(block, w_proj, near_home, far_home)
+    half = mine.shape[0] // 2
+    my_half = lax.dynamic_slice_in_dim(mine, g * half, half, axis=0)
+
+    across, near_even, near_odd, mine, my_half = lax.optimization_barrier(
+        (across, near_even, near_odd, mine, my_half)
+    )
+    near_home = sent_home(near_even, near_odd, 0)
+    across, other, *near_home = lax.optimization_barrier((across, over_core(across), *near_home))
+    far = down([across, other], w_think, planes)
+    far_even, far_odd = add(odd, lax.all_to_all(far, "mp", 0, 0))
+
+    my_half = over_section(after(my_half, far))
+    other_half = over_groups(my_half)
+
+    far_home = sent_home(far_even, far_odd, 1)
+    slots, other_half = lax.optimization_barrier((talker_slot, other_half))
+    thinker_out, *projected = project(here, slots, w_proj, near_home, far_home)
     terms = projected[:1]
     for d in range(1, planes):
         terms.append(lax.ppermute(projected[d], "mp", [(p, p ^ d) for p in range(planes)]))
-    other = after(other, *far_home)
-    weights = [mine, over_core(mine), other, over_core(other)]
-    new_kv, ctx = talker(block, terms, talker_gain, weights, kv_len, kv_cache)
-
-    place = (jnp.arange(planes)[:, None] ^ m) * owned + jnp.arange(owned)[None, :]
-    pick = (slots[:, None] == place.reshape(-1)[None, :]).astype(jnp.bfloat16)
-    thinker_out = jnp.dot(
-        pick, home.reshape(planes * owned, -1), preferred_element_type=jnp.float32
-    )
-    return (thinker_out.astype(jnp.bfloat16), new_kv, ctx)
+    weights = [mine, over_core(mine), my_half, other_half, over_core(my_half), over_core(other_half)]
+    new_kv, ctx = talker(here, terms, talker_gain, weights, kv_len, kv_cache)
+    return (thinker_out, new_kv, ctx)
 
 
 def solution(mesh):

time: 139 us -> 149 us (1.072)
  waiting for transfers between devices: 50 us -> 64.2 us
  local copies, waits for them, and re-layouts: 13.9 us -> 7.01 us
  starting transfers between devices: 41 us -> 44.5 us
    all_to_all x2, waiting for transfers between devices: 0.01 us -> 16.4 us  [the longest x1 16.4 us: four_planes(): near_even, near_odd = add(odd, lax.all_to_all(near, 'mp', 0, 0))]
    ppermute x2 -> x1, waiting for transfers between devices: 2.91 us -> 13.3 us  [over_groups(): return lax.ppermute(x, 'groups', [(0, 1), (1, 0)])]
    unnamed x52 -> x32, local copies, waits for them, and re-layouts: 13.8 us -> 6.08 us
    ppermute x8, waiting for transfers between devices: 17.7 us -> 10.3 us  [sent_home(): out.append(lax.ppermute(odd if k % 2 else even, GROUP, pairs))]
    ppermute x2, waiting for transfers between devices: 22.5 us -> 17.3 us  [over_section(): return lax.ppermute(x, 'section', [(0, 1), (1, 0)])]
    ppermute x8, starting transfers between devices: 19 us -> 21.7 us  [sent_home(): out.append(lax.ppermute(odd if k % 2 else even, GROUP, pairs))]
    ppermute x3, starting transfers between devices: 5.19 us -> 7.08 us  [four_planes(): lax.ppermute(projected[d], 'mp', [(p, p ^ d) for p in range(planes)])]
  transfers between devices with their start and end apart: 22 -> 21, of which waited for: 9 -> 9; matrix products, arithmetic and copies ran while one was open for 1% -> 1% of each run, Pallas kernels for 7% -> 7%
where the time goes in v14:
time: 149 us; the launch traced here: 148 us
  waiting for transfers between devices  64.2 us (43%)
  starting transfers between devices  44.5 us (30%)
  Pallas kernels  31.3 us (21%)
  local copies, waits for them, and re-layouts  7.01 us (5%)
    ppermute x8, starting transfers between devices, sent_home(): out.append(lax.ppermute(odd if k % 2 else even, GROUP, pairs))  21.7 us
    ppermute x2, waiting for transfers between devices, over_section(): return lax.ppermute(x, 'section', [(0, 1), (1, 0)])  17.3 us
    all_to_all x1, waiting for transfers between devices, four_planes(): near_even, near_odd = add(odd, lax.all_to_all(near, 'mp', 0, 0))  16.4 us
    pallas_call x2, Pallas kernels, down(): pl.pallas_call(functools.partial(down_kernel, planes, list(zip(ends[:-1],...  15.4 us
    ppermute x1, waiting for transfers between devices, over_groups(): return lax.ppermute(x, 'groups', [(0, 1), (1, 0)])  13.3 us
    pallas_call x1, Pallas kernels, talker(): pl.pallas_call(talker_kernel, out_shape=(jax.ShapeDtypeStruct((rows, kv_w...  12.4 us
    ppermute x8, waiting for transfers between devices, sent_home(): out.append(lax.ppermute(odd if k % 2 else even, GROUP, pairs))  10.3 us
    ppermute x3, starting transfers between devices, four_planes(): lax.ppermute(projected[d], 'mp', [(p, p ^ d) for p in range(planes)])  7.08 us
  transfers between devices with their start and end apart: 21, of which 9 were waited for; matrix products, arithmetic and copies ran while one was open for 1% of the time, Pallas kernels for 7%

profile of v14, /device:TPU:0, one launch (start us, length us, event | category | flops | bytes accessed | tf_op | source)
XLA Modules:
  0.0 148.1 jit_solution(13353784347761931054)
XLA Ops:
  1.1 2.6 %collective-permute-start = (bf16[192,4736]{1,0:T(8,128)(2,1)}, bf16[192,4736]{1,0:T(8,128)(2,1)}, u32[]{:S(2)}, u32[]{:S(2)}) collective-permute-start(bf16[192,4736]{1,0:T(8,128)(2,1)} %refs_0_.1), channel_id=1, source_target_pairs={{0,2},{2,0},{1,3},{3,1},{4,6},{6,4},{5,7},{7,5},{8,10},{10,8},{9,1... | collective-permute-start | bytes 5455880 | tf_op jit(solution)/shard_map/ppermute | solution.py:414
  6.0 7.7 %shard_map.121 = bf16[4,96,896]{2,1,0:T(8,128)(2,1)} custom-call(bf16[192,4736]{1,0:T(8,128)(2,1)} %refs_0_.1, bf16[192,4736]{1,0:T(8,128)(2,1)} %copy-done.10, bf16[4736,896]{1,0:T(8,128)(2,1)} %refs_2_.3), custom_call_target="tpu_custom_call" | custom-call | flops 1 | bytes 1 | tf_op jit(solution)/shard_map/pallas_call | solution.py:51
  13.7 6.4 %all-to-all-start = ((bf16[4,96,896]{2,1,0:T(8,128)(2,1)}), bf16[4,96,896]{2,1,0:T(8,128)(2,1)S(1)}, u32[]{:S(2)}, u32[]{:S(2)}) async-start(bf16[4,96,896]{2,1,0:T(8,128)(2,1)} %shard_map.121), calls=%async_computation | async-start | bytes 1376256 | tf_op jit(solution)/shard_map/all_to_all | solution.py:460
  22.0 16.4 %all-to-all-done.terms = bf16[4,96,896]{2,1,0:T(8,128)(2,1)S(1)} async-done(((bf16[4,96,896]{2,1,0:T(8,128)(2,1)}), bf16[4,96,896]{2,1,0:T(8,128)(2,1)S(1)}, u32[]{:S(2)}, u32[]{:S(2)}) %all-to-all-start) | async-done | bytes 688160 | tf_op jit(solution)/shard_map/all_to_all | solution.py:460
  38.5 5.8 %collective-permute-done.refs_0_ = bf16[192,4736]{1,0:T(8,128)(2,1)} collective-permute-done((bf16[192,4736]{1,0:T(8,128)(2,1)}, bf16[192,4736]{1,0:T(8,128)(2,1)}, u32[]{:S(2)}, u32[]{:S(2)}) %collective-permute-start) | collective-permute-done | bytes 1818656 | tf_op jit(solution)/shard_map/ppermute | solution.py:414
  44.9 5.2 %collective-permute-start.4 = (bf16[48,896]{1,0:T(8,128)(2,1)S(1)}, bf16[48,896]{1,0:T(8,128)(2,1)S(1)}, u32[]{:S(2)}, u32[]{:S(2)}) collective-permute-start(bf16[48,896]{1,0:T(8,128)(2,1)S(1)} %get-tuple-element.33), channel_id=1, source_target_pairs={{0,1},{1,4},{2,11},{3,14},{4,0},{5,5},{6,10},{7,15},{16,17},{17,20... | collective-permute-start | bytes 258056 | tf_op jit(solution)/shard_map/ppermute | solution.py:434
  50.2 1.3 collective-permute-start.5
  51.5 1.3 collective-permute-start.6
  52.8 8.2 %collective-permute-done.5.refs_2_ = bf16[48,896]{1,0:T(8,128)(2,1)S(1)} collective-permute-done((bf16[48,896]{1,0:T(8,128)(2,1)S(1)}, bf16[48,896]{1,0:T(8,128)(2,1)S(1)}, u32[]{:S(2)}, u32[]{:S(2)}) %collective-permute-start.5) | collective-permute-done | bytes 86048 | tf_op jit(solution)/shard_map/ppermute | solution.py:434
  61.0 1.2 copy-done.9
  62.3 7.7 %shard_map.123 = bf16[4,96,896]{2,1,0:T(8,128)(2,1)} custom-call(bf16[192,4736]{1,0:T(8,128)(2,1)} %collective-permute-done.refs_0_, bf16[192,4736]{1,0:T(8,128)(2,1)} %copy-done.9, bf16[4736,896]{1,0:T(8,128)(2,1)} %refs_2_.3), custom_call_target="tpu_custom_call" | custom-call | flops 1 | bytes 1 | tf_op jit(solution)/shard_map/pallas_call | solution.py:51
  70.1 3.6 %all-to-all-start.1 = ((bf16[4,96,896]{2,1,0:T(8,128)(2,1)}), bf16[4,96,896]{2,1,0:T(8,128)(2,1)S(1)}, u32[]{:S(2)}, u32[]{:S(2)}) async-start(bf16[4,96,896]{2,1,0:T(8,128)(2,1)} %shard_map.123), calls=%async_computation.1 | async-start | bytes 1376256 | tf_op jit(solution)/shard_map/all_to_all | solution.py:471
  74.6 11.5 %collective-permute-done.7.refs_2_ = bf16[448,640]{1,0:T(8,128)(2,1)} collective-permute-done((bf16[448,640]{1,0:T(8,128)(2,1)}, bf16[448,640]{1,0:T(8,128)(2,1)}, u32[]{:S(2)}, u32[]{:S(2)}) %collective-permute-start.7) | collective-permute-done | bytes 573472 | tf_op jit(solution)/shard_map/ppermute | solution.py:414
  86.0 1.8 %collective-permute-start.8 = (bf16[448,640]{1,0:T(8,128)(2,1)}, bf16[448,640]{1,0:T(8,128)(2,1)}, u32[]{:S(2)}, u32[]{:S(2)}) collective-permute-start(bf16[448,640]{1,0:T(8,128)(2,1)} %collective-permute-done.7.refs_2_), channel_id=1, source_target_pairs={{0,16},{16,0},{1,17},{17,1},{2,18},{18,2},{3,19},{19,3},{4,20},{20... | collective-permute-start | bytes 1720328 | tf_op jit(solution)/shard_map/ppermute | solution.py:422
  87.8 13.3 %collective-permute-done.8.refs_3_ = bf16[448,640]{1,0:T(8,128)(2,1)} collective-permute-done((bf16[448,640]{1,0:T(8,128)(2,1)}, bf16[448,640]{1,0:T(8,128)(2,1)}, u32[]{:S(2)}, u32[]{:S(2)}) %collective-permute-start.8) | collective-permute-done | bytes 573472 | tf_op jit(solution)/shard_map/ppermute | solution.py:422
  103.3 9.4 %collective-permute-start.11 = (bf16[48,896]{1,0:T(8,128)(2,1)}, bf16[48,896]{1,0:T(8,128)(2,1)S(1)}, u32[]{:S(2)}, u32[]{:S(2)}) collective-permute-start(bf16[48,896]{1,0:T(8,128)(2,1)} %get-tuple-element.42), channel_id=1, source_target_pairs={{0,2},{1,7},{2,8},{3,13},{4,3},{5,6},{6,9},{7,12},{16,18},{17,23},... | collective-permute-start | bytes 258056 | tf_op jit(solution)/shard_map/ppermute | solution.py:434
  112.7 2.5 %collective-permute-start.12 = (bf16[48,896]{1,0:T(8,128)(2,1)}, bf16[48,896]{1,0:T(8,128)(2,1)S(1)}, u32[]{:S(2)}, u32[]{:S(2)}) collective-permute-start(bf16[48,896]{1,0:T(8,128)(2,1)} %get-tuple-element.43), channel_id=1, source_target_pairs={{0,3},{1,6},{2,9},{3,12},{4,2},{5,7},{6,8},{7,13},{16,19},{17,22},... | collective-permute-start | bytes 258056 | tf_op jit(solution)/shard_map/ppermute | solution.py:434
  115.3 2.1 %collective-permute-done.12.refs_7_ = bf16[48,896]{1,0:T(8,128)(2,1)S(1)} collective-permute-done((bf16[48,896]{1,0:T(8,128)(2,1)}, bf16[48,896]{1,0:T(8,128)(2,1)S(1)}, u32[]{:S(2)}, u32[]{:S(2)}) %collective-permute-start.12) | collective-permute-done | bytes 86048 | tf_op jit(solution)/shard_map/ppermute | solution.py:434
  120.1 2.5 %shard_map.125 = (bf16[192,896]{1,0:T(8,128)(2,1)}, bf16[48,896]{1,0:T(8,128)(2,1)S(1)}, bf16[48,896]{1,0:T(8,128)(2,1)S(1)}, bf16[48,896]{1,0:T(8,128)(2,1)S(1)}, bf16[48,896]{1,0:T(8,128)(2,1)S(1)}) custom-call(s32[3]{0:T(128)S(1)} %pad_add_fusion.here_ref, s32[1,192]{1,0:T(1,128)S(1)} %copy-done.7, bf16[896,896]{1,0:T(8,128)(2,1)S(1)} %copy-done, ...), custom_call_target="tpu_custom_call" | custom-call | flops 1 | bytes 1 | tf_op jit(solution)/shard_map/pallas_call | solution.py:122
  122.6 2.1 %collective-permute-start.16 = (bf16[48,896]{1,0:T(8,128)(2,1)S(1)}, bf16[48,896]{1,0:T(8,128)(2,1)S(1)}, u32[]{:S(2)}, u32[]{:S(2)}) collective-permute-start(bf16[48,896]{1,0:T(8,128)(2,1)S(1)} %get-tuple-element.48), channel_id=1, source_target_pairs={{0,4},{4,0},{8,12},{12,8},{1,5},{5,1},{9,13},{13,9},{2,6},{6,2},{1... | collective-permute-start | bytes 258056 | tf_op jit(solution)/shard_map/ppermute | solution.py:481
  124.7 4.5 %collective-permute-start.17 = (bf16[48,896]{1,0:T(8,128)(2,1)S(1)}, bf16[48,896]{1,0:T(8,128)(2,1)S(1)}, u32[]{:S(2)}, u32[]{:S(2)}) collective-permute-start(bf16[48,896]{1,0:T(8,128)(2,1)S(1)} %get-tuple-element.49), channel_id=1, source_target_pairs={{0,8},{4,12},{8,0},{12,4},{1,9},{5,13},{9,1},{13,5},{2,10},{6,14},... | collective-permute-start | bytes 258056 | tf_op jit(solution)/shard_map/ppermute | solution.py:481
  129.7 3.5 %collective-permute-done.17.refs_8_ = bf16[48,896]{1,0:T(8,128)(2,1)S(1)} collective-permute-done((bf16[48,896]{1,0:T(8,128)(2,1)S(1)}, bf16[48,896]{1,0:T(8,128)(2,1)S(1)}, u32[]{:S(2)}, u32[]{:S(2)}) %collective-permute-start.17) | collective-permute-done | bytes 86048 | tf_op jit(solution)/shard_map/ppermute | solution.py:481
  133.3 2.2 %collective-permute-done.18.refs_9_ = bf16[48,896]{1,0:T(8,128)(2,1)S(1)} collective-permute-done((bf16[48,896]{1,0:T(8,128)(2,1)S(1)}, bf16[48,896]{1,0:T(8,128)(2,1)S(1)}, u32[]{:S(2)}, u32[]{:S(2)}) %collective-permute-start.18) | collective-permute-done | bytes 86048 | tf_op jit(solution)/shard_map/ppermute | solution.py:481
  135.5 12.4 %shard_map.126 = (bf16[48,1024]{1,0:T(8,128)(2,1)}, f32[48,1536]{1,0:T(8,128)}) custom-call(s32[3]{0:T(128)S(1)} %pad_add_fusion.here_ref, s32[48]{0:T(128)S(1)} %copy-done.8, f32[1,896]{1,0:T(1,128)S(1)} %reshape.13.gain, bf16[896,640]{1,0:T(8,128)(2,1)S(1)} %constant_dynamic-update-slice_fusion.refs_0_, bf16[896,640]{1,0:T(8,128)(2,1)} %collective-permute-done.13.refs_1_, ...), custom_call_target="tpu_custom_call" | custom-call | flops 1 | bytes 1 | tf_op jit(solution)/shard_map/pallas_call | solution.py:304
  (60 shorter events, 11.6 us)
Async XLA Ops:
  0.6 4.1 %collective-permute-start.1 = (bf16[192,4736]{1,0:T(8,128)(2,1)}, bf16[192,4736]{1,0:T(8,128)(2,1)S(1)}, u32[]{:S(2)}, u32[]{:S(2)}) collective-permute-start(bf16[192,4736]{1,0:T(8,128)(2,1)} %refs_0_.1), channel_id=1, source_target_pairs={{0,1},{1,0},{2,3},{3,2},{4,5},{5,4},{6,7},{7,6},{8,9},{9,8},{10,11... | collective-permute-start | bytes 5455880 | tf_op jit(solution)/shard_map/ppermute | solution.py:410
  1.1 43.1 %collective-permute-start = (bf16[192,4736]{1,0:T(8,128)(2,1)}, bf16[192,4736]{1,0:T(8,128)(2,1)}, u32[]{:S(2)}, u32[]{:S(2)}) collective-permute-start(bf16[192,4736]{1,0:T(8,128)(2,1)} %refs_0_.1), channel_id=1, source_target_pairs={{0,2},{2,0},{1,3},{3,1},{4,6},{6,4},{5,7},{7,5},{8,10},{10,8},{9,1... | collective-permute-start | bytes 5455880 | tf_op jit(solution)/shard_map/ppermute | solution.py:414
  13.7 24.7 %all-to-all-start = ((bf16[4,96,896]{2,1,0:T(8,128)(2,1)}), bf16[4,96,896]{2,1,0:T(8,128)(2,1)S(1)}, u32[]{:S(2)}, u32[]{:S(2)}) async-start(bf16[4,96,896]{2,1,0:T(8,128)(2,1)} %shard_map.121), calls=%async_computation | async-start | bytes 1376256 | tf_op jit(solution)/shard_map/all_to_all | solution.py:460
  44.3 16.7 %collective-permute-start.2 = (bf16[192,4736]{1,0:T(8,128)(2,1)}, bf16[192,4736]{1,0:T(8,128)(2,1)S(1)}, u32[]{:S(2)}, u32[]{:S(2)}) collective-permute-start(bf16[192,4736]{1,0:T(8,128)(2,1)} %collective-permute-done.refs_0_), channel_id=1, source_target_pairs={{0,1},{1,0},{2,3},{3,2},{4,5},{5,4},{6,7},{7,6},{8,9},{9,8},{10,11... | collective-permute-start | bytes 5455880 | tf_op jit(solution)/shard_map/ppermute | solution.py:410
  44.3 8.5 %collective-permute-start.3 = (bf16[48,896]{1,0:T(8,128)(2,1)S(1)}, bf16[48,896]{1,0:T(8,128)(2,1)S(1)}, u32[]{:S(2)}, u32[]{:S(2)}) collective-permute-start(bf16[48,896]{1,0:T(8,128)(2,1)S(1)} %get-tuple-element.32), channel_id=1, source_target_pairs={{0,0},{1,5},{2,10},{3,15},{4,1},{5,4},{6,11},{7,14},{16,16},{17,21... | collective-permute-start | bytes 258056 | tf_op jit(solution)/shard_map/ppermute | solution.py:434
  44.9 7.8 %collective-permute-start.4 = (bf16[48,896]{1,0:T(8,128)(2,1)S(1)}, bf16[48,896]{1,0:T(8,128)(2,1)S(1)}, u32[]{:S(2)}, u32[]{:S(2)}) collective-permute-start(bf16[48,896]{1,0:T(8,128)(2,1)S(1)} %get-tuple-element.33), channel_id=1, source_target_pairs={{0,1},{1,4},{2,11},{3,14},{4,0},{5,5},{6,10},{7,15},{16,17},{17,20... | collective-permute-start | bytes 258056 | tf_op jit(solution)/shard_map/ppermute | solution.py:434
  50.2 10.8 %collective-permute-start.5 = (bf16[48,896]{1,0:T(8,128)(2,1)S(1)}, bf16[48,896]{1,0:T(8,128)(2,1)S(1)}, u32[]{:S(2)}, u32[]{:S(2)}) collective-permute-start(bf16[48,896]{1,0:T(8,128)(2,1)S(1)} %get-tuple-element.32), channel_id=1, source_target_pairs={{8,0},{9,5},{10,10},{11,15},{12,1},{13,4},{14,11},{15,14},{24,16},... | collective-permute-start | bytes 258056 | tf_op jit(solution)/shard_map/ppermute | solution.py:434
  51.5 9.5 %collective-permute-start.6 = (bf16[48,896]{1,0:T(8,128)(2,1)S(1)}, bf16[48,896]{1,0:T(8,128)(2,1)S(1)}, u32[]{:S(2)}, u32[]{:S(2)}) collective-permute-start(bf16[48,896]{1,0:T(8,128)(2,1)S(1)} %get-tuple-element.33), channel_id=1, source_target_pairs={{8,1},{9,4},{10,11},{11,14},{12,0},{13,5},{14,10},{15,15},{24,17},... | collective-permute-start | bytes 258056 | tf_op jit(solution)/shard_map/ppermute | solution.py:434
  70.0 47.4 %copy-start = (bf16[896,896]{1,0:T(8,128)(2,1)S(1)}, bf16[896,896]{1,0:T(8,128)(2,1)}, u32[]{:S(2)}) copy-start(bf16[896,896]{1,0:T(8,128)(2,1)} %w_hbm.1) | copy-start | bytes 4816900
  70.0 47.4 %copy-start.7 = (s32[1,192]{1,0:T(1,128)S(1)}, s32[1,192]{1,0:T(1,128)}, u32[]{:S(2)}) copy-start(s32[1,192]{1,0:T(1,128)} %slots) | copy-start | bytes 2308
  70.1 16.0 %collective-permute-start.7 = (bf16[448,640]{1,0:T(8,128)(2,1)}, bf16[448,640]{1,0:T(8,128)(2,1)}, u32[]{:S(2)}, u32[]{:S(2)}) collective-permute-start(bf16[448,640]{1,0:T(8,128)(2,1)} %constant_dynamic-slice_fusion), channel_id=1, source_target_pairs={{0,2},{2,0},{1,3},{3,1},{4,6},{6,4},{5,7},{7,5},{8,10},{10,8},{9,1... | collective-permute-start | bytes 1720328 | tf_op jit(solution)/shard_map/ppermute | solution.py:414
  70.1 31.0 %all-to-all-start.1 = ((bf16[4,96,896]{2,1,0:T(8,128)(2,1)}), bf16[4,96,896]{2,1,0:T(8,128)(2,1)S(1)}, u32[]{:S(2)}, u32[]{:S(2)}) async-start(bf16[4,96,896]{2,1,0:T(8,128)(2,1)} %shard_map.123), calls=%async_computation.1 | async-start | bytes 1376256 | tf_op jit(solution)/shard_map/all_to_all | solution.py:471
  73.8 55.5 %collective-permute-start.13 = (bf16[896,640]{1,0:T(8,128)(2,1)S(1)}, bf16[896,640]{1,0:T(8,128)(2,1)}, u32[]{:S(2)}, u32[]{:S(2)}) collective-permute-start(bf16[896,640]{1,0:T(8,128)(2,1)S(1)} %constant_dynamic-update-slice_fusion.refs_0_), channel_id=1, source_target_pairs={{0,1},{1,0},{2,3},{3,2},{4,5},{5,4},{6,7},{7,6},{8,9},{9,8},{10,11... | collective-permute-start | bytes 3440648 | tf_op jit(solution)/shard_map/ppermute | solution.py:410
  86.0 15.1 %collective-permute-start.8 = (bf16[448,640]{1,0:T(8,128)(2,1)}, bf16[448,640]{1,0:T(8,128)(2,1)}, u32[]{:S(2)}, u32[]{:S(2)}) collective-permute-start(bf16[448,640]{1,0:T(8,128)(2,1)} %collective-permute-done.7.refs_2_), channel_id=1, source_target_pairs={{0,16},{16,0},{1,17},{17,1},{2,18},{18,2},{3,19},{19,3},{4,20},{20... | collective-permute-start | bytes 1720328 | tf_op jit(solution)/shard_map/ppermute | solution.py:422
  87.8 41.9 %collective-permute-start.14 = (bf16[448,640]{1,0:T(8,128)(2,1)}, bf16[448,640]{1,0:T(8,128)(2,1)}, u32[]{:S(2)}, u32[]{:S(2)}) collective-permute-start(bf16[448,640]{1,0:T(8,128)(2,1)} %collective-permute-done.7.refs_2_), channel_id=1, source_target_pairs={{0,1},{1,0},{2,3},{3,2},{4,5},{5,4},{6,7},{7,6},{8,9},{9,8},{10,11... | collective-permute-start | bytes 1720328 | tf_op jit(solution)/shard_map/ppermute | solution.py:410
  101.1 34.4 %collective-permute-start.15 = (bf16[448,640]{1,0:T(8,128)(2,1)}, bf16[448,640]{1,0:T(8,128)(2,1)}, u32[]{:S(2)}, u32[]{:S(2)}) collective-permute-start(bf16[448,640]{1,0:T(8,128)(2,1)} %collective-permute-done.8.refs_3_), channel_id=1, source_target_pairs={{0,1},{1,0},{2,3},{3,2},{4,5},{5,4},{6,7},{7,6},{8,9},{9,8},{10,11... | collective-permute-start | bytes 1720328 | tf_op jit(solution)/shard_map/ppermute | solution.py:410
  101.9 1.3 collective-permute-start.9
  102.6 10.1 %collective-permute-start.10 = (bf16[48,896]{1,0:T(8,128)(2,1)}, bf16[48,896]{1,0:T(8,128)(2,1)S(1)}, u32[]{:S(2)}, u32[]{:S(2)}) collective-permute-start(bf16[48,896]{1,0:T(8,128)(2,1)} %get-tuple-element.43), channel_id=1, source_target_pairs={{8,3},{9,6},{10,9},{11,12},{12,2},{13,7},{14,8},{15,13},{24,19},{2... | collective-permute-start | bytes 258056 | tf_op jit(solution)/shard_map/ppermute | solution.py:434
  103.3 12.0 %collective-permute-start.11 = (bf16[48,896]{1,0:T(8,128)(2,1)}, bf16[48,896]{1,0:T(8,128)(2,1)S(1)}, u32[]{:S(2)}, u32[]{:S(2)}) collective-permute-start(bf16[48,896]{1,0:T(8,128)(2,1)} %get-tuple-element.42), channel_id=1, source_target_pairs={{0,2},{1,7},{2,8},{3,13},{4,3},{5,6},{6,9},{7,12},{16,18},{17,23},... | collective-permute-start | bytes 258056 | tf_op jit(solution)/shard_map/ppermute | solution.py:434
  112.7 4.8 %collective-permute-start.12 = (bf16[48,896]{1,0:T(8,128)(2,1)}, bf16[48,896]{1,0:T(8,128)(2,1)S(1)}, u32[]{:S(2)}, u32[]{:S(2)}) collective-permute-start(bf16[48,896]{1,0:T(8,128)(2,1)} %get-tuple-element.43), channel_id=1, source_target_pairs={{0,3},{1,6},{2,9},{3,12},{4,2},{5,7},{6,8},{7,13},{16,19},{17,22},... | collective-permute-start | bytes 258056 | tf_op jit(solution)/shard_map/ppermute | solution.py:434
  115.2 20.3 %copy-start.8 = (s32[48]{0:T(128)S(1)}, s32[48]{0:T(128)}, u32[]{:S(2)}) copy-start(s32[48]{0:T(128)} %len_ref.1) | copy-start | bytes 580
  122.6 7.1 %collective-permute-start.16 = (bf16[48,896]{1,0:T(8,128)(2,1)S(1)}, bf16[48,896]{1,0:T(8,128)(2,1)S(1)}, u32[]{:S(2)}, u32[]{:S(2)}) collective-permute-start(bf16[48,896]{1,0:T(8,128)(2,1)S(1)} %get-tuple-element.48), channel_id=1, source_target_pairs={{0,4},{4,0},{8,12},{12,8},{1,5},{5,1},{9,13},{13,9},{2,6},{6,2},{1... | collective-permute-start | bytes 258056 | tf_op jit(solution)/shard_map/ppermute | solution.py:481
  124.7 8.6 %collective-permute-start.17 = (bf16[48,896]{1,0:T(8,128)(2,1)S(1)}, bf16[48,896]{1,0:T(8,128)(2,1)S(1)}, u32[]{:S(2)}, u32[]{:S(2)}) collective-permute-start(bf16[48,896]{1,0:T(8,128)(2,1)S(1)} %get-tuple-element.49), channel_id=1, source_target_pairs={{0,8},{4,12},{8,0},{12,4},{1,9},{5,13},{9,1},{13,5},{2,10},{6,14},... | collective-permute-start | bytes 258056 | tf_op jit(solution)/shard_map/ppermute | solution.py:481
  129.2 6.3 %collective-permute-start.18 = (bf16[48,896]{1,0:T(8,128)(2,1)S(1)}, bf16[48,896]{1,0:T(8,128)(2,1)S(1)}, u32[]{:S(2)}, u32[]{:S(2)}) collective-permute-start(bf16[48,896]{1,0:T(8,128)(2,1)S(1)} %get-tuple-element.50), channel_id=1, source_target_pairs={{0,12},{4,8},{8,4},{12,0},{1,13},{5,9},{9,5},{13,1},{2,14},{6,10},... | collective-permute-start | bytes 258056 | tf_op jit(solution)/shard_map/ppermute | solution.py:481
  (12 other events, 63.8 us)

commit v15 on v14

--- a/solution.py
+++ b/solution.py
@@ -12,7 +12,10 @@
 LANES = 128
 PAGES = 2
 SHORT = pl.CostEstimate(flops=1, bytes_accessed=1, transcendentals=0)
-MOST_VMEM = 56 * 1024 * 1024
+
+
+def in_hbm(x):
+    return pltpu.with_memory_space_constraint(x, pltpu.HBM)
 
 
 def down_kernel(planes, cuts, groups, *refs):
@@ -61,49 +64,73 @@
             pltpu.SemaphoreType.DMA((parts,)),
         ],
         cost_estimate=SHORT,
-        compiler_params=pltpu.CompilerParams(vmem_limit_bytes=MOST_VMEM),
-    )(*xs, w)
-
-
-def add_kernel(odd_ref, terms, even_out, odd_out):
+        compiler_params=pltpu.CompilerParams(vmem_limit_bytes=24 * 1024 * 1024),
+    )(*xs, in_hbm(w))
+
+
+def add_kernel(terms, out):
     total = terms[0].astype(jnp.float32)
     for k in range(1, terms.shape[0]):
         total = total + terms[k].astype(jnp.float32)
-    n = even_out.shape[0]
-    first, second = total[:n].astype(jnp.bfloat16), total[n:].astype(jnp.bfloat16)
-    odd = odd_ref[0] != 0
-    even_out[...] = jnp.where(odd, second, first)
-    odd_out[...] = jnp.where(odd, first, second)
-
-
-def add(odd, terms):
-    _, rows, columns = terms.shape
-    part = jax.ShapeDtypeStruct((rows // 2, columns), jnp.bfloat16)
+    out[...] = total.astype(jnp.bfloat16)
+
+
+def add(terms):
     vmem = pl.BlockSpec(memory_space=pltpu.VMEM)
     return pl.pallas_call(
         add_kernel,
-        out_shape=(part, part),
-        in_specs=[pl.BlockSpec(memory_space=pltpu.SMEM), vmem],
-        out_specs=(vmem, vmem),
+        out_shape=jax.ShapeDtypeStruct(terms.shape[1:], jnp.bfloat16),
+        in_specs=[vmem],
+        out_specs=vmem,
         cost_estimate=SHORT,
         compiler_params=pltpu.CompilerParams(vmem_limit_bytes=16 * 1024 * 1024),
-    )(odd, terms)
+    )(terms)
+
+
+def add_and_deal_kernel(plane_ref, near, terms, *refs):
+    outs, sums = refs[:-1], refs[-1]
+    total = terms[0].astype(jnp.float32)
+    for k in range(1, terms.shape[0]):
+        total = total + terms[k].astype(jnp.float32)
+    rows = sums.shape[1]
+    half = len(outs) // 2
+    for e in range(half):
+        sums[e] = near[e * rows : (e + 1) * rows, :]
+        sums[half + e] = total[e * rows : (e + 1) * rows].astype(jnp.bfloat16)
+    for k, out in enumerate(outs):
+        out[...] = sums[plane_ref[0] ^ k]
+
+
+def add_and_deal(plane, near, terms):
+    rows, columns = near.shape
+    blocks = 4
+    part = jax.ShapeDtypeStruct((2 * rows // blocks, columns), jnp.bfloat16)
+    vmem = pl.BlockSpec(memory_space=pltpu.VMEM)
+    return pl.pallas_call(
+        add_and_deal_kernel,
+        out_shape=(part,) * blocks,
+        in_specs=[pl.BlockSpec(memory_space=pltpu.SMEM), vmem, vmem],
+        out_specs=(vmem,) * blocks,
+        scratch_shapes=[pltpu.VMEM((blocks, *part.shape), jnp.bfloat16)],
+        cost_estimate=SHORT,
+        compiler_params=pltpu.CompilerParams(vmem_limit_bytes=16 * 1024 * 1024),
+    )(plane, near, terms)
 
 
 def project_kernel(planes, here_ref, slots, w_hbm, *refs):
-    came, refs = refs[: 2 * planes], refs[2 * planes :]
-    home, outs, (two, w, sem, w_sem) = refs[0], refs[1 : planes + 1], refs[planes + 1 :]
+    came, refs = refs[:planes], refs[planes:]
+    home, outs, (parts, w, sem, w_sem) = refs[0], refs[1 : planes + 1], refs[planes + 1 :]
     plane, block = here_ref[0], here_ref[1]
     copies = [pltpu.make_async_copy(w_hbm, w, w_sem)]
-    for i in range(2 * planes):
-        to = two.at[i // planes, plane ^ block ^ (i % planes)]
-        copies.append(pltpu.make_async_copy(came[i], to, sem.at[i]))
+    for k in range(planes):
+        copies.append(pltpu.make_async_copy(came[k], parts.at[plane ^ block ^ k], sem.at[k]))
     for copy in copies:
         copy.start()
     for copy in copies:
         copy.wait()
-    rows = two.shape[2]
-    home[...] = (two[0] + two[1]).reshape(home.shape)
+    rows = parts.shape[1]
+    for p in range(planes):
+        home[p * rows : (p + 1) * rows, :] = parts[p]
     n = home.shape[0]
     place = lax.broadcasted_iota(jnp.int32, (n, n), 0)
     place = ((place // rows) ^ plane) * rows + place % rows
@@ -114,26 +141,26 @@
         outs[d][...] = made[d * rows : (d + 1) * rows]
 
 
-def project(here, slots, w_proj, near, far):
-    planes = len(near)
-    rows, columns = near[0].shape
+def project(here, slots, w_proj, came):
+    planes = len(came)
+    rows, columns = came[0].shape
     vmem = pl.BlockSpec(memory_space=pltpu.VMEM)
     made = jax.ShapeDtypeStruct((rows, w_proj.shape[1]), jnp.bfloat16)
     return pl.pallas_call(
         functools.partial(project_kernel, planes),
         out_shape=(jax.ShapeDtypeStruct((planes * rows, columns), jnp.bfloat16), *[made] * planes),
         in_specs=[pl.BlockSpec(memory_space=pltpu.SMEM), vmem]
-        + [pl.BlockSpec(memory_space=pl.ANY)] * (1 + 2 * planes),
+        + [pl.BlockSpec(memory_space=pl.ANY)] * (1 + planes),
         out_specs=(vmem,) * (1 + planes),
         scratch_shapes=[
-            pltpu.VMEM((2, planes, rows, columns), jnp.bfloat16),
+            pltpu.VMEM((planes, rows, columns), jnp.bfloat16),
             pltpu.VMEM(w_proj.shape, w_proj.dtype),
-            pltpu.SemaphoreType.DMA((2 * planes,)),
+            pltpu.SemaphoreType.DMA((planes,)),
             pltpu.SemaphoreType.DMA,
         ],
         cost_estimate=SHORT,
         compiler_params=pltpu.CompilerParams(vmem_limit_bytes=16 * 1024 * 1024),
-    )(here, slots, w_proj, *near, *far)
+    )(here, slots, in_hbm(w_proj), *came)
 
 
 def page_copies(len_ref, kv_hbm, kv_ref, sem, r):
@@ -322,8 +349,8 @@
             pltpu.VMEM((sets, LANES, HEAD_DIM), jnp.float32),
         ],
         cost_estimate=SHORT,
-        compiler_params=pltpu.CompilerParams(vmem_limit_bytes=48 * 1024 * 1024),
-    )(here, kv_len, talker_gain.reshape(1, wide), *weights, *terms, kv_cache)
+        compiler_params=pltpu.CompilerParams(vmem_limit_bytes=40 * 1024 * 1024),
+    )(here, kv_len, talker_gain.reshape(1, wide), *weights, *terms, in_hbm(kv_cache))
 
 
 def rms_norm(talker_in, talker_gain):
@@ -422,19 +449,6 @@
     return lax.ppermute(x, "groups", [(0, 1), (1, 0)])
 
 
-def sent_home(even, odd, upper):
-    out = []
-    for k in range(4):
-        pairs = [
-            (p * 4 + c, c * 4 + (c ^ p ^ k))
-            for p in range(4)
-            for c in range(4)
-            if (p ^ k) // 2 == upper
-        ]
-        out.append(lax.ppermute(odd if k % 2 else even, GROUP, pairs))
-    return out
-
-
 def after(x, *others):
     return lax.optimization_barrier((x, *others))[0]
 
@@ -453,33 +467,37 @@
 ):
     planes = 4
     g, m, c = lax.axis_index("groups"), lax.axis_index("mp"), lax.axis_index(PLANE)
-    here, odd = jnp.stack([m, c, g]), (m & 1).reshape(1)
+    here, plane = jnp.stack([m, c, g]), m.reshape(1)
 
     across, peer = over_section(thinker_act), over_core(thinker_act)
-    near = down([thinker_act, peer], w_think, planes)
-    near_even, near_odd = add(odd, lax.all_to_all(near, "mp", 0, 0))
+    near = down([in_hbm(thinker_act), peer], w_think, planes)
+    near_terms = lax.all_to_all(near, "mp", 0, 0)
     mine = jnp.concatenate([w_query, w_key, w_value], axis=1)
     half = mine.shape[0] // 2
     my_half = lax.dynamic_slice_in_dim(mine, g * half, half, axis=0)
 
-    across, near_even, near_odd, mine, my_half = lax.optimization_barrier(
-        (across, near_even, near_odd, mine, my_half)
-    )
-    near_home = sent_home(near_even, near_odd, 0)
-    across, other, *near_home = lax.optimization_barrier((across, over_core(across), *near_home))
-    far = down([across, other], w_think, planes)
-    far_even, far_odd = add(odd, lax.all_to_all(far, "mp", 0, 0))
+    across, near_terms, mine, my_half = lax.optimization_barrier(
+        (across, near_terms, mine, my_half)
+    )
+    far = down([across, over_core(across)], w_think, planes)
+    far_terms = lax.all_to_all(far, "mp", 0, 0)
 
     my_half = over_section(after(my_half, far))
-    other_half = over_groups(my_half)
-
-    far_home = sent_home(far_even, far_odd, 1)
-    slots, other_half = lax.optimization_barrier((talker_slot, other_half))
-    thinker_out, *projected = project(here, slots, w_proj, near_home, far_home)
+    near_sums = add(after(near_terms, far))
+
+    came = [
+        lax.ppermute(x, GROUP, [(p * 4 + b, b * 4 + (b ^ p ^ k)) for p in range(4) for b in range(4)])
+        for k, x in enumerate(add_and_deal(plane, near_sums, far_terms))
+    ]
+    my_half = after(my_half, near_sums)
+    came[0], other_half = lax.optimization_barrier((came[0], over_groups(my_half)))
+    thinker_out, *projected = project(here, talker_slot, w_proj, came)
     terms = projected[:1]
     for d in range(1, planes):
         terms.append(lax.ppermute(projected[d], "mp", [(p, p ^ d) for p in range(planes)]))
-    weights = [mine, over_core(mine), my_half, other_half, over_core(my_half), over_core(other_half)]
+    other_half = after(other_half, projected[0])
+    halves = [my_half, other_half, over_core(my_half), over_core(other_half)]
+    weights = [mine, over_core(mine), *halves]
     new_kv, ctx = talker(here, terms, talker_gain, weights, kv_len, kv_cache)
     return (thinker_out, new_kv, ctx)
 

time: 149 us -> 124 us (0.83)
  waiting for transfers between devices: 64.2 us -> 54.6 us
  starting transfers between devices: 44.5 us -> 36.8 us
  local copies, waits for them, and re-layouts: 7.01 us -> 1.87 us
  Pallas kernels: 31.3 us -> 29.7 us
    ppermute x2, waiting for transfers between devices: 17.3 us -> 37.4 us  [over_section(): return lax.ppermute(x, 'section', [(0, 1), (1, 0)])]
    all_to_all x2, waiting for transfers between devices: 16.4 us -> 1.83 us  [the longest x1 1.83 us: four_planes(): far_terms = lax.all_to_all(far, 'mp', 0, 0)]
    ppermute x1, waiting for transfers between devices: 13.3 us -> 0.01 us  [over_groups(): return lax.ppermute(x, 'groups', [(0, 1), (1, 0)])]
    ppermute x8 -> x4, starting transfers between devices: 21.7 us -> 14 us  [four_planes(): lax.ppermute(x, GROUP, [(p * 4 + b, b * 4 + (b ^ p ^ k)) for p in range(4...]
    ppermute x8 -> x4, waiting for transfers between devices: 10.3 us -> 4.8 us  [four_planes(): lax.ppermute(x, GROUP, [(p * 4 + b, b * 4 + (b ^ p ^ k)) for p in range(4...]
    unnamed x32 -> x14, local copies, waits for them, and re-layouts: 6.08 us -> 0.94 us
    ppermute x5, waiting for transfers between devices: 1.04 us -> 5.01 us  [over_core(): return lax.ppermute(x, 'rows', [(0, 1), (1, 0)])]
    ppermute x3, starting transfers between devices: 7.08 us -> 4.39 us  [four_planes(): lax.ppermute(projected[d], 'mp', [(p, p ^ d) for p in range(planes)])]
  transfers between devices with their start and end apart: 21 -> 17, of which waited for: 9 -> 8; matrix products, arithmetic and copies ran while one was open for 1% -> 1% of each run, Pallas kernels for 7% -> 8%
where the time goes in v15:
time: 124 us
  waiting for transfers between devices  54.6 us (44%)
  starting transfers between devices  36.8 us (30%)
  Pallas kernels  29.7 us (24%)
  local copies, waits for them, and re-layouts  1.87 us (2%)
    ppermute x2, waiting for transfers between devices, over_section(): return lax.ppermute(x, 'section', [(0, 1), (1, 0)])  37.4 us
    pallas_call x2, Pallas kernels, down(): pl.pallas_call(functools.partial(down_kernel, planes, list(zip(ends[:-1],...  14.4 us
    ppermute x4, starting transfers between devices, four_planes(): lax.ppermute(x, GROUP, [(p * 4 + b, b * 4 + (b ^ p ^ k)) for p in range(4...  14 us
    pallas_call x1, Pallas kernels, talker(): pl.pallas_call(talker_kernel, out_shape=(jax.ShapeDtypeStruct((rows, kv_w...  12.3 us
    all_to_all x1, starting transfers between devices, four_planes(): near_terms = lax.all_to_all(near, 'mp', 0, 0)  6.38 us
    ppermute x3, waiting for transfers between devices, four_planes(): lax.ppermute(projected[d], 'mp', [(p, p ^ d) for p in range(planes)])  5.53 us
    all_to_all x1, starting transfers between devices, four_planes(): far_terms = lax.all_to_all(far, 'mp', 0, 0)  5.14 us
    ppermute x5, waiting for transfers between devices, over_core(): return lax.ppermute(x, 'rows', [(0, 1), (1, 0)])  5.01 us
  transfers between devices with their start and end apart: 17, of which 8 were waited for; matrix products, arithmetic and copies ran while one was open for 1% of the time, Pallas kernels for 8%

profile of v15, /device:TPU:0, one launch (start us, length us, event | category | flops | bytes accessed | tf_op | source)
XLA Modules:
  0.0 124.1 jit_solution(3594025671619574476)
XLA Ops:
  1.1 2.6 %collective-permute-start = (bf16[192,4736]{1,0:T(8,128)(2,1)}, bf16[192,4736]{1,0:T(8,128)(2,1)}, u32[]{:S(2)}, u32[]{:S(2)}) collective-permute-start(bf16[192,4736]{1,0:T(8,128)(2,1)} %refs_0_.1), channel_id=1, source_target_pairs={{0,2},{2,0},{1,3},{3,1},{4,6},{6,4},{5,7},{7,5},{8,10},{10,8},{9,1... | collective-permute-start | bytes 5455880 | tf_op jit(solution)/shard_map/ppermute | solution.py:441
  3.7 1.0 collective-permute-done.1.refs_1_
  4.7 7.2 %shard_map.121 = bf16[4,96,896]{2,1,0:T(8,128)(2,1)} custom-call(bf16[192,4736]{1,0:T(8,128)(2,1)} %refs_0_.1, bf16[192,4736]{1,0:T(8,128)(2,1)S(1)} %collective-permute-done.1.refs_1_, bf16[4736,896]{1,0:T(8,128)(2,1)} %refs_2_.3), custom_call_target="tpu_custom_call" | custom-call | flops 1 | bytes 1 | tf_op jit(solution)/shard_map/pallas_call | solution.py:54
  12.0 6.4 %all-to-all-start = ((bf16[4,96,896]{2,1,0:T(8,128)(2,1)}), bf16[4,96,896]{2,1,0:T(8,128)(2,1)S(1)}, u32[]{:S(2)}, u32[]{:S(2)}) async-start(bf16[4,96,896]{2,1,0:T(8,128)(2,1)} %shard_map.121), calls=%async_computation | async-start | bytes 1376256 | tf_op jit(solution)/shard_map/all_to_all | solution.py:474
  19.4 0.9 constant_dynamic-slice_fusion
  20.2 24.0 %collective-permute-done.refs_0_ = bf16[192,4736]{1,0:T(8,128)(2,1)} collective-permute-done((bf16[192,4736]{1,0:T(8,128)(2,1)}, bf16[192,4736]{1,0:T(8,128)(2,1)}, u32[]{:S(2)}, u32[]{:S(2)}) %collective-permute-start) | collective-permute-done | bytes 1818656 | tf_op jit(solution)/shard_map/ppermute | solution.py:441
  44.3 4.0 %collective-permute-done.2.refs_1_ = bf16[192,4736]{1,0:T(8,128)(2,1)S(1)} collective-permute-done((bf16[192,4736]{1,0:T(8,128)(2,1)}, bf16[192,4736]{1,0:T(8,128)(2,1)S(1)}, u32[]{:S(2)}, u32[]{:S(2)}) %collective-permute-start.2) | collective-permute-done | bytes 1818656 | tf_op jit(solution)/shard_map/ppermute | solution.py:437
  48.3 7.2 %shard_map.122 = bf16[4,96,896]{2,1,0:T(8,128)(2,1)} custom-call(bf16[192,4736]{1,0:T(8,128)(2,1)} %collective-permute-done.refs_0_, bf16[192,4736]{1,0:T(8,128)(2,1)S(1)} %collective-permute-done.2.refs_1_, bf16[4736,896]{1,0:T(8,128)(2,1)} %refs_2_.3), custom_call_target="tpu_custom_call" | custom-call | flops 1 | bytes 1 | tf_op jit(solution)/shard_map/pallas_call | solution.py:54
  55.5 5.1 %all-to-all-start.1 = ((bf16[4,96,896]{2,1,0:T(8,128)(2,1)}), bf16[4,96,896]{2,1,0:T(8,128)(2,1)S(1)}, u32[]{:S(2)}, u32[]{:S(2)}) async-start(bf16[4,96,896]{2,1,0:T(8,128)(2,1)} %shard_map.122), calls=%async_computation.1 | async-start | bytes 1376256 | tf_op jit(solution)/shard_map/all_to_all | solution.py:483
  60.6 1.5 %collective-permute-start.4 = (bf16[448,640]{1,0:T(8,128)(2,1)}, bf16[448,640]{1,0:T(8,128)(2,1)S(1)}, u32[]{:S(2)}, u32[]{:S(2)}) collective-permute-start(bf16[448,640]{1,0:T(8,128)(2,1)} %constant_dynamic-slice_fusion), channel_id=1, source_target_pairs={{0,2},{2,0},{1,3},{3,1},{4,6},{6,4},{5,7},{7,5},{8,10},{10,8},{9,1... | collective-permute-start | bytes 1720328 | tf_op jit(solution)/shard_map/ppermute | solution.py:441
  62.2 13.4 %collective-permute-done.4.refs_2_ = bf16[448,640]{1,0:T(8,128)(2,1)S(1)} collective-permute-done((bf16[448,640]{1,0:T(8,128)(2,1)}, bf16[448,640]{1,0:T(8,128)(2,1)S(1)}, u32[]{:S(2)}, u32[]{:S(2)}) %collective-permute-start.4) | collective-permute-done | bytes 573472 | tf_op jit(solution)/shard_map/ppermute | solution.py:441
  75.6 1.5 %collective-permute-start.5 = (bf16[448,640]{1,0:T(8,128)(2,1)S(1)}, bf16[448,640]{1,0:T(8,128)(2,1)S(1)}, u32[]{:S(2)}, u32[]{:S(2)}) collective-permute-start(bf16[448,640]{1,0:T(8,128)(2,1)S(1)} %collective-permute-done.4.refs_2_), channel_id=1, source_target_pairs={{0,16},{16,0},{1,17},{17,1},{2,18},{18,2},{3,19},{19,3},{4,20},{20... | collective-permute-start | bytes 1720328 | tf_op jit(solution)/shard_map/ppermute | solution.py:449
  77.1 1.8 %all-to-all-done.1.terms = bf16[4,96,896]{2,1,0:T(8,128)(2,1)S(1)} async-done(((bf16[4,96,896]{2,1,0:T(8,128)(2,1)}), bf16[4,96,896]{2,1,0:T(8,128)(2,1)S(1)}, u32[]{:S(2)}, u32[]{:S(2)}) %all-to-all-start.1) | async-done | bytes 688160 | tf_op jit(solution)/shard_map/all_to_all | solution.py:483
  79.8 2.3 %collective-permute-start.6 = (bf16[48,896]{1,0:T(8,128)(2,1)S(1)}, bf16[48,896]{1,0:T(8,128)(2,1)S(1)}, u32[]{:S(2)}, u32[]{:S(2)}) collective-permute-start(bf16[48,896]{1,0:T(8,128)(2,1)S(1)} %get-tuple-element.32), channel_id=1, source_target_pairs={{0,1},{1,4},{2,11},{3,14},{4,0},{5,5},{6,10},{7,15},{8,3},{9,6},{1... | collective-permute-start | bytes 258056 | tf_op jit(solution)/shard_map/ppermute | solution.py:489
  82.1 5.1 %collective-permute-start.7 = (bf16[48,896]{1,0:T(8,128)(2,1)S(1)}, bf16[48,896]{1,0:T(8,128)(2,1)S(1)}, u32[]{:S(2)}, u32[]{:S(2)}) collective-permute-start(bf16[48,896]{1,0:T(8,128)(2,1)S(1)} %get-tuple-element.33), channel_id=1, source_target_pairs={{0,2},{1,7},{2,8},{3,13},{4,3},{5,6},{6,9},{7,12},{8,0},{9,5},{10,... | collective-permute-start | bytes 258056 | tf_op jit(solution)/shard_map/ppermute | solution.py:489
  87.2 6.0 %collective-permute-start.8 = (bf16[48,896]{1,0:T(8,128)(2,1)S(1)}, bf16[48,896]{1,0:T(8,128)(2,1)S(1)}, u32[]{:S(2)}, u32[]{:S(2)}) collective-permute-start(bf16[48,896]{1,0:T(8,128)(2,1)S(1)} %get-tuple-element.34), channel_id=1, source_target_pairs={{0,3},{1,6},{2,9},{3,12},{4,2},{5,7},{6,8},{7,13},{8,1},{9,4},{10,... | collective-permute-start | bytes 258056 | tf_op jit(solution)/shard_map/ppermute | solution.py:489
  93.3 4.8 %collective-permute-done.7.refs_2_ = bf16[48,896]{1,0:T(8,128)(2,1)S(1)} collective-permute-done((bf16[48,896]{1,0:T(8,128)(2,1)S(1)}, bf16[48,896]{1,0:T(8,128)(2,1)S(1)}, u32[]{:S(2)}, u32[]{:S(2)}) %collective-permute-start.7) | collective-permute-done | bytes 86048 | tf_op jit(solution)/shard_map/ppermute | solution.py:489
  98.1 2.8 %shard_map.125 = (bf16[192,896]{1,0:T(8,128)(2,1)}, bf16[48,896]{1,0:T(8,128)(2,1)S(1)}, bf16[48,896]{1,0:T(8,128)(2,1)S(1)}, bf16[48,896]{1,0:T(8,128)(2,1)S(1)}, bf16[48,896]{1,0:T(8,128)(2,1)S(1)}) custom-call(s32[3]{0:T(128)S(1)} %pad_add_fusion.here_ref, s32[1,192]{1,0:T(1,128)S(1)} %copy-done, bf16[896,896]{1,0:T(8,128)(2,1)} %w_hbm.1, ...), custom_call_target="tpu_custom_call" | custom-call | flops 1 | bytes 1 | tf_op jit(solution)/shard_map/pallas_call | solution.py:149
  100.9 0.8 collective-permute-start.11
  101.7 3.0 %collective-permute-start.13 = (bf16[48,896]{1,0:T(8,128)(2,1)S(1)}, bf16[48,896]{1,0:T(8,128)(2,1)S(1)}, u32[]{:S(2)}, u32[]{:S(2)}) collective-permute-start(bf16[48,896]{1,0:T(8,128)(2,1)S(1)} %get-tuple-element.41), channel_id=1, source_target_pairs={{0,8},{4,12},{8,0},{12,4},{1,9},{5,13},{9,1},{13,5},{2,10},{6,14},... | collective-permute-start | bytes 258056 | tf_op jit(solution)/shard_map/ppermute | solution.py:497
  104.7 1.4 %collective-permute-start.14 = (bf16[48,896]{1,0:T(8,128)(2,1)S(1)}, bf16[48,896]{1,0:T(8,128)(2,1)S(1)}, u32[]{:S(2)}, u32[]{:S(2)}) collective-permute-start(bf16[48,896]{1,0:T(8,128)(2,1)S(1)} %get-tuple-element.42), channel_id=1, source_target_pairs={{0,12},{4,8},{8,4},{12,0},{1,13},{5,9},{9,5},{13,1},{2,14},{6,10},... | collective-permute-start | bytes 258056 | tf_op jit(solution)/shard_map/ppermute | solution.py:497
  106.1 1.5 %collective-permute-done.12.refs_7_ = bf16[48,896]{1,0:T(8,128)(2,1)S(1)} collective-permute-done((bf16[48,896]{1,0:T(8,128)(2,1)S(1)}, bf16[48,896]{1,0:T(8,128)(2,1)S(1)}, u32[]{:S(2)}, u32[]{:S(2)}) %collective-permute-start.12) | collective-permute-done | bytes 86048 | tf_op jit(solution)/shard_map/ppermute | solution.py:497
  107.6 4.0 %collective-permute-done.13.refs_8_ = bf16[48,896]{1,0:T(8,128)(2,1)S(1)} collective-permute-done((bf16[48,896]{1,0:T(8,128)(2,1)S(1)}, bf16[48,896]{1,0:T(8,128)(2,1)S(1)}, u32[]{:S(2)}, u32[]{:S(2)}) %collective-permute-start.13) | collective-permute-done | bytes 86048 | tf_op jit(solution)/shard_map/ppermute | solution.py:497
  111.6 12.3 %shard_map.126 = (bf16[48,1024]{1,0:T(8,128)(2,1)}, f32[48,1536]{1,0:T(8,128)}) custom-call(s32[3]{0:T(128)S(1)} %pad_add_fusion.here_ref, s32[48]{0:T(128)S(1)} %copy-done.1, f32[1,896]{1,0:T(1,128)S(1)} %reshape.10.gain, bf16[896,640]{1,0:T(8,128)(2,1)S(1)} %constant_dynamic-update-slice_fusion.refs_0_, bf16[896,640]{1,0:T(8,128)(2,1)} %collective-permute-done.9.refs_1_, ...), custom_call_target="tpu_custom_call" | custom-call | flops 1 | bytes 1 | tf_op jit(solution)/shard_map/pallas_call | solution.py:331
  (34 shorter events, 2.6 us)
Async XLA Ops:
  0.6 4.1 %collective-permute-start.1 = (bf16[192,4736]{1,0:T(8,128)(2,1)}, bf16[192,4736]{1,0:T(8,128)(2,1)S(1)}, u32[]{:S(2)}, u32[]{:S(2)}) collective-permute-start(bf16[192,4736]{1,0:T(8,128)(2,1)} %refs_0_.1), channel_id=1, source_target_pairs={{0,1},{1,0},{2,3},{3,2},{4,5},{5,4},{6,7},{7,6},{8,9},{9,8},{10,11... | collective-permute-start | bytes 5455880 | tf_op jit(solution)/shard_map/ppermute | solution.py:437
  1.1 43.1 %collective-permute-start = (bf16[192,4736]{1,0:T(8,128)(2,1)}, bf16[192,4736]{1,0:T(8,128)(2,1)}, u32[]{:S(2)}, u32[]{:S(2)}) collective-permute-start(bf16[192,4736]{1,0:T(8,128)(2,1)} %refs_0_.1), channel_id=1, source_target_pairs={{0,2},{2,0},{1,3},{3,1},{4,6},{6,4},{5,7},{7,5},{8,10},{10,8},{9,1... | collective-permute-start | bytes 5455880 | tf_op jit(solution)/shard_map/ppermute | solution.py:441
  12.0 6.4 %copy-start.2 = (bf16[896,384]{1,0:T(8,128)(2,1)S(1)}, bf16[896,384]{1,0:T(8,128)(2,1)}, u32[]{:S(2)}) copy-start(bf16[896,384]{1,0:T(8,128)(2,1)} %param.14) | copy-start | bytes 2064388
  12.0 6.5 %copy-start.3 = (bf16[896,128]{1,0:T(8,128)(2,1)S(1)}, bf16[896,128]{1,0:T(8,128)(2,1)}, u32[]{:S(2)}) copy-start(bf16[896,128]{1,0:T(8,128)(2,1)} %param.15) | copy-start | bytes 688132
  12.0 32.3 %all-to-all-start = ((bf16[4,96,896]{2,1,0:T(8,128)(2,1)}), bf16[4,96,896]{2,1,0:T(8,128)(2,1)S(1)}, u32[]{:S(2)}, u32[]{:S(2)}) async-start(bf16[4,96,896]{2,1,0:T(8,128)(2,1)} %shard_map.121), calls=%async_computation | async-start | bytes 1376256 | tf_op jit(solution)/shard_map/all_to_all | solution.py:474
  18.4 0.9 copy-start.4
  44.3 4.0 %collective-permute-start.2 = (bf16[192,4736]{1,0:T(8,128)(2,1)}, bf16[192,4736]{1,0:T(8,128)(2,1)S(1)}, u32[]{:S(2)}, u32[]{:S(2)}) collective-permute-start(bf16[192,4736]{1,0:T(8,128)(2,1)} %collective-permute-done.refs_0_), channel_id=1, source_target_pairs={{0,1},{1,0},{2,3},{3,2},{4,5},{5,4},{6,7},{7,6},{8,9},{9,8},{10,11... | collective-permute-start | bytes 5455880 | tf_op jit(solution)/shard_map/ppermute | solution.py:437
  55.5 23.5 %all-to-all-start.1 = ((bf16[4,96,896]{2,1,0:T(8,128)(2,1)}), bf16[4,96,896]{2,1,0:T(8,128)(2,1)S(1)}, u32[]{:S(2)}, u32[]{:S(2)}) async-start(bf16[4,96,896]{2,1,0:T(8,128)(2,1)} %shard_map.122), calls=%async_computation.1 | async-start | bytes 1376256 | tf_op jit(solution)/shard_map/all_to_all | solution.py:483
  60.6 37.5 %copy-start = (s32[1,192]{1,0:T(1,128)S(1)}, s32[1,192]{1,0:T(1,128)}, u32[]{:S(2)}) copy-start(s32[1,192]{1,0:T(1,128)} %slots.1) | copy-start | bytes 2308
  60.6 15.0 %collective-permute-start.4 = (bf16[448,640]{1,0:T(8,128)(2,1)}, bf16[448,640]{1,0:T(8,128)(2,1)S(1)}, u32[]{:S(2)}, u32[]{:S(2)}) collective-permute-start(bf16[448,640]{1,0:T(8,128)(2,1)} %constant_dynamic-slice_fusion), channel_id=1, source_target_pairs={{0,2},{2,0},{1,3},{3,1},{4,6},{6,4},{5,7},{7,5},{8,10},{10,8},{9,1... | collective-permute-start | bytes 1720328 | tf_op jit(solution)/shard_map/ppermute | solution.py:441
  62.1 42.5 %collective-permute-start.9 = (bf16[896,640]{1,0:T(8,128)(2,1)S(1)}, bf16[896,640]{1,0:T(8,128)(2,1)}, u32[]{:S(2)}, u32[]{:S(2)}) collective-permute-start(bf16[896,640]{1,0:T(8,128)(2,1)S(1)} %constant_dynamic-update-slice_fusion.refs_0_), channel_id=1, source_target_pairs={{0,1},{1,0},{2,3},{3,2},{4,5},{5,4},{6,7},{7,6},{8,9},{9,8},{10,11... | collective-permute-start | bytes 3440648 | tf_op jit(solution)/shard_map/ppermute | solution.py:437
  75.6 17.7 %collective-permute-start.5 = (bf16[448,640]{1,0:T(8,128)(2,1)S(1)}, bf16[448,640]{1,0:T(8,128)(2,1)S(1)}, u32[]{:S(2)}, u32[]{:S(2)}) collective-permute-start(bf16[448,640]{1,0:T(8,128)(2,1)S(1)} %collective-permute-done.4.refs_2_), channel_id=1, source_target_pairs={{0,16},{16,0},{1,17},{17,1},{2,18},{18,2},{3,19},{19,3},{4,20},{20... | collective-permute-start | bytes 1720328 | tf_op jit(solution)/shard_map/ppermute | solution.py:449
  79.1 27.0 %copy-start.5 = (f32[896]{0:T(1024)S(1)}, f32[896]{0:T(1024)}, u32[]{:S(2)}) copy-start(f32[896]{0:T(1024)} %param.13) | copy-start | bytes 10756
  79.1 32.5 %copy-start.1 = (s32[48]{0:T(128)S(1)}, s32[48]{0:T(128)}, u32[]{:S(2)}) copy-start(s32[48]{0:T(128)} %len_ref.1) | copy-start | bytes 580
  79.1 8.1 %collective-permute-start.3 = (bf16[48,896]{1,0:T(8,128)(2,1)S(1)}, bf16[48,896]{1,0:T(8,128)(2,1)S(1)}, u32[]{:S(2)}, u32[]{:S(2)}) collective-permute-start(bf16[48,896]{1,0:T(8,128)(2,1)S(1)} %get-tuple-element.27), channel_id=1, source_target_pairs={{0,0},{1,5},{2,10},{3,15},{4,1},{5,4},{6,11},{7,14},{8,2},{9,7},{1... | collective-permute-start | bytes 258056 | tf_op jit(solution)/shard_map/ppermute | solution.py:489
  79.8 13.5 %collective-permute-start.6 = (bf16[48,896]{1,0:T(8,128)(2,1)S(1)}, bf16[48,896]{1,0:T(8,128)(2,1)S(1)}, u32[]{:S(2)}, u32[]{:S(2)}) collective-permute-start(bf16[48,896]{1,0:T(8,128)(2,1)S(1)} %get-tuple-element.32), channel_id=1, source_target_pairs={{0,1},{1,4},{2,11},{3,14},{4,0},{5,5},{6,10},{7,15},{8,3},{9,6},{1... | collective-permute-start | bytes 258056 | tf_op jit(solution)/shard_map/ppermute | solution.py:489
  82.1 16.0 %collective-permute-start.7 = (bf16[48,896]{1,0:T(8,128)(2,1)S(1)}, bf16[48,896]{1,0:T(8,128)(2,1)S(1)}, u32[]{:S(2)}, u32[]{:S(2)}) collective-permute-start(bf16[48,896]{1,0:T(8,128)(2,1)S(1)} %get-tuple-element.33), channel_id=1, source_target_pairs={{0,2},{1,7},{2,8},{3,13},{4,3},{5,6},{6,9},{7,12},{8,0},{9,5},{10,... | collective-permute-start | bytes 258056 | tf_op jit(solution)/shard_map/ppermute | solution.py:489
  87.2 10.9 %collective-permute-start.8 = (bf16[48,896]{1,0:T(8,128)(2,1)S(1)}, bf16[48,896]{1,0:T(8,128)(2,1)S(1)}, u32[]{:S(2)}, u32[]{:S(2)}) collective-permute-start(bf16[48,896]{1,0:T(8,128)(2,1)S(1)} %get-tuple-element.34), channel_id=1, source_target_pairs={{0,3},{1,6},{2,9},{3,12},{4,2},{5,7},{6,8},{7,13},{8,1},{9,4},{10,... | collective-permute-start | bytes 258056 | tf_op jit(solution)/shard_map/ppermute | solution.py:489
  93.2 12.8 %collective-permute-start.10 = (bf16[448,640]{1,0:T(8,128)(2,1)S(1)}, bf16[448,640]{1,0:T(8,128)(2,1)S(1)}, u32[]{:S(2)}, u32[]{:S(2)}) collective-permute-start(bf16[448,640]{1,0:T(8,128)(2,1)S(1)} %collective-permute-done.4.refs_2_), channel_id=1, source_target_pairs={{0,1},{1,0},{2,3},{3,2},{4,5},{5,4},{6,7},{7,6},{8,9},{9,8},{10,11... | collective-permute-start | bytes 1720328 | tf_op jit(solution)/shard_map/ppermute | solution.py:437
  100.9 10.7 %collective-permute-start.11 = (bf16[448,640]{1,0:T(8,128)(2,1)S(1)}, bf16[448,640]{1,0:T(8,128)(2,1)S(1)}, u32[]{:S(2)}, u32[]{:S(2)}) collective-permute-start(bf16[448,640]{1,0:T(8,128)(2,1)S(1)} %collective-permute-done.5.refs_3_), channel_id=1, source_target_pairs={{0,1},{1,0},{2,3},{3,2},{4,5},{5,4},{6,7},{7,6},{8,9},{9,8},{10,11... | collective-permute-start | bytes 1720328 | tf_op jit(solution)/shard_map/ppermute | solution.py:437
  101.7 5.9 %collective-permute-start.12 = (bf16[48,896]{1,0:T(8,128)(2,1)S(1)}, bf16[48,896]{1,0:T(8,128)(2,1)S(1)}, u32[]{:S(2)}, u32[]{:S(2)}) collective-permute-start(bf16[48,896]{1,0:T(8,128)(2,1)S(1)} %get-tuple-element.40), channel_id=1, source_target_pairs={{0,4},{4,0},{8,12},{12,8},{1,5},{5,1},{9,13},{13,9},{2,6},{6,2},{1... | collective-permute-start | bytes 258056 | tf_op jit(solution)/shard_map/ppermute | solution.py:497
  101.7 9.9 %collective-permute-start.13 = (bf16[48,896]{1,0:T(8,128)(2,1)S(1)}, bf16[48,896]{1,0:T(8,128)(2,1)S(1)}, u32[]{:S(2)}, u32[]{:S(2)}) collective-permute-start(bf16[48,896]{1,0:T(8,128)(2,1)S(1)} %get-tuple-element.41), channel_id=1, source_target_pairs={{0,8},{4,12},{8,0},{12,4},{1,9},{5,13},{9,1},{13,5},{2,10},{6,14},... | collective-permute-start | bytes 258056 | tf_op jit(solution)/shard_map/ppermute | solution.py:497
  104.7 6.9 %collective-permute-start.14 = (bf16[48,896]{1,0:T(8,128)(2,1)S(1)}, bf16[48,896]{1,0:T(8,128)(2,1)S(1)}, u32[]{:S(2)}, u32[]{:S(2)}) collective-permute-start(bf16[48,896]{1,0:T(8,128)(2,1)S(1)} %get-tuple-element.42), channel_id=1, source_target_pairs={{0,12},{4,8},{8,4},{12,0},{1,13},{5,9},{9,5},{13,1},{2,14},{6,10},... | collective-permute-start | bytes 258056 | tf_op jit(solution)/shard_map/ppermute | solution.py:497

commit v16 on v15

--- a/solution.py
+++ b/solution.py
@@ -18,7 +18,7 @@
     return pltpu.with_memory_space_constraint(x, pltpu.HBM)
 
 
-def down_kernel(planes, cuts, groups, *refs):
+def down_kernel(planes, cuts, groups, spans, *refs):
     xs, (w, out, x_all, w_all, acc, x_sem, w_sem) = refs[:groups], refs[groups:]
     n = xs[0].shape[0]
     loads = []
@@ -39,20 +39,23 @@
             copy.wait()
         part = jnp.dot(x_all[:, lo:hi], w_all[lo:hi, :], preferred_element_type=jnp.float32)
         acc[...] = part if s == 0 else acc[...] + part
-    part = n // planes
+    row = 0
     for i in range(groups):
-        for p in range(planes):
-            at = i * n + p * part
-            out[p, i * part : (i + 1) * part, :] = acc[at : at + part, :].astype(out.dtype)
-
-
-def down(xs, w, planes):
+        for start, length in spans:
+            part = length // planes
+            for p in range(planes):
+                at = i * n + start + p * part
+                out[p, row : row + part, :] = acc[at : at + part, :].astype(out.dtype)
+            row += part
+
+
+def down(xs, w, planes, spans):
     depth, columns = w.shape
     groups, n = len(xs), xs[0].shape[0]
     tiles, parts = depth // LANES, 6
     ends = [LANES * (tiles * i // parts) for i in range(parts)] + [depth]
     return pl.pallas_call(
-        functools.partial(down_kernel, planes, list(zip(ends[:-1], ends[1:])), groups),
+        functools.partial(down_kernel, planes, list(zip(ends[:-1], ends[1:])), groups, spans),
         out_shape=jax.ShapeDtypeStruct((planes, groups * n // planes, columns), jnp.bfloat16),
         in_specs=[pl.BlockSpec(memory_space=pl.ANY)] * (groups + 1),
         out_specs=pl.BlockSpec(memory_space=pltpu.VMEM),
@@ -87,21 +90,28 @@
     )(terms)
 
 
-def add_and_deal_kernel(plane_ref, near, terms, *refs):
-    outs, sums = refs[:-1], refs[-1]
-    total = terms[0].astype(jnp.float32)
-    for k in range(1, terms.shape[0]):
-        total = total + terms[k].astype(jnp.float32)
+def add_and_deal_kernel(plane_ref, near, *refs):
+    chunks, outs, sums = refs[:-5], refs[-5:-1], refs[-1]
     rows = sums.shape[1]
     half = len(outs) // 2
     for e in range(half):
         sums[e] = near[e * rows : (e + 1) * rows, :]
-        sums[half + e] = total[e * rows : (e + 1) * rows].astype(jnp.bfloat16)
+    row = 0
+    for terms in chunks:
+        total = terms[0].astype(jnp.float32)
+        for k in range(1, terms.shape[0]):
+            total = total + terms[k].astype(jnp.float32)
+        part = total.shape[0] // half
+        for e in range(half):
+            sums[half + e, row : row + part, :] = total[e * part : (e + 1) * part].astype(
+                jnp.bfloat16
+            )
+        row += part
     for k, out in enumerate(outs):
         out[...] = sums[plane_ref[0] ^ k]
 
 
-def add_and_deal(plane, near, terms):
+def add_and_deal(plane, near, chunks):
     rows, columns = near.shape
     blocks = 4
     part = jax.ShapeDtypeStruct((2 * rows // blocks, columns), jnp.bfloat16)
@@ -109,15 +119,15 @@
     return pl.pallas_call(
         add_and_deal_kernel,
         out_shape=(part,) * blocks,
-        in_specs=[pl.BlockSpec(memory_space=pltpu.SMEM), vmem, vmem],
+        in_specs=[pl.BlockSpec(memory_space=pltpu.SMEM), vmem] + [vmem] * len(chunks),
         out_specs=(vmem,) * blocks,
         scratch_shapes=[pltpu.VMEM((blocks, *part.shape), jnp.bfloat16)],
         cost_estimate=SHORT,
         compiler_params=pltpu.CompilerParams(vmem_limit_bytes=16 * 1024 * 1024),
-    )(plane, near, terms)
-
-
-def project_kernel(planes, here_ref, slots, w_hbm, *refs):
+    )(plane, near, *chunks)
+
+
+def project_kernel(planes, spans, here_ref, slots, w_hbm, *refs):
     came, refs = refs[:planes], refs[planes:]
     home, outs, (parts, w, sem, w_sem) = refs[0], refs[1 : planes + 1], refs[planes + 1 :]
     plane, block = here_ref[0], here_ref[1]
@@ -129,8 +139,13 @@
     for copy in copies:
         copy.wait()
     rows = parts.shape[1]
-    for p in range(planes):
-        home[p * rows : (p + 1) * rows, :] = parts[p]
+    row = 0
+    for start, length in spans:
+        part = length // planes
+        for p in range(planes):
+            at = start + p * part
+            home[at : at + part, :] = parts[p, row : row + part, :]
+        row += part
     n = home.shape[0]
     place = lax.broadcasted_iota(jnp.int32, (n, n), 0)
     place = ((place // rows) ^ plane) * rows + place % rows
@@ -141,13 +156,13 @@
         outs[d][...] = made[d * rows : (d + 1) * rows]
 
 
-def project(here, slots, w_proj, came):
+def project(here, slots, w_proj, came, spans):
     planes = len(came)
     rows, columns = came[0].shape
     vmem = pl.BlockSpec(memory_space=pltpu.VMEM)
     made = jax.ShapeDtypeStruct((rows, w_proj.shape[1]), jnp.bfloat16)
     return pl.pallas_call(
-        functools.partial(project_kernel, planes),
+        functools.partial(project_kernel, planes, spans),
         out_shape=(jax.ShapeDtypeStruct((planes * rows, columns), jnp.bfloat16), *[made] * planes),
         in_specs=[pl.BlockSpec(memory_space=pltpu.SMEM), vmem]
         + [pl.BlockSpec(memory_space=pl.ANY)] * (1 + planes),
@@ -469,18 +484,21 @@
     g, m, c = lax.axis_index("groups"), lax.axis_index("mp"), lax.axis_index(PLANE)
     here, plane = jnp.stack([m, c, g]), m.reshape(1)
 
-    across, peer = over_section(thinker_act), over_core(thinker_act)
-    near = down([in_hbm(thinker_act), peer], w_think, planes)
+    rows = thinker_act.shape[0]
+    spans = [(0, rows // 3), (rows // 3, rows - rows // 3)]
+    across = [over_section(thinker_act[start : start + n]) for start, n in spans]
+    near = down([in_hbm(thinker_act), over_core(thinker_act)], w_think, planes, spans)
     near_terms = lax.all_to_all(near, "mp", 0, 0)
     mine = jnp.concatenate([w_query, w_key, w_value], axis=1)
     half = mine.shape[0] // 2
     my_half = lax.dynamic_slice_in_dim(mine, g * half, half, axis=0)
 
-    across, near_terms, mine, my_half = lax.optimization_barrier(
-        (across, near_terms, mine, my_half)
-    )
-    far = down([across, over_core(across)], w_think, planes)
-    far_terms = lax.all_to_all(far, "mp", 0, 0)
+    ready, far_terms = (near,), []
+    for x, (_, n) in zip(across, spans):
+        x = after(x, *ready)
+        far = down([x, over_core(x)], w_think, planes, [(0, n)])
+        far_terms.append(lax.all_to_all(far, "mp", 0, 0))
+        ready = (near_terms, far_terms[0], mine, my_half)
 
     my_half = over_section(after(my_half, far))
     near_sums = add(after(near_terms, far))
@@ -491,7 +509,7 @@
     ]
     my_half = after(my_half, near_sums)
     came[0], other_half = lax.optimization_barrier((came[0], over_groups(my_half)))
-    thinker_out, *projected = project(here, talker_slot, w_proj, came)
+    thinker_out, *projected = project(here, talker_slot, w_proj, came, spans)
     terms = projected[:1]
     for d in range(1, planes):
         terms.append(lax.ppermute(projected[d], "mp", [(p, p ^ d) for p in range(planes)]))

time: 124 us -> 138 us (1.11)
  local copies, waits for them, and re-layouts: 1.87 us -> 8.28 us
  Pallas kernels: 29.7 us -> 33.7 us
  starting transfers between devices: 36.8 us -> 39.7 us
    all_to_all x1 -> x2, waiting for transfers between devices: 1.83 us -> 8.42 us  [four_planes(): far_terms.append(lax.all_to_all(far, 'mp', 0, 0))]
    ppermute x2 -> x3, waiting for transfers between devices: 37.4 us -> 30.9 us  [over_section(): return lax.ppermute(x, 'section', [(0, 1), (1, 0)])]
    all_to_all x1 -> x2, starting transfers between devices: 5.14 us -> 9.95 us  [four_planes(): far_terms.append(lax.all_to_all(far, 'mp', 0, 0))]
    unnamed x14 -> x26, local copies, waits for them, and re-layouts: 0.94 us -> 5.09 us
    pallas_call x2 -> x3, Pallas kernels: 14.4 us -> 17.9 us  [down(): pl.pallas_call(functools.partial(down_kernel, planes, list(zip(ends[:-1],...]
    all_to_all x1, starting transfers between devices: 6.38 us -> 3.48 us  [four_planes(): near_terms = lax.all_to_all(near, 'mp', 0, 0)]
    slice x0 -> x2, local copies, waits for them, and re-layouts: none -> 2.25 us  [four_planes(): across = [over_section(thinker_act[start:start + n]) for start, n in spans]]
    ppermute x2 -> x3, starting transfers between devices: 4.06 us -> 5.62 us  [over_section(): return lax.ppermute(x, 'section', [(0, 1), (1, 0)])]
  transfers between devices with their start and end apart: 17 -> 20, of which waited for: 8 -> 10; matrix products, arithmetic and copies ran while one was open for 1% -> 3% of each run, Pallas kernels for 8% -> 8%
where the time goes in v16:
time: 138 us
  waiting for transfers between devices  54.8 us (40%)
  starting transfers between devices  39.7 us (29%)
  Pallas kernels  33.7 us (24%)
  local copies, waits for them, and re-layouts  8.28 us (6%)
    ppermute x3, waiting for transfers between devices, over_section(): return lax.ppermute(x, 'section', [(0, 1), (1, 0)])  30.9 us
    pallas_call x3, Pallas kernels, down(): pl.pallas_call(functools.partial(down_kernel, planes, list(zip(ends[:-1],...  17.9 us
    ppermute x4, starting transfers between devices, four_planes(): lax.ppermute(x, GROUP, [(p * 4 + b, b * 4 + (b ^ p ^ k)) for p in range(4...  13.4 us
    pallas_call x1, Pallas kernels, talker(): pl.pallas_call(talker_kernel, out_shape=(jax.ShapeDtypeStruct((rows, kv_w...  12.1 us
    all_to_all x2, starting transfers between devices, four_planes(): far_terms.append(lax.all_to_all(far, 'mp', 0, 0))  9.95 us
    all_to_all x2, waiting for transfers between devices, four_planes(): far_terms.append(lax.all_to_all(far, 'mp', 0, 0))  8.42 us
    ppermute x3, starting transfers between devices, over_section(): return lax.ppermute(x, 'section', [(0, 1), (1, 0)])  5.62 us
    ppermute x3, waiting for transfers between devices, four_planes(): lax.ppermute(projected[d], 'mp', [(p, p ^ d) for p in range(planes)])  5.57 us
  transfers between devices with their start and end apart: 20, of which 10 were waited for; matrix products, arithmetic and copies ran while one was open for 3% of the time, Pallas kernels for 8%

profile of v16, /device:TPU:0, one launch (start us, length us, event | category | flops | bytes accessed | tf_op | source)
XLA Modules:
  0.0 137.6 jit_solution(1941357190644214921)
XLA Ops:
  2.3 2.6 %collective-permute-start.2 = (bf16[64,4736]{1,0:T(8,128)(2,1)S(1)}, bf16[64,4736]{1,0:T(8,128)(2,1)S(1)}, u32[]{:S(2)}, u32[]{:S(2)}) collective-permute-start(bf16[64,4736]{1,0:T(8,128)(2,1)S(1)} %slice.7), channel_id=1, source_target_pairs={{0,2},{2,0},{1,3},{3,1},{4,6},{6,4},{5,7},{7,5},{8,10},{10,8},{9,1... | collective-permute-start | bytes 1818632 | tf_op jit(solution)/shard_map/ppermute | solution.py:456
  4.8 7.2 %shard_map.121 = bf16[4,96,896]{2,1,0:T(8,128)(2,1)} custom-call(bf16[192,4736]{1,0:T(8,128)(2,1)} %refs_0_.1, bf16[192,4736]{1,0:T(8,128)(2,1)S(1)} %collective-permute-done.refs_1_, bf16[4736,896]{1,0:T(8,128)(2,1)} %refs_2_.5), custom_call_target="tpu_custom_call" | custom-call | flops 1 | bytes 1 | tf_op jit(solution)/shard_map/pallas_call | solution.py:57
  12.0 7.1 %collective-permute-done.2.refs_0_ = bf16[64,4736]{1,0:T(8,128)(2,1)S(1)} collective-permute-done((bf16[64,4736]{1,0:T(8,128)(2,1)S(1)}, bf16[64,4736]{1,0:T(8,128)(2,1)S(1)}, u32[]{:S(2)}, u32[]{:S(2)}) %collective-permute-start.2) | collective-permute-done | bytes 606240 | tf_op jit(solution)/shard_map/ppermute | solution.py:456
  19.2 2.0 %collective-permute-done.3.refs_1_ = bf16[64,4736]{1,0:T(8,128)(2,1)S(1)} collective-permute-done((bf16[64,4736]{1,0:T(8,128)(2,1)S(1)}, bf16[64,4736]{1,0:T(8,128)(2,1)S(1)}, u32[]{:S(2)}, u32[]{:S(2)}) %collective-permute-start.3) | collective-permute-done | bytes 606240 | tf_op jit(solution)/shard_map/ppermute | solution.py:452
  21.2 4.9 %shard_map.122 = bf16[4,32,896]{2,1,0:T(8,128)(2,1)} custom-call(bf16[64,4736]{1,0:T(8,128)(2,1)S(1)} %collective-permute-done.2.refs_0_, bf16[64,4736]{1,0:T(8,128)(2,1)S(1)} %collective-permute-done.3.refs_1_, bf16[4736,896]{1,0:T(8,128)(2,1)} %refs_2_.5), custom_call_target="tpu_custom_call" | custom-call | flops 1 | bytes 1 | tf_op jit(solution)/shard_map/pallas_call | solution.py:57
  26.1 5.1 %all-to-all-start.1 = ((bf16[4,32,896]{2,1,0:T(8,128)(2,1)}), bf16[4,32,896]{2,1,0:T(8,128)(2,1)S(1)}, u32[]{:S(2)}, u32[]{:S(2)}) async-start(bf16[4,32,896]{2,1,0:T(8,128)(2,1)} %shard_map.122), calls=%async_computation.1 | async-start | bytes 458752 | tf_op jit(solution)/shard_map/all_to_all | solution.py:500
  33.9 5.9 %all-to-all-done.1.refs_0_ = bf16[4,32,896]{2,1,0:T(8,128)(2,1)S(1)} async-done(((bf16[4,32,896]{2,1,0:T(8,128)(2,1)}), bf16[4,32,896]{2,1,0:T(8,128)(2,1)S(1)}, u32[]{:S(2)}, u32[]{:S(2)}) %all-to-all-start.1) | async-done | bytes 229408 | tf_op jit(solution)/shard_map/all_to_all | solution.py:500
  39.8 3.5 %all-to-all-start = ((bf16[4,96,896]{2,1,0:T(8,128)(2,1)}), bf16[4,96,896]{2,1,0:T(8,128)(2,1)S(1)}, u32[]{:S(2)}, u32[]{:S(2)}) async-start(bf16[4,96,896]{2,1,0:T(8,128)(2,1)} %shard_map.121), calls=%async_computation | async-start | bytes 1376256 | tf_op jit(solution)/shard_map/all_to_all | solution.py:491
  45.5 15.5 %collective-permute-done.1.refs_0_ = bf16[128,4736]{1,0:T(8,128)(2,1)S(1)} collective-permute-done((bf16[128,4736]{1,0:T(8,128)(2,1)}, bf16[128,4736]{1,0:T(8,128)(2,1)S(1)}, u32[]{:S(2)}, u32[]{:S(2)}) %collective-permute-start.1) | collective-permute-done | bytes 1212448 | tf_op jit(solution)/shard_map/ppermute | solution.py:456
  61.0 2.9 %collective-permute-done.4.refs_1_ = bf16[128,4736]{1,0:T(8,128)(2,1)S(1)} collective-permute-done((bf16[128,4736]{1,0:T(8,128)(2,1)S(1)}, bf16[128,4736]{1,0:T(8,128)(2,1)S(1)}, u32[]{:S(2)}, u32[]{:S(2)}) %collective-permute-start.4) | collective-permute-done | bytes 1212448 | tf_op jit(solution)/shard_map/ppermute | solution.py:452
  63.9 5.8 %shard_map.123 = bf16[4,64,896]{2,1,0:T(8,128)(2,1)} custom-call(bf16[128,4736]{1,0:T(8,128)(2,1)S(1)} %collective-permute-done.1.refs_0_, bf16[128,4736]{1,0:T(8,128)(2,1)S(1)} %collective-permute-done.4.refs_1_, bf16[4736,896]{1,0:T(8,128)(2,1)} %refs_2_.5), custom_call_target="tpu_custom_call" | custom-call | flops 1 | bytes 1 | tf_op jit(solution)/shard_map/pallas_call | solution.py:57
  69.8 1.6 %collective-permute-start.6 = (bf16[448,640]{1,0:T(8,128)(2,1)}, bf16[448,640]{1,0:T(8,128)(2,1)}, u32[]{:S(2)}, u32[]{:S(2)}) collective-permute-start(bf16[448,640]{1,0:T(8,128)(2,1)} %constant_dynamic-slice_fusion), channel_id=1, source_target_pairs={{0,2},{2,0},{1,3},{3,1},{4,6},{6,4},{5,7},{7,5},{8,10},{10,8},{9,1... | collective-permute-start | bytes 1720328 | tf_op jit(solution)/shard_map/ppermute | solution.py:456
  71.3 4.8 %all-to-all-start.2 = ((bf16[4,64,896]{2,1,0:T(8,128)(2,1)}), bf16[4,64,896]{2,1,0:T(8,128)(2,1)S(1)}, u32[]{:S(2)}, u32[]{:S(2)}) async-start(bf16[4,64,896]{2,1,0:T(8,128)(2,1)} %shard_map.123), calls=%async_computation.2 | async-start | bytes 917504 | tf_op jit(solution)/shard_map/all_to_all | solution.py:500
  76.9 8.3 %collective-permute-done.6.refs_2_ = bf16[448,640]{1,0:T(8,128)(2,1)} collective-permute-done((bf16[448,640]{1,0:T(8,128)(2,1)}, bf16[448,640]{1,0:T(8,128)(2,1)}, u32[]{:S(2)}, u32[]{:S(2)}) %collective-permute-start.6) | collective-permute-done | bytes 573472 | tf_op jit(solution)/shard_map/ppermute | solution.py:456
  86.7 2.6 %all-to-all-done.2.refs_1_ = bf16[4,64,896]{2,1,0:T(8,128)(2,1)S(1)} async-done(((bf16[4,64,896]{2,1,0:T(8,128)(2,1)}), bf16[4,64,896]{2,1,0:T(8,128)(2,1)S(1)}, u32[]{:S(2)}, u32[]{:S(2)}) %all-to-all-start.2) | async-done | bytes 458784 | tf_op jit(solution)/shard_map/all_to_all | solution.py:500
  93.2 1.7 %collective-permute-start.5 = (bf16[48,896]{1,0:T(8,128)(2,1)}, bf16[48,896]{1,0:T(8,128)(2,1)S(1)}, u32[]{:S(2)}, u32[]{:S(2)}) collective-permute-start(bf16[48,896]{1,0:T(8,128)(2,1)} %get-tuple-element.25), channel_id=1, source_target_pairs={{0,0},{1,5},{2,10},{3,15},{4,1},{5,4},{6,11},{7,14},{8,2},{9,7},{1... | collective-permute-start | bytes 258056 | tf_op jit(solution)/shard_map/ppermute | solution.py:507
  94.8 1.9 %collective-permute-start.8 = (bf16[48,896]{1,0:T(8,128)(2,1)}, bf16[48,896]{1,0:T(8,128)(2,1)S(1)}, u32[]{:S(2)}, u32[]{:S(2)}) collective-permute-start(bf16[48,896]{1,0:T(8,128)(2,1)} %copy-done.7), channel_id=1, source_target_pairs={{0,1},{1,4},{2,11},{3,14},{4,0},{5,5},{6,10},{7,15},{8,3},{9,6},{1... | collective-permute-start | bytes 258056 | tf_op jit(solution)/shard_map/ppermute | solution.py:507
  96.8 3.9 %collective-permute-start.9 = (bf16[48,896]{1,0:T(8,128)(2,1)}, bf16[48,896]{1,0:T(8,128)(2,1)S(1)}, u32[]{:S(2)}, u32[]{:S(2)}) collective-permute-start(bf16[48,896]{1,0:T(8,128)(2,1)} %copy-done.6), channel_id=1, source_target_pairs={{0,2},{1,7},{2,8},{3,13},{4,3},{5,6},{6,9},{7,12},{8,0},{9,5},{10,... | collective-permute-start | bytes 258056 | tf_op jit(solution)/shard_map/ppermute | solution.py:507
  100.7 6.0 %collective-permute-start.10 = (bf16[48,896]{1,0:T(8,128)(2,1)S(1)}, bf16[48,896]{1,0:T(8,128)(2,1)S(1)}, u32[]{:S(2)}, u32[]{:S(2)}) collective-permute-start(bf16[48,896]{1,0:T(8,128)(2,1)S(1)} %get-tuple-element.31), channel_id=1, source_target_pairs={{0,3},{1,6},{2,9},{3,12},{4,2},{5,7},{6,8},{7,13},{8,1},{9,4},{10,... | collective-permute-start | bytes 258056 | tf_op jit(solution)/shard_map/ppermute | solution.py:507
  106.8 5.0 %collective-permute-done.9.refs_2_ = bf16[48,896]{1,0:T(8,128)(2,1)S(1)} collective-permute-done((bf16[48,896]{1,0:T(8,128)(2,1)}, bf16[48,896]{1,0:T(8,128)(2,1)S(1)}, u32[]{:S(2)}, u32[]{:S(2)}) %collective-permute-start.9) | collective-permute-done | bytes 86048 | tf_op jit(solution)/shard_map/ppermute | solution.py:507
  111.8 2.8 %shard_map.126 = (bf16[192,896]{1,0:T(8,128)(2,1)}, bf16[48,896]{1,0:T(8,128)(2,1)S(1)}, bf16[48,896]{1,0:T(8,128)(2,1)S(1)}, bf16[48,896]{1,0:T(8,128)(2,1)S(1)}, bf16[48,896]{1,0:T(8,128)(2,1)S(1)}) custom-call(s32[3]{0:T(128)S(1)} %pad_add_fusion.here_ref, s32[1,192]{1,0:T(1,128)S(1)} %copy-done.4, bf16[896,896]{1,0:T(8,128)(2,1)} %w_hbm.1, ...), custom_call_target="tpu_custom_call" | custom-call | flops 1 | bytes 1 | tf_op jit(solution)/shard_map/pallas_call | solution.py:164
  115.4 3.0 %collective-permute-start.15 = (bf16[48,896]{1,0:T(8,128)(2,1)S(1)}, bf16[48,896]{1,0:T(8,128)(2,1)S(1)}, u32[]{:S(2)}, u32[]{:S(2)}) collective-permute-start(bf16[48,896]{1,0:T(8,128)(2,1)S(1)} %get-tuple-element.37), channel_id=1, source_target_pairs={{0,8},{4,12},{8,0},{12,4},{1,9},{5,13},{9,1},{13,5},{2,10},{6,14},... | collective-permute-start | bytes 258056 | tf_op jit(solution)/shard_map/ppermute | solution.py:515
  121.3 4.1 %collective-permute-done.15.refs_8_ = bf16[48,896]{1,0:T(8,128)(2,1)S(1)} collective-permute-done((bf16[48,896]{1,0:T(8,128)(2,1)S(1)}, bf16[48,896]{1,0:T(8,128)(2,1)S(1)}, u32[]{:S(2)}, u32[]{:S(2)}) %collective-permute-start.15) | collective-permute-done | bytes 86048 | tf_op jit(solution)/shard_map/ppermute | solution.py:515
  125.3 12.1 %shard_map.127 = (bf16[48,1024]{1,0:T(8,128)(2,1)}, f32[48,1536]{1,0:T(8,128)}) custom-call(s32[3]{0:T(128)S(1)} %pad_add_fusion.here_ref, s32[48]{0:T(128)S(1)} %copy-done.5, f32[1,896]{1,0:T(1,128)S(1)} %reshape.10.gain, bf16[896,640]{1,0:T(8,128)(2,1)S(1)} %constant_dynamic-update-slice_fusion.refs_0_, ...), custom_call_target="tpu_custom_call" | custom-call | flops 1 | bytes 1 | tf_op jit(solution)/shard_map/pallas_call | solution.py:346
  (55 shorter events, 16.5 us)
Async XLA Ops:
  0.6 4.2 %collective-permute-start = (bf16[192,4736]{1,0:T(8,128)(2,1)}, bf16[192,4736]{1,0:T(8,128)(2,1)S(1)}, u32[]{:S(2)}, u32[]{:S(2)}) collective-permute-start(bf16[192,4736]{1,0:T(8,128)(2,1)} %refs_0_.1), channel_id=1, source_target_pairs={{0,1},{1,0},{2,3},{3,2},{4,5},{5,4},{6,7},{7,6},{8,9},{9,8},{10,11... | collective-permute-start | bytes 5455880 | tf_op jit(solution)/shard_map/ppermute | solution.py:452
  2.3 16.9 %collective-permute-start.2 = (bf16[64,4736]{1,0:T(8,128)(2,1)S(1)}, bf16[64,4736]{1,0:T(8,128)(2,1)S(1)}, u32[]{:S(2)}, u32[]{:S(2)}) collective-permute-start(bf16[64,4736]{1,0:T(8,128)(2,1)S(1)} %slice.7), channel_id=1, source_target_pairs={{0,2},{2,0},{1,3},{3,1},{4,6},{6,4},{5,7},{7,5},{8,10},{10,8},{9,1... | collective-permute-start | bytes 1818632 | tf_op jit(solution)/shard_map/ppermute | solution.py:456
  19.2 2.0 %collective-permute-start.3 = (bf16[64,4736]{1,0:T(8,128)(2,1)S(1)}, bf16[64,4736]{1,0:T(8,128)(2,1)S(1)}, u32[]{:S(2)}, u32[]{:S(2)}) collective-permute-start(bf16[64,4736]{1,0:T(8,128)(2,1)S(1)} %collective-permute-done.2.refs_0_), channel_id=1, source_target_pairs={{0,1},{1,0},{2,3},{3,2},{4,5},{5,4},{6,7},{7,6},{8,9},{9,8},{10,11... | collective-permute-start | bytes 1818632 | tf_op jit(solution)/shard_map/ppermute | solution.py:452
  26.1 13.7 %all-to-all-start.1 = ((bf16[4,32,896]{2,1,0:T(8,128)(2,1)}), bf16[4,32,896]{2,1,0:T(8,128)(2,1)S(1)}, u32[]{:S(2)}, u32[]{:S(2)}) async-start(bf16[4,32,896]{2,1,0:T(8,128)(2,1)} %shard_map.122), calls=%async_computation.1 | async-start | bytes 458752 | tf_op jit(solution)/shard_map/all_to_all | solution.py:500
  32.4 12.1 %copy-start.9 = (bf16[896,128]{1,0:T(8,128)(2,1)S(1)}, bf16[896,128]{1,0:T(8,128)(2,1)}, u32[]{:S(2)}) copy-start(bf16[896,128]{1,0:T(8,128)(2,1)} %param.15) | copy-start | bytes 688132
  32.4 28.6 %collective-permute-start.1 = (bf16[128,4736]{1,0:T(8,128)(2,1)}, bf16[128,4736]{1,0:T(8,128)(2,1)S(1)}, u32[]{:S(2)}, u32[]{:S(2)}) collective-permute-start(bf16[128,4736]{1,0:T(8,128)(2,1)} %slice.6), channel_id=1, source_target_pairs={{0,2},{2,0},{1,3},{3,1},{4,6},{6,4},{5,7},{7,5},{8,10},{10,8},{9,1... | collective-permute-start | bytes 3637256 | tf_op jit(solution)/shard_map/ppermute | solution.py:456
  39.8 21.3 %all-to-all-start = ((bf16[4,96,896]{2,1,0:T(8,128)(2,1)}), bf16[4,96,896]{2,1,0:T(8,128)(2,1)S(1)}, u32[]{:S(2)}, u32[]{:S(2)}) async-start(bf16[4,96,896]{2,1,0:T(8,128)(2,1)} %shard_map.121), calls=%async_computation | async-start | bytes 1376256 | tf_op jit(solution)/shard_map/all_to_all | solution.py:491
  61.0 2.9 %collective-permute-start.4 = (bf16[128,4736]{1,0:T(8,128)(2,1)S(1)}, bf16[128,4736]{1,0:T(8,128)(2,1)S(1)}, u32[]{:S(2)}, u32[]{:S(2)}) collective-permute-start(bf16[128,4736]{1,0:T(8,128)(2,1)S(1)} %collective-permute-done.1.refs_0_), channel_id=1, source_target_pairs={{0,1},{1,0},{2,3},{3,2},{4,5},{5,4},{6,7},{7,6},{8,9},{9,8},{10,11... | collective-permute-start | bytes 3637256 | tf_op jit(solution)/shard_map/ppermute | solution.py:452
  69.8 42.0 %copy-start.4 = (s32[1,192]{1,0:T(1,128)S(1)}, s32[1,192]{1,0:T(1,128)}, u32[]{:S(2)}) copy-start(s32[1,192]{1,0:T(1,128)} %slots.1) | copy-start | bytes 2308
  69.8 15.4 %collective-permute-start.6 = (bf16[448,640]{1,0:T(8,128)(2,1)}, bf16[448,640]{1,0:T(8,128)(2,1)}, u32[]{:S(2)}, u32[]{:S(2)}) collective-permute-start(bf16[448,640]{1,0:T(8,128)(2,1)} %constant_dynamic-slice_fusion), channel_id=1, source_target_pairs={{0,2},{2,0},{1,3},{3,1},{4,6},{6,4},{5,7},{7,5},{8,10},{10,8},{9,1... | collective-permute-start | bytes 1720328 | tf_op jit(solution)/shard_map/ppermute | solution.py:456
  71.3 17.9 %all-to-all-start.2 = ((bf16[4,64,896]{2,1,0:T(8,128)(2,1)}), bf16[4,64,896]{2,1,0:T(8,128)(2,1)S(1)}, u32[]{:S(2)}, u32[]{:S(2)}) async-start(bf16[4,64,896]{2,1,0:T(8,128)(2,1)} %shard_map.123), calls=%async_computation.2 | async-start | bytes 917504 | tf_op jit(solution)/shard_map/all_to_all | solution.py:500
  76.2 42.2 %collective-permute-start.11 = (bf16[896,640]{1,0:T(8,128)(2,1)S(1)}, bf16[896,640]{1,0:T(8,128)(2,1)S(1)}, u32[]{:S(2)}, u32[]{:S(2)}) collective-permute-start(bf16[896,640]{1,0:T(8,128)(2,1)S(1)} %constant_dynamic-update-slice_fusion.refs_0_), channel_id=1, source_target_pairs={{0,1},{1,0},{2,3},{3,2},{4,5},{5,4},{6,7},{7,6},{8,9},{9,8},{10,11... | collective-permute-start | bytes 3440648 | tf_op jit(solution)/shard_map/ppermute | solution.py:452
  85.2 21.5 %collective-permute-start.7 = (bf16[448,640]{1,0:T(8,128)(2,1)}, bf16[448,640]{1,0:T(8,128)(2,1)S(1)}, u32[]{:S(2)}, u32[]{:S(2)}) collective-permute-start(bf16[448,640]{1,0:T(8,128)(2,1)} %collective-permute-done.6.refs_2_), channel_id=1, source_target_pairs={{0,16},{16,0},{1,17},{17,1},{2,18},{18,2},{3,19},{19,3},{4,20},{20... | collective-permute-start | bytes 1720328 | tf_op jit(solution)/shard_map/ppermute | solution.py:464
  93.2 26.6 %copy-start.11 = (f32[896]{0:T(1024)S(1)}, f32[896]{0:T(1024)}, u32[]{:S(2)}) copy-start(f32[896]{0:T(1024)} %param.13) | copy-start | bytes 10756
  93.2 32.1 %copy-start.5 = (s32[48]{0:T(128)S(1)}, s32[48]{0:T(128)}, u32[]{:S(2)}) copy-start(s32[48]{0:T(128)} %len_ref.1) | copy-start | bytes 580
  93.2 7.5 %collective-permute-start.5 = (bf16[48,896]{1,0:T(8,128)(2,1)}, bf16[48,896]{1,0:T(8,128)(2,1)S(1)}, u32[]{:S(2)}, u32[]{:S(2)}) collective-permute-start(bf16[48,896]{1,0:T(8,128)(2,1)} %get-tuple-element.25), channel_id=1, source_target_pairs={{0,0},{1,5},{2,10},{3,15},{4,1},{5,4},{6,11},{7,14},{8,2},{9,7},{1... | collective-permute-start | bytes 258056 | tf_op jit(solution)/shard_map/ppermute | solution.py:507
  94.8 11.9 %collective-permute-start.8 = (bf16[48,896]{1,0:T(8,128)(2,1)}, bf16[48,896]{1,0:T(8,128)(2,1)S(1)}, u32[]{:S(2)}, u32[]{:S(2)}) collective-permute-start(bf16[48,896]{1,0:T(8,128)(2,1)} %copy-done.7), channel_id=1, source_target_pairs={{0,1},{1,4},{2,11},{3,14},{4,0},{5,5},{6,10},{7,15},{8,3},{9,6},{1... | collective-permute-start | bytes 258056 | tf_op jit(solution)/shard_map/ppermute | solution.py:507
  96.8 15.0 %collective-permute-start.9 = (bf16[48,896]{1,0:T(8,128)(2,1)}, bf16[48,896]{1,0:T(8,128)(2,1)S(1)}, u32[]{:S(2)}, u32[]{:S(2)}) collective-permute-start(bf16[48,896]{1,0:T(8,128)(2,1)} %copy-done.6), channel_id=1, source_target_pairs={{0,2},{1,7},{2,8},{3,13},{4,3},{5,6},{6,9},{7,12},{8,0},{9,5},{10,... | collective-permute-start | bytes 258056 | tf_op jit(solution)/shard_map/ppermute | solution.py:507
  100.7 11.1 %collective-permute-start.10 = (bf16[48,896]{1,0:T(8,128)(2,1)S(1)}, bf16[48,896]{1,0:T(8,128)(2,1)S(1)}, u32[]{:S(2)}, u32[]{:S(2)}) collective-permute-start(bf16[48,896]{1,0:T(8,128)(2,1)S(1)} %get-tuple-element.31), channel_id=1, source_target_pairs={{0,3},{1,6},{2,9},{3,12},{4,2},{5,7},{6,8},{7,13},{8,1},{9,4},{10,... | collective-permute-start | bytes 258056 | tf_op jit(solution)/shard_map/ppermute | solution.py:507
  106.7 13.0 %collective-permute-start.12 = (bf16[448,640]{1,0:T(8,128)(2,1)}, bf16[448,640]{1,0:T(8,128)(2,1)S(1)}, u32[]{:S(2)}, u32[]{:S(2)}) collective-permute-start(bf16[448,640]{1,0:T(8,128)(2,1)} %collective-permute-done.6.refs_2_), channel_id=1, source_target_pairs={{0,1},{1,0},{2,3},{3,2},{4,5},{5,4},{6,7},{7,6},{8,9},{9,8},{10,11... | collective-permute-start | bytes 1720328 | tf_op jit(solution)/shard_map/ppermute | solution.py:452
  114.5 10.8 %collective-permute-start.13 = (bf16[448,640]{1,0:T(8,128)(2,1)S(1)}, bf16[448,640]{1,0:T(8,128)(2,1)S(1)}, u32[]{:S(2)}, u32[]{:S(2)}) collective-permute-start(bf16[448,640]{1,0:T(8,128)(2,1)S(1)} %collective-permute-done.7.refs_3_), channel_id=1, source_target_pairs={{0,1},{1,0},{2,3},{3,2},{4,5},{5,4},{6,7},{7,6},{8,9},{9,8},{10,11... | collective-permute-start | bytes 1720328 | tf_op jit(solution)/shard_map/ppermute | solution.py:452
  115.3 5.9 %collective-permute-start.14 = (bf16[48,896]{1,0:T(8,128)(2,1)S(1)}, bf16[48,896]{1,0:T(8,128)(2,1)S(1)}, u32[]{:S(2)}, u32[]{:S(2)}) collective-permute-start(bf16[48,896]{1,0:T(8,128)(2,1)S(1)} %get-tuple-element.36), channel_id=1, source_target_pairs={{0,4},{4,0},{8,12},{12,8},{1,5},{5,1},{9,13},{13,9},{2,6},{6,2},{1... | collective-permute-start | bytes 258056 | tf_op jit(solution)/shard_map/ppermute | solution.py:515
  115.4 10.0 %collective-permute-start.15 = (bf16[48,896]{1,0:T(8,128)(2,1)S(1)}, bf16[48,896]{1,0:T(8,128)(2,1)S(1)}, u32[]{:S(2)}, u32[]{:S(2)}) collective-permute-start(bf16[48,896]{1,0:T(8,128)(2,1)S(1)} %get-tuple-element.37), channel_id=1, source_target_pairs={{0,8},{4,12},{8,0},{12,4},{1,9},{5,13},{9,1},{13,5},{2,10},{6,14},... | collective-permute-start | bytes 258056 | tf_op jit(solution)/shard_map/ppermute | solution.py:515
  118.4 6.9 %collective-permute-start.16 = (bf16[48,896]{1,0:T(8,128)(2,1)S(1)}, bf16[48,896]{1,0:T(8,128)(2,1)S(1)}, u32[]{:S(2)}, u32[]{:S(2)}) collective-permute-start(bf16[48,896]{1,0:T(8,128)(2,1)S(1)} %get-tuple-element.38), channel_id=1, source_target_pairs={{0,12},{4,8},{8,4},{12,0},{1,13},{5,9},{9,5},{13,1},{2,14},{6,10},... | collective-permute-start | bytes 258056 | tf_op jit(solution)/shard_map/ppermute | solution.py:515
  (8 other events, 18.7 us)

commit v17 on v15

--- a/solution.py
+++ b/solution.py
@@ -163,19 +163,31 @@
     )(here, slots, in_hbm(w_proj), *came)
 
 
-def page_copies(len_ref, kv_hbm, kv_ref, sem, r):
+def page_copies(len_ref, kv_hbm, kv_ref, first_sem, sem, at):
     page = kv_ref.shape[1] // PAGES
-    out = []
-    for p in range(PAGES):
-        at = pl.ds(p * page, page)
-        copy = pltpu.make_async_copy(kv_hbm.at[r, at], kv_ref.at[r, at], sem.at[r, p])
-        out.append((copy, len_ref[r] > p * page))
+    rows, first = pl.ds(at, ROW_STEP), pl.ds(0, page)
+    out = [
+        (
+            pltpu.make_async_copy(
+                kv_hbm.at[rows, first], kv_ref.at[rows, first], first_sem.at[at // ROW_STEP]
+            ),
+            None,
+            None,
+        )
+    ]
+    for r in range(ROW_STEP):
+        for p in range(1, PAGES):
+            here = pl.ds(p * page, page)
+            copy = pltpu.make_async_copy(
+                kv_hbm.at[at + r, here], kv_ref.at[at + r, here], sem.at[at + r, p]
+            )
+            out.append((copy, len_ref[at + r] > p * page, (at + r, here)))
     return out
 
 
 def talker_kernel(here_ref, len_ref, gain, *refs):
-    w_hbm, terms, refs = refs[:6], refs[6:-10], refs[-10:]
-    kv_hbm, new_kv, out_ref, kv_ref, sem, w_ref, w_sem, qkv, spreads, gathereds = refs
+    w_hbm, terms, refs = refs[:6], refs[6:-11], refs[-11:]
+    kv_hbm, new_kv, out_ref, kv_ref, first_sem, sem, w_ref, w_sem, qkv, spreads, gathereds = refs
     block, turn = here_ref[1], here_ref[2]
     blocks = qkv.shape[0]
     rows, cached, kv_width = kv_ref.shape
@@ -205,10 +217,11 @@
             w_copies[-1][-1].start()
             at += 1
 
-    @pl.loop(0, rows)
-    def _(r):
-        for p, (copy, needed) in enumerate(page_copies(len_ref, kv_hbm, kv_ref, sem, r)):
-            if p == 0:
+    @pl.loop(0, rows // ROW_STEP)
+    def _(i):
+        at = pl.multiple_of(i * ROW_STEP, ROW_STEP)
+        for copy, needed, _ in page_copies(len_ref, kv_hbm, kv_ref, first_sem, sem, at):
+            if needed is None:
                 copy.start()
             else:
                 pl.when(needed)(copy.start)
@@ -299,21 +312,20 @@
     @pl.loop(0, rows // (sets * ROW_STEP))
     def _(i):
         first = pl.multiple_of(i * sets * ROW_STEP, sets * ROW_STEP)
-        for k in range(sets * ROW_STEP):
-            r = first + k
-            for p, (copy, needed) in enumerate(page_copies(len_ref, kv_hbm, kv_ref, sem, r)):
-                if p == 0:
+        ats = [pl.multiple_of(first + k * ROW_STEP, ROW_STEP) for k in range(sets)]
+        for at in ats:
+            for copy, needed, place in page_copies(
+                len_ref, kv_hbm, kv_ref, first_sem, sem, at
+            ):
+                if needed is None:
                     copy.wait()
                     continue
                 pl.when(needed)(copy.wait)
 
                 @pl.when(jnp.logical_not(needed))
-                def _(p=p, r=r):
-                    kv_ref[r, p * page : (p + 1) * page, :] = jnp.zeros(
-                        (page, kv_width), kv_ref.dtype
-                    )
-
-        ats = [pl.multiple_of(first + k * ROW_STEP, ROW_STEP) for k in range(sets)]
+                def _(place=place):
+                    kv_ref[place[0], place[1], :] = jnp.zeros((page, kv_width), kv_ref.dtype)
+
         scored = [scores_of(at, spreads.at[k]) for k, at in enumerate(ats)]
         weighed = [softmax(at, *s) for at, s in zip(ats, scored)]
         for k, at in enumerate(ats):
@@ -325,7 +337,7 @@
     wide, columns = weights[0].shape
     blocks = 4
     q_width = blocks * columns - kv_width
-    sets = 2
+    sets = 3
     vmem = pl.BlockSpec(memory_space=pltpu.VMEM)
     smem = pl.BlockSpec(memory_space=pltpu.SMEM)
     return pl.pallas_call(
@@ -341,6 +353,7 @@
         out_specs=(vmem, vmem),
         scratch_shapes=[
             pltpu.VMEM((rows, cached, kv_width), jnp.bfloat16),
+            pltpu.SemaphoreType.DMA((rows // ROW_STEP,)),
             pltpu.SemaphoreType.DMA((rows, PAGES)),
             pltpu.VMEM((blocks, wide, columns), jnp.bfloat16),
             pltpu.SemaphoreType.DMA((len(weights),)),

time: 124 us -> 125 us (level)
  no operation moved by 1% of the time
where the time goes in v17:
time: 125 us; the launch traced here: 124 us
  waiting for transfers between devices  54.6 us (44%)
  starting transfers between devices  36.8 us (29%)
  Pallas kernels  29.7 us (24%)
  local copies, waits for them, and re-layouts  1.87 us (1%)
    ppermute x2, waiting for transfers between devices, over_section(): return lax.ppermute(x, 'section', [(0, 1), (1, 0)])  37.4 us
    pallas_call x2, Pallas kernels, down(): pl.pallas_call(functools.partial(down_kernel, planes, list(zip(ends[:-1],...  14.4 us
    ppermute x4, starting transfers between devices, four_planes(): lax.ppermute(x, GROUP, [(p * 4 + b, b * 4 + (b ^ p ^ k)) for p in range(4...  14 us
    pallas_call x1, Pallas kernels, talker(): pl.pallas_call(talker_kernel, out_shape=(jax.ShapeDtypeStruct((rows, kv_w...  12.3 us
    all_to_all x1, starting transfers between devices, four_planes(): near_terms = lax.all_to_all(near, 'mp', 0, 0)  6.38 us
    ppermute x3, waiting for transfers between devices, four_planes(): lax.ppermute(projected[d], 'mp', [(p, p ^ d) for p in range(planes)])  5.53 us
    all_to_all x1, starting transfers between devices, four_planes(): far_terms = lax.all_to_all(far, 'mp', 0, 0)  5.14 us
    ppermute x5, waiting for transfers between devices, over_core(): return lax.ppermute(x, 'rows', [(0, 1), (1, 0)])  5.01 us
  transfers between devices with their start and end apart: 17, of which 8 were waited for; matrix products, arithmetic and copies ran while one was open for 1% of the time, Pallas kernels for 8%

profile of v17, /device:TPU:0, one launch (start us, length us, event | category | flops | bytes accessed | tf_op | source)
XLA Modules:
  0.0 124.1 jit_solution(8051964067695121816)
XLA Ops:
  1.1 2.6 %collective-permute-start = (bf16[192,4736]{1,0:T(8,128)(2,1)}, bf16[192,4736]{1,0:T(8,128)(2,1)}, u32[]{:S(2)}, u32[]{:S(2)}) collective-permute-start(bf16[192,4736]{1,0:T(8,128)(2,1)} %refs_0_.1), channel_id=1, source_target_pairs={{0,2},{2,0},{1,3},{3,1},{4,6},{6,4},{5,7},{7,5},{8,10},{10,8},{9,1... | collective-permute-start | bytes 5455880 | tf_op jit(solution)/shard_map/ppermute | solution.py:454
  3.7 1.0 collective-permute-done.1.refs_1_
  4.7 7.2 %shard_map.121 = bf16[4,96,896]{2,1,0:T(8,128)(2,1)} custom-call(bf16[192,4736]{1,0:T(8,128)(2,1)} %refs_0_.1, bf16[192,4736]{1,0:T(8,128)(2,1)S(1)} %collective-permute-done.1.refs_1_, bf16[4736,896]{1,0:T(8,128)(2,1)} %refs_2_.3), custom_call_target="tpu_custom_call" | custom-call | flops 1 | bytes 1 | tf_op jit(solution)/shard_map/pallas_call | solution.py:54
  12.0 6.4 %all-to-all-start = ((bf16[4,96,896]{2,1,0:T(8,128)(2,1)}), bf16[4,96,896]{2,1,0:T(8,128)(2,1)S(1)}, u32[]{:S(2)}, u32[]{:S(2)}) async-start(bf16[4,96,896]{2,1,0:T(8,128)(2,1)} %shard_map.121), calls=%async_computation | async-start | bytes 1376256 | tf_op jit(solution)/shard_map/all_to_all | solution.py:487
  19.4 0.9 constant_dynamic-slice_fusion
  20.2 24.0 %collective-permute-done.refs_0_ = bf16[192,4736]{1,0:T(8,128)(2,1)} collective-permute-done((bf16[192,4736]{1,0:T(8,128)(2,1)}, bf16[192,4736]{1,0:T(8,128)(2,1)}, u32[]{:S(2)}, u32[]{:S(2)}) %collective-permute-start) | collective-permute-done | bytes 1818656 | tf_op jit(solution)/shard_map/ppermute | solution.py:454
  44.3 4.0 %collective-permute-done.2.refs_1_ = bf16[192,4736]{1,0:T(8,128)(2,1)S(1)} collective-permute-done((bf16[192,4736]{1,0:T(8,128)(2,1)}, bf16[192,4736]{1,0:T(8,128)(2,1)S(1)}, u32[]{:S(2)}, u32[]{:S(2)}) %collective-permute-start.2) | collective-permute-done | bytes 1818656 | tf_op jit(solution)/shard_map/ppermute | solution.py:450
  48.3 7.2 %shard_map.122 = bf16[4,96,896]{2,1,0:T(8,128)(2,1)} custom-call(bf16[192,4736]{1,0:T(8,128)(2,1)} %collective-permute-done.refs_0_, bf16[192,4736]{1,0:T(8,128)(2,1)S(1)} %collective-permute-done.2.refs_1_, bf16[4736,896]{1,0:T(8,128)(2,1)} %refs_2_.3), custom_call_target="tpu_custom_call" | custom-call | flops 1 | bytes 1 | tf_op jit(solution)/shard_map/pallas_call | solution.py:54
  55.5 5.1 %all-to-all-start.1 = ((bf16[4,96,896]{2,1,0:T(8,128)(2,1)}), bf16[4,96,896]{2,1,0:T(8,128)(2,1)S(1)}, u32[]{:S(2)}, u32[]{:S(2)}) async-start(bf16[4,96,896]{2,1,0:T(8,128)(2,1)} %shard_map.122), calls=%async_computation.1 | async-start | bytes 1376256 | tf_op jit(solution)/shard_map/all_to_all | solution.py:496
  60.6 1.5 %collective-permute-start.4 = (bf16[448,640]{1,0:T(8,128)(2,1)}, bf16[448,640]{1,0:T(8,128)(2,1)S(1)}, u32[]{:S(2)}, u32[]{:S(2)}) collective-permute-start(bf16[448,640]{1,0:T(8,128)(2,1)} %constant_dynamic-slice_fusion), channel_id=1, source_target_pairs={{0,2},{2,0},{1,3},{3,1},{4,6},{6,4},{5,7},{7,5},{8,10},{10,8},{9,1... | collective-permute-start | bytes 1720328 | tf_op jit(solution)/shard_map/ppermute | solution.py:454
  62.2 13.4 %collective-permute-done.4.refs_2_ = bf16[448,640]{1,0:T(8,128)(2,1)S(1)} collective-permute-done((bf16[448,640]{1,0:T(8,128)(2,1)}, bf16[448,640]{1,0:T(8,128)(2,1)S(1)}, u32[]{:S(2)}, u32[]{:S(2)}) %collective-permute-start.4) | collective-permute-done | bytes 573472 | tf_op jit(solution)/shard_map/ppermute | solution.py:454
  75.6 1.5 %collective-permute-start.5 = (bf16[448,640]{1,0:T(8,128)(2,1)S(1)}, bf16[448,640]{1,0:T(8,128)(2,1)S(1)}, u32[]{:S(2)}, u32[]{:S(2)}) collective-permute-start(bf16[448,640]{1,0:T(8,128)(2,1)S(1)} %collective-permute-done.4.refs_2_), channel_id=1, source_target_pairs={{0,16},{16,0},{1,17},{17,1},{2,18},{18,2},{3,19},{19,3},{4,20},{20... | collective-permute-start | bytes 1720328 | tf_op jit(solution)/shard_map/ppermute | solution.py:462
  77.1 1.8 %all-to-all-done.1.terms = bf16[4,96,896]{2,1,0:T(8,128)(2,1)S(1)} async-done(((bf16[4,96,896]{2,1,0:T(8,128)(2,1)}), bf16[4,96,896]{2,1,0:T(8,128)(2,1)S(1)}, u32[]{:S(2)}, u32[]{:S(2)}) %all-to-all-start.1) | async-done | bytes 688160 | tf_op jit(solution)/shard_map/all_to_all | solution.py:496
  79.8 2.3 %collective-permute-start.6 = (bf16[48,896]{1,0:T(8,128)(2,1)S(1)}, bf16[48,896]{1,0:T(8,128)(2,1)S(1)}, u32[]{:S(2)}, u32[]{:S(2)}) collective-permute-start(bf16[48,896]{1,0:T(8,128)(2,1)S(1)} %get-tuple-element.32), channel_id=1, source_target_pairs={{0,1},{1,4},{2,11},{3,14},{4,0},{5,5},{6,10},{7,15},{8,3},{9,6},{1... | collective-permute-start | bytes 258056 | tf_op jit(solution)/shard_map/ppermute | solution.py:502
  82.1 5.1 %collective-permute-start.7 = (bf16[48,896]{1,0:T(8,128)(2,1)S(1)}, bf16[48,896]{1,0:T(8,128)(2,1)S(1)}, u32[]{:S(2)}, u32[]{:S(2)}) collective-permute-start(bf16[48,896]{1,0:T(8,128)(2,1)S(1)} %get-tuple-element.33), channel_id=1, source_target_pairs={{0,2},{1,7},{2,8},{3,13},{4,3},{5,6},{6,9},{7,12},{8,0},{9,5},{10,... | collective-permute-start | bytes 258056 | tf_op jit(solution)/shard_map/ppermute | solution.py:502
  87.2 6.0 %collective-permute-start.8 = (bf16[48,896]{1,0:T(8,128)(2,1)S(1)}, bf16[48,896]{1,0:T(8,128)(2,1)S(1)}, u32[]{:S(2)}, u32[]{:S(2)}) collective-permute-start(bf16[48,896]{1,0:T(8,128)(2,1)S(1)} %get-tuple-element.34), channel_id=1, source_target_pairs={{0,3},{1,6},{2,9},{3,12},{4,2},{5,7},{6,8},{7,13},{8,1},{9,4},{10,... | collective-permute-start | bytes 258056 | tf_op jit(solution)/shard_map/ppermute | solution.py:502
  93.3 4.8 %collective-permute-done.7.refs_2_ = bf16[48,896]{1,0:T(8,128)(2,1)S(1)} collective-permute-done((bf16[48,896]{1,0:T(8,128)(2,1)S(1)}, bf16[48,896]{1,0:T(8,128)(2,1)S(1)}, u32[]{:S(2)}, u32[]{:S(2)}) %collective-permute-start.7) | collective-permute-done | bytes 86048 | tf_op jit(solution)/shard_map/ppermute | solution.py:502
  98.1 2.8 %shard_map.125 = (bf16[192,896]{1,0:T(8,128)(2,1)}, bf16[48,896]{1,0:T(8,128)(2,1)S(1)}, bf16[48,896]{1,0:T(8,128)(2,1)S(1)}, bf16[48,896]{1,0:T(8,128)(2,1)S(1)}, bf16[48,896]{1,0:T(8,128)(2,1)S(1)}) custom-call(s32[3]{0:T(128)S(1)} %pad_add_fusion.here_ref, s32[1,192]{1,0:T(1,128)S(1)} %copy-done, bf16[896,896]{1,0:T(8,128)(2,1)} %w_hbm.1, ...), custom_call_target="tpu_custom_call" | custom-call | flops 1 | bytes 1 | tf_op jit(solution)/shard_map/pallas_call | solution.py:149
  100.9 0.8 collective-permute-start.11
  101.7 3.0 %collective-permute-start.13 = (bf16[48,896]{1,0:T(8,128)(2,1)S(1)}, bf16[48,896]{1,0:T(8,128)(2,1)S(1)}, u32[]{:S(2)}, u32[]{:S(2)}) collective-permute-start(bf16[48,896]{1,0:T(8,128)(2,1)S(1)} %get-tuple-element.41), channel_id=1, source_target_pairs={{0,8},{4,12},{8,0},{12,4},{1,9},{5,13},{9,1},{13,5},{2,10},{6,14},... | collective-permute-start | bytes 258056 | tf_op jit(solution)/shard_map/ppermute | solution.py:510
  104.7 1.4 %collective-permute-start.14 = (bf16[48,896]{1,0:T(8,128)(2,1)S(1)}, bf16[48,896]{1,0:T(8,128)(2,1)S(1)}, u32[]{:S(2)}, u32[]{:S(2)}) collective-permute-start(bf16[48,896]{1,0:T(8,128)(2,1)S(1)} %get-tuple-element.42), channel_id=1, source_target_pairs={{0,12},{4,8},{8,4},{12,0},{1,13},{5,9},{9,5},{13,1},{2,14},{6,10},... | collective-permute-start | bytes 258056 | tf_op jit(solution)/shard_map/ppermute | solution.py:510
  106.1 1.5 %collective-permute-done.12.refs_7_ = bf16[48,896]{1,0:T(8,128)(2,1)S(1)} collective-permute-done((bf16[48,896]{1,0:T(8,128)(2,1)S(1)}, bf16[48,896]{1,0:T(8,128)(2,1)S(1)}, u32[]{:S(2)}, u32[]{:S(2)}) %collective-permute-start.12) | collective-permute-done | bytes 86048 | tf_op jit(solution)/shard_map/ppermute | solution.py:510
  107.6 4.0 %collective-permute-done.13.refs_8_ = bf16[48,896]{1,0:T(8,128)(2,1)S(1)} collective-permute-done((bf16[48,896]{1,0:T(8,128)(2,1)S(1)}, bf16[48,896]{1,0:T(8,128)(2,1)S(1)}, u32[]{:S(2)}, u32[]{:S(2)}) %collective-permute-start.13) | collective-permute-done | bytes 86048 | tf_op jit(solution)/shard_map/ppermute | solution.py:510
  111.6 12.3 %shard_map.126 = (bf16[48,1024]{1,0:T(8,128)(2,1)}, f32[48,1536]{1,0:T(8,128)}) custom-call(s32[3]{0:T(128)S(1)} %pad_add_fusion.here_ref, s32[48]{0:T(128)S(1)} %copy-done.1, f32[1,896]{1,0:T(1,128)S(1)} %reshape.10.gain, bf16[896,640]{1,0:T(8,128)(2,1)S(1)} %constant_dynamic-update-slice_fusion.refs_0_, bf16[896,640]{1,0:T(8,128)(2,1)} %collective-permute-done.9.refs_1_, ...), custom_call_target="tpu_custom_call" | custom-call | flops 1 | bytes 1 | tf_op jit(solution)/shard_map/pallas_call | solution.py:343
  (34 shorter events, 2.6 us)
Async XLA Ops:
  0.6 4.1 %collective-permute-start.1 = (bf16[192,4736]{1,0:T(8,128)(2,1)}, bf16[192,4736]{1,0:T(8,128)(2,1)S(1)}, u32[]{:S(2)}, u32[]{:S(2)}) collective-permute-start(bf16[192,4736]{1,0:T(8,128)(2,1)} %refs_0_.1), channel_id=1, source_target_pairs={{0,1},{1,0},{2,3},{3,2},{4,5},{5,4},{6,7},{7,6},{8,9},{9,8},{10,11... | collective-permute-start | bytes 5455880 | tf_op jit(solution)/shard_map/ppermute | solution.py:450
  1.1 43.1 %collective-permute-start = (bf16[192,4736]{1,0:T(8,128)(2,1)}, bf16[192,4736]{1,0:T(8,128)(2,1)}, u32[]{:S(2)}, u32[]{:S(2)}) collective-permute-start(bf16[192,4736]{1,0:T(8,128)(2,1)} %refs_0_.1), channel_id=1, source_target_pairs={{0,2},{2,0},{1,3},{3,1},{4,6},{6,4},{5,7},{7,5},{8,10},{10,8},{9,1... | collective-permute-start | bytes 5455880 | tf_op jit(solution)/shard_map/ppermute | solution.py:454
  12.0 6.4 %copy-start.2 = (bf16[896,384]{1,0:T(8,128)(2,1)S(1)}, bf16[896,384]{1,0:T(8,128)(2,1)}, u32[]{:S(2)}) copy-start(bf16[896,384]{1,0:T(8,128)(2,1)} %param.14) | copy-start | bytes 2064388
  12.0 6.5 %copy-start.3 = (bf16[896,128]{1,0:T(8,128)(2,1)S(1)}, bf16[896,128]{1,0:T(8,128)(2,1)}, u32[]{:S(2)}) copy-start(bf16[896,128]{1,0:T(8,128)(2,1)} %param.15) | copy-start | bytes 688132
  12.0 32.3 %all-to-all-start = ((bf16[4,96,896]{2,1,0:T(8,128)(2,1)}), bf16[4,96,896]{2,1,0:T(8,128)(2,1)S(1)}, u32[]{:S(2)}, u32[]{:S(2)}) async-start(bf16[4,96,896]{2,1,0:T(8,128)(2,1)} %shard_map.121), calls=%async_computation | async-start | bytes 1376256 | tf_op jit(solution)/shard_map/all_to_all | solution.py:487
  18.4 0.9 copy-start.4
  44.3 4.0 %collective-permute-start.2 = (bf16[192,4736]{1,0:T(8,128)(2,1)}, bf16[192,4736]{1,0:T(8,128)(2,1)S(1)}, u32[]{:S(2)}, u32[]{:S(2)}) collective-permute-start(bf16[192,4736]{1,0:T(8,128)(2,1)} %collective-permute-done.refs_0_), channel_id=1, source_target_pairs={{0,1},{1,0},{2,3},{3,2},{4,5},{5,4},{6,7},{7,6},{8,9},{9,8},{10,11... | collective-permute-start | bytes 5455880 | tf_op jit(solution)/shard_map/ppermute | solution.py:450
  55.5 23.5 %all-to-all-start.1 = ((bf16[4,96,896]{2,1,0:T(8,128)(2,1)}), bf16[4,96,896]{2,1,0:T(8,128)(2,1)S(1)}, u32[]{:S(2)}, u32[]{:S(2)}) async-start(bf16[4,96,896]{2,1,0:T(8,128)(2,1)} %shard_map.122), calls=%async_computation.1 | async-start | bytes 1376256 | tf_op jit(solution)/shard_map/all_to_all | solution.py:496
  60.6 37.5 %copy-start = (s32[1,192]{1,0:T(1,128)S(1)}, s32[1,192]{1,0:T(1,128)}, u32[]{:S(2)}) copy-start(s32[1,192]{1,0:T(1,128)} %slots.1) | copy-start | bytes 2308
  60.6 15.0 %collective-permute-start.4 = (bf16[448,640]{1,0:T(8,128)(2,1)}, bf16[448,640]{1,0:T(8,128)(2,1)S(1)}, u32[]{:S(2)}, u32[]{:S(2)}) collective-permute-start(bf16[448,640]{1,0:T(8,128)(2,1)} %constant_dynamic-slice_fusion), channel_id=1, source_target_pairs={{0,2},{2,0},{1,3},{3,1},{4,6},{6,4},{5,7},{7,5},{8,10},{10,8},{9,1... | collective-permute-start | bytes 1720328 | tf_op jit(solution)/shard_map/ppermute | solution.py:454
  62.1 42.5 %collective-permute-start.9 = (bf16[896,640]{1,0:T(8,128)(2,1)S(1)}, bf16[896,640]{1,0:T(8,128)(2,1)}, u32[]{:S(2)}, u32[]{:S(2)}) collective-permute-start(bf16[896,640]{1,0:T(8,128)(2,1)S(1)} %constant_dynamic-update-slice_fusion.refs_0_), channel_id=1, source_target_pairs={{0,1},{1,0},{2,3},{3,2},{4,5},{5,4},{6,7},{7,6},{8,9},{9,8},{10,11... | collective-permute-start | bytes 3440648 | tf_op jit(solution)/shard_map/ppermute | solution.py:450
  75.6 17.7 %collective-permute-start.5 = (bf16[448,640]{1,0:T(8,128)(2,1)S(1)}, bf16[448,640]{1,0:T(8,128)(2,1)S(1)}, u32[]{:S(2)}, u32[]{:S(2)}) collective-permute-start(bf16[448,640]{1,0:T(8,128)(2,1)S(1)} %collective-permute-done.4.refs_2_), channel_id=1, source_target_pairs={{0,16},{16,0},{1,17},{17,1},{2,18},{18,2},{3,19},{19,3},{4,20},{20... | collective-permute-start | bytes 1720328 | tf_op jit(solution)/shard_map/ppermute | solution.py:462
  79.1 27.0 %copy-start.5 = (f32[896]{0:T(1024)S(1)}, f32[896]{0:T(1024)}, u32[]{:S(2)}) copy-start(f32[896]{0:T(1024)} %param.13) | copy-start | bytes 10756
  79.1 32.5 %copy-start.1 = (s32[48]{0:T(128)S(1)}, s32[48]{0:T(128)}, u32[]{:S(2)}) copy-start(s32[48]{0:T(128)} %len_ref.1) | copy-start | bytes 580
  79.1 8.1 %collective-permute-start.3 = (bf16[48,896]{1,0:T(8,128)(2,1)S(1)}, bf16[48,896]{1,0:T(8,128)(2,1)S(1)}, u32[]{:S(2)}, u32[]{:S(2)}) collective-permute-start(bf16[48,896]{1,0:T(8,128)(2,1)S(1)} %get-tuple-element.27), channel_id=1, source_target_pairs={{0,0},{1,5},{2,10},{3,15},{4,1},{5,4},{6,11},{7,14},{8,2},{9,7},{1... | collective-permute-start | bytes 258056 | tf_op jit(solution)/shard_map/ppermute | solution.py:502
  79.8 13.5 %collective-permute-start.6 = (bf16[48,896]{1,0:T(8,128)(2,1)S(1)}, bf16[48,896]{1,0:T(8,128)(2,1)S(1)}, u32[]{:S(2)}, u32[]{:S(2)}) collective-permute-start(bf16[48,896]{1,0:T(8,128)(2,1)S(1)} %get-tuple-element.32), channel_id=1, source_target_pairs={{0,1},{1,4},{2,11},{3,14},{4,0},{5,5},{6,10},{7,15},{8,3},{9,6},{1... | collective-permute-start | bytes 258056 | tf_op jit(solution)/shard_map/ppermute | solution.py:502
  82.1 16.0 %collective-permute-start.7 = (bf16[48,896]{1,0:T(8,128)(2,1)S(1)}, bf16[48,896]{1,0:T(8,128)(2,1)S(1)}, u32[]{:S(2)}, u32[]{:S(2)}) collective-permute-start(bf16[48,896]{1,0:T(8,128)(2,1)S(1)} %get-tuple-element.33), channel_id=1, source_target_pairs={{0,2},{1,7},{2,8},{3,13},{4,3},{5,6},{6,9},{7,12},{8,0},{9,5},{10,... | collective-permute-start | bytes 258056 | tf_op jit(solution)/shard_map/ppermute | solution.py:502
  87.2 10.9 %collective-permute-start.8 = (bf16[48,896]{1,0:T(8,128)(2,1)S(1)}, bf16[48,896]{1,0:T(8,128)(2,1)S(1)}, u32[]{:S(2)}, u32[]{:S(2)}) collective-permute-start(bf16[48,896]{1,0:T(8,128)(2,1)S(1)} %get-tuple-element.34), channel_id=1, source_target_pairs={{0,3},{1,6},{2,9},{3,12},{4,2},{5,7},{6,8},{7,13},{8,1},{9,4},{10,... | collective-permute-start | bytes 258056 | tf_op jit(solution)/shard_map/ppermute | solution.py:502
  93.2 12.8 %collective-permute-start.10 = (bf16[448,640]{1,0:T(8,128)(2,1)S(1)}, bf16[448,640]{1,0:T(8,128)(2,1)S(1)}, u32[]{:S(2)}, u32[]{:S(2)}) collective-permute-start(bf16[448,640]{1,0:T(8,128)(2,1)S(1)} %collective-permute-done.4.refs_2_), channel_id=1, source_target_pairs={{0,1},{1,0},{2,3},{3,2},{4,5},{5,4},{6,7},{7,6},{8,9},{9,8},{10,11... | collective-permute-start | bytes 1720328 | tf_op jit(solution)/shard_map/ppermute | solution.py:450
  100.9 10.7 %collective-permute-start.11 = (bf16[448,640]{1,0:T(8,128)(2,1)S(1)}, bf16[448,640]{1,0:T(8,128)(2,1)S(1)}, u32[]{:S(2)}, u32[]{:S(2)}) collective-permute-start(bf16[448,640]{1,0:T(8,128)(2,1)S(1)} %collective-permute-done.5.refs_3_), channel_id=1, source_target_pairs={{0,1},{1,0},{2,3},{3,2},{4,5},{5,4},{6,7},{7,6},{8,9},{9,8},{10,11... | collective-permute-start | bytes 1720328 | tf_op jit(solution)/shard_map/ppermute | solution.py:450
  101.7 5.9 %collective-permute-start.12 = (bf16[48,896]{1,0:T(8,128)(2,1)S(1)}, bf16[48,896]{1,0:T(8,128)(2,1)S(1)}, u32[]{:S(2)}, u32[]{:S(2)}) collective-permute-start(bf16[48,896]{1,0:T(8,128)(2,1)S(1)} %get-tuple-element.40), channel_id=1, source_target_pairs={{0,4},{4,0},{8,12},{12,8},{1,5},{5,1},{9,13},{13,9},{2,6},{6,2},{1... | collective-permute-start | bytes 258056 | tf_op jit(solution)/shard_map/ppermute | solution.py:510
  101.7 9.9 %collective-permute-start.13 = (bf16[48,896]{1,0:T(8,128)(2,1)S(1)}, bf16[48,896]{1,0:T(8,128)(2,1)S(1)}, u32[]{:S(2)}, u32[]{:S(2)}) collective-permute-start(bf16[48,896]{1,0:T(8,128)(2,1)S(1)} %get-tuple-element.41), channel_id=1, source_target_pairs={{0,8},{4,12},{8,0},{12,4},{1,9},{5,13},{9,1},{13,5},{2,10},{6,14},... | collective-permute-start | bytes 258056 | tf_op jit(solution)/shard_map/ppermute | solution.py:510
  104.7 6.9 %collective-permute-start.14 = (bf16[48,896]{1,0:T(8,128)(2,1)S(1)}, bf16[48,896]{1,0:T(8,128)(2,1)S(1)}, u32[]{:S(2)}, u32[]{:S(2)}) collective-permute-start(bf16[48,896]{1,0:T(8,128)(2,1)S(1)} %get-tuple-element.42), channel_id=1, source_target_pairs={{0,12},{4,8},{8,4},{12,0},{1,13},{5,9},{9,5},{13,1},{2,14},{6,10},... | collective-permute-start | bytes 258056 | tf_op jit(solution)/shard_map/ppermute | solution.py:510

commit v18 on v15

--- a/solution.py
+++ b/solution.py
@@ -93,25 +93,28 @@
     for k in range(1, terms.shape[0]):
         total = total + terms[k].astype(jnp.float32)
     rows = sums.shape[1]
-    half = len(outs) // 2
+    half = sums.shape[0] // 2
     for e in range(half):
         sums[e] = near[e * rows : (e + 1) * rows, :]
         sums[half + e] = total[e * rows : (e + 1) * rows].astype(jnp.bfloat16)
+    low = plane_ref[0] & 1
     for k, out in enumerate(outs):
-        out[...] = sums[plane_ref[0] ^ k]
+        section = (plane_ref[0] // 2) ^ k
+        out[0] = sums[2 * section + low]
+        out[1] = sums[2 * section + 1 - low]
 
 
 def add_and_deal(plane, near, terms):
     rows, columns = near.shape
     blocks = 4
-    part = jax.ShapeDtypeStruct((2 * rows // blocks, columns), jnp.bfloat16)
+    pair = jax.ShapeDtypeStruct((2, 2 * rows // blocks, columns), jnp.bfloat16)
     vmem = pl.BlockSpec(memory_space=pltpu.VMEM)
     return pl.pallas_call(
         add_and_deal_kernel,
-        out_shape=(part,) * blocks,
+        out_shape=(pair,) * 2,
         in_specs=[pl.BlockSpec(memory_space=pltpu.SMEM), vmem, vmem],
-        out_specs=(vmem,) * blocks,
-        scratch_shapes=[pltpu.VMEM((blocks, *part.shape), jnp.bfloat16)],
+        out_specs=(vmem,) * 2,
+        scratch_shapes=[pltpu.VMEM((blocks, *pair.shape[1:]), jnp.bfloat16)],
         cost_estimate=SHORT,
         compiler_params=pltpu.CompilerParams(vmem_limit_bytes=16 * 1024 * 1024),
     )(plane, near, terms)
@@ -123,7 +126,8 @@
     plane, block = here_ref[0], here_ref[1]
     copies = [pltpu.make_async_copy(w_hbm, w, w_sem)]
     for k in range(planes):
-        copies.append(pltpu.make_async_copy(came[k], parts.at[plane ^ block ^ k], sem.at[k]))
+        mine = came[k].at[k % 2]
+        copies.append(pltpu.make_async_copy(mine, parts.at[plane ^ block ^ k], sem.at[k]))
     for copy in copies:
         copy.start()
     for copy in copies:
@@ -143,7 +147,7 @@
 
 def project(here, slots, w_proj, came):
     planes = len(came)
-    rows, columns = came[0].shape
+    _, rows, columns = came[0].shape
     vmem = pl.BlockSpec(memory_space=pltpu.VMEM)
     made = jax.ShapeDtypeStruct((rows, w_proj.shape[1]), jnp.bfloat16)
     return pl.pallas_call(
@@ -485,10 +489,11 @@
     my_half = over_section(after(my_half, far))
     near_sums = add(after(near_terms, far))
 
-    came = [
-        lax.ppermute(x, GROUP, [(p * 4 + b, b * 4 + (b ^ p ^ k)) for p in range(4) for b in range(4)])
-        for k, x in enumerate(add_and_deal(plane, near_sums, far_terms))
-    ]
+    came = []
+    for k, pair in enumerate(add_and_deal(plane, near_sums, far_terms)):
+        route = [(p * 4 + b, b * 4 + (b ^ p ^ (2 * k))) for p in range(4) for b in range(4)]
+        pair = lax.ppermute(pair, GROUP, route)
+        came += [pair, over_core(pair)]
     my_half = after(my_half, near_sums)
     came[0], other_half = lax.optimization_barrier((came[0], over_groups(my_half)))
     thinker_out, *projected = project(here, talker_slot, w_proj, came)

time: 124 us -> 125 us (level)
  waiting for transfers between devices: 54.6 us -> 62.7 us
  starting transfers between devices: 36.8 us -> 29.9 us
    ppermute x4 -> x2, starting transfers between devices: 14 us -> 6.3 us  [four_planes(): pair = lax.ppermute(pair, GROUP, route)]
    ppermute x4 -> x2, waiting for transfers between devices: 4.8 us -> 11.8 us  [four_planes(): pair = lax.ppermute(pair, GROUP, route)]
    ppermute x5 -> x7, waiting for transfers between devices: 5.01 us -> 5.93 us  [over_core(): return lax.ppermute(x, 'rows', [(0, 1), (1, 0)])]
  transfers between devices with their start and end apart: 17 -> 17, of which waited for: 8 -> 9; matrix products, arithmetic and copies ran while one was open for 1% -> 1% of each run, Pallas kernels for 8% -> 8%
where the time goes in v18:
time: 125 us
  waiting for transfers between devices  62.7 us (50%)
  starting transfers between devices  29.9 us (24%)
  Pallas kernels  29.4 us (24%)
  local copies, waits for them, and re-layouts  1.87 us (1%)
    ppermute x2, waiting for transfers between devices, over_section(): return lax.ppermute(x, 'section', [(0, 1), (1, 0)])  37.4 us
    pallas_call x2, Pallas kernels, down(): pl.pallas_call(functools.partial(down_kernel, planes, list(zip(ends[:-1],...  14.4 us
    pallas_call x1, Pallas kernels, talker(): pl.pallas_call(talker_kernel, out_shape=(jax.ShapeDtypeStruct((rows, kv_w...  12 us
    ppermute x2, waiting for transfers between devices, four_planes(): pair = lax.ppermute(pair, GROUP, route)  11.8 us
    all_to_all x1, starting transfers between devices, four_planes(): near_terms = lax.all_to_all(near, 'mp', 0, 0)  6.38 us
    ppermute x2, starting transfers between devices, four_planes(): pair = lax.ppermute(pair, GROUP, route)  6.3 us
    ppermute x7, waiting for transfers between devices, over_core(): return lax.ppermute(x, 'rows', [(0, 1), (1, 0)])  5.93 us
    ppermute x3, waiting for transfers between devices, four_planes(): lax.ppermute(projected[d], 'mp', [(p, p ^ d) for p in range(planes)])  5.65 us
  transfers between devices with their start and end apart: 17, of which 9 were waited for; matrix products, arithmetic and copies ran while one was open for 1% of the time, Pallas kernels for 8%

profile of v18, /device:TPU:0, one launch (start us, length us, event | category | flops | bytes accessed | tf_op | source)
XLA Modules:
  0.0 124.8 jit_solution(7208439195083144272)
XLA Ops:
  1.1 2.6 %collective-permute-start = (bf16[192,4736]{1,0:T(8,128)(2,1)}, bf16[192,4736]{1,0:T(8,128)(2,1)}, u32[]{:S(2)}, u32[]{:S(2)}) collective-permute-start(bf16[192,4736]{1,0:T(8,128)(2,1)} %refs_0_.1), channel_id=1, source_target_pairs={{0,2},{2,0},{1,3},{3,1},{4,6},{6,4},{5,7},{7,5},{8,10},{10,8},{9,1... | collective-permute-start | bytes 5455880 | tf_op jit(solution)/shard_map/ppermute | solution.py:445
  3.7 1.0 collective-permute-done.1.refs_1_
  4.7 7.2 %shard_map.121 = bf16[4,96,896]{2,1,0:T(8,128)(2,1)} custom-call(bf16[192,4736]{1,0:T(8,128)(2,1)} %refs_0_.1, bf16[192,4736]{1,0:T(8,128)(2,1)S(1)} %collective-permute-done.1.refs_1_, bf16[4736,896]{1,0:T(8,128)(2,1)} %refs_2_.3), custom_call_target="tpu_custom_call" | custom-call | flops 1 | bytes 1 | tf_op jit(solution)/shard_map/pallas_call | solution.py:54
  12.0 6.4 %all-to-all-start = ((bf16[4,96,896]{2,1,0:T(8,128)(2,1)}), bf16[4,96,896]{2,1,0:T(8,128)(2,1)S(1)}, u32[]{:S(2)}, u32[]{:S(2)}) async-start(bf16[4,96,896]{2,1,0:T(8,128)(2,1)} %shard_map.121), calls=%async_computation | async-start | bytes 1376256 | tf_op jit(solution)/shard_map/all_to_all | solution.py:478
  18.5 0.8 copy-done.4
  19.4 0.9 constant_dynamic-slice_fusion
  20.2 24.0 %collective-permute-done.refs_0_ = bf16[192,4736]{1,0:T(8,128)(2,1)} collective-permute-done((bf16[192,4736]{1,0:T(8,128)(2,1)}, bf16[192,4736]{1,0:T(8,128)(2,1)}, u32[]{:S(2)}, u32[]{:S(2)}) %collective-permute-start) | collective-permute-done | bytes 1818656 | tf_op jit(solution)/shard_map/ppermute | solution.py:445
  44.3 4.0 %collective-permute-done.2.refs_1_ = bf16[192,4736]{1,0:T(8,128)(2,1)S(1)} collective-permute-done((bf16[192,4736]{1,0:T(8,128)(2,1)}, bf16[192,4736]{1,0:T(8,128)(2,1)S(1)}, u32[]{:S(2)}, u32[]{:S(2)}) %collective-permute-start.2) | collective-permute-done | bytes 1818656 | tf_op jit(solution)/shard_map/ppermute | solution.py:441
  48.3 7.2 %shard_map.122 = bf16[4,96,896]{2,1,0:T(8,128)(2,1)} custom-call(bf16[192,4736]{1,0:T(8,128)(2,1)} %collective-permute-done.refs_0_, bf16[192,4736]{1,0:T(8,128)(2,1)S(1)} %collective-permute-done.2.refs_1_, bf16[4736,896]{1,0:T(8,128)(2,1)} %refs_2_.3), custom_call_target="tpu_custom_call" | custom-call | flops 1 | bytes 1 | tf_op jit(solution)/shard_map/pallas_call | solution.py:54
  55.5 5.1 %all-to-all-start.1 = ((bf16[4,96,896]{2,1,0:T(8,128)(2,1)}), bf16[4,96,896]{2,1,0:T(8,128)(2,1)S(1)}, u32[]{:S(2)}, u32[]{:S(2)}) async-start(bf16[4,96,896]{2,1,0:T(8,128)(2,1)} %shard_map.122), calls=%async_computation.1 | async-start | bytes 1376256 | tf_op jit(solution)/shard_map/all_to_all | solution.py:487
  60.6 1.5 %collective-permute-start.4 = (bf16[448,640]{1,0:T(8,128)(2,1)}, bf16[448,640]{1,0:T(8,128)(2,1)S(1)}, u32[]{:S(2)}, u32[]{:S(2)}) collective-permute-start(bf16[448,640]{1,0:T(8,128)(2,1)} %constant_dynamic-slice_fusion), channel_id=1, source_target_pairs={{0,2},{2,0},{1,3},{3,1},{4,6},{6,4},{5,7},{7,5},{8,10},{10,8},{9,1... | collective-permute-start | bytes 1720328 | tf_op jit(solution)/shard_map/ppermute | solution.py:445
  62.2 13.4 %collective-permute-done.4.refs_2_ = bf16[448,640]{1,0:T(8,128)(2,1)S(1)} collective-permute-done((bf16[448,640]{1,0:T(8,128)(2,1)}, bf16[448,640]{1,0:T(8,128)(2,1)S(1)}, u32[]{:S(2)}, u32[]{:S(2)}) %collective-permute-start.4) | collective-permute-done | bytes 573472 | tf_op jit(solution)/shard_map/ppermute | solution.py:445
  75.6 1.5 %collective-permute-start.5 = (bf16[448,640]{1,0:T(8,128)(2,1)S(1)}, bf16[448,640]{1,0:T(8,128)(2,1)S(1)}, u32[]{:S(2)}, u32[]{:S(2)}) collective-permute-start(bf16[448,640]{1,0:T(8,128)(2,1)S(1)} %collective-permute-done.4.refs_2_), channel_id=1, source_target_pairs={{0,16},{16,0},{1,17},{17,1},{2,18},{18,2},{3,19},{19,3},{4,20},{20... | collective-permute-start | bytes 1720328 | tf_op jit(solution)/shard_map/ppermute | solution.py:453
  77.1 1.8 %all-to-all-done.1.terms = bf16[4,96,896]{2,1,0:T(8,128)(2,1)S(1)} async-done(((bf16[4,96,896]{2,1,0:T(8,128)(2,1)}), bf16[4,96,896]{2,1,0:T(8,128)(2,1)S(1)}, u32[]{:S(2)}, u32[]{:S(2)}) %all-to-all-start.1) | async-done | bytes 688160 | tf_op jit(solution)/shard_map/all_to_all | solution.py:487
  79.8 5.6 %collective-permute-start.7 = (bf16[2,48,896]{2,1,0:T(8,128)(2,1)S(1)}, bf16[2,48,896]{2,1,0:T(8,128)(2,1)S(1)}, u32[]{:S(2)}, u32[]{:S(2)}) collective-permute-start(bf16[2,48,896]{2,1,0:T(8,128)(2,1)S(1)} %get-tuple-element.30), channel_id=1, source_target_pairs={{0,2},{1,7},{2,8},{3,13},{4,3},{5,6},{6,9},{7,12},{8,0},{9,5},{10,... | collective-permute-start | bytes 516104 | tf_op jit(solution)/shard_map/ppermute | solution.py:495
  85.4 0.8 collective-permute-start.6
  86.2 11.8 %collective-permute-done.7.refs_2_ = bf16[2,48,896]{2,1,0:T(8,128)(2,1)S(1)} collective-permute-done((bf16[2,48,896]{2,1,0:T(8,128)(2,1)S(1)}, bf16[2,48,896]{2,1,0:T(8,128)(2,1)S(1)}, u32[]{:S(2)}, u32[]{:S(2)}) %collective-permute-start.7) | collective-permute-done | bytes 172064 | tf_op jit(solution)/shard_map/ppermute | solution.py:495
  98.7 0.9 collective-permute-done.8.refs_3_
  99.6 2.8 %shard_map.125 = (bf16[192,896]{1,0:T(8,128)(2,1)}, bf16[48,896]{1,0:T(8,128)(2,1)S(1)}, bf16[48,896]{1,0:T(8,128)(2,1)S(1)}, bf16[48,896]{1,0:T(8,128)(2,1)S(1)}, bf16[48,896]{1,0:T(8,128)(2,1)S(1)}) custom-call(s32[3]{0:T(128)S(1)} %pad_add_fusion.here_ref, s32[1,192]{1,0:T(1,128)S(1)} %copy-done, bf16[896,896]{1,0:T(8,128)(2,1)} %w_hbm.1, ...), custom_call_target="tpu_custom_call" | custom-call | flops 1 | bytes 1 | tf_op jit(solution)/shard_map/pallas_call | solution.py:153
  102.6 3.0 %collective-permute-start.13 = (bf16[48,896]{1,0:T(8,128)(2,1)S(1)}, bf16[48,896]{1,0:T(8,128)(2,1)S(1)}, u32[]{:S(2)}, u32[]{:S(2)}) collective-permute-start(bf16[48,896]{1,0:T(8,128)(2,1)S(1)} %get-tuple-element.37), channel_id=1, source_target_pairs={{0,8},{4,12},{8,0},{12,4},{1,9},{5,13},{9,1},{13,5},{2,10},{6,14},... | collective-permute-start | bytes 258056 | tf_op jit(solution)/shard_map/ppermute | solution.py:502
  105.6 1.4 %collective-permute-start.14 = (bf16[48,896]{1,0:T(8,128)(2,1)S(1)}, bf16[48,896]{1,0:T(8,128)(2,1)S(1)}, u32[]{:S(2)}, u32[]{:S(2)}) collective-permute-start(bf16[48,896]{1,0:T(8,128)(2,1)S(1)} %get-tuple-element.38), channel_id=1, source_target_pairs={{0,12},{4,8},{8,4},{12,0},{1,13},{5,9},{9,5},{13,1},{2,14},{6,10},... | collective-permute-start | bytes 258056 | tf_op jit(solution)/shard_map/ppermute | solution.py:502
  107.0 1.8 %collective-permute-done.12.refs_7_ = bf16[48,896]{1,0:T(8,128)(2,1)S(1)} collective-permute-done((bf16[48,896]{1,0:T(8,128)(2,1)S(1)}, bf16[48,896]{1,0:T(8,128)(2,1)S(1)}, u32[]{:S(2)}, u32[]{:S(2)}) %collective-permute-start.12) | collective-permute-done | bytes 86048 | tf_op jit(solution)/shard_map/ppermute | solution.py:502
  108.8 3.8 %collective-permute-done.13.refs_8_ = bf16[48,896]{1,0:T(8,128)(2,1)S(1)} collective-permute-done((bf16[48,896]{1,0:T(8,128)(2,1)S(1)}, bf16[48,896]{1,0:T(8,128)(2,1)S(1)}, u32[]{:S(2)}, u32[]{:S(2)}) %collective-permute-start.13) | collective-permute-done | bytes 86048 | tf_op jit(solution)/shard_map/ppermute | solution.py:502
  112.7 12.0 %shard_map.126 = (bf16[48,1024]{1,0:T(8,128)(2,1)}, f32[48,1536]{1,0:T(8,128)}) custom-call(s32[3]{0:T(128)S(1)} %pad_add_fusion.here_ref, s32[48]{0:T(128)S(1)} %copy-done.1, f32[1,896]{1,0:T(1,128)S(1)} %reshape.10.gain, bf16[896,640]{1,0:T(8,128)(2,1)S(1)} %constant_dynamic-update-slice_fusion.refs_0_, bf16[896,640]{1,0:T(8,128)(2,1)} %collective-permute-done.9.refs_1_, ...), custom_call_target="tpu_custom_call" | custom-call | flops 1 | bytes 1 | tf_op jit(solution)/shard_map/pallas_call | solution.py:335
  (34 shorter events, 2.5 us)
Async XLA Ops:
  0.6 4.1 %collective-permute-start.1 = (bf16[192,4736]{1,0:T(8,128)(2,1)}, bf16[192,4736]{1,0:T(8,128)(2,1)S(1)}, u32[]{:S(2)}, u32[]{:S(2)}) collective-permute-start(bf16[192,4736]{1,0:T(8,128)(2,1)} %refs_0_.1), channel_id=1, source_target_pairs={{0,1},{1,0},{2,3},{3,2},{4,5},{5,4},{6,7},{7,6},{8,9},{9,8},{10,11... | collective-permute-start | bytes 5455880 | tf_op jit(solution)/shard_map/ppermute | solution.py:441
  1.1 43.1 %collective-permute-start = (bf16[192,4736]{1,0:T(8,128)(2,1)}, bf16[192,4736]{1,0:T(8,128)(2,1)}, u32[]{:S(2)}, u32[]{:S(2)}) collective-permute-start(bf16[192,4736]{1,0:T(8,128)(2,1)} %refs_0_.1), channel_id=1, source_target_pairs={{0,2},{2,0},{1,3},{3,1},{4,6},{6,4},{5,7},{7,5},{8,10},{10,8},{9,1... | collective-permute-start | bytes 5455880 | tf_op jit(solution)/shard_map/ppermute | solution.py:445
  12.0 6.4 %copy-start.2 = (bf16[896,384]{1,0:T(8,128)(2,1)S(1)}, bf16[896,384]{1,0:T(8,128)(2,1)}, u32[]{:S(2)}) copy-start(bf16[896,384]{1,0:T(8,128)(2,1)} %param.14) | copy-start | bytes 2064388
  12.0 6.5 %copy-start.3 = (bf16[896,128]{1,0:T(8,128)(2,1)S(1)}, bf16[896,128]{1,0:T(8,128)(2,1)}, u32[]{:S(2)}) copy-start(bf16[896,128]{1,0:T(8,128)(2,1)} %param.15) | copy-start | bytes 688132
  12.0 32.3 %all-to-all-start = ((bf16[4,96,896]{2,1,0:T(8,128)(2,1)}), bf16[4,96,896]{2,1,0:T(8,128)(2,1)S(1)}, u32[]{:S(2)}, u32[]{:S(2)}) async-start(bf16[4,96,896]{2,1,0:T(8,128)(2,1)} %shard_map.121), calls=%async_computation | async-start | bytes 1376256 | tf_op jit(solution)/shard_map/all_to_all | solution.py:478
  18.4 0.9 copy-start.4
  44.3 4.0 %collective-permute-start.2 = (bf16[192,4736]{1,0:T(8,128)(2,1)}, bf16[192,4736]{1,0:T(8,128)(2,1)S(1)}, u32[]{:S(2)}, u32[]{:S(2)}) collective-permute-start(bf16[192,4736]{1,0:T(8,128)(2,1)} %collective-permute-done.refs_0_), channel_id=1, source_target_pairs={{0,1},{1,0},{2,3},{3,2},{4,5},{5,4},{6,7},{7,6},{8,9},{9,8},{10,11... | collective-permute-start | bytes 5455880 | tf_op jit(solution)/shard_map/ppermute | solution.py:441
  55.5 23.5 %all-to-all-start.1 = ((bf16[4,96,896]{2,1,0:T(8,128)(2,1)}), bf16[4,96,896]{2,1,0:T(8,128)(2,1)S(1)}, u32[]{:S(2)}, u32[]{:S(2)}) async-start(bf16[4,96,896]{2,1,0:T(8,128)(2,1)} %shard_map.122), calls=%async_computation.1 | async-start | bytes 1376256 | tf_op jit(solution)/shard_map/all_to_all | solution.py:487
  60.6 39.0 %copy-start = (s32[1,192]{1,0:T(1,128)S(1)}, s32[1,192]{1,0:T(1,128)}, u32[]{:S(2)}) copy-start(s32[1,192]{1,0:T(1,128)} %slots.1) | copy-start | bytes 2308
  60.6 15.0 %collective-permute-start.4 = (bf16[448,640]{1,0:T(8,128)(2,1)}, bf16[448,640]{1,0:T(8,128)(2,1)S(1)}, u32[]{:S(2)}, u32[]{:S(2)}) collective-permute-start(bf16[448,640]{1,0:T(8,128)(2,1)} %constant_dynamic-slice_fusion), channel_id=1, source_target_pairs={{0,2},{2,0},{1,3},{3,1},{4,6},{6,4},{5,7},{7,5},{8,10},{10,8},{9,1... | collective-permute-start | bytes 1720328 | tf_op jit(solution)/shard_map/ppermute | solution.py:445
  62.1 43.5 %collective-permute-start.9 = (bf16[896,640]{1,0:T(8,128)(2,1)S(1)}, bf16[896,640]{1,0:T(8,128)(2,1)}, u32[]{:S(2)}, u32[]{:S(2)}) collective-permute-start(bf16[896,640]{1,0:T(8,128)(2,1)S(1)} %constant_dynamic-update-slice_fusion.refs_0_), channel_id=1, source_target_pairs={{0,1},{1,0},{2,3},{3,2},{4,5},{5,4},{6,7},{7,6},{8,9},{9,8},{10,11... | collective-permute-start | bytes 3440648 | tf_op jit(solution)/shard_map/ppermute | solution.py:441
  75.6 23.1 %collective-permute-start.5 = (bf16[448,640]{1,0:T(8,128)(2,1)S(1)}, bf16[448,640]{1,0:T(8,128)(2,1)S(1)}, u32[]{:S(2)}, u32[]{:S(2)}) collective-permute-start(bf16[448,640]{1,0:T(8,128)(2,1)S(1)} %collective-permute-done.4.refs_2_), channel_id=1, source_target_pairs={{0,16},{16,0},{1,17},{17,1},{2,18},{18,2},{3,19},{19,3},{4,20},{20... | collective-permute-start | bytes 1720328 | tf_op jit(solution)/shard_map/ppermute | solution.py:453
  79.1 6.3 %collective-permute-start.3 = (bf16[2,48,896]{2,1,0:T(8,128)(2,1)S(1)}, bf16[2,48,896]{2,1,0:T(8,128)(2,1)S(1)}, u32[]{:S(2)}, u32[]{:S(2)}) collective-permute-start(bf16[2,48,896]{2,1,0:T(8,128)(2,1)S(1)} %get-tuple-element.25), channel_id=1, source_target_pairs={{0,0},{1,5},{2,10},{3,15},{4,1},{5,4},{6,11},{7,14},{8,2},{9,7},{1... | collective-permute-start | bytes 516104 | tf_op jit(solution)/shard_map/ppermute | solution.py:495
  79.8 18.3 %collective-permute-start.7 = (bf16[2,48,896]{2,1,0:T(8,128)(2,1)S(1)}, bf16[2,48,896]{2,1,0:T(8,128)(2,1)S(1)}, u32[]{:S(2)}, u32[]{:S(2)}) collective-permute-start(bf16[2,48,896]{2,1,0:T(8,128)(2,1)S(1)} %get-tuple-element.30), channel_id=1, source_target_pairs={{0,2},{1,7},{2,8},{3,13},{4,3},{5,6},{6,9},{7,12},{8,0},{9,5},{10,... | collective-permute-start | bytes 516104 | tf_op jit(solution)/shard_map/ppermute | solution.py:495
  85.4 13.3 %collective-permute-start.6 = (bf16[2,48,896]{2,1,0:T(8,128)(2,1)S(1)}, bf16[2,48,896]{2,1,0:T(8,128)(2,1)S(1)}, u32[]{:S(2)}, u32[]{:S(2)}) collective-permute-start(bf16[2,48,896]{2,1,0:T(8,128)(2,1)S(1)} %collective-permute-done.3.refs_0_), channel_id=1, source_target_pairs={{0,1},{1,0},{2,3},{3,2},{4,5},{5,4},{6,7},{7,6},{8,9},{9,8},{10,11... | collective-permute-start | bytes 516104 | tf_op jit(solution)/shard_map/ppermute | solution.py:441
  98.1 1.5 %collective-permute-start.8 = (bf16[2,48,896]{2,1,0:T(8,128)(2,1)S(1)}, bf16[2,48,896]{2,1,0:T(8,128)(2,1)}, u32[]{:S(2)}, u32[]{:S(2)}) collective-permute-start(bf16[2,48,896]{2,1,0:T(8,128)(2,1)S(1)} %collective-permute-done.7.refs_2_), channel_id=1, source_target_pairs={{0,1},{1,0},{2,3},{3,2},{4,5},{5,4},{6,7},{7,6},{8,9},{9,8},{10,11... | collective-permute-start | bytes 516104 | tf_op jit(solution)/shard_map/ppermute | solution.py:441
  98.1 8.9 %copy-start.5 = (f32[896]{0:T(1024)S(1)}, f32[896]{0:T(1024)}, u32[]{:S(2)}) copy-start(f32[896]{0:T(1024)} %param.13) | copy-start | bytes 10756
  98.1 14.5 %copy-start.1 = (s32[48]{0:T(128)S(1)}, s32[48]{0:T(128)}, u32[]{:S(2)}) copy-start(s32[48]{0:T(128)} %len_ref.1) | copy-start | bytes 580
  98.1 8.9 %collective-permute-start.10 = (bf16[448,640]{1,0:T(8,128)(2,1)S(1)}, bf16[448,640]{1,0:T(8,128)(2,1)S(1)}, u32[]{:S(2)}, u32[]{:S(2)}) collective-permute-start(bf16[448,640]{1,0:T(8,128)(2,1)S(1)} %collective-permute-done.4.refs_2_), channel_id=1, source_target_pairs={{0,1},{1,0},{2,3},{3,2},{4,5},{5,4},{6,7},{7,6},{8,9},{9,8},{10,11... | collective-permute-start | bytes 1720328 | tf_op jit(solution)/shard_map/ppermute | solution.py:441
  102.4 10.3 %collective-permute-start.11 = (bf16[448,640]{1,0:T(8,128)(2,1)S(1)}, bf16[448,640]{1,0:T(8,128)(2,1)S(1)}, u32[]{:S(2)}, u32[]{:S(2)}) collective-permute-start(bf16[448,640]{1,0:T(8,128)(2,1)S(1)} %collective-permute-done.5.refs_3_), channel_id=1, source_target_pairs={{0,1},{1,0},{2,3},{3,2},{4,5},{5,4},{6,7},{7,6},{8,9},{9,8},{10,11... | collective-permute-start | bytes 1720328 | tf_op jit(solution)/shard_map/ppermute | solution.py:441
  102.6 6.3 %collective-permute-start.12 = (bf16[48,896]{1,0:T(8,128)(2,1)S(1)}, bf16[48,896]{1,0:T(8,128)(2,1)S(1)}, u32[]{:S(2)}, u32[]{:S(2)}) collective-permute-start(bf16[48,896]{1,0:T(8,128)(2,1)S(1)} %get-tuple-element.36), channel_id=1, source_target_pairs={{0,4},{4,0},{8,12},{12,8},{1,5},{5,1},{9,13},{13,9},{2,6},{6,2},{1... | collective-permute-start | bytes 258056 | tf_op jit(solution)/shard_map/ppermute | solution.py:502
  102.6 10.1 %collective-permute-start.13 = (bf16[48,896]{1,0:T(8,128)(2,1)S(1)}, bf16[48,896]{1,0:T(8,128)(2,1)S(1)}, u32[]{:S(2)}, u32[]{:S(2)}) collective-permute-start(bf16[48,896]{1,0:T(8,128)(2,1)S(1)} %get-tuple-element.37), channel_id=1, source_target_pairs={{0,8},{4,12},{8,0},{12,4},{1,9},{5,13},{9,1},{13,5},{2,10},{6,14},... | collective-permute-start | bytes 258056 | tf_op jit(solution)/shard_map/ppermute | solution.py:502
  105.6 7.1 %collective-permute-start.14 = (bf16[48,896]{1,0:T(8,128)(2,1)S(1)}, bf16[48,896]{1,0:T(8,128)(2,1)S(1)}, u32[]{:S(2)}, u32[]{:S(2)}) collective-permute-start(bf16[48,896]{1,0:T(8,128)(2,1)S(1)} %get-tuple-element.38), channel_id=1, source_target_pairs={{0,12},{4,8},{8,4},{12,0},{1,13},{5,9},{9,5},{13,1},{2,14},{6,10},... | collective-permute-start | bytes 258056 | tf_op jit(solution)/shard_map/ppermute | solution.py:502

commit v19 on v15

--- a/solution.py
+++ b/solution.py
@@ -173,14 +173,52 @@
     return out
 
 
+def stage_kernel(len_ref, kv_hbm, kv_ref, sem):
+    rows, cached, kv_width = kv_ref.shape
+    page = cached // PAGES
+
+    @pl.loop(0, rows)
+    def _(r):
+        for p, (copy, needed) in enumerate(page_copies(len_ref, kv_hbm, kv_ref, sem, r)):
+            if p == 0:
+                copy.start()
+            else:
+                pl.when(needed)(copy.start)
+
+                @pl.when(jnp.logical_not(needed))
+                def _(p=p, r=r):
+                    kv_ref[r, p * page : (p + 1) * page, :] = jnp.zeros(
+                        (page, kv_width), kv_ref.dtype
+                    )
+
+    @pl.loop(0, rows)
+    def _(r):
+        for p, (copy, needed) in enumerate(page_copies(len_ref, kv_hbm, kv_ref, sem, r)):
+            if p == 0:
+                copy.wait()
+            else:
+                pl.when(needed)(copy.wait)
+
+
+def stage(kv_len, kv_cache):
+    return pl.pallas_call(
+        stage_kernel,
+        out_shape=pltpu.VMEM(kv_cache.shape, kv_cache.dtype),
+        in_specs=[pl.BlockSpec(memory_space=pltpu.SMEM), pl.BlockSpec(memory_space=pl.ANY)],
+        out_specs=pl.BlockSpec(memory_space=pltpu.VMEM),
+        scratch_shapes=[pltpu.SemaphoreType.DMA((kv_cache.shape[0], PAGES))],
+        cost_estimate=SHORT,
+        compiler_params=pltpu.CompilerParams(vmem_limit_bytes=8 * 1024 * 1024),
+    )(kv_len, in_hbm(kv_cache))
+
+
 def talker_kernel(here_ref, len_ref, gain, *refs):
-    w_hbm, terms, refs = refs[:6], refs[6:-10], refs[-10:]
-    kv_hbm, new_kv, out_ref, kv_ref, sem, w_ref, w_sem, qkv, spreads, gathereds = refs
+    w_hbm, terms, refs = refs[:6], refs[6:-8], refs[-8:]
+    kv_ref, new_kv, out_ref, w_ref, w_sem, qkv, spreads, gathereds = refs
     block, turn = here_ref[1], here_ref[2]
     blocks = qkv.shape[0]
     rows, cached, kv_width = kv_ref.shape
     width = kv_width // 2
-    page = cached // PAGES
     heads = out_ref.shape[1] // HEAD_DIM
     group = heads // blocks
     slot = LANES // ROW_STEP
@@ -204,14 +242,6 @@
             w_copies[-1].append(pltpu.make_async_copy(w_hbm[at], part, w_sem.at[at]))
             w_copies[-1][-1].start()
             at += 1
-
-    @pl.loop(0, rows)
-    def _(r):
-        for p, (copy, needed) in enumerate(page_copies(len_ref, kv_hbm, kv_ref, sem, r)):
-            if p == 0:
-                copy.start()
-            else:
-                pl.when(needed)(copy.start)
 
     total = terms[0][...].astype(jnp.float32)
     for term in terms[1:]:
@@ -299,20 +329,6 @@
     @pl.loop(0, rows // (sets * ROW_STEP))
     def _(i):
         first = pl.multiple_of(i * sets * ROW_STEP, sets * ROW_STEP)
-        for k in range(sets * ROW_STEP):
-            r = first + k
-            for p, (copy, needed) in enumerate(page_copies(len_ref, kv_hbm, kv_ref, sem, r)):
-                if p == 0:
-                    copy.wait()
-                    continue
-                pl.when(needed)(copy.wait)
-
-                @pl.when(jnp.logical_not(needed))
-                def _(p=p, r=r):
-                    kv_ref[r, p * page : (p + 1) * page, :] = jnp.zeros(
-                        (page, kv_width), kv_ref.dtype
-                    )
-
         ats = [pl.multiple_of(first + k * ROW_STEP, ROW_STEP) for k in range(sets)]
         scored = [scores_of(at, spreads.at[k]) for k, at in enumerate(ats)]
         weighed = [softmax(at, *s) for at, s in zip(ats, scored)]
@@ -337,11 +353,9 @@
         in_specs=[smem, smem, vmem]
         + [pl.BlockSpec(memory_space=pl.ANY)] * len(weights)
         + [vmem] * len(terms)
-        + [pl.BlockSpec(memory_space=pl.ANY)],
+        + [vmem],
         out_specs=(vmem, vmem),
         scratch_shapes=[
-            pltpu.VMEM((rows, cached, kv_width), jnp.bfloat16),
-            pltpu.SemaphoreType.DMA((rows, PAGES)),
             pltpu.VMEM((blocks, wide, columns), jnp.bfloat16),
             pltpu.SemaphoreType.DMA((len(weights),)),
             pltpu.VMEM((blocks, rows, columns), jnp.float32),
@@ -349,8 +363,8 @@
             pltpu.VMEM((sets, LANES, HEAD_DIM), jnp.float32),
         ],
         cost_estimate=SHORT,
-        compiler_params=pltpu.CompilerParams(vmem_limit_bytes=40 * 1024 * 1024),
-    )(here, kv_len, talker_gain.reshape(1, wide), *weights, *terms, in_hbm(kv_cache))
+        compiler_params=pltpu.CompilerParams(vmem_limit_bytes=16 * 1024 * 1024),
+    )(here, kv_len, talker_gain.reshape(1, wide), *weights, *terms, kv_cache)
 
 
 def rms_norm(talker_in, talker_gain):
@@ -498,7 +512,8 @@
     other_half = after(other_half, projected[0])
     halves = [my_half, other_half, over_core(my_half), over_core(other_half)]
     weights = [mine, over_core(mine), *halves]
-    new_kv, ctx = talker(here, terms, talker_gain, weights, kv_len, kv_cache)
+    staged = stage(after(kv_len, projected[0]), kv_cache)
+    new_kv, ctx = talker(here, terms, talker_gain, weights, kv_len, staged)
     return (thinker_out, new_kv, ctx)
 
 

time: 124 us -> 124 us (level)
  waiting for transfers between devices: 54.6 us -> 49.1 us
  Pallas kernels: 29.7 us -> 34.9 us
    pallas_call x0 -> x1, Pallas kernels: none -> 7.7 us  [stage(): pl.pallas_call(stage_kernel, out_shape=pltpu.VMEM(kv_cache.shape, kv_cach...]
    ppermute x3, waiting for transfers between devices: 5.53 us -> 0.01 us  [four_planes(): lax.ppermute(projected[d], 'mp', [(p, p ^ d) for p in range(planes)])]
    pallas_call x1, Pallas kernels: 12.3 us -> 9.8 us  [talker(): pl.pallas_call(talker_kernel, out_shape=(jax.ShapeDtypeStruct((rows, kv_w...]
  transfers between devices with their start and end apart: 17 -> 17, of which waited for: 8 -> 6; matrix products, arithmetic and copies ran while one was open for 1% -> 1% of each run, Pallas kernels for 8% -> 14%
where the time goes in v19:
time: 124 us
  waiting for transfers between devices  49.1 us (40%)
  starting transfers between devices  36.8 us (30%)
  Pallas kernels  34.9 us (28%)
  local copies, waits for them, and re-layouts  1.87 us (2%)
    ppermute x2, waiting for transfers between devices, over_section(): return lax.ppermute(x, 'section', [(0, 1), (1, 0)])  37.4 us
    pallas_call x2, Pallas kernels, down(): pl.pallas_call(functools.partial(down_kernel, planes, list(zip(ends[:-1],...  14.4 us
    ppermute x4, starting transfers between devices, four_planes(): lax.ppermute(x, GROUP, [(p * 4 + b, b * 4 + (b ^ p ^ k)) for p in range(4...  14 us
    pallas_call x1, Pallas kernels, talker(): pl.pallas_call(talker_kernel, out_shape=(jax.ShapeDtypeStruct((rows, kv_w...  9.8 us
    pallas_call x1, Pallas kernels, stage(): pl.pallas_call(stage_kernel, out_shape=pltpu.VMEM(kv_cache.shape, kv_cach...  7.7 us
    all_to_all x1, starting transfers between devices, four_planes(): near_terms = lax.all_to_all(near, 'mp', 0, 0)  6.38 us
    all_to_all x1, starting transfers between devices, four_planes(): far_terms = lax.all_to_all(far, 'mp', 0, 0)  5.14 us
    ppermute x5, waiting for transfers between devices, over_core(): return lax.ppermute(x, 'rows', [(0, 1), (1, 0)])  5.01 us
  transfers between devices with their start and end apart: 17, of which 6 were waited for; matrix products, arithmetic and copies ran while one was open for 1% of the time, Pallas kernels for 14%

profile of v19, /device:TPU:0, one launch (start us, length us, event | category | flops | bytes accessed | tf_op | source)
XLA Modules:
  0.0 123.8 jit_solution(1310300281607375375)
XLA Ops:
  1.1 2.6 %collective-permute-start = (bf16[192,4736]{1,0:T(8,128)(2,1)}, bf16[192,4736]{1,0:T(8,128)(2,1)}, u32[]{:S(2)}, u32[]{:S(2)}) collective-permute-start(bf16[192,4736]{1,0:T(8,128)(2,1)} %refs_0_.1), channel_id=1, source_target_pairs={{0,2},{2,0},{1,3},{3,1},{4,6},{6,4},{5,7},{7,5},{8,10},{10,8},{9,1... | collective-permute-start | bytes 5455880 | tf_op jit(solution)/shard_map/ppermute | solution.py:455
  3.7 1.0 collective-permute-done.1.refs_1_
  4.7 7.2 %shard_map.121 = bf16[4,96,896]{2,1,0:T(8,128)(2,1)} custom-call(bf16[192,4736]{1,0:T(8,128)(2,1)} %refs_0_.1, bf16[192,4736]{1,0:T(8,128)(2,1)S(1)} %collective-permute-done.1.refs_1_, bf16[4736,896]{1,0:T(8,128)(2,1)} %refs_2_.3), custom_call_target="tpu_custom_call" | custom-call | flops 1 | bytes 1 | tf_op jit(solution)/shard_map/pallas_call | solution.py:54
  12.0 6.4 %all-to-all-start = ((bf16[4,96,896]{2,1,0:T(8,128)(2,1)}), bf16[4,96,896]{2,1,0:T(8,128)(2,1)S(1)}, u32[]{:S(2)}, u32[]{:S(2)}) async-start(bf16[4,96,896]{2,1,0:T(8,128)(2,1)} %shard_map.121), calls=%async_computation | async-start | bytes 1376256 | tf_op jit(solution)/shard_map/all_to_all | solution.py:488
  18.5 0.8 copy-done.4
  19.4 0.9 constant_dynamic-slice_fusion
  20.2 24.0 %collective-permute-done.refs_0_ = bf16[192,4736]{1,0:T(8,128)(2,1)} collective-permute-done((bf16[192,4736]{1,0:T(8,128)(2,1)}, bf16[192,4736]{1,0:T(8,128)(2,1)}, u32[]{:S(2)}, u32[]{:S(2)}) %collective-permute-start) | collective-permute-done | bytes 1818656 | tf_op jit(solution)/shard_map/ppermute | solution.py:455
  44.3 4.0 %collective-permute-done.2.refs_1_ = bf16[192,4736]{1,0:T(8,128)(2,1)S(1)} collective-permute-done((bf16[192,4736]{1,0:T(8,128)(2,1)}, bf16[192,4736]{1,0:T(8,128)(2,1)S(1)}, u32[]{:S(2)}, u32[]{:S(2)}) %collective-permute-start.2) | collective-permute-done | bytes 1818656 | tf_op jit(solution)/shard_map/ppermute | solution.py:451
  48.3 7.2 %shard_map.122 = bf16[4,96,896]{2,1,0:T(8,128)(2,1)} custom-call(bf16[192,4736]{1,0:T(8,128)(2,1)} %collective-permute-done.refs_0_, bf16[192,4736]{1,0:T(8,128)(2,1)S(1)} %collective-permute-done.2.refs_1_, bf16[4736,896]{1,0:T(8,128)(2,1)} %refs_2_.3), custom_call_target="tpu_custom_call" | custom-call | flops 1 | bytes 1 | tf_op jit(solution)/shard_map/pallas_call | solution.py:54
  55.5 5.1 %all-to-all-start.1 = ((bf16[4,96,896]{2,1,0:T(8,128)(2,1)}), bf16[4,96,896]{2,1,0:T(8,128)(2,1)S(1)}, u32[]{:S(2)}, u32[]{:S(2)}) async-start(bf16[4,96,896]{2,1,0:T(8,128)(2,1)} %shard_map.122), calls=%async_computation.1 | async-start | bytes 1376256 | tf_op jit(solution)/shard_map/all_to_all | solution.py:497
  60.6 1.5 %collective-permute-start.4 = (bf16[448,640]{1,0:T(8,128)(2,1)}, bf16[448,640]{1,0:T(8,128)(2,1)S(1)}, u32[]{:S(2)}, u32[]{:S(2)}) collective-permute-start(bf16[448,640]{1,0:T(8,128)(2,1)} %constant_dynamic-slice_fusion), channel_id=1, source_target_pairs={{0,2},{2,0},{1,3},{3,1},{4,6},{6,4},{5,7},{7,5},{8,10},{10,8},{9,1... | collective-permute-start | bytes 1720328 | tf_op jit(solution)/shard_map/ppermute | solution.py:455
  62.2 13.4 %collective-permute-done.4.refs_2_ = bf16[448,640]{1,0:T(8,128)(2,1)S(1)} collective-permute-done((bf16[448,640]{1,0:T(8,128)(2,1)}, bf16[448,640]{1,0:T(8,128)(2,1)S(1)}, u32[]{:S(2)}, u32[]{:S(2)}) %collective-permute-start.4) | collective-permute-done | bytes 573472 | tf_op jit(solution)/shard_map/ppermute | solution.py:455
  75.6 1.5 %collective-permute-start.5 = (bf16[448,640]{1,0:T(8,128)(2,1)S(1)}, bf16[448,640]{1,0:T(8,128)(2,1)S(1)}, u32[]{:S(2)}, u32[]{:S(2)}) collective-permute-start(bf16[448,640]{1,0:T(8,128)(2,1)S(1)} %collective-permute-done.4.refs_2_), channel_id=1, source_target_pairs={{0,16},{16,0},{1,17},{17,1},{2,18},{18,2},{3,19},{19,3},{4,20},{20... | collective-permute-start | bytes 1720328 | tf_op jit(solution)/shard_map/ppermute | solution.py:463
  77.1 1.8 %all-to-all-done.1.terms = bf16[4,96,896]{2,1,0:T(8,128)(2,1)S(1)} async-done(((bf16[4,96,896]{2,1,0:T(8,128)(2,1)}), bf16[4,96,896]{2,1,0:T(8,128)(2,1)S(1)}, u32[]{:S(2)}, u32[]{:S(2)}) %all-to-all-start.1) | async-done | bytes 688160 | tf_op jit(solution)/shard_map/all_to_all | solution.py:497
  79.8 2.3 %collective-permute-start.6 = (bf16[48,896]{1,0:T(8,128)(2,1)S(1)}, bf16[48,896]{1,0:T(8,128)(2,1)S(1)}, u32[]{:S(2)}, u32[]{:S(2)}) collective-permute-start(bf16[48,896]{1,0:T(8,128)(2,1)S(1)} %get-tuple-element.33), channel_id=1, source_target_pairs={{0,1},{1,4},{2,11},{3,14},{4,0},{5,5},{6,10},{7,15},{8,3},{9,6},{1... | collective-permute-start | bytes 258056 | tf_op jit(solution)/shard_map/ppermute | solution.py:503
  82.1 5.1 %collective-permute-start.7 = (bf16[48,896]{1,0:T(8,128)(2,1)S(1)}, bf16[48,896]{1,0:T(8,128)(2,1)S(1)}, u32[]{:S(2)}, u32[]{:S(2)}) collective-permute-start(bf16[48,896]{1,0:T(8,128)(2,1)S(1)} %get-tuple-element.34), channel_id=1, source_target_pairs={{0,2},{1,7},{2,8},{3,13},{4,3},{5,6},{6,9},{7,12},{8,0},{9,5},{10,... | collective-permute-start | bytes 258056 | tf_op jit(solution)/shard_map/ppermute | solution.py:503
  87.2 6.0 %collective-permute-start.8 = (bf16[48,896]{1,0:T(8,128)(2,1)S(1)}, bf16[48,896]{1,0:T(8,128)(2,1)S(1)}, u32[]{:S(2)}, u32[]{:S(2)}) collective-permute-start(bf16[48,896]{1,0:T(8,128)(2,1)S(1)} %get-tuple-element.35), channel_id=1, source_target_pairs={{0,3},{1,6},{2,9},{3,12},{4,2},{5,7},{6,8},{7,13},{8,1},{9,4},{10,... | collective-permute-start | bytes 258056 | tf_op jit(solution)/shard_map/ppermute | solution.py:503
  93.3 4.8 %collective-permute-done.7.refs_2_ = bf16[48,896]{1,0:T(8,128)(2,1)S(1)} collective-permute-done((bf16[48,896]{1,0:T(8,128)(2,1)S(1)}, bf16[48,896]{1,0:T(8,128)(2,1)S(1)}, u32[]{:S(2)}, u32[]{:S(2)}) %collective-permute-start.7) | collective-permute-done | bytes 86048 | tf_op jit(solution)/shard_map/ppermute | solution.py:503
  98.1 2.8 %shard_map.125 = (bf16[192,896]{1,0:T(8,128)(2,1)}, bf16[48,896]{1,0:T(8,128)(2,1)S(1)}, bf16[48,896]{1,0:T(8,128)(2,1)S(1)}, bf16[48,896]{1,0:T(8,128)(2,1)S(1)}, bf16[48,896]{1,0:T(8,128)(2,1)S(1)}) custom-call(s32[3]{0:T(128)S(1)} %pad_add_fusion.here_ref, s32[1,192]{1,0:T(1,128)S(1)} %copy-done.1, bf16[896,896]{1,0:T(8,128)(2,1)} %w_hbm.1, ...), custom_call_target="tpu_custom_call" | custom-call | flops 1 | bytes 1 | tf_op jit(solution)/shard_map/pallas_call | solution.py:149
  100.9 0.8 collective-permute-start.11
  101.7 3.0 %collective-permute-start.13 = (bf16[48,896]{1,0:T(8,128)(2,1)S(1)}, bf16[48,896]{1,0:T(8,128)(2,1)S(1)}, u32[]{:S(2)}, u32[]{:S(2)}) collective-permute-start(bf16[48,896]{1,0:T(8,128)(2,1)S(1)} %get-tuple-element.42), channel_id=1, source_target_pairs={{0,8},{4,12},{8,0},{12,4},{1,9},{5,13},{9,1},{13,5},{2,10},{6,14},... | collective-permute-start | bytes 258056 | tf_op jit(solution)/shard_map/ppermute | solution.py:511
  104.7 1.4 %collective-permute-start.14 = (bf16[48,896]{1,0:T(8,128)(2,1)S(1)}, bf16[48,896]{1,0:T(8,128)(2,1)S(1)}, u32[]{:S(2)}, u32[]{:S(2)}) collective-permute-start(bf16[48,896]{1,0:T(8,128)(2,1)S(1)} %get-tuple-element.43), channel_id=1, source_target_pairs={{0,12},{4,8},{8,4},{12,0},{1,13},{5,9},{9,5},{13,1},{2,14},{6,10},... | collective-permute-start | bytes 258056 | tf_op jit(solution)/shard_map/ppermute | solution.py:511
  106.1 7.7 %shard_map.126.refs_10_ = bf16[48,256,1024]{2,1,0:T(8,128)(2,1)S(1)} custom-call(s32[48]{0:T(128)S(1)} %copy-done, bf16[48,256,1024]{2,1,0:T(8,128)(2,1)} %kv_hbm.1), custom_call_target="tpu_custom_call" | custom-call | flops 1 | bytes 1 | tf_op jit(solution)/shard_map/pallas_call | solution.py:204
  113.8 9.8 %shard_map.127 = (bf16[48,1024]{1,0:T(8,128)(2,1)}, f32[48,1536]{1,0:T(8,128)}) custom-call(s32[3]{0:T(128)S(1)} %pad_add_fusion.here_ref, s32[48]{0:T(128)S(1)} %copy-done, f32[1,896]{1,0:T(1,128)S(1)} %reshape.10.gain, bf16[896,640]{1,0:T(8,128)(2,1)S(1)} %constant_dynamic-update-slice_fusion.refs_0_, bf16[896,640]{1,0:T(8,128)(2,1)} %collective-permute-done.9.refs_1_, ...), custom_call_target="tpu_custom_call" | custom-call | flops 1 | bytes 1 | tf_op jit(solution)/shard_map/pallas_call | solution.py:347
  (35 shorter events, 1.8 us)
Async XLA Ops:
  0.6 4.1 %collective-permute-start.1 = (bf16[192,4736]{1,0:T(8,128)(2,1)}, bf16[192,4736]{1,0:T(8,128)(2,1)S(1)}, u32[]{:S(2)}, u32[]{:S(2)}) collective-permute-start(bf16[192,4736]{1,0:T(8,128)(2,1)} %refs_0_.1), channel_id=1, source_target_pairs={{0,1},{1,0},{2,3},{3,2},{4,5},{5,4},{6,7},{7,6},{8,9},{9,8},{10,11... | collective-permute-start | bytes 5455880 | tf_op jit(solution)/shard_map/ppermute | solution.py:451
  1.1 43.1 %collective-permute-start = (bf16[192,4736]{1,0:T(8,128)(2,1)}, bf16[192,4736]{1,0:T(8,128)(2,1)}, u32[]{:S(2)}, u32[]{:S(2)}) collective-permute-start(bf16[192,4736]{1,0:T(8,128)(2,1)} %refs_0_.1), channel_id=1, source_target_pairs={{0,2},{2,0},{1,3},{3,1},{4,6},{6,4},{5,7},{7,5},{8,10},{10,8},{9,1... | collective-permute-start | bytes 5455880 | tf_op jit(solution)/shard_map/ppermute | solution.py:455
  12.0 6.4 %copy-start.2 = (bf16[896,384]{1,0:T(8,128)(2,1)S(1)}, bf16[896,384]{1,0:T(8,128)(2,1)}, u32[]{:S(2)}) copy-start(bf16[896,384]{1,0:T(8,128)(2,1)} %param.14) | copy-start | bytes 2064388
  12.0 6.5 %copy-start.3 = (bf16[896,128]{1,0:T(8,128)(2,1)S(1)}, bf16[896,128]{1,0:T(8,128)(2,1)}, u32[]{:S(2)}) copy-start(bf16[896,128]{1,0:T(8,128)(2,1)} %param.15) | copy-start | bytes 688132
  12.0 32.3 %all-to-all-start = ((bf16[4,96,896]{2,1,0:T(8,128)(2,1)}), bf16[4,96,896]{2,1,0:T(8,128)(2,1)S(1)}, u32[]{:S(2)}, u32[]{:S(2)}) async-start(bf16[4,96,896]{2,1,0:T(8,128)(2,1)} %shard_map.121), calls=%async_computation | async-start | bytes 1376256 | tf_op jit(solution)/shard_map/all_to_all | solution.py:488
  18.4 0.9 copy-start.4
  44.3 4.0 %collective-permute-start.2 = (bf16[192,4736]{1,0:T(8,128)(2,1)}, bf16[192,4736]{1,0:T(8,128)(2,1)S(1)}, u32[]{:S(2)}, u32[]{:S(2)}) collective-permute-start(bf16[192,4736]{1,0:T(8,128)(2,1)} %collective-permute-done.refs_0_), channel_id=1, source_target_pairs={{0,1},{1,0},{2,3},{3,2},{4,5},{5,4},{6,7},{7,6},{8,9},{9,8},{10,11... | collective-permute-start | bytes 5455880 | tf_op jit(solution)/shard_map/ppermute | solution.py:451
  55.5 23.5 %all-to-all-start.1 = ((bf16[4,96,896]{2,1,0:T(8,128)(2,1)}), bf16[4,96,896]{2,1,0:T(8,128)(2,1)S(1)}, u32[]{:S(2)}, u32[]{:S(2)}) async-start(bf16[4,96,896]{2,1,0:T(8,128)(2,1)} %shard_map.122), calls=%async_computation.1 | async-start | bytes 1376256 | tf_op jit(solution)/shard_map/all_to_all | solution.py:497
  60.6 37.5 %copy-start.1 = (s32[1,192]{1,0:T(1,128)S(1)}, s32[1,192]{1,0:T(1,128)}, u32[]{:S(2)}) copy-start(s32[1,192]{1,0:T(1,128)} %slots.1) | copy-start | bytes 2308
  60.6 15.0 %collective-permute-start.4 = (bf16[448,640]{1,0:T(8,128)(2,1)}, bf16[448,640]{1,0:T(8,128)(2,1)S(1)}, u32[]{:S(2)}, u32[]{:S(2)}) collective-permute-start(bf16[448,640]{1,0:T(8,128)(2,1)} %constant_dynamic-slice_fusion), channel_id=1, source_target_pairs={{0,2},{2,0},{1,3},{3,1},{4,6},{6,4},{5,7},{7,5},{8,10},{10,8},{9,1... | collective-permute-start | bytes 1720328 | tf_op jit(solution)/shard_map/ppermute | solution.py:455
  62.1 42.5 %collective-permute-start.9 = (bf16[896,640]{1,0:T(8,128)(2,1)S(1)}, bf16[896,640]{1,0:T(8,128)(2,1)}, u32[]{:S(2)}, u32[]{:S(2)}) collective-permute-start(bf16[896,640]{1,0:T(8,128)(2,1)S(1)} %constant_dynamic-update-slice_fusion.refs_0_), channel_id=1, source_target_pairs={{0,1},{1,0},{2,3},{3,2},{4,5},{5,4},{6,7},{7,6},{8,9},{9,8},{10,11... | collective-permute-start | bytes 3440648 | tf_op jit(solution)/shard_map/ppermute | solution.py:451
  75.6 17.7 %collective-permute-start.5 = (bf16[448,640]{1,0:T(8,128)(2,1)S(1)}, bf16[448,640]{1,0:T(8,128)(2,1)S(1)}, u32[]{:S(2)}, u32[]{:S(2)}) collective-permute-start(bf16[448,640]{1,0:T(8,128)(2,1)S(1)} %collective-permute-done.4.refs_2_), channel_id=1, source_target_pairs={{0,16},{16,0},{1,17},{17,1},{2,18},{18,2},{3,19},{19,3},{4,20},{20... | collective-permute-start | bytes 1720328 | tf_op jit(solution)/shard_map/ppermute | solution.py:463
  79.1 27.0 %copy-start.5 = (f32[896]{0:T(1024)S(1)}, f32[896]{0:T(1024)}, u32[]{:S(2)}) copy-start(f32[896]{0:T(1024)} %param.13) | copy-start | bytes 10756
  79.1 27.0 %copy-start = (s32[48]{0:T(128)S(1)}, s32[48]{0:T(128)}, u32[]{:S(2)}) copy-start(s32[48]{0:T(128)} %len_ref.2) | copy-start | bytes 580
  79.1 8.1 %collective-permute-start.3 = (bf16[48,896]{1,0:T(8,128)(2,1)S(1)}, bf16[48,896]{1,0:T(8,128)(2,1)S(1)}, u32[]{:S(2)}, u32[]{:S(2)}) collective-permute-start(bf16[48,896]{1,0:T(8,128)(2,1)S(1)} %get-tuple-element.28), channel_id=1, source_target_pairs={{0,0},{1,5},{2,10},{3,15},{4,1},{5,4},{6,11},{7,14},{8,2},{9,7},{1... | collective-permute-start | bytes 258056 | tf_op jit(solution)/shard_map/ppermute | solution.py:503
  79.8 13.5 %collective-permute-start.6 = (bf16[48,896]{1,0:T(8,128)(2,1)S(1)}, bf16[48,896]{1,0:T(8,128)(2,1)S(1)}, u32[]{:S(2)}, u32[]{:S(2)}) collective-permute-start(bf16[48,896]{1,0:T(8,128)(2,1)S(1)} %get-tuple-element.33), channel_id=1, source_target_pairs={{0,1},{1,4},{2,11},{3,14},{4,0},{5,5},{6,10},{7,15},{8,3},{9,6},{1... | collective-permute-start | bytes 258056 | tf_op jit(solution)/shard_map/ppermute | solution.py:503
  82.1 16.0 %collective-permute-start.7 = (bf16[48,896]{1,0:T(8,128)(2,1)S(1)}, bf16[48,896]{1,0:T(8,128)(2,1)S(1)}, u32[]{:S(2)}, u32[]{:S(2)}) collective-permute-start(bf16[48,896]{1,0:T(8,128)(2,1)S(1)} %get-tuple-element.34), channel_id=1, source_target_pairs={{0,2},{1,7},{2,8},{3,13},{4,3},{5,6},{6,9},{7,12},{8,0},{9,5},{10,... | collective-permute-start | bytes 258056 | tf_op jit(solution)/shard_map/ppermute | solution.py:503
  87.2 10.9 %collective-permute-start.8 = (bf16[48,896]{1,0:T(8,128)(2,1)S(1)}, bf16[48,896]{1,0:T(8,128)(2,1)S(1)}, u32[]{:S(2)}, u32[]{:S(2)}) collective-permute-start(bf16[48,896]{1,0:T(8,128)(2,1)S(1)} %get-tuple-element.35), channel_id=1, source_target_pairs={{0,3},{1,6},{2,9},{3,12},{4,2},{5,7},{6,8},{7,13},{8,1},{9,4},{10,... | collective-permute-start | bytes 258056 | tf_op jit(solution)/shard_map/ppermute | solution.py:503
  93.2 20.5 %collective-permute-start.10 = (bf16[448,640]{1,0:T(8,128)(2,1)S(1)}, bf16[448,640]{1,0:T(8,128)(2,1)S(1)}, u32[]{:S(2)}, u32[]{:S(2)}) collective-permute-start(bf16[448,640]{1,0:T(8,128)(2,1)S(1)} %collective-permute-done.4.refs_2_), channel_id=1, source_target_pairs={{0,1},{1,0},{2,3},{3,2},{4,5},{5,4},{6,7},{7,6},{8,9},{9,8},{10,11... | collective-permute-start | bytes 1720328 | tf_op jit(solution)/shard_map/ppermute | solution.py:451
  100.9 13.0 %collective-permute-start.11 = (bf16[448,640]{1,0:T(8,128)(2,1)S(1)}, bf16[448,640]{1,0:T(8,128)(2,1)S(1)}, u32[]{:S(2)}, u32[]{:S(2)}) collective-permute-start(bf16[448,640]{1,0:T(8,128)(2,1)S(1)} %collective-permute-done.5.refs_3_), channel_id=1, source_target_pairs={{0,1},{1,0},{2,3},{3,2},{4,5},{5,4},{6,7},{7,6},{8,9},{9,8},{10,11... | collective-permute-start | bytes 1720328 | tf_op jit(solution)/shard_map/ppermute | solution.py:451
  101.7 12.1 %collective-permute-start.12 = (bf16[48,896]{1,0:T(8,128)(2,1)S(1)}, bf16[48,896]{1,0:T(8,128)(2,1)S(1)}, u32[]{:S(2)}, u32[]{:S(2)}) collective-permute-start(bf16[48,896]{1,0:T(8,128)(2,1)S(1)} %get-tuple-element.41), channel_id=1, source_target_pairs={{0,4},{4,0},{8,12},{12,8},{1,5},{5,1},{9,13},{13,9},{2,6},{6,2},{1... | collective-permute-start | bytes 258056 | tf_op jit(solution)/shard_map/ppermute | solution.py:511
  101.7 12.1 %collective-permute-start.13 = (bf16[48,896]{1,0:T(8,128)(2,1)S(1)}, bf16[48,896]{1,0:T(8,128)(2,1)S(1)}, u32[]{:S(2)}, u32[]{:S(2)}) collective-permute-start(bf16[48,896]{1,0:T(8,128)(2,1)S(1)} %get-tuple-element.42), channel_id=1, source_target_pairs={{0,8},{4,12},{8,0},{12,4},{1,9},{5,13},{9,1},{13,5},{2,10},{6,14},... | collective-permute-start | bytes 258056 | tf_op jit(solution)/shard_map/ppermute | solution.py:511
  104.7 9.2 %collective-permute-start.14 = (bf16[48,896]{1,0:T(8,128)(2,1)S(1)}, bf16[48,896]{1,0:T(8,128)(2,1)S(1)}, u32[]{:S(2)}, u32[]{:S(2)}) collective-permute-start(bf16[48,896]{1,0:T(8,128)(2,1)S(1)} %get-tuple-element.43), channel_id=1, source_target_pairs={{0,12},{4,8},{8,4},{12,0},{1,13},{5,9},{9,5},{13,1},{2,14},{6,10},... | collective-permute-start | bytes 258056 | tf_op jit(solution)/shard_map/ppermute | solution.py:511

commit v20 on v19

--- a/solution.py
+++ b/solution.py
@@ -83,7 +83,7 @@
         in_specs=[vmem],
         out_specs=vmem,
         cost_estimate=SHORT,
-        compiler_params=pltpu.CompilerParams(vmem_limit_bytes=16 * 1024 * 1024),
+        compiler_params=pltpu.CompilerParams(vmem_limit_bytes=10 * 1024 * 1024),
     )(terms)
 
 
@@ -113,7 +113,7 @@
         out_specs=(vmem,) * blocks,
         scratch_shapes=[pltpu.VMEM((blocks, *part.shape), jnp.bfloat16)],
         cost_estimate=SHORT,
-        compiler_params=pltpu.CompilerParams(vmem_limit_bytes=16 * 1024 * 1024),
+        compiler_params=pltpu.CompilerParams(vmem_limit_bytes=10 * 1024 * 1024),
     )(plane, near, terms)
 
 
@@ -159,7 +159,7 @@
             pltpu.SemaphoreType.DMA,
         ],
         cost_estimate=SHORT,
-        compiler_params=pltpu.CompilerParams(vmem_limit_bytes=16 * 1024 * 1024),
+        compiler_params=pltpu.CompilerParams(vmem_limit_bytes=10 * 1024 * 1024),
     )(here, slots, in_hbm(w_proj), *came)
 
 
@@ -363,7 +363,7 @@
             pltpu.VMEM((sets, LANES, HEAD_DIM), jnp.float32),
         ],
         cost_estimate=SHORT,
-        compiler_params=pltpu.CompilerParams(vmem_limit_bytes=16 * 1024 * 1024),
+        compiler_params=pltpu.CompilerParams(vmem_limit_bytes=10 * 1024 * 1024),
     )(here, kv_len, talker_gain.reshape(1, wide), *weights, *terms, kv_cache)
 
 
@@ -498,6 +498,8 @@
 
     my_half = over_section(after(my_half, far))
     near_sums = add(after(near_terms, far))
+    staged = stage(after(kv_len, far), kv_cache)
+    far_terms, staged = lax.optimization_barrier((far_terms, staged))
 
     came = [
         lax.ppermute(x, GROUP, [(p * 4 + b, b * 4 + (b ^ p ^ k)) for p in range(4) for b in range(4)])
@@ -512,7 +514,6 @@
     other_half = after(other_half, projected[0])
     halves = [my_half, other_half, over_core(my_half), over_core(other_half)]
     weights = [mine, over_core(mine), *halves]
-    staged = stage(after(kv_len, projected[0]), kv_cache)
     new_kv, ctx = talker(here, terms, talker_gain, weights, kv_len, staged)
     return (thinker_out, new_kv, ctx)
 

time: 124 us -> 146 us (1.18)
  local copies, waits for them, and re-layouts: 1.87 us -> 18.3 us
  waiting for transfers between devices: 49.1 us -> 51.9 us
  starting transfers between devices: 36.8 us -> 39.3 us
    unnamed x14 -> x18, local copies, waits for them, and re-layouts: 0.94 us -> 17.4 us
    ppermute x3, waiting for transfers between devices: 0.01 us -> 5.82 us  [four_planes(): lax.ppermute(projected[d], 'mp', [(p, p ^ d) for p in range(planes)])]
    ppermute x4, starting transfers between devices: 14 us -> 16.1 us  [four_planes(): lax.ppermute(x, GROUP, [(p * 4 + b, b * 4 + (b ^ p ^ k)) for p in range(4...]
    all_to_all x1, waiting for transfers between devices: 1.83 us -> 0.01 us  [four_planes(): far_terms = lax.all_to_all(far, 'mp', 0, 0)]
  transfers between devices with their start and end apart: 17 -> 17, of which waited for: 6 -> 7; matrix products, arithmetic and copies ran while one was open for 1% -> 1% of each run, Pallas kernels for 14% -> 12%
where the time goes in v20:
time: 146 us; the launch traced here: 145 us
  waiting for transfers between devices  51.9 us (36%)
  starting transfers between devices  39.3 us (27%)
  Pallas kernels  34.7 us (24%)
  local copies, waits for them, and re-layouts  18.3 us (13%)
    ppermute x2, waiting for transfers between devices, over_section(): return lax.ppermute(x, 'section', [(0, 1), (1, 0)])  37.4 us
    unnamed x18, local copies, waits for them, and re-layouts  17.4 us
    ppermute x4, starting transfers between devices, four_planes(): lax.ppermute(x, GROUP, [(p * 4 + b, b * 4 + (b ^ p ^ k)) for p in range(4...  16.1 us
    pallas_call x2, Pallas kernels, down(): pl.pallas_call(functools.partial(down_kernel, planes, list(zip(ends[:-1],...  14.4 us
    pallas_call x1, Pallas kernels, talker(): pl.pallas_call(talker_kernel, out_shape=(jax.ShapeDtypeStruct((rows, kv_w...  9.8 us
    pallas_call x1, Pallas kernels, stage(): pl.pallas_call(stage_kernel, out_shape=pltpu.VMEM(kv_cache.shape, kv_cach...  7.47 us
    all_to_all x1, starting transfers between devices, four_planes(): near_terms = lax.all_to_all(near, 'mp', 0, 0)  6.38 us
    ppermute x3, waiting for transfers between devices, four_planes(): lax.ppermute(projected[d], 'mp', [(p, p ^ d) for p in range(planes)])  5.82 us
  transfers between devices with their start and end apart: 17, of which 7 were waited for; matrix products, arithmetic and copies ran while one was open for 1% of the time, Pallas kernels for 12%

profile of v20, /device:TPU:0, one launch (start us, length us, event | category | flops | bytes accessed | tf_op | source)
XLA Modules:
  0.0 145.3 jit_solution(3119770808572030224)
XLA Ops:
  1.1 2.6 %collective-permute-start = (bf16[192,4736]{1,0:T(8,128)(2,1)}, bf16[192,4736]{1,0:T(8,128)(2,1)}, u32[]{:S(2)}, u32[]{:S(2)}) collective-permute-start(bf16[192,4736]{1,0:T(8,128)(2,1)} %refs_0_.1), channel_id=1, source_target_pairs={{0,2},{2,0},{1,3},{3,1},{4,6},{6,4},{5,7},{7,5},{8,10},{10,8},{9,1... | collective-permute-start | bytes 5455880 | tf_op jit(solution)/shard_map/ppermute | solution.py:455
  4.7 7.2 %shard_map.121 = bf16[4,96,896]{2,1,0:T(8,128)(2,1)} custom-call(bf16[192,4736]{1,0:T(8,128)(2,1)} %refs_0_.1, bf16[192,4736]{1,0:T(8,128)(2,1)S(1)} %collective-permute-done.1.refs_1_, bf16[4736,896]{1,0:T(8,128)(2,1)} %refs_2_.3), custom_call_target="tpu_custom_call" | custom-call | flops 1 | bytes 1 | tf_op jit(solution)/shard_map/pallas_call | solution.py:54
  12.0 6.4 %all-to-all-start = ((bf16[4,96,896]{2,1,0:T(8,128)(2,1)}), bf16[4,96,896]{2,1,0:T(8,128)(2,1)S(1)}, u32[]{:S(2)}, u32[]{:S(2)}) async-start(bf16[4,96,896]{2,1,0:T(8,128)(2,1)} %shard_map.121), calls=%async_computation | async-start | bytes 1376256 | tf_op jit(solution)/shard_map/all_to_all | solution.py:488
  20.2 24.0 %collective-permute-done.refs_0_ = bf16[192,4736]{1,0:T(8,128)(2,1)} collective-permute-done((bf16[192,4736]{1,0:T(8,128)(2,1)}, bf16[192,4736]{1,0:T(8,128)(2,1)}, u32[]{:S(2)}, u32[]{:S(2)}) %collective-permute-start) | collective-permute-done | bytes 1818656 | tf_op jit(solution)/shard_map/ppermute | solution.py:455
  44.3 4.0 %collective-permute-done.2.refs_1_ = bf16[192,4736]{1,0:T(8,128)(2,1)S(1)} collective-permute-done((bf16[192,4736]{1,0:T(8,128)(2,1)}, bf16[192,4736]{1,0:T(8,128)(2,1)S(1)}, u32[]{:S(2)}, u32[]{:S(2)}) %collective-permute-start.2) | collective-permute-done | bytes 1818656 | tf_op jit(solution)/shard_map/ppermute | solution.py:451
  48.3 7.2 %shard_map.122 = bf16[4,96,896]{2,1,0:T(8,128)(2,1)} custom-call(bf16[192,4736]{1,0:T(8,128)(2,1)} %collective-permute-done.refs_0_, bf16[192,4736]{1,0:T(8,128)(2,1)S(1)} %collective-permute-done.2.refs_1_, bf16[4736,896]{1,0:T(8,128)(2,1)} %refs_2_.3), custom_call_target="tpu_custom_call" | custom-call | flops 1 | bytes 1 | tf_op jit(solution)/shard_map/pallas_call | solution.py:54
  55.5 5.1 %all-to-all-start.1 = ((bf16[4,96,896]{2,1,0:T(8,128)(2,1)}), bf16[4,96,896]{2,1,0:T(8,128)(2,1)S(1)}, u32[]{:S(2)}, u32[]{:S(2)}) async-start(bf16[4,96,896]{2,1,0:T(8,128)(2,1)} %shard_map.122), calls=%async_computation.1 | async-start | bytes 1376256 | tf_op jit(solution)/shard_map/all_to_all | solution.py:497
  60.6 1.5 %collective-permute-start.4 = (bf16[448,640]{1,0:T(8,128)(2,1)}, bf16[448,640]{1,0:T(8,128)(2,1)S(1)}, u32[]{:S(2)}, u32[]{:S(2)}) collective-permute-start(bf16[448,640]{1,0:T(8,128)(2,1)} %constant_dynamic-slice_fusion), channel_id=1, source_target_pairs={{0,2},{2,0},{1,3},{3,1},{4,6},{6,4},{5,7},{7,5},{8,10},{10,8},{9,1... | collective-permute-start | bytes 1720328 | tf_op jit(solution)/shard_map/ppermute | solution.py:455
  62.2 13.4 %collective-permute-done.4.refs_2_ = bf16[448,640]{1,0:T(8,128)(2,1)S(1)} collective-permute-done((bf16[448,640]{1,0:T(8,128)(2,1)}, bf16[448,640]{1,0:T(8,128)(2,1)S(1)}, u32[]{:S(2)}, u32[]{:S(2)}) %collective-permute-start.4) | collective-permute-done | bytes 573472 | tf_op jit(solution)/shard_map/ppermute | solution.py:455
  75.6 1.5 %collective-permute-start.5 = (bf16[448,640]{1,0:T(8,128)(2,1)S(1)}, bf16[448,640]{1,0:T(8,128)(2,1)S(1)}, u32[]{:S(2)}, u32[]{:S(2)}) collective-permute-start(bf16[448,640]{1,0:T(8,128)(2,1)S(1)} %collective-permute-done.4.refs_2_), channel_id=1, source_target_pairs={{0,16},{16,0},{1,17},{17,1},{2,18},{18,2},{3,19},{19,3},{4,20},{20... | collective-permute-start | bytes 1720328 | tf_op jit(solution)/shard_map/ppermute | solution.py:463
  77.1 7.5 %shard_map.124.refs_10_ = bf16[48,256,1024]{2,1,0:T(8,128)(2,1)S(1)} custom-call(s32[48]{0:T(128)S(1)} %copy-done.2, bf16[48,256,1024]{2,1,0:T(8,128)(2,1)} %kv_hbm.1), custom_call_target="tpu_custom_call" | custom-call | flops 1 | bytes 1 | tf_op jit(solution)/shard_map/pallas_call | solution.py:204
  84.6 8.3 %copy-done = bf16[48,256,1024]{2,1,0:T(8,128)(2,1)} copy-done((bf16[48,256,1024]{2,1,0:T(8,128)(2,1)}, bf16[48,256,1024]{2,1,0:T(8,128)(2,1)S(1)}, u32[]{:S(2)}) %copy-start) | copy-done | bytes 25165848
  93.8 2.8 %collective-permute-start.6 = (bf16[48,896]{1,0:T(8,128)(2,1)S(1)}, bf16[48,896]{1,0:T(8,128)(2,1)S(1)}, u32[]{:S(2)}, u32[]{:S(2)}) collective-permute-start(bf16[48,896]{1,0:T(8,128)(2,1)S(1)} %get-tuple-element.37), channel_id=1, source_target_pairs={{0,1},{1,4},{2,11},{3,14},{4,0},{5,5},{6,10},{7,15},{8,3},{9,6},{1... | collective-permute-start | bytes 258056 | tf_op jit(solution)/shard_map/ppermute | solution.py:505
  96.6 6.5 %collective-permute-start.7 = (bf16[48,896]{1,0:T(8,128)(2,1)S(1)}, bf16[48,896]{1,0:T(8,128)(2,1)S(1)}, u32[]{:S(2)}, u32[]{:S(2)}) collective-permute-start(bf16[48,896]{1,0:T(8,128)(2,1)S(1)} %get-tuple-element.38), channel_id=1, source_target_pairs={{0,2},{1,7},{2,8},{3,13},{4,3},{5,6},{6,9},{7,12},{8,0},{9,5},{10,... | collective-permute-start | bytes 258056 | tf_op jit(solution)/shard_map/ppermute | solution.py:505
  103.1 6.2 %collective-permute-start.8 = (bf16[48,896]{1,0:T(8,128)(2,1)S(1)}, bf16[48,896]{1,0:T(8,128)(2,1)S(1)}, u32[]{:S(2)}, u32[]{:S(2)}) collective-permute-start(bf16[48,896]{1,0:T(8,128)(2,1)S(1)} %get-tuple-element.39), channel_id=1, source_target_pairs={{0,3},{1,6},{2,9},{3,12},{4,2},{5,7},{6,8},{7,13},{8,1},{9,4},{10,... | collective-permute-start | bytes 258056 | tf_op jit(solution)/shard_map/ppermute | solution.py:505
  109.4 3.6 %collective-permute-done.7.refs_2_ = bf16[48,896]{1,0:T(8,128)(2,1)S(1)} collective-permute-done((bf16[48,896]{1,0:T(8,128)(2,1)S(1)}, bf16[48,896]{1,0:T(8,128)(2,1)S(1)}, u32[]{:S(2)}, u32[]{:S(2)}) %collective-permute-start.7) | collective-permute-done | bytes 86048 | tf_op jit(solution)/shard_map/ppermute | solution.py:505
  113.0 2.8 %shard_map.126 = (bf16[192,896]{1,0:T(8,128)(2,1)}, bf16[48,896]{1,0:T(8,128)(2,1)S(1)}, bf16[48,896]{1,0:T(8,128)(2,1)S(1)}, bf16[48,896]{1,0:T(8,128)(2,1)S(1)}, bf16[48,896]{1,0:T(8,128)(2,1)S(1)}) custom-call(s32[3]{0:T(128)S(1)} %pad_add_fusion.here_ref, s32[1,192]{1,0:T(1,128)S(1)} %copy-done.3, bf16[896,896]{1,0:T(8,128)(2,1)} %w_hbm.1, ...), custom_call_target="tpu_custom_call" | custom-call | flops 1 | bytes 1 | tf_op jit(solution)/shard_map/pallas_call | solution.py:149
  115.8 1.1 collective-permute-start.11
  117.1 2.9 %collective-permute-start.13 = (bf16[48,896]{1,0:T(8,128)(2,1)S(1)}, bf16[48,896]{1,0:T(8,128)(2,1)S(1)}, u32[]{:S(2)}, u32[]{:S(2)}) collective-permute-start(bf16[48,896]{1,0:T(8,128)(2,1)S(1)} %get-tuple-element.46), channel_id=1, source_target_pairs={{0,8},{4,12},{8,0},{12,4},{1,9},{5,13},{9,1},{13,5},{2,10},{6,14},... | collective-permute-start | bytes 258056 | tf_op jit(solution)/shard_map/ppermute | solution.py:513
  120.0 1.3 collective-permute-start.14
  121.3 1.4 collective-permute-done.12.refs_7_
  122.7 4.5 %collective-permute-done.13.refs_8_ = bf16[48,896]{1,0:T(8,128)(2,1)S(1)} collective-permute-done((bf16[48,896]{1,0:T(8,128)(2,1)S(1)}, bf16[48,896]{1,0:T(8,128)(2,1)S(1)}, u32[]{:S(2)}, u32[]{:S(2)}) %collective-permute-start.13) | collective-permute-done | bytes 86048 | tf_op jit(solution)/shard_map/ppermute | solution.py:513
  127.2 8.2 %copy-done.1 = bf16[48,256,1024]{2,1,0:T(8,128)(2,1)S(1)} copy-done((bf16[48,256,1024]{2,1,0:T(8,128)(2,1)S(1)}, bf16[48,256,1024]{2,1,0:T(8,128)(2,1)}, u32[]{:S(2)}) %copy-start.1) | copy-done | bytes 25165848
  135.3 9.8 %shard_map.127 = (bf16[48,1024]{1,0:T(8,128)(2,1)}, f32[48,1536]{1,0:T(8,128)}) custom-call(s32[3]{0:T(128)S(1)} %pad_add_fusion.here_ref, s32[48]{0:T(128)S(1)} %copy-done.2, f32[1,896]{1,0:T(1,128)S(1)} %reshape.10.gain, bf16[896,640]{1,0:T(8,128)(2,1)S(1)} %constant_dynamic-update-slice_fusion.refs_0_, bf16[896,640]{1,0:T(8,128)(2,1)} %collective-permute-done.9.refs_1_, ...), custom_call_target="tpu_custom_call" | custom-call | flops 1 | bytes 1 | tf_op jit(solution)/shard_map/pallas_call | solution.py:347
  (39 shorter events, 4.7 us)
Async XLA Ops:
  0.6 4.1 %collective-permute-start.1 = (bf16[192,4736]{1,0:T(8,128)(2,1)}, bf16[192,4736]{1,0:T(8,128)(2,1)S(1)}, u32[]{:S(2)}, u32[]{:S(2)}) collective-permute-start(bf16[192,4736]{1,0:T(8,128)(2,1)} %refs_0_.1), channel_id=1, source_target_pairs={{0,1},{1,0},{2,3},{3,2},{4,5},{5,4},{6,7},{7,6},{8,9},{9,8},{10,11... | collective-permute-start | bytes 5455880 | tf_op jit(solution)/shard_map/ppermute | solution.py:451
  1.1 43.1 %collective-permute-start = (bf16[192,4736]{1,0:T(8,128)(2,1)}, bf16[192,4736]{1,0:T(8,128)(2,1)}, u32[]{:S(2)}, u32[]{:S(2)}) collective-permute-start(bf16[192,4736]{1,0:T(8,128)(2,1)} %refs_0_.1), channel_id=1, source_target_pairs={{0,2},{2,0},{1,3},{3,1},{4,6},{6,4},{5,7},{7,5},{8,10},{10,8},{9,1... | collective-permute-start | bytes 5455880 | tf_op jit(solution)/shard_map/ppermute | solution.py:455
  12.0 6.4 %copy-start.4 = (bf16[896,384]{1,0:T(8,128)(2,1)S(1)}, bf16[896,384]{1,0:T(8,128)(2,1)}, u32[]{:S(2)}) copy-start(bf16[896,384]{1,0:T(8,128)(2,1)} %param.14) | copy-start | bytes 2064388
  12.0 6.5 %copy-start.5 = (bf16[896,128]{1,0:T(8,128)(2,1)S(1)}, bf16[896,128]{1,0:T(8,128)(2,1)}, u32[]{:S(2)}) copy-start(bf16[896,128]{1,0:T(8,128)(2,1)} %param.15) | copy-start | bytes 688132
  12.0 32.3 %all-to-all-start = ((bf16[4,96,896]{2,1,0:T(8,128)(2,1)}), bf16[4,96,896]{2,1,0:T(8,128)(2,1)S(1)}, u32[]{:S(2)}, u32[]{:S(2)}) async-start(bf16[4,96,896]{2,1,0:T(8,128)(2,1)} %shard_map.121), calls=%async_computation | async-start | bytes 1376256 | tf_op jit(solution)/shard_map/all_to_all | solution.py:488
  44.3 4.0 %collective-permute-start.2 = (bf16[192,4736]{1,0:T(8,128)(2,1)}, bf16[192,4736]{1,0:T(8,128)(2,1)S(1)}, u32[]{:S(2)}, u32[]{:S(2)}) collective-permute-start(bf16[192,4736]{1,0:T(8,128)(2,1)} %collective-permute-done.refs_0_), channel_id=1, source_target_pairs={{0,1},{1,0},{2,3},{3,2},{4,5},{5,4},{6,7},{7,6},{8,9},{9,8},{10,11... | collective-permute-start | bytes 5455880 | tf_op jit(solution)/shard_map/ppermute | solution.py:451
  55.5 21.6 %copy-start.2 = (s32[48]{0:T(128)S(1)}, s32[48]{0:T(128)}, u32[]{:S(2)}) copy-start(s32[48]{0:T(128)} %len_ref.2) | copy-start | bytes 580
  55.5 37.4 %all-to-all-start.1 = ((bf16[4,96,896]{2,1,0:T(8,128)(2,1)}), bf16[4,96,896]{2,1,0:T(8,128)(2,1)S(1)}, u32[]{:S(2)}, u32[]{:S(2)}) async-start(bf16[4,96,896]{2,1,0:T(8,128)(2,1)} %shard_map.122), calls=%async_computation.1 | async-start | bytes 1376256 | tf_op jit(solution)/shard_map/all_to_all | solution.py:497
  60.6 15.0 %collective-permute-start.4 = (bf16[448,640]{1,0:T(8,128)(2,1)}, bf16[448,640]{1,0:T(8,128)(2,1)S(1)}, u32[]{:S(2)}, u32[]{:S(2)}) collective-permute-start(bf16[448,640]{1,0:T(8,128)(2,1)} %constant_dynamic-slice_fusion), channel_id=1, source_target_pairs={{0,2},{2,0},{1,3},{3,1},{4,6},{6,4},{5,7},{7,5},{8,10},{10,8},{9,1... | collective-permute-start | bytes 1720328 | tf_op jit(solution)/shard_map/ppermute | solution.py:455
  62.1 57.9 %collective-permute-start.9 = (bf16[896,640]{1,0:T(8,128)(2,1)S(1)}, bf16[896,640]{1,0:T(8,128)(2,1)}, u32[]{:S(2)}, u32[]{:S(2)}) collective-permute-start(bf16[896,640]{1,0:T(8,128)(2,1)S(1)} %constant_dynamic-update-slice_fusion.refs_0_), channel_id=1, source_target_pairs={{0,1},{1,0},{2,3},{3,2},{4,5},{5,4},{6,7},{7,6},{8,9},{9,8},{10,11... | collective-permute-start | bytes 3440648 | tf_op jit(solution)/shard_map/ppermute | solution.py:451
  75.6 33.7 %collective-permute-start.5 = (bf16[448,640]{1,0:T(8,128)(2,1)S(1)}, bf16[448,640]{1,0:T(8,128)(2,1)S(1)}, u32[]{:S(2)}, u32[]{:S(2)}) collective-permute-start(bf16[448,640]{1,0:T(8,128)(2,1)S(1)} %collective-permute-done.4.refs_2_), channel_id=1, source_target_pairs={{0,16},{16,0},{1,17},{17,1},{2,18},{18,2},{3,19},{19,3},{4,20},{20... | collective-permute-start | bytes 1720328 | tf_op jit(solution)/shard_map/ppermute | solution.py:463
  77.1 35.9 %copy-start.3 = (s32[1,192]{1,0:T(1,128)S(1)}, s32[1,192]{1,0:T(1,128)}, u32[]{:S(2)}) copy-start(s32[1,192]{1,0:T(1,128)} %slots.1) | copy-start | bytes 2308
  84.6 8.3 %copy-start = (bf16[48,256,1024]{2,1,0:T(8,128)(2,1)}, bf16[48,256,1024]{2,1,0:T(8,128)(2,1)S(1)}, u32[]{:S(2)}) copy-start(bf16[48,256,1024]{2,1,0:T(8,128)(2,1)S(1)} %shard_map.124.refs_10_) | copy-start | bytes 75497472
  93.1 28.3 %copy-start.7 = (f32[896]{0:T(1024)S(1)}, f32[896]{0:T(1024)}, u32[]{:S(2)}) copy-start(f32[896]{0:T(1024)} %param.13) | copy-start | bytes 10756
  93.1 10.0 %collective-permute-start.3 = (bf16[48,896]{1,0:T(8,128)(2,1)S(1)}, bf16[48,896]{1,0:T(8,128)(2,1)S(1)}, u32[]{:S(2)}, u32[]{:S(2)}) collective-permute-start(bf16[48,896]{1,0:T(8,128)(2,1)S(1)} %get-tuple-element.32), channel_id=1, source_target_pairs={{0,0},{1,5},{2,10},{3,15},{4,1},{5,4},{6,11},{7,14},{8,2},{9,7},{1... | collective-permute-start | bytes 258056 | tf_op jit(solution)/shard_map/ppermute | solution.py:505
  93.8 15.6 %collective-permute-start.6 = (bf16[48,896]{1,0:T(8,128)(2,1)S(1)}, bf16[48,896]{1,0:T(8,128)(2,1)S(1)}, u32[]{:S(2)}, u32[]{:S(2)}) collective-permute-start(bf16[48,896]{1,0:T(8,128)(2,1)S(1)} %get-tuple-element.37), channel_id=1, source_target_pairs={{0,1},{1,4},{2,11},{3,14},{4,0},{5,5},{6,10},{7,15},{8,3},{9,6},{1... | collective-permute-start | bytes 258056 | tf_op jit(solution)/shard_map/ppermute | solution.py:505
  96.6 16.5 %collective-permute-start.7 = (bf16[48,896]{1,0:T(8,128)(2,1)S(1)}, bf16[48,896]{1,0:T(8,128)(2,1)S(1)}, u32[]{:S(2)}, u32[]{:S(2)}) collective-permute-start(bf16[48,896]{1,0:T(8,128)(2,1)S(1)} %get-tuple-element.38), channel_id=1, source_target_pairs={{0,2},{1,7},{2,8},{3,13},{4,3},{5,6},{6,9},{7,12},{8,0},{9,5},{10,... | collective-permute-start | bytes 258056 | tf_op jit(solution)/shard_map/ppermute | solution.py:505
  103.1 10.0 %collective-permute-start.8 = (bf16[48,896]{1,0:T(8,128)(2,1)S(1)}, bf16[48,896]{1,0:T(8,128)(2,1)S(1)}, u32[]{:S(2)}, u32[]{:S(2)}) collective-permute-start(bf16[48,896]{1,0:T(8,128)(2,1)S(1)} %get-tuple-element.39), channel_id=1, source_target_pairs={{0,3},{1,6},{2,9},{3,12},{4,2},{5,7},{6,8},{7,13},{8,1},{9,4},{10,... | collective-permute-start | bytes 258056 | tf_op jit(solution)/shard_map/ppermute | solution.py:505
  109.3 12.0 %collective-permute-start.10 = (bf16[448,640]{1,0:T(8,128)(2,1)S(1)}, bf16[448,640]{1,0:T(8,128)(2,1)S(1)}, u32[]{:S(2)}, u32[]{:S(2)}) collective-permute-start(bf16[448,640]{1,0:T(8,128)(2,1)S(1)} %collective-permute-done.4.refs_2_), channel_id=1, source_target_pairs={{0,1},{1,0},{2,3},{3,2},{4,5},{5,4},{6,7},{7,6},{8,9},{9,8},{10,11... | collective-permute-start | bytes 1720328 | tf_op jit(solution)/shard_map/ppermute | solution.py:451
  115.8 11.4 %collective-permute-start.11 = (bf16[448,640]{1,0:T(8,128)(2,1)S(1)}, bf16[448,640]{1,0:T(8,128)(2,1)S(1)}, u32[]{:S(2)}, u32[]{:S(2)}) collective-permute-start(bf16[448,640]{1,0:T(8,128)(2,1)S(1)} %collective-permute-done.5.refs_3_), channel_id=1, source_target_pairs={{0,1},{1,0},{2,3},{3,2},{4,5},{5,4},{6,7},{7,6},{8,9},{9,8},{10,11... | collective-permute-start | bytes 1720328 | tf_op jit(solution)/shard_map/ppermute | solution.py:451
  116.9 5.8 %collective-permute-start.12 = (bf16[48,896]{1,0:T(8,128)(2,1)S(1)}, bf16[48,896]{1,0:T(8,128)(2,1)S(1)}, u32[]{:S(2)}, u32[]{:S(2)}) collective-permute-start(bf16[48,896]{1,0:T(8,128)(2,1)S(1)} %get-tuple-element.45), channel_id=1, source_target_pairs={{0,4},{4,0},{8,12},{12,8},{1,5},{5,1},{9,13},{13,9},{2,6},{6,2},{1... | collective-permute-start | bytes 258056 | tf_op jit(solution)/shard_map/ppermute | solution.py:513
  117.1 10.0 %collective-permute-start.13 = (bf16[48,896]{1,0:T(8,128)(2,1)S(1)}, bf16[48,896]{1,0:T(8,128)(2,1)S(1)}, u32[]{:S(2)}, u32[]{:S(2)}) collective-permute-start(bf16[48,896]{1,0:T(8,128)(2,1)S(1)} %get-tuple-element.46), channel_id=1, source_target_pairs={{0,8},{4,12},{8,0},{12,4},{1,9},{5,13},{9,1},{13,5},{2,10},{6,14},... | collective-permute-start | bytes 258056 | tf_op jit(solution)/shard_map/ppermute | solution.py:513
  120.0 7.2 %collective-permute-start.14 = (bf16[48,896]{1,0:T(8,128)(2,1)S(1)}, bf16[48,896]{1,0:T(8,128)(2,1)S(1)}, u32[]{:S(2)}, u32[]{:S(2)}) collective-permute-start(bf16[48,896]{1,0:T(8,128)(2,1)S(1)} %get-tuple-element.47), channel_id=1, source_target_pairs={{0,12},{4,8},{8,4},{12,0},{1,13},{5,9},{9,5},{13,1},{2,14},{6,10},... | collective-permute-start | bytes 258056 | tf_op jit(solution)/shard_map/ppermute | solution.py:513
  127.2 8.2 %copy-start.1 = (bf16[48,256,1024]{2,1,0:T(8,128)(2,1)S(1)}, bf16[48,256,1024]{2,1,0:T(8,128)(2,1)}, u32[]{:S(2)}) copy-start(bf16[48,256,1024]{2,1,0:T(8,128)(2,1)} %copy-done) | copy-start | bytes 75497472
  (1 other events, 0.9 us)
